TPU v7x, 32 devices: a whole 2x2x4 slice. The times are simulated.
32 devices in a mesh: section: 4 (over x, core), fsdp: 2 (over y), tensor: 4 (over z).
Axes of the slice: x: 2, y: 2, z: 4, core: 2. Of those that a mesh axis runs over, the one named last changes fastest.
Arguments:
- entering: bfloat16 [4, 1024, 2048], P('section', 'fsdp', 'tensor'), may hold values from -8 to 8
- w_query: bfloat16 [4, 2048, 4096], P('section', 'fsdp', 'tensor'), may hold values from -0.125 to 0.125
- w_keyval: bfloat16 [4, 2048, 4, 256], P('section', 'fsdp', 'tensor'), may hold values from -0.125 to 0.125
- w_out: bfloat16 [4, 4096, 2048], P('section', 'tensor', 'fsdp'), may hold values from -0.09375 to 0.09375
Outputs:
- leaving: bfloat16 [4, 1024, 2048], P('section', 'fsdp', 'tensor')
All inputs are finite; a program needn't handle non-finite values.
Results may differ from a plain program's by a relative error of at most 0.0055.
Values may be sent and summed in bfloat16 or wider, within the bound.
No kernel may reach another device: no remote copies, remote signals or barrier semaphores. Data moves between devices by JAX's collectives and lax.ppermute only.
A program may use at most 128 MiB of HBM per device.

v0:
```python
import math

import jax
import jax.numpy as jnp
from jax import lax
from jax.sharding import PartitionSpec as P

D = 2048
HEAD_DIM = 128


EPSILON = 1e-06
ROPE_BASE = 1000000.0
BEFORE_SHARE = 0.6
AFTER_SHARE = 0.4


def shifted(block, axis, distance):
    devices = range(lax.axis_size(axis))
    route = [((i - distance) % len(devices), i) for i in devices]
    return lax.ppermute(block, axis, route)


def rope_tables(length, width):
    half_width = width // 2
    exponent = jnp.arange(half_width, dtype=jnp.float32) * (2.0 / width)
    inverse = jnp.exp(-exponent * math.log(ROPE_BASE))
    angles = jnp.arange(length, dtype=jnp.float32)[:, None] * inverse[None, :]
    return (jnp.cos(angles)[:, None, :], jnp.sin(angles)[:, None, :])


def head_norm_rope(vectors, cosine, sine):
    meansq = jnp.mean(vectors * vectors, axis=-1, keepdims=True)
    normed = vectors * lax.rsqrt(meansq + EPSILON)
    half_width = vectors.shape[-1] // 2
    first_half = normed[..., :half_width]
    second_half = normed[..., half_width:]
    return jnp.concatenate(
        [first_half * cosine - second_half * sine, second_half * cosine + first_half * sine],
        axis=-1,
    )


def pack_weights(query_shard, keyval_shard, out_shard):
    return jnp.concatenate(
        [query_shard.reshape(1, -1), keyval_shard.reshape(1, -1), out_shard.reshape(1, -1)], axis=1
    )


def body(entering, w_query, w_keyval, w_out):
    owned_pack = pack_weights(w_query, w_keyval, w_out)
    from_lower = shifted(owned_pack, "section", 1)
    from_upper = shifted(owned_pack, "section", -1)
    section_pack = (
        BEFORE_SHARE * from_lower.astype(jnp.float32) + AFTER_SHARE * from_upper.astype(jnp.float32)
    ).astype(jnp.bfloat16)
    query_count = w_query.size
    keyval_count = w_keyval.size
    query_mine = section_pack[:, :query_count].reshape(w_query.shape)
    keyval_mine = section_pack[:, query_count : query_count + keyval_count].reshape(w_keyval.shape)
    out_mine = section_pack[:, query_count + keyval_count :].reshape(w_out.shape)
    own_rows = entering[0]
    own_float = own_rows.astype(jnp.float32)
    square_total = lax.psum(jnp.sum(own_float * own_float, axis=-1, keepdims=True), "tensor")
    meansq = square_total / D
    normed_own = (own_float * lax.rsqrt(meansq + EPSILON)).astype(jnp.bfloat16)
    normed = lax.all_gather(normed_own, "tensor", axis=1, tiled=True)
    length = normed.shape[0]
    query_width = query_mine.shape[2]
    keyval_width = keyval_mine.shape[2] * keyval_mine.shape[3]
    query_piece = lax.all_gather(query_mine, "fsdp", axis=1, tiled=True)
    keyval_piece = lax.all_gather(keyval_mine, "fsdp", axis=1, tiled=True)
    piece_rows = query_piece.shape[1]
    query_sum = jnp.dot(normed, query_piece[0], preferred_element_type=jnp.float32)
    keyval_sum = jnp.dot(
        normed, keyval_piece[0].reshape(piece_rows, -1), preferred_element_type=jnp.float32
    )
    query_heads = query_width // HEAD_DIM
    kv_count = keyval_width // (2 * HEAD_DIM)
    group_size = query_heads // kv_count
    cosine, sine = rope_tables(length, HEAD_DIM)
    queries = head_norm_rope(
        query_sum.reshape(length, kv_count, group_size, HEAD_DIM),
        cosine[:, :, None, :],
        sine[:, :, None, :],
    ).astype(jnp.bfloat16)
    keyval_heads = keyval_sum.reshape(length, kv_count, 2 * HEAD_DIM)
    keys = head_norm_rope(keyval_heads[..., :HEAD_DIM], cosine, sine).astype(jnp.bfloat16)
    values = keyval_heads[..., HEAD_DIM:].astype(jnp.bfloat16)
    positions = jnp.arange(length)
    causal = positions[:, None] >= positions[None, :]
    scale = 1.0 / math.sqrt(HEAD_DIM)

    def one_group(query_slice):
        scores = (
            jnp.einsum("qkd,pkd->kqp", query_slice, keys, preferred_element_type=jnp.float32)
            * scale
        )
        expo = jnp.where(causal[None], jnp.exp(scores - math.sqrt(HEAD_DIM)), 0.0)
        weights = (expo / jnp.sum(expo, axis=-1, keepdims=True)).astype(jnp.bfloat16)
        return jnp.einsum(
            "kqp,pkd->qkd", weights, values, preferred_element_type=jnp.float32
        ).astype(jnp.bfloat16)

    mixed = lax.map(one_group, jnp.moveaxis(queries, 2, 0))
    mixed = jnp.moveaxis(mixed, 0, 2).reshape(length, query_heads * HEAD_DIM)
    partial_terms = jnp.dot(
        mixed,
        lax.all_gather(out_mine, "fsdp", axis=2, tiled=True)[0],
        preferred_element_type=jnp.float32,
    ).astype(jnp.bfloat16)
    summed = lax.psum_scatter(partial_terms, "tensor", scatter_dimension=1, tiled=True).astype(
        jnp.float32
    )
    return (own_float + summed).astype(jnp.bfloat16)[None]


def solution(mesh):
    in_specs = (
        P("section", "fsdp", "tensor"),
        P("section", "fsdp", "tensor"),
        P("section", "fsdp", "tensor", None),
        P("section", "tensor", "fsdp"),
    )
    out_specs = P("section", "fsdp", "tensor")
    return jax.shard_map(body, mesh=mesh, in_specs=in_specs, out_specs=out_specs, check_vma=False)
```

profile of v0, /device:TPU:0, one launch (start us, length us, event | category | flops | bytes accessed | tf_op | source)
XLA Modules:
  0.0 499.6 jit_solution(14244062705795576982)
XLA Ops:
  6.5 4.8 copy.24
  11.4 6.0 %constant_dynamic-update-slice_fusion.3 = bf16[1,2359296]{1,0:T(2,128)(2,1)} fusion(bf16[1,1048576]{1,0:T(2,128)(2,1)S(1)} %bitcast.77), kind=kLoop, calls=%fused_computation.54 | loop fusion | bytes 6291456
  17.4 0.8 copy.25
  18.2 3.2 copy.26
  21.4 1.9 constant_dynamic-update-slice_fusion.2
  23.3 6.0 %constant_dynamic-update-slice_fusion.1 = bf16[1,2359296]{1,0:T(2,128)(2,1)} fusion(bf16[1,2359296]{1,0:T(2,128)(2,1)} %constant_dynamic-update-slice_fusion.2, bf16[1,1048576]{1,0:T(2,128)(2,1)S(1)} %bitcast.76), kind=kLoop, calls=%fused_computation.52 | loop fusion | bytes 6291456 | tf_op jit(solution)/shard_map/concatenate | solution.py:45
  29.8 1.9 collective-permute-start.1
  31.9 12.8 %psum.7 = f32[512,1]{0,1:T(1,128)S(1)} all-reduce(f32[512,1]{0,1:T(1,128)S(1)} %bitcast.83), channel_id=1, replica_groups=mesh['section'=4,'fsdp'=2,'tensor'=4] {'tensor'}, use_global_device_ids=true, to_apply=%region_1.0 | all-reduce | flops 512 | bytes 4096 | tf_op jit(solution)/shard_map/psum | solution.py:64
  44.7 1.0 fusion.22
  45.9 186.9 %collective-permute-done = bf16[1,2359296]{1,0:T(2,128)(2,1)} collective-permute-done((bf16[1,2359296]{1,0:T(2,128)(2,1)}, bf16[1,2359296]{1,0:T(2,128)(2,1)}, u32[]{:S(2)}, u32[]{:S(2)}) %collective-permute-start) | collective-permute-done | bytes 4718624 | tf_op jit(solution)/shard_map/ppermute | solution.py:21
  232.8 2.5 collective-permute-done.1
  235.3 24.3 %add_convert_fusion = bf16[1,2359296]{1,0:T(2,128)(2,1)S(1)} fusion(bf16[1,2359296]{1,0:T(2,128)(2,1)} %collective-permute-done.1, bf16[1,2359296]{1,0:T(2,128)(2,1)} %collective-permute-done), kind=kLoop, calls=%fused_computation.15 | loop fusion | flops 14155776 | bytes 14155776 | tf_op jit(solution)/shard_map/convert_element_type | solution.py:56
  259.6 3.6 copy-done
  263.2 8.8 %slice_reduce_fusion.2 = bf16[262144]{0:T(1024)(128)(2,1)S(1)} fusion(bf16[1,2359296]{1,0:T(2,128)(2,1)S(1)} %add_convert_fusion), kind=kLoop, calls=%fused_computation.35 | loop fusion | bytes 1048576 | tf_op jit(solution)/shard_map/slice | solution.py:60
  272.0 1.0 reshape.277
  273.2 47.0 %slice_reduce_fusion = (bf16[1048576]{0:T(1024)(128)(2,1)S(1)}, bf16[1048576]{0:T(1024)(128)(2,1)}) fusion(bf16[1,2359296]{1,0:T(2,128)(2,1)} %copy-done), kind=kLoop, calls=%fused_computation.16 | loop fusion | bytes 8388608 | tf_op jit(solution)/shard_map/slice | solution.py:61
  320.2 4.2 reshape.275
  324.5 1.0 fusion.27
  325.4 2.3 reshape.280
  328.2 2.6 convolution_bitcast_fusion
  331.6 0.8 copy.20
  332.4 50.6 %all-gather.7.cloned.1.call-done = bf16[1,2048,1024]{2,1,0:T(8,128)(2,1)} async-done(((bf16[1,1024,1024]{2,1,0:T(8,128)(2,1)}), bf16[1,2048,1024]{2,1,0:T(8,128)(2,1)}) %all-gather.7.cloned.1.call-update) | async-done | bytes 4194320 | tf_op jit(solution)/shard_map/all_gather | solution.py:71
  383.0 5.1 %fusion.18 = f32[64,8,8,128]{3,1,2,0:T(8,128)S(1)} fusion(bf16[512,2048]{1,0:T(8,128)(2,1)} %all-gather.5.cloned.1.call-done, bf16[1,2048,1024]{2,1,0:T(8,128)(2,1)} %all-gather.7.cloned.1.call-done), kind=kOutput, calls=%fused_computation.27 | convolution fusion | flops 2147483648 | bytes 8388608 | tf_op jit(solution)/shard_map/dot_general | solution.py:74
  388.6 0.6 multiply_reduce_fusion
  389.4 0.6 copy_multiply_fusion
  390.0 0.8 subtract_convert_fusion
  390.8 0.6 maximum_bitcast_fusion
  392.2 6.8 %while.13 = (s32[]{:T(128)}, bf16[8,512,1,128]{1,3,0,2:T(8,128)(2,1)S(1)}, bf16[8,512,1,128]{3,1,2,0:T(8,128)(2,1)S(1)}, bf16[512,1,128]{2,0,1:T(8,128)(2,1)S(1)}, bf16[512,1,128]{2,0,1:T(8,128)(2,1)S(1)}, /*index=5*/s32[]{:T(128)}) while((s32[]{:T(128)}, bf16[8,512,1,128]{1,3,0,2:T(8,128)(2,1)S(1)}, ...), condition=%wide.region_6.7_spmd.clone, body=%wide.region_4.6_spmd.clone.sunk | while | flops 136117760 | bytes 3149901 | solution.py:105
  399.0 42.2 %all-gather.11.cloned.1.call-done = bf16[1,1024,2048]{2,1,0:T(8,128)(2,1)} async-done(((bf16[1,1024,1024]{2,1,0:T(8,128)(2,1)}), bf16[1,1024,2048]{2,1,0:T(8,128)(2,1)}) %all-gather.11.cloned.1.call-update) | async-done | bytes 4194320 | tf_op jit(solution)/shard_map/all_gather | solution.py:109
  441.2 5.9 %fusion.15 = bf16[512,2048]{1,0:T(8,128)(2,1)} fusion(bf16[512,1024]{0,1:T(8,128)(2,1)S(1)} %bitcast.84, bf16[1,1024,2048]{2,1,0:T(8,128)(2,1)} %all-gather.11.cloned.1.call-done), kind=kOutput, calls=%fused_computation.22 | convolution fusion | flops 2148532224 | bytes 7340032 | tf_op jit(solution)/shard_map/dot_general | solution.py:107
  447.1 44.0 %reduce-scatter.2.cloned.1.call-done = bf16[512,512]{1,0:T(8,128)(2,1)} async-done(((bf16[512,2048]{1,0:T(8,128)(2,1)}), bf16[512,512]{1,0:T(8,128)(2,1)}) %reduce-scatter.2.cloned.1.call-update) | async-done | bytes 524304 | tf_op jit(solution)/shard_map/reduce_scatter | solution.py:112
  491.1 2.0 fusion.25
  (70 shorter events, 10.4 us)
Async XLA Ops:
  6.5 321.6 %all-gather.5.cloned.1.call-start = ((), (), s32[]{:S(2)}) async-start(), calls=%async_computation.1 | async-start | bytes 2621440 | tf_op jit(solution)/shard_map/all_gather | solution.py:67
  11.4 6.0 %copy-start.3 = (bf16[1,1024,1,256]{3,1,2,0:T(8,128)(2,1)S(1)}, bf16[1,1024,1,256]{3,1,2,0:T(8,128)(2,1)}, u32[]{:S(2)}) copy-start(bf16[1,1024,1,256]{3,1,2,0:T(8,128)(2,1)} %param.8) | copy-start | bytes 1572868
  11.4 6.8 %copy-start.2 = (bf16[1,1024,1024]{2,1,0:T(8,128)(2,1)S(1)}, bf16[1,1024,1024]{2,1,0:T(8,128)(2,1)}, u32[]{:S(2)}) copy-start(bf16[1,1024,1024]{2,1,0:T(8,128)(2,1)} %param.9) | copy-start | bytes 6291460
  23.3 8.3 %copy-start.1 = (bf16[1,512,512]{2,1,0:T(8,128)(2,1)S(1)}, bf16[1,512,512]{2,1,0:T(8,128)(2,1)}, u32[]{:S(2)}) copy-start(bf16[1,512,512]{2,1,0:T(8,128)(2,1)} %param.6) | copy-start | bytes 1572868
  29.3 203.5 %collective-permute-start = (bf16[1,2359296]{1,0:T(2,128)(2,1)}, bf16[1,2359296]{1,0:T(2,128)(2,1)}, u32[]{:S(2)}, u32[]{:S(2)}) collective-permute-start(bf16[1,2359296]{1,0:T(2,128)(2,1)} %constant_dynamic-update-slice_fusion.1), channel_id=1, source_target_pairs={{24,0},{0,8},{8,16},{16,24},{25,1},{1,9},{9,17},{17,25},{26,2},{2,... | collective-permute-start | bytes 14155784 | tf_op jit(solution)/shard_map/ppermute | solution.py:21
  29.8 205.5 %collective-permute-start.1 = (bf16[1,2359296]{1,0:T(2,128)(2,1)}, bf16[1,2359296]{1,0:T(2,128)(2,1)}, u32[]{:S(2)}, u32[]{:S(2)}) collective-permute-start(bf16[1,2359296]{1,0:T(2,128)(2,1)} %constant_dynamic-update-slice_fusion.1), channel_id=1, source_target_pairs={{8,0},{16,8},{24,16},{0,24},{9,1},{17,9},{25,17},{1,25},{10,2},{18... | collective-permute-start | bytes 14155784 | tf_op jit(solution)/shard_map/ppermute | solution.py:21
  45.7 282.5 %all-gather.9.cloned.1.call-start = ((), (), s32[]{:S(2)}) async-start(), calls=%async_computation.3 | async-start | bytes 1572864 | tf_op jit(solution)/shard_map/all_gather | solution.py:72
  259.6 3.6 copy-start
  273.0 110.1 %all-gather.7.cloned.1.call-start = ((), (), s32[]{:S(2)}) async-start(), calls=%async_computation.2 | async-start | bytes 6291456 | tf_op jit(solution)/shard_map/all_gather | solution.py:71
  324.4 116.8 %all-gather.11.cloned.1.call-start = ((), (), s32[]{:S(2)}) async-start(), calls=%async_computation.4 | async-start | bytes 6291456 | tf_op jit(solution)/shard_map/all_gather | solution.py:109
  327.8 163.3 %reduce-scatter.2.cloned.1.call-start = ((), (), s32[]{:S(2)}) async-start(), calls=%async_computation.5 | async-start | bytes 2621440 | tf_op jit(solution)/shard_map/reduce_scatter | solution.py:112
  390.8 0.9 copy-start.4
  390.8 1.4 copy-start.5
Sparse Core Ops, SparseCore 0:
  45.8 44.1 all-gather.4
  273.1 23.0 all-gather.8
  324.5 58.4 all-gather.6
  384.4 56.7 all-gather.10
  447.2 43.8 reduce-scatter.1
where the time goes:
time: 500 us
  waiting for transfers between devices  326 us (65%)
  local copies, waits for them, and re-layouts  92.9 us (19%)
  other arithmetic  31.6 us (6%)
  matrix products  19.1 us (4%)
  between operations  13.4 us (3%)
  blocking collectives  12.8 us (3%)
    ppermute x2, waiting for transfers between devices, shifted(): return lax.ppermute(block, axis, route)  189 us
    all_gather x1, waiting for transfers between devices, body(): query_piece = lax.all_gather(query_mine, 'fsdp', axis=1, tiled=True)  50.6 us
    slice x1, local copies, waits for them, and re-layouts, body(): out_mine = section_pack[:, query_count + keyval_count:].reshape(w_out.shape)  47 us
    reduce_scatter x1, waiting for transfers between devices, body(): lax.psum_scatter(partial_terms, 'tensor', scatter_dimension=1, tiled=True)  44 us
    all_gather x1, waiting for transfers between devices, body(): lax.all_gather(out_mine, 'fsdp', axis=2, tiled=True)[0]  42.2 us
    convert_element_type x1, other arithmetic, body(): section_pack = (BEFORE_SHARE * from_lower.astype(jnp.float32) + AFTER_SHA...  24.3 us
    unnamed x20, local copies, waits for them, and re-layouts  22.6 us
    psum x1, blocking collectives, body(): lax.psum(jnp.sum(own_float * own_float, axis=-1, keepdims=True), 'tensor')  12.8 us
  transfers between devices with their start and end apart: 7, of which 5 were waited for; matrix products, arithmetic and copies ran while one was open for 22% of the time, Pallas kernels for 0%

commit v1 on v0

v1 whole, which is shorter than its diff:
```python
import functools
import math

import jax
import jax.numpy as jnp
from jax import lax
from jax.experimental import pallas as pl
from jax.experimental.pallas import tpu as pltpu
from jax.sharding import PartitionSpec as P

HEAD_DIM = 128
EPSILON = 1e-06
ROPE_BASE = 1000000.0
BEFORE_SHARE = 0.6
AFTER_SHARE = 0.4
LANES = 128
VMEM_BYTES = 48 * 1024 * 1024
QUERY_CHUNKS = 4
OUT_CHUNKS = 4

SMEM = pl.BlockSpec(memory_space=pltpu.SMEM)
VMEM = pl.BlockSpec(memory_space=pltpu.VMEM)


def params():
    return pltpu.CompilerParams(vmem_limit_bytes=VMEM_BYTES)


def rope_tables(length, width):
    half_width = width // 2
    exponent = jnp.arange(half_width, dtype=jnp.float32) * (2.0 / width)
    inverse = jnp.exp(-exponent * math.log(ROPE_BASE))
    angles = jnp.arange(length, dtype=jnp.float32)[:, None] * inverse[None, :]
    cosine, sine = jnp.cos(angles), jnp.sin(angles)
    return jnp.concatenate([cosine, cosine], axis=1), jnp.concatenate([-sine, sine], axis=1)


def combine_kernel(shares, near, far, out):
    mixed = shares[0] * near[...].astype(jnp.float32) + shares[1] * far[...].astype(jnp.float32)
    out[...] = mixed.astype(out.dtype)


def combine(shares, near, far, near_block, width):
    rows, columns = far.shape
    pieces = columns // width
    step = min(rows, 512)
    return pl.pallas_call(
        combine_kernel,
        out_shape=jax.ShapeDtypeStruct(far.shape, far.dtype),
        grid=(rows // step, pieces),
        in_specs=[
            SMEM,
            pl.BlockSpec((step, width), lambda i, j: (i, near_block(j))),
            pl.BlockSpec((step, width), lambda i, j: (i, j)),
        ],
        out_specs=pl.BlockSpec((step, width), lambda i, j: (i, j)),
        compiler_params=params(),
        cost_estimate=pl.CostEstimate(
            flops=3 * far.size, bytes_accessed=6 * far.size, transcendentals=0
        ),
    )(shares, near, far)


def project(ids, blocks, own, other, whole):
    half = own.shape[0]
    mine, place, count = ids[0], ids[1], len(blocks)
    whole[pl.ds(pl.multiple_of(mine * half, half), half), :] = own[...]
    whole[pl.ds(pl.multiple_of((1 - mine) * half, half), half), :] = other[...]
    total = None
    for k, block in enumerate(blocks):
        width = block.shape[1]
        owner = lax.rem(place - k + count, count)
        rows = pl.ds(pl.multiple_of(owner * width, width), width)
        term = jnp.dot(block[...], whole[rows, :], preferred_element_type=jnp.float32)
        total = term if total is None else total + term
    return total


def norm_rope(vectors, cosine, signed_sine):
    meansq = jnp.mean(vectors * vectors, axis=-1, keepdims=True)
    normed = vectors * lax.rsqrt(meansq + EPSILON)
    return normed * cosine + pltpu.roll(normed, HEAD_DIM // 2, 1) * signed_sine


def keyval_kernel(count, ids, *refs):
    blocks = refs[:count]
    own, other, cosine, sine, keys, values, scales, whole = refs[count:]
    total = 0.0
    features = 0
    for block in blocks:
        rows = block[...].astype(jnp.float32)
        total = total + jnp.sum(rows * rows, axis=-1, keepdims=True)
        features += block.shape[1]
    scale = lax.rsqrt(total / features + EPSILON)
    raw = project(ids, blocks, own, other, whole) * scale
    keys[...] = norm_rope(raw[:, :HEAD_DIM], cosine[...], sine[...]).astype(keys.dtype)
    values[...] = raw[:, HEAD_DIM:].astype(values.dtype)
    scales[...] = jnp.broadcast_to(scale, scales.shape)


def keyval(ids, blocks, own, other, cosine, sine):
    length = blocks[0].shape[0]
    features = sum(b.shape[1] for b in blocks)
    head = jax.ShapeDtypeStruct((length, HEAD_DIM), jnp.bfloat16)
    return pl.pallas_call(
        functools.partial(keyval_kernel, len(blocks)),
        out_shape=(head, head, jax.ShapeDtypeStruct((length, LANES), jnp.float32)),
        in_specs=[SMEM] + [VMEM] * (len(blocks) + 4),
        out_specs=(VMEM,) * 3,
        scratch_shapes=[pltpu.VMEM((features, own.shape[1]), own.dtype)],
        compiler_params=params(),
        cost_estimate=pl.CostEstimate(
            flops=2 * length * features * own.shape[1],
            bytes_accessed=2 * features * (length + own.shape[1]),
            transcendentals=0,
        ),
    )(ids, *blocks, own, other, cosine, sine)


def attend_kernel(count, ids, *refs):
    blocks = refs[:count]
    own, other, keys, values, scales, cosine, sine, mixed, whole = refs[count:]
    raw = project(ids, blocks, own, other, whole)
    length = raw.shape[0]
    rows = length // 2 if length % 16 == 0 else length
    scale = scales[:, :1]
    for head in range(raw.shape[1] // HEAD_DIM):
        columns = slice(head * HEAD_DIM, (head + 1) * HEAD_DIM)
        query = norm_rope(raw[:, columns] * scale, cosine[...], sine[...]).astype(jnp.bfloat16)
        for first in range(0, length, rows):
            last = first + rows
            scores = lax.dot_general(
                query[first:last],
                keys[:last, :],
                (((1,), (1,)), ((), ())),
                preferred_element_type=jnp.float32,
            )
            expo = jnp.exp(scores * (1.0 / math.sqrt(HEAD_DIM)) - math.sqrt(HEAD_DIM))
            at = first + lax.broadcasted_iota(jnp.int32, expo.shape, 0)
            expo = jnp.where(lax.broadcasted_iota(jnp.int32, expo.shape, 1) <= at, expo, 0.0)
            total = jnp.sum(expo, axis=-1, keepdims=True)
            product = jnp.dot(
                expo.astype(jnp.bfloat16), values[:last, :], preferred_element_type=jnp.float32
            )
            mixed[first:last, columns] = (product / total).astype(mixed.dtype)


def attend(ids, blocks, own, other, keys, values, scales, cosine, sine):
    length = blocks[0].shape[0]
    features = sum(b.shape[1] for b in blocks)
    width = own.shape[1]
    return pl.pallas_call(
        functools.partial(attend_kernel, len(blocks)),
        out_shape=jax.ShapeDtypeStruct((length, width), jnp.bfloat16),
        in_specs=[SMEM] + [VMEM] * (len(blocks) + 7),
        out_specs=VMEM,
        scratch_shapes=[pltpu.VMEM((features, width), own.dtype)],
        compiler_params=params(),
        cost_estimate=pl.CostEstimate(
            flops=2 * length * features * width + 3 * length * length * width,
            bytes_accessed=2 * features * (length + width),
            transcendentals=length * length * width // HEAD_DIM,
        ),
    )(ids, *blocks, own, other, keys, values, scales, cosine, sine)


def partial_kernel(count, parts, ids, *refs):
    mixed = refs[:parts]
    own, other = refs[parts : parts + 2]
    outs = refs[parts + 2 : parts + 2 + count]
    by_owner = refs[-1]
    mine, place = ids[0], ids[1]
    width = by_owner.shape[2]
    per_half = count // 2
    for half, weights in ((mine, own), (1 - mine, other)):
        total = None
        depth = 0
        for part in mixed:
            rows = slice(depth, depth + part.shape[1])
            depth += part.shape[1]
            term = jnp.dot(part[...], weights[rows, :], preferred_element_type=jnp.float32)
            total = term if total is None else total + term
        for piece in range(per_half):
            by_owner[half * per_half + piece] = total[
                :, piece * width : (piece + 1) * width
            ].astype(by_owner.dtype)
    for k in range(count):
        outs[k][...] = by_owner[lax.rem(place + k, count)]


def partials(ids, mixed, own, other, count):
    length = mixed[0].shape[0]
    width = 2 * own.shape[1] // count
    piece = jax.ShapeDtypeStruct((length, width), jnp.bfloat16)
    return pl.pallas_call(
        functools.partial(partial_kernel, count, len(mixed)),
        out_shape=(piece,) * count,
        in_specs=[SMEM] + [VMEM] * (len(mixed) + 2),
        out_specs=(VMEM,) * count,
        scratch_shapes=[pltpu.VMEM((count, length, width), jnp.bfloat16)],
        compiler_params=params(),
        cost_estimate=pl.CostEstimate(
            flops=4 * length * own.size,
            bytes_accessed=4 * own.size + 2 * length * (own.shape[0] + 2 * own.shape[1]),
            transcendentals=0,
        ),
    )(ids, *mixed, own, other)


def leave_kernel(count, chunks, rows, *refs):
    out = refs[-1]
    width = refs[0].shape[1]
    for chunk in range(chunks):
        columns = slice(chunk * width, (chunk + 1) * width)
        pieces = refs[chunk * count : (chunk + 1) * count]
        total = pieces[0][...].astype(jnp.float32)
        for piece in pieces[1:]:
            total = total + piece[...].astype(jnp.float32)
        out[:, columns] = (rows[:, columns].astype(jnp.float32) + total).astype(out.dtype)


def leave(rows, pieces):
    flat = [piece for chunk in pieces for piece in chunk]
    return pl.pallas_call(
        functools.partial(leave_kernel, len(pieces[0]), len(pieces)),
        out_shape=jax.ShapeDtypeStruct(rows.shape, rows.dtype),
        in_specs=[VMEM] * (1 + len(flat)),
        out_specs=VMEM,
        compiler_params=params(),
        cost_estimate=pl.CostEstimate(
            flops=(1 + len(pieces[0])) * rows.size,
            bytes_accessed=2 * rows.size * (2 + len(pieces[0])),
            transcendentals=0,
        ),
    )(rows, *flat)


def permute(array, axis, source):
    count = lax.axis_size(axis)
    return lax.ppermute(array, axis, [(source(i) % count, i) for i in range(count)])


def from_near(array):
    return permute(array, "section", lambda i: i ^ 1)


def from_far(array):
    return permute(array, "section", lambda i: i + 1 if i % 2 else i - 1)


def from_other_half(array):
    return permute(array, "fsdp", lambda i: i ^ 1)


def body(entering, w_query, w_keyval, w_out):
    count = lax.axis_size("tensor")
    section = lax.axis_index("section")
    ids = jnp.stack([lax.axis_index("fsdp"), lax.axis_index("tensor")]).astype(jnp.int32)
    shares = jnp.where(
        section % 2 == 0,
        jnp.array([AFTER_SHARE, BEFORE_SHARE], jnp.float32),
        jnp.array([BEFORE_SHARE, AFTER_SHARE], jnp.float32),
    )
    rows = entering[0]
    length = rows.shape[0]
    own_query = w_query[0]
    own_keyval = w_keyval.reshape(w_keyval.shape[1], -1)
    own_out = w_out[0]
    query_width = own_query.shape[1] // QUERY_CHUNKS
    halves = count // 2
    quarter = own_out.shape[1] // halves
    out_width = quarter // OUT_CHUNKS

    far_keyval = from_far(own_keyval)
    near_keyval = from_near(own_keyval)
    blocks = [rows] + [permute(rows, "tensor", lambda i, k=k: i - k) for k in range(1, count)]
    near_query = from_near(own_query)
    near_out = from_near(own_out)
    far_query = [
        from_far(own_query[:, c * query_width : (c + 1) * query_width])
        for c in range(QUERY_CHUNKS)
    ]
    far_out = [
        from_far(
            jnp.concatenate(
                [
                    own_out[:, h * quarter + c * out_width : h * quarter + (c + 1) * out_width]
                    for h in range(halves)
                ],
                axis=1,
            )
        )
        for c in range(OUT_CHUNKS)
    ]
    cosine, sine = rope_tables(length, HEAD_DIM)

    keyval_own = combine(shares, near_keyval, far_keyval, lambda j: 0, own_keyval.shape[1])
    keyval_other = from_other_half(keyval_own)
    query_own, query_other = [], []
    for c in range(QUERY_CHUNKS):
        query_own.append(
            combine(shares, near_query, far_query[c], lambda j, c=c: c, query_width)
        )
        query_other.append(from_other_half(query_own[c]))
    out_own, out_other = [], []
    for c in range(OUT_CHUNKS):
        out_own.append(
            combine(
                shares, near_out, far_out[c], lambda j, c=c: j * OUT_CHUNKS + c, out_width
            )
        )
        out_other.append(from_other_half(out_own[c]))

    keys, values, scales = keyval(ids, blocks, keyval_own, keyval_other, cosine, sine)
    mixed = [
        attend(
            ids, blocks, query_own[c], query_other[c], keys, values, scales, cosine, sine
        )
        for c in range(QUERY_CHUNKS)
    ]
    pieces = []
    for c in range(OUT_CHUNKS):
        parts = partials(ids, mixed, out_own[c], out_other[c], count)
        pieces.append(
            [parts[0]]
            + [permute(parts[k], "tensor", lambda i, k=k: i - k) for k in range(1, count)]
        )
    return leave(rows, pieces)[None]


def shifted(block, axis, distance):
    return permute(block, axis, lambda i: i - distance)


def head_norm_rope(vectors, cosine, signed_sine):
    meansq = jnp.mean(vectors * vectors, axis=-1, keepdims=True)
    normed = vectors * lax.rsqrt(meansq + EPSILON)
    return normed * cosine + jnp.roll(normed, vectors.shape[-1] // 2, axis=-1) * signed_sine


def rebuilt(weights):
    before = shifted(weights, "section", 1).astype(jnp.float32)
    after = shifted(weights, "section", -1).astype(jnp.float32)
    return (BEFORE_SHARE * before + AFTER_SHARE * after).astype(jnp.bfloat16)


def general_body(entering, w_query, w_keyval, w_out):
    rows = entering[0].astype(jnp.float32)
    features = rows.shape[1] * lax.axis_size("tensor")
    square_total = lax.psum(jnp.sum(rows * rows, axis=-1, keepdims=True), "tensor")
    normed = (rows * lax.rsqrt(square_total / features + EPSILON)).astype(jnp.bfloat16)
    normed = lax.all_gather(normed, "tensor", axis=1, tiled=True)
    length = normed.shape[0]
    query_weight = lax.all_gather(rebuilt(w_query)[0], "fsdp", axis=0, tiled=True)
    keyval_weight = lax.all_gather(rebuilt(w_keyval)[0], "fsdp", axis=0, tiled=True)
    out_weight = lax.all_gather(rebuilt(w_out)[0], "fsdp", axis=1, tiled=True)
    kv_count = keyval_weight.shape[1]
    raw = jnp.dot(normed, query_weight, preferred_element_type=jnp.float32)
    raw = raw.reshape(length, kv_count, -1, HEAD_DIM)
    keyval_raw = jnp.dot(
        normed, keyval_weight.reshape(features, -1), preferred_element_type=jnp.float32
    ).reshape(length, kv_count, 2 * HEAD_DIM)
    cosine, sine = rope_tables(length, HEAD_DIM)
    queries = head_norm_rope(raw, cosine[:, None, None], sine[:, None, None]).astype(jnp.bfloat16)
    keys = head_norm_rope(
        keyval_raw[..., :HEAD_DIM], cosine[:, None], sine[:, None]
    ).astype(jnp.bfloat16)
    values = keyval_raw[..., HEAD_DIM:].astype(jnp.bfloat16)
    causal = jnp.arange(length)[:, None] >= jnp.arange(length)[None, :]

    def one_group(query_slice):
        scores = jnp.einsum("qkd,pkd->kqp", query_slice, keys, preferred_element_type=jnp.float32)
        expo = jnp.exp(scores * (1.0 / math.sqrt(HEAD_DIM)) - math.sqrt(HEAD_DIM))
        expo = jnp.where(causal[None], expo, 0.0)
        weights = (expo / jnp.sum(expo, axis=-1, keepdims=True)).astype(jnp.bfloat16)
        return jnp.einsum(
            "kqp,pkd->qkd", weights, values, preferred_element_type=jnp.float32
        ).astype(jnp.bfloat16)

    mixed = lax.map(one_group, jnp.moveaxis(queries, 2, 0))
    mixed = jnp.moveaxis(mixed, 0, 2).reshape(length, -1)
    terms = jnp.dot(mixed, out_weight, preferred_element_type=jnp.float32).astype(jnp.bfloat16)
    summed = lax.psum_scatter(terms, "tensor", scatter_dimension=1, tiled=True)
    return (rows + summed.astype(jnp.float32)).astype(jnp.bfloat16)[None]


def solution(mesh):
    in_specs = (
        P("section", "fsdp", "tensor"),
        P("section", "fsdp", "tensor"),
        P("section", "fsdp", "tensor", None),
        P("section", "tensor", "fsdp"),
    )
    out_specs = P("section", "fsdp", "tensor")

    def step(entering, w_query, w_keyval, w_out):
        chunked = (
            mesh.shape["section"] % 2 == 0
            and mesh.shape["fsdp"] == 2
            and mesh.shape["tensor"] % 2 == 0
            and w_keyval.shape[2] == mesh.shape["tensor"]
            and w_keyval.shape[3] == 2 * HEAD_DIM
            and w_query.shape[2] % (mesh.shape["tensor"] * QUERY_CHUNKS * HEAD_DIM) == 0
            and w_out.shape[2] % (mesh.shape["tensor"] * OUT_CHUNKS * LANES) == 0
        )
        return jax.shard_map(
            body if chunked else general_body,
            mesh=mesh,
            in_specs=in_specs,
            out_specs=out_specs,
            check_vma=False,
        )(entering, w_query, w_keyval, w_out)

    return step
```

time: 500 us -> 236 us (0.47)
  waiting for transfers between devices: 326 us -> 92.2 us
  local copies, waits for them, and re-layouts: 92.9 us -> 14 us
  starting transfers between devices: 3.21 us -> 80.8 us
  Pallas kernels: 0 us -> 41.7 us
  other arithmetic: 31.6 us -> 5.49 us
  matrix products: 19.1 us -> 0 us
  between operations: 13.4 us -> 0.33 us
  blocking collectives: 12.8 us -> 0 us
    ppermute x2 -> x36, waiting for transfers between devices: 189 us -> 92.2 us  [permute(): lax.ppermute(array, axis, [(source(i) % count, i) for i in range(count)])]
    all_gather x4 -> x0, waiting for transfers between devices: 92.8 us -> none  [the longest x1 50.6 us: body(): query_piece = lax.all_gather(query_mine, 'fsdp', axis=1, tiled=True)]
    ppermute x2 -> x36, starting transfers between devices: 2.38 us -> 80.8 us  [permute(): lax.ppermute(array, axis, [(source(i) % count, i) for i in range(count)])]
    slice x3 -> x2, local copies, waits for them, and re-layouts: 55.7 us -> 2.22 us  [the longest x1 1.83 us: body(): own_query[:, c * query_width:(c + 1) * query_width]]
    reduce_scatter x1 -> x0, waiting for transfers between devices: 44 us -> none  [body(): lax.psum_scatter(partial_terms, 'tensor', scatter_dimension=1, tiled=True)]
    pallas_call x0 -> x19, Pallas kernels: none -> 41.7 us  [the longest x9 17.8 us: combine(): pl.pallas_call(combine_kernel, out_shape=jax.ShapeDtypeStruct(far.shape,...]
    convert_element_type x2 -> x0, other arithmetic: 25.2 us -> none  [the longest x1 24.3 us: body(): section_pack = (BEFORE_SHARE * from_lower.astype(jnp.float32) + AFTER_SHA...]
    dot_general x19 -> x0, matrix products: 19.1 us -> none  [the longest x1 5.87 us: body(): jnp.dot(mixed, lax.all_gather(out_mine, 'fsdp', axis=2, tiled=True)[0], p...]
  transfers between devices with their start and end apart: 7 -> 36, of which waited for: 5 -> 11; matrix products, arithmetic and copies ran while one was open for 22% -> 3% of each run, Pallas kernels for 0% -> 17%
where the time goes in v1:
time: 236 us; the launch traced here: 235 us
  waiting for transfers between devices  92.2 us (39%)
  starting transfers between devices  80.8 us (34%)
  Pallas kernels  41.7 us (18%)
  local copies, waits for them, and re-layouts  14 us (6%)
  other arithmetic  5.49 us (2%)
    ppermute x36, waiting for transfers between devices, permute(): lax.ppermute(array, axis, [(source(i) % count, i) for i in range(count)])  92.2 us
    ppermute x36, starting transfers between devices, permute(): lax.ppermute(array, axis, [(source(i) % count, i) for i in range(count)])  80.8 us
    pallas_call x9, Pallas kernels, combine(): pl.pallas_call(combine_kernel, out_shape=jax.ShapeDtypeStruct(far.shape,...  17.8 us
    pallas_call x4, Pallas kernels, attend(): pl.pallas_call(functools.partial(attend_kernel, len(blocks)), out_shape=j...  14.4 us
    unnamed x62, local copies, waits for them, and re-layouts  11.8 us
    pallas_call x4, Pallas kernels, partials(): pl.pallas_call(functools.partial(partial_kernel, count, len(mixed)), out_...  6.54 us
  transfers between devices with their start and end apart: 36, of which 11 were waited for; matrix products, arithmetic and copies ran while one was open for 3% of the time, Pallas kernels for 17%

profile of v1, /device:TPU:0, one launch (start us, length us, event | category | flops | bytes accessed | tf_op | source)
XLA Modules:
  0.0 234.5 jit_solution(16881449858351791340)
XLA Ops:
  0.5 2.5 %collective-permute-start.7 = (bf16[1024,256]{1,0:T(8,128)(2,1)}, bf16[1024,256]{1,0:T(8,128)(2,1)S(1)}, u32[]{:S(2)}, u32[]{:S(2)}) collective-permute-start(bf16[1024,256]{1,0:T(8,128)(2,1)} %bitcast.21), channel_id=1, source_target_pairs={{24,0},{16,8},{8,16},{0,24},{25,1},{17,9},{9,17},{1,25},{26,2},{18... | collective-permute-start | bytes 1572872 | tf_op jit(solution)/shard_map/ppermute | solution.py:240
  4.6 2.6 %collective-permute-start.1 = (bf16[512,512]{1,0:T(8,128)(2,1)}, bf16[512,512]{1,0:T(8,128)(2,1)S(1)}, u32[]{:S(2)}, u32[]{:S(2)}) collective-permute-start(bf16[512,512]{1,0:T(8,128)(2,1)} %bitcast.8), channel_id=1, source_target_pairs={{2,0},{3,1},{0,2},{1,3},{6,4},{7,5},{4,6},{5,7},{10,8},{11,9},{8,1... | collective-permute-start | bytes 1572872 | tf_op jit(solution)/shard_map/ppermute | solution.py:240
  9.9 5.6 %collective-permute-done.7.far = bf16[1024,256]{1,0:T(8,128)(2,1)S(1)} collective-permute-done((bf16[1024,256]{1,0:T(8,128)(2,1)}, bf16[1024,256]{1,0:T(8,128)(2,1)S(1)}, u32[]{:S(2)}, u32[]{:S(2)}) %collective-permute-start.7) | collective-permute-done | bytes 524320 | tf_op jit(solution)/shard_map/ppermute | solution.py:240
  16.3 4.3 %collective-permute-start.2 = (bf16[512,512]{1,0:T(8,128)(2,1)S(1)}, bf16[512,512]{1,0:T(8,128)(2,1)S(1)}, u32[]{:S(2)}, u32[]{:S(2)}) collective-permute-start(bf16[512,512]{1,0:T(8,128)(2,1)S(1)} %bitcast.9), channel_id=1, source_target_pairs={{1,0},{2,1},{3,2},{0,3},{5,4},{6,5},{7,6},{4,7},{9,8},{10,9},{11,1... | collective-permute-start | bytes 1572872 | tf_op jit(solution)/shard_map/ppermute | solution.py:240
  21.7 20.3 %collective-permute-done.1.refs_2_ = bf16[512,512]{1,0:T(8,128)(2,1)S(1)} collective-permute-done((bf16[512,512]{1,0:T(8,128)(2,1)}, bf16[512,512]{1,0:T(8,128)(2,1)S(1)}, u32[]{:S(2)}, u32[]{:S(2)}) %collective-permute-start.1) | collective-permute-done | bytes 524320 | tf_op jit(solution)/shard_map/ppermute | solution.py:240
  47.8 8.3 %collective-permute-done.11.far = bf16[1024,256]{1,0:T(8,128)(2,1)S(1)} collective-permute-done((bf16[1024,256]{1,0:T(8,128)(2,1)S(1)}, bf16[1024,256]{1,0:T(8,128)(2,1)S(1)}, u32[]{:S(2)}, u32[]{:S(2)}) %collective-permute-start.11) | collective-permute-done | bytes 524320 | tf_op jit(solution)/shard_map/ppermute | solution.py:240
  56.7 10.6 %collective-permute-done.9.far = bf16[1024,256]{1,0:T(8,128)(2,1)S(1)} collective-permute-done((bf16[1024,256]{1,0:T(8,128)(2,1)S(1)}, bf16[1024,256]{1,0:T(8,128)(2,1)S(1)}, u32[]{:S(2)}, u32[]{:S(2)}) %collective-permute-start.9) | collective-permute-done | bytes 524320 | tf_op jit(solution)/shard_map/ppermute | solution.py:240
  69.7 8.9 %collective-permute-done.4.far = bf16[1024,256]{1,0:T(8,128)(2,1)S(1)} collective-permute-done((bf16[1024,256]{1,0:T(8,128)(2,1)S(1)}, bf16[1024,256]{1,0:T(8,128)(2,1)S(1)}, u32[]{:S(2)}, u32[]{:S(2)}) %collective-permute-start.4) | collective-permute-done | bytes 524320 | tf_op jit(solution)/shard_map/ppermute | solution.py:240
  91.4 9.7 %collective-permute-done.26.far = bf16[1024,256]{1,0:T(8,128)(2,1)} collective-permute-done((bf16[1024,256]{1,0:T(8,128)(2,1)}, bf16[1024,256]{1,0:T(8,128)(2,1)}, u32[]{:S(2)}, u32[]{:S(2)}) %collective-permute-start.26) | collective-permute-done | bytes 524320 | tf_op jit(solution)/shard_map/ppermute | solution.py:240
  105.7 6.6 %collective-permute-done.21.far = bf16[1024,256]{1,0:T(8,128)(2,1)} collective-permute-done((bf16[1024,256]{1,0:T(8,128)(2,1)}, bf16[1024,256]{1,0:T(8,128)(2,1)}, u32[]{:S(2)}, u32[]{:S(2)}) %collective-permute-start.21) | collective-permute-done | bytes 524320 | tf_op jit(solution)/shard_map/ppermute | solution.py:240
  113.9 9.7 %collective-permute-done.16.far = bf16[1024,256]{1,0:T(8,128)(2,1)} collective-permute-done((bf16[1024,256]{1,0:T(8,128)(2,1)}, bf16[1024,256]{1,0:T(8,128)(2,1)}, u32[]{:S(2)}, u32[]{:S(2)}) %collective-permute-start.16) | collective-permute-done | bytes 524320 | tf_op jit(solution)/shard_map/ppermute | solution.py:240
  128.2 3.4 %shard_map.80.refs_4_ = bf16[1024,256]{1,0:T(8,128)(2,1)} custom-call(f32[2]{0:T(128)S(1)} %broadcast_select_fusion.shares, bf16[1024,1024]{1,0:T(8,128)(2,1)S(1)} %collective-permute-done.15.near, bf16[1024,256]{1,0:T(8,128)(2,1)} %collective-permute-done.31.far), custom_call_target="tpu_custom_call" | custom-call | flops 786432 | bytes 1572864 | tf_op jit(solution)/shard_map/pallas_call | solution.py:47
  131.6 3.3 %shard_map.78.refs_4_ = bf16[1024,256]{1,0:T(8,128)(2,1)} custom-call(f32[2]{0:T(128)S(1)} %broadcast_select_fusion.shares, bf16[1024,1024]{1,0:T(8,128)(2,1)S(1)} %collective-permute-done.15.near, bf16[1024,256]{1,0:T(8,128)(2,1)} %collective-permute-done.26.far), custom_call_target="tpu_custom_call" | custom-call | flops 786432 | bytes 1572864 | tf_op jit(solution)/shard_map/pallas_call | solution.py:47
  139.5 2.2 shard_map.76.refs_4_
  141.8 2.6 %shard_map.74.refs_4_ = bf16[1024,256]{1,0:T(8,128)(2,1)S(1)} custom-call(f32[2]{0:T(128)S(1)} %broadcast_select_fusion.shares, bf16[1024,1024]{1,0:T(8,128)(2,1)S(1)} %collective-permute-done.15.near, bf16[1024,256]{1,0:T(8,128)(2,1)} %collective-permute-done.16.far), custom_call_target="tpu_custom_call" | custom-call | flops 786432 | bytes 1572864 | tf_op jit(solution)/shard_map/pallas_call | solution.py:47
  148.5 3.1 %shard_map.73.refs_3_ = bf16[512,256]{1,0:T(8,128)(2,1)S(1)} custom-call(s32[2]{0:T(128)S(1)} %pad_add_fusion.ids, bf16[512,512]{1,0:T(8,128)(2,1)S(1)} %bitcast.11, bf16[512,512]{1,0:T(8,128)(2,1)S(1)} %collective-permute-done.refs_1_, bf16[512,512]{1,0:T(8,128)(2,1)S(1)} %copy-done.4, bf16[512,512]{1,0:T(8,128)(2,1)S(1)} %copy-done.6, ...), custom_call_target="tpu_custom_call" | custom-call | flops 738197504 | bytes 3145728 | tf_op jit(solution)/shard_map/pallas_call | solution.py:152
  151.6 3.8 %shard_map.71.refs_2_ = bf16[512,256]{1,0:T(8,128)(2,1)S(1)} custom-call(s32[2]{0:T(128)S(1)} %pad_add_fusion.ids, bf16[512,512]{1,0:T(8,128)(2,1)S(1)} %bitcast.12, bf16[512,512]{1,0:T(8,128)(2,1)S(1)} %collective-permute-done.refs_1_, bf16[512,512]{1,0:T(8,128)(2,1)S(1)} %copy-done.4, bf16[512,512]{1,0:T(8,128)(2,1)S(1)} %copy-done.6, ...), custom_call_target="tpu_custom_call" | custom-call | flops 738197504 | bytes 3145728 | tf_op jit(solution)/shard_map/pallas_call | solution.py:152
  155.4 3.8 %shard_map.69.refs_1_ = bf16[512,256]{1,0:T(8,128)(2,1)S(1)} custom-call(s32[2]{0:T(128)S(1)} %pad_add_fusion.ids, bf16[512,512]{1,0:T(8,128)(2,1)S(1)} %bitcast.13, bf16[512,512]{1,0:T(8,128)(2,1)S(1)} %collective-permute-done.refs_1_, bf16[512,512]{1,0:T(8,128)(2,1)S(1)} %copy-done.4, bf16[512,512]{1,0:T(8,128)(2,1)S(1)} %copy-done.6, ...), custom_call_target="tpu_custom_call" | custom-call | flops 738197504 | bytes 3145728 | tf_op jit(solution)/shard_map/pallas_call | solution.py:152
  159.2 3.8 %shard_map.67.refs_0_ = bf16[512,256]{1,0:T(8,128)(2,1)S(1)} custom-call(s32[2]{0:T(128)S(1)} %pad_add_fusion.ids, bf16[512,512]{1,0:T(8,128)(2,1)S(1)} %bitcast.14, bf16[512,512]{1,0:T(8,128)(2,1)S(1)} %collective-permute-done.refs_1_, bf16[512,512]{1,0:T(8,128)(2,1)S(1)} %copy-done.4, bf16[512,512]{1,0:T(8,128)(2,1)S(1)} %copy-done.6, ...), custom_call_target="tpu_custom_call" | custom-call | flops 738197504 | bytes 3145728 | tf_op jit(solution)/shard_map/pallas_call | solution.py:152
  162.9 2.0 shard_map.81
  164.9 10.2 %collective-permute-start.33 = (bf16[512,128]{1,0:T(8,128)(2,1)S(1)}, bf16[512,128]{1,0:T(8,128)(2,1)S(1)}, u32[]{:S(2)}, u32[]{:S(2)}) collective-permute-start(bf16[512,128]{1,0:T(8,128)(2,1)S(1)} %get-tuple-element.40), channel_id=1, source_target_pairs={{3,0},{0,1},{1,2},{2,3},{7,4},{4,5},{5,6},{6,7},{11,8},{8,9},{9,10... | collective-permute-start | bytes 393224 | tf_op jit(solution)/shard_map/ppermute | solution.py:240
  175.1 3.3 %collective-permute-start.34 = (bf16[512,128]{1,0:T(8,128)(2,1)S(1)}, bf16[512,128]{1,0:T(8,128)(2,1)S(1)}, u32[]{:S(2)}, u32[]{:S(2)}) collective-permute-start(bf16[512,128]{1,0:T(8,128)(2,1)S(1)} %get-tuple-element.41), channel_id=1, source_target_pairs={{2,0},{3,1},{0,2},{1,3},{6,4},{7,5},{4,6},{5,7},{10,8},{11,9},{8,1... | collective-permute-start | bytes 393224 | tf_op jit(solution)/shard_map/ppermute | solution.py:240
  178.3 6.9 %collective-permute-start.35 = (bf16[512,128]{1,0:T(8,128)(2,1)S(1)}, bf16[512,128]{1,0:T(8,128)(2,1)S(1)}, u32[]{:S(2)}, u32[]{:S(2)}) collective-permute-start(bf16[512,128]{1,0:T(8,128)(2,1)S(1)} %get-tuple-element.42), channel_id=1, source_target_pairs={{1,0},{2,1},{3,2},{0,3},{5,4},{6,5},{7,6},{4,7},{9,8},{10,9},{11,1... | collective-permute-start | bytes 393224 | tf_op jit(solution)/shard_map/ppermute | solution.py:240
  185.3 2.0 shard_map.79
  187.2 6.4 %collective-permute-start.28 = (bf16[512,128]{1,0:T(8,128)(2,1)S(1)}, bf16[512,128]{1,0:T(8,128)(2,1)S(1)}, u32[]{:S(2)}, u32[]{:S(2)}) collective-permute-start(bf16[512,128]{1,0:T(8,128)(2,1)S(1)} %get-tuple-element.36), channel_id=1, source_target_pairs={{3,0},{0,1},{1,2},{2,3},{7,4},{4,5},{5,6},{6,7},{11,8},{8,9},{9,10... | collective-permute-start | bytes 393224 | tf_op jit(solution)/shard_map/ppermute | solution.py:240
  195.0 9.6 %collective-permute-start.29 = (bf16[512,128]{1,0:T(8,128)(2,1)S(1)}, bf16[512,128]{1,0:T(8,128)(2,1)S(1)}, u32[]{:S(2)}, u32[]{:S(2)}) collective-permute-start(bf16[512,128]{1,0:T(8,128)(2,1)S(1)} %get-tuple-element.37), channel_id=1, source_target_pairs={{2,0},{3,1},{0,2},{1,3},{6,4},{7,5},{4,6},{5,7},{10,8},{11,9},{8,1... | collective-permute-start | bytes 393224 | tf_op jit(solution)/shard_map/ppermute | solution.py:240
  204.6 2.1 collective-permute-start.30
  210.1 2.9 %collective-permute-start.25 = (bf16[512,128]{1,0:T(8,128)(2,1)S(1)}, bf16[512,128]{1,0:T(8,128)(2,1)S(1)}, u32[]{:S(2)}, u32[]{:S(2)}) collective-permute-start(bf16[512,128]{1,0:T(8,128)(2,1)S(1)} %get-tuple-element.34), channel_id=1, source_target_pairs={{1,0},{2,1},{3,2},{0,3},{5,4},{6,5},{7,6},{4,7},{9,8},{10,9},{11,1... | collective-permute-start | bytes 393224 | tf_op jit(solution)/shard_map/ppermute | solution.py:240
  213.0 2.0 collective-permute-start.18
  215.0 7.1 %collective-permute-start.19 = (bf16[512,128]{1,0:T(8,128)(2,1)S(1)}, bf16[512,128]{1,0:T(8,128)(2,1)S(1)}, u32[]{:S(2)}, u32[]{:S(2)}) collective-permute-start(bf16[512,128]{1,0:T(8,128)(2,1)S(1)} %get-tuple-element.29), channel_id=1, source_target_pairs={{2,0},{3,1},{0,2},{1,3},{6,4},{7,5},{4,6},{5,7},{10,8},{11,9},{8,1... | collective-permute-start | bytes 393224 | tf_op jit(solution)/shard_map/ppermute | solution.py:240
  222.2 5.6 %collective-permute-done.24.refs_6_ = bf16[512,128]{1,0:T(8,128)(2,1)S(1)} collective-permute-done((bf16[512,128]{1,0:T(8,128)(2,1)S(1)}, bf16[512,128]{1,0:T(8,128)(2,1)S(1)}, u32[]{:S(2)}, u32[]{:S(2)}) %collective-permute-start.24) | collective-permute-done | bytes 131104 | tf_op jit(solution)/shard_map/ppermute | solution.py:240
  227.8 5.6 %collective-permute-done.19.refs_2_ = bf16[512,128]{1,0:T(8,128)(2,1)S(1)} collective-permute-done((bf16[512,128]{1,0:T(8,128)(2,1)S(1)}, bf16[512,128]{1,0:T(8,128)(2,1)S(1)}, u32[]{:S(2)}, u32[]{:S(2)}) %collective-permute-start.19) | collective-permute-done | bytes 131104 | tf_op jit(solution)/shard_map/ppermute | solution.py:240
  (132 shorter events, 53.3 us)
Async XLA Ops:
  0.5 79.6 %collective-permute-start.3 = (bf16[1024,1024]{1,0:T(8,128)(2,1)}, bf16[1024,1024]{1,0:T(8,128)(2,1)S(1)}, u32[]{:S(2)}, u32[]{:S(2)}) collective-permute-start(bf16[1024,1024]{1,0:T(8,128)(2,1)} %bitcast.16), channel_id=1, source_target_pairs={{8,0},{0,8},{24,16},{16,24},{9,1},{1,9},{25,17},{17,25},{10,2},{2,... | collective-permute-start | bytes 6291464 | tf_op jit(solution)/shard_map/ppermute | solution.py:240
  0.5 15.0 %collective-permute-start.7 = (bf16[1024,256]{1,0:T(8,128)(2,1)}, bf16[1024,256]{1,0:T(8,128)(2,1)S(1)}, u32[]{:S(2)}, u32[]{:S(2)}) collective-permute-start(bf16[1024,256]{1,0:T(8,128)(2,1)} %bitcast.21), channel_id=1, source_target_pairs={{24,0},{16,8},{8,16},{0,24},{25,1},{17,9},{9,17},{1,25},{26,2},{18... | collective-permute-start | bytes 1572872 | tf_op jit(solution)/shard_map/ppermute | solution.py:240
  3.1 17.6 %collective-permute-start = (bf16[512,512]{1,0:T(8,128)(2,1)}, bf16[512,512]{1,0:T(8,128)(2,1)S(1)}, u32[]{:S(2)}, u32[]{:S(2)}) collective-permute-start(bf16[512,512]{1,0:T(8,128)(2,1)} %bitcast.7), channel_id=1, source_target_pairs={{3,0},{0,1},{1,2},{2,3},{7,4},{4,5},{5,6},{6,7},{11,8},{8,9},{9,10... | collective-permute-start | bytes 1572872 | tf_op jit(solution)/shard_map/ppermute | solution.py:240
  4.6 37.4 %collective-permute-start.1 = (bf16[512,512]{1,0:T(8,128)(2,1)}, bf16[512,512]{1,0:T(8,128)(2,1)S(1)}, u32[]{:S(2)}, u32[]{:S(2)}) collective-permute-start(bf16[512,512]{1,0:T(8,128)(2,1)} %bitcast.8), channel_id=1, source_target_pairs={{2,0},{3,1},{0,2},{1,3},{6,4},{7,5},{4,6},{5,7},{10,8},{11,9},{8,1... | collective-permute-start | bytes 1572872 | tf_op jit(solution)/shard_map/ppermute | solution.py:240
  8.0 118.7 %collective-permute-start.15 = (bf16[1024,1024]{1,0:T(8,128)(2,1)}, bf16[1024,1024]{1,0:T(8,128)(2,1)S(1)}, u32[]{:S(2)}, u32[]{:S(2)}) collective-permute-start(bf16[1024,1024]{1,0:T(8,128)(2,1)} %bitcast.18), channel_id=1, source_target_pairs={{8,0},{0,8},{24,16},{16,24},{9,1},{1,9},{25,17},{17,25},{10,2},{2,... | collective-permute-start | bytes 6291464 | tf_op jit(solution)/shard_map/ppermute | solution.py:240
  16.3 25.9 %collective-permute-start.2 = (bf16[512,512]{1,0:T(8,128)(2,1)S(1)}, bf16[512,512]{1,0:T(8,128)(2,1)S(1)}, u32[]{:S(2)}, u32[]{:S(2)}) collective-permute-start(bf16[512,512]{1,0:T(8,128)(2,1)S(1)} %bitcast.9), channel_id=1, source_target_pairs={{1,0},{2,1},{3,2},{0,3},{5,4},{6,5},{7,6},{4,7},{9,8},{10,9},{11,1... | collective-permute-start | bytes 1572872 | tf_op jit(solution)/shard_map/ppermute | solution.py:240
  20.6 24.0 %collective-permute-start.13 = (bf16[1024,256]{1,0:T(8,128)(2,1)S(1)}, bf16[1024,256]{1,0:T(8,128)(2,1)S(1)}, u32[]{:S(2)}, u32[]{:S(2)}) collective-permute-start(bf16[1024,256]{1,0:T(8,128)(2,1)S(1)} %get-tuple-element.51), channel_id=1, source_target_pairs={{24,0},{16,8},{8,16},{0,24},{25,1},{17,9},{9,17},{1,25},{26,2},{18... | collective-permute-start | bytes 1572872 | tf_op jit(solution)/shard_map/ppermute | solution.py:240
  43.0 24.3 %collective-permute-start.9 = (bf16[1024,256]{1,0:T(8,128)(2,1)S(1)}, bf16[1024,256]{1,0:T(8,128)(2,1)S(1)}, u32[]{:S(2)}, u32[]{:S(2)}) collective-permute-start(bf16[1024,256]{1,0:T(8,128)(2,1)S(1)} %get-tuple-element.53), channel_id=1, source_target_pairs={{24,0},{16,8},{8,16},{0,24},{25,1},{17,9},{9,17},{1,25},{26,2},{18... | collective-permute-start | bytes 1572872 | tf_op jit(solution)/shard_map/ppermute | solution.py:240
  45.4 33.1 %collective-permute-start.4 = (bf16[1024,256]{1,0:T(8,128)(2,1)S(1)}, bf16[1024,256]{1,0:T(8,128)(2,1)S(1)}, u32[]{:S(2)}, u32[]{:S(2)}) collective-permute-start(bf16[1024,256]{1,0:T(8,128)(2,1)S(1)} %get-tuple-element.54), channel_id=1, source_target_pairs={{24,0},{16,8},{8,16},{0,24},{25,1},{17,9},{9,17},{1,25},{26,2},{18... | collective-permute-start | bytes 1572872 | tf_op jit(solution)/shard_map/ppermute | solution.py:240
  56.1 33.8 %collective-permute-start.31 = (bf16[1024,256]{1,0:T(8,128)(2,1)}, bf16[1024,256]{1,0:T(8,128)(2,1)}, u32[]{:S(2)}, u32[]{:S(2)}) collective-permute-start(bf16[1024,256]{1,0:T(8,128)(2,1)} %pad_maximum_fusion.3), channel_id=1, source_target_pairs={{24,0},{16,8},{8,16},{0,24},{25,1},{17,9},{9,17},{1,25},{26,2},{18... | collective-permute-start | bytes 1572872 | tf_op jit(solution)/shard_map/ppermute | solution.py:240
  67.4 33.8 %collective-permute-start.26 = (bf16[1024,256]{1,0:T(8,128)(2,1)}, bf16[1024,256]{1,0:T(8,128)(2,1)}, u32[]{:S(2)}, u32[]{:S(2)}) collective-permute-start(bf16[1024,256]{1,0:T(8,128)(2,1)} %pad_maximum_fusion.2), channel_id=1, source_target_pairs={{24,0},{16,8},{8,16},{0,24},{25,1},{17,9},{9,17},{1,25},{26,2},{18... | collective-permute-start | bytes 1572872 | tf_op jit(solution)/shard_map/ppermute | solution.py:240
  79.4 33.0 %collective-permute-start.21 = (bf16[1024,256]{1,0:T(8,128)(2,1)}, bf16[1024,256]{1,0:T(8,128)(2,1)}, u32[]{:S(2)}, u32[]{:S(2)}) collective-permute-start(bf16[1024,256]{1,0:T(8,128)(2,1)} %pad_maximum_fusion.1), channel_id=1, source_target_pairs={{24,0},{16,8},{8,16},{0,24},{25,1},{17,9},{9,17},{1,25},{26,2},{18... | collective-permute-start | bytes 1572872 | tf_op jit(solution)/shard_map/ppermute | solution.py:240
  81.4 42.3 %collective-permute-start.16 = (bf16[1024,256]{1,0:T(8,128)(2,1)}, bf16[1024,256]{1,0:T(8,128)(2,1)}, u32[]{:S(2)}, u32[]{:S(2)}) collective-permute-start(bf16[1024,256]{1,0:T(8,128)(2,1)} %pad_maximum_fusion), channel_id=1, source_target_pairs={{24,0},{16,8},{8,16},{0,24},{25,1},{17,9},{9,17},{1,25},{26,2},{18... | collective-permute-start | bytes 1572872 | tf_op jit(solution)/shard_map/ppermute | solution.py:240
  89.9 45.0 %collective-permute-start.8 = (bf16[1024,256]{1,0:T(8,128)(2,1)S(1)}, bf16[1024,256]{1,0:T(8,128)(2,1)S(1)}, u32[]{:S(2)}, u32[]{:S(2)}) collective-permute-start(bf16[1024,256]{1,0:T(8,128)(2,1)S(1)} %shard_map.65.refs_4_), channel_id=1, source_target_pairs={{4,0},{0,4},{5,1},{1,5},{6,2},{2,6},{7,3},{3,7},{12,8},{8,12},{13,... | collective-permute-start | bytes 1572872 | tf_op jit(solution)/shard_map/ppermute | solution.py:240
  101.2 36.2 %collective-permute-start.14 = (bf16[1024,256]{1,0:T(8,128)(2,1)S(1)}, bf16[1024,256]{1,0:T(8,128)(2,1)S(1)}, u32[]{:S(2)}, u32[]{:S(2)}) collective-permute-start(bf16[1024,256]{1,0:T(8,128)(2,1)S(1)} %shard_map.72.refs_4_), channel_id=1, source_target_pairs={{4,0},{0,4},{5,1},{1,5},{6,2},{2,6},{7,3},{3,7},{12,8},{8,12},{13,... | collective-permute-start | bytes 1572872 | tf_op jit(solution)/shard_map/ppermute | solution.py:240
  112.4 32.0 %collective-permute-start.12 = (bf16[1024,256]{1,0:T(8,128)(2,1)}, bf16[1024,256]{1,0:T(8,128)(2,1)}, u32[]{:S(2)}, u32[]{:S(2)}) collective-permute-start(bf16[1024,256]{1,0:T(8,128)(2,1)} %shard_map.70.refs_4_), channel_id=1, source_target_pairs={{4,0},{0,4},{5,1},{1,5},{6,2},{2,6},{7,3},{3,7},{12,8},{8,12},{13,... | collective-permute-start | bytes 1572872 | tf_op jit(solution)/shard_map/ppermute | solution.py:240
  123.6 22.4 %collective-permute-start.10 = (bf16[1024,256]{1,0:T(8,128)(2,1)}, bf16[1024,256]{1,0:T(8,128)(2,1)}, u32[]{:S(2)}, u32[]{:S(2)}) collective-permute-start(bf16[1024,256]{1,0:T(8,128)(2,1)} %shard_map.68.refs_4_), channel_id=1, source_target_pairs={{4,0},{0,4},{5,1},{1,5},{6,2},{2,6},{7,3},{3,7},{12,8},{8,12},{13,... | collective-permute-start | bytes 1572872 | tf_op jit(solution)/shard_map/ppermute | solution.py:240
  126.7 32.4 %collective-permute-start.5 = (bf16[1024,256]{1,0:T(8,128)(2,1)}, bf16[1024,256]{1,0:T(8,128)(2,1)}, u32[]{:S(2)}, u32[]{:S(2)}) collective-permute-start(bf16[1024,256]{1,0:T(8,128)(2,1)} %shard_map.64.refs_4_), channel_id=1, source_target_pairs={{4,0},{0,4},{5,1},{1,5},{6,2},{2,6},{7,3},{3,7},{12,8},{8,12},{13,... | collective-permute-start | bytes 1572872 | tf_op jit(solution)/shard_map/ppermute | solution.py:240
  135.8 27.1 %collective-permute-start.32 = (bf16[1024,256]{1,0:T(8,128)(2,1)}, bf16[1024,256]{1,0:T(8,128)(2,1)}, u32[]{:S(2)}, u32[]{:S(2)}) collective-permute-start(bf16[1024,256]{1,0:T(8,128)(2,1)} %shard_map.80.refs_4_), channel_id=1, source_target_pairs={{4,0},{0,4},{5,1},{1,5},{6,2},{2,6},{7,3},{3,7},{12,8},{8,12},{13,... | collective-permute-start | bytes 1572872 | tf_op jit(solution)/shard_map/ppermute | solution.py:240
  138.1 40.2 %collective-permute-start.27 = (bf16[1024,256]{1,0:T(8,128)(2,1)}, bf16[1024,256]{1,0:T(8,128)(2,1)}, u32[]{:S(2)}, u32[]{:S(2)}) collective-permute-start(bf16[1024,256]{1,0:T(8,128)(2,1)} %shard_map.78.refs_4_), channel_id=1, source_target_pairs={{4,0},{0,4},{5,1},{1,5},{6,2},{2,6},{7,3},{3,7},{12,8},{8,12},{13,... | collective-permute-start | bytes 1572872 | tf_op jit(solution)/shard_map/ppermute | solution.py:240
  144.5 42.8 %collective-permute-start.22 = (bf16[1024,256]{1,0:T(8,128)(2,1)S(1)}, bf16[1024,256]{1,0:T(8,128)(2,1)S(1)}, u32[]{:S(2)}, u32[]{:S(2)}) collective-permute-start(bf16[1024,256]{1,0:T(8,128)(2,1)S(1)} %shard_map.76.refs_4_), channel_id=1, source_target_pairs={{4,0},{0,4},{5,1},{1,5},{6,2},{2,6},{7,3},{3,7},{12,8},{8,12},{13,... | collective-permute-start | bytes 1572872 | tf_op jit(solution)/shard_map/ppermute | solution.py:240
  146.0 48.9 %collective-permute-start.17 = (bf16[1024,256]{1,0:T(8,128)(2,1)S(1)}, bf16[1024,256]{1,0:T(8,128)(2,1)S(1)}, u32[]{:S(2)}, u32[]{:S(2)}) collective-permute-start(bf16[1024,256]{1,0:T(8,128)(2,1)S(1)} %shard_map.74.refs_4_), channel_id=1, source_target_pairs={{4,0},{0,4},{5,1},{1,5},{6,2},{2,6},{7,3},{3,7},{12,8},{8,12},{13,... | collective-permute-start | bytes 1572872 | tf_op jit(solution)/shard_map/ppermute | solution.py:240
  164.9 39.6 %collective-permute-start.33 = (bf16[512,128]{1,0:T(8,128)(2,1)S(1)}, bf16[512,128]{1,0:T(8,128)(2,1)S(1)}, u32[]{:S(2)}, u32[]{:S(2)}) collective-permute-start(bf16[512,128]{1,0:T(8,128)(2,1)S(1)} %get-tuple-element.40), channel_id=1, source_target_pairs={{3,0},{0,1},{1,2},{2,3},{7,4},{4,5},{5,6},{6,7},{11,8},{8,9},{9,10... | collective-permute-start | bytes 393224 | tf_op jit(solution)/shard_map/ppermute | solution.py:240
  175.1 31.6 %collective-permute-start.34 = (bf16[512,128]{1,0:T(8,128)(2,1)S(1)}, bf16[512,128]{1,0:T(8,128)(2,1)S(1)}, u32[]{:S(2)}, u32[]{:S(2)}) collective-permute-start(bf16[512,128]{1,0:T(8,128)(2,1)S(1)} %get-tuple-element.41), channel_id=1, source_target_pairs={{2,0},{3,1},{0,2},{1,3},{6,4},{7,5},{4,6},{5,7},{10,8},{11,9},{8,1... | collective-permute-start | bytes 393224 | tf_op jit(solution)/shard_map/ppermute | solution.py:240
  178.3 30.3 %collective-permute-start.35 = (bf16[512,128]{1,0:T(8,128)(2,1)S(1)}, bf16[512,128]{1,0:T(8,128)(2,1)S(1)}, u32[]{:S(2)}, u32[]{:S(2)}) collective-permute-start(bf16[512,128]{1,0:T(8,128)(2,1)S(1)} %get-tuple-element.42), channel_id=1, source_target_pairs={{1,0},{2,1},{3,2},{0,3},{5,4},{6,5},{7,6},{4,7},{9,8},{10,9},{11,1... | collective-permute-start | bytes 393224 | tf_op jit(solution)/shard_map/ppermute | solution.py:240
  187.2 22.9 %collective-permute-start.28 = (bf16[512,128]{1,0:T(8,128)(2,1)S(1)}, bf16[512,128]{1,0:T(8,128)(2,1)S(1)}, u32[]{:S(2)}, u32[]{:S(2)}) collective-permute-start(bf16[512,128]{1,0:T(8,128)(2,1)S(1)} %get-tuple-element.36), channel_id=1, source_target_pairs={{3,0},{0,1},{1,2},{2,3},{7,4},{4,5},{5,6},{6,7},{11,8},{8,9},{9,10... | collective-permute-start | bytes 393224 | tf_op jit(solution)/shard_map/ppermute | solution.py:240
  195.0 18.0 %collective-permute-start.29 = (bf16[512,128]{1,0:T(8,128)(2,1)S(1)}, bf16[512,128]{1,0:T(8,128)(2,1)S(1)}, u32[]{:S(2)}, u32[]{:S(2)}) collective-permute-start(bf16[512,128]{1,0:T(8,128)(2,1)S(1)} %get-tuple-element.37), channel_id=1, source_target_pairs={{2,0},{3,1},{0,2},{1,3},{6,4},{7,5},{4,6},{5,7},{10,8},{11,9},{8,1... | collective-permute-start | bytes 393224 | tf_op jit(solution)/shard_map/ppermute | solution.py:240
  206.7 15.5 %collective-permute-start.23 = (bf16[512,128]{1,0:T(8,128)(2,1)S(1)}, bf16[512,128]{1,0:T(8,128)(2,1)S(1)}, u32[]{:S(2)}, u32[]{:S(2)}) collective-permute-start(bf16[512,128]{1,0:T(8,128)(2,1)S(1)} %get-tuple-element.32), channel_id=1, source_target_pairs={{3,0},{0,1},{1,2},{2,3},{7,4},{4,5},{5,6},{6,7},{11,8},{8,9},{9,10... | collective-permute-start | bytes 393224 | tf_op jit(solution)/shard_map/ppermute | solution.py:240
  208.6 19.1 %collective-permute-start.24 = (bf16[512,128]{1,0:T(8,128)(2,1)S(1)}, bf16[512,128]{1,0:T(8,128)(2,1)S(1)}, u32[]{:S(2)}, u32[]{:S(2)}) collective-permute-start(bf16[512,128]{1,0:T(8,128)(2,1)S(1)} %get-tuple-element.33), channel_id=1, source_target_pairs={{2,0},{3,1},{0,2},{1,3},{6,4},{7,5},{4,6},{5,7},{10,8},{11,9},{8,1... | collective-permute-start | bytes 393224 | tf_op jit(solution)/shard_map/ppermute | solution.py:240
  210.1 17.7 %collective-permute-start.25 = (bf16[512,128]{1,0:T(8,128)(2,1)S(1)}, bf16[512,128]{1,0:T(8,128)(2,1)S(1)}, u32[]{:S(2)}, u32[]{:S(2)}) collective-permute-start(bf16[512,128]{1,0:T(8,128)(2,1)S(1)} %get-tuple-element.34), channel_id=1, source_target_pairs={{1,0},{2,1},{3,2},{0,3},{5,4},{6,5},{7,6},{4,7},{9,8},{10,9},{11,1... | collective-permute-start | bytes 393224 | tf_op jit(solution)/shard_map/ppermute | solution.py:240
  213.0 14.7 %collective-permute-start.18 = (bf16[512,128]{1,0:T(8,128)(2,1)S(1)}, bf16[512,128]{1,0:T(8,128)(2,1)S(1)}, u32[]{:S(2)}, u32[]{:S(2)}) collective-permute-start(bf16[512,128]{1,0:T(8,128)(2,1)S(1)} %get-tuple-element.28), channel_id=1, source_target_pairs={{3,0},{0,1},{1,2},{2,3},{7,4},{4,5},{5,6},{6,7},{11,8},{8,9},{9,10... | collective-permute-start | bytes 393224 | tf_op jit(solution)/shard_map/ppermute | solution.py:240
  215.0 18.3 %collective-permute-start.19 = (bf16[512,128]{1,0:T(8,128)(2,1)S(1)}, bf16[512,128]{1,0:T(8,128)(2,1)S(1)}, u32[]{:S(2)}, u32[]{:S(2)}) collective-permute-start(bf16[512,128]{1,0:T(8,128)(2,1)S(1)} %get-tuple-element.29), channel_id=1, source_target_pairs={{2,0},{3,1},{0,2},{1,3},{6,4},{7,5},{4,6},{5,7},{10,8},{11,9},{8,1... | collective-permute-start | bytes 393224 | tf_op jit(solution)/shard_map/ppermute | solution.py:240
  (35 other events, 336.5 us)

commit v2 on v1

--- a/solution.py
+++ b/solution.py
@@ -35,30 +35,30 @@
     return jnp.concatenate([cosine, cosine], axis=1), jnp.concatenate([-sine, sine], axis=1)
 
 
-def combine_kernel(shares, near, far, out):
+ANY = pl.BlockSpec(memory_space=pl.ANY)
+
+
+def combine_kernel(shares, near, far, *rest):
+    out = rest[-1]
     mixed = shares[0] * near[...].astype(jnp.float32) + shares[1] * far[...].astype(jnp.float32)
     out[...] = mixed.astype(out.dtype)
 
 
-def combine(shares, near, far, near_block, width):
+def combine(shares, near, far, after=()):
     rows, columns = far.shape
-    pieces = columns // width
     step = min(rows, 512)
+    block = pl.BlockSpec((step, columns), lambda i: (i, 0))
     return pl.pallas_call(
         combine_kernel,
         out_shape=jax.ShapeDtypeStruct(far.shape, far.dtype),
-        grid=(rows // step, pieces),
-        in_specs=[
-            SMEM,
-            pl.BlockSpec((step, width), lambda i, j: (i, near_block(j))),
-            pl.BlockSpec((step, width), lambda i, j: (i, j)),
-        ],
-        out_specs=pl.BlockSpec((step, width), lambda i, j: (i, j)),
+        grid=(rows // step,),
+        in_specs=[SMEM, block, block] + [ANY] * len(after),
+        out_specs=block,
         compiler_params=params(),
         cost_estimate=pl.CostEstimate(
             flops=3 * far.size, bytes_accessed=6 * far.size, transcendentals=0
         ),
-    )(shares, near, far)
+    )(shares, near, far, *after)
 
 
 def project(ids, blocks, own, other, whole):
@@ -84,7 +84,8 @@
 
 def keyval_kernel(count, ids, *refs):
     blocks = refs[:count]
-    own, other, cosine, sine, keys, values, scales, whole = refs[count:]
+    own, other, cosine, sine = refs[count : count + 4]
+    keys, values, scales, whole = refs[-4:]
     total = 0.0
     features = 0
     for block in blocks:
@@ -98,14 +99,14 @@
     scales[...] = jnp.broadcast_to(scale, scales.shape)
 
 
-def keyval(ids, blocks, own, other, cosine, sine):
+def keyval(ids, blocks, own, other, cosine, sine, after=()):
     length = blocks[0].shape[0]
     features = sum(b.shape[1] for b in blocks)
     head = jax.ShapeDtypeStruct((length, HEAD_DIM), jnp.bfloat16)
     return pl.pallas_call(
         functools.partial(keyval_kernel, len(blocks)),
         out_shape=(head, head, jax.ShapeDtypeStruct((length, LANES), jnp.float32)),
-        in_specs=[SMEM] + [VMEM] * (len(blocks) + 4),
+        in_specs=[SMEM] + [VMEM] * (len(blocks) + 4) + [ANY] * len(after),
         out_specs=(VMEM,) * 3,
         scratch_shapes=[pltpu.VMEM((features, own.shape[1]), own.dtype)],
         compiler_params=params(),
@@ -114,12 +115,13 @@
             bytes_accessed=2 * features * (length + own.shape[1]),
             transcendentals=0,
         ),
-    )(ids, *blocks, own, other, cosine, sine)
+    )(ids, *blocks, own, other, cosine, sine, *after)
 
 
 def attend_kernel(count, ids, *refs):
     blocks = refs[:count]
-    own, other, keys, values, scales, cosine, sine, mixed, whole = refs[count:]
+    own, other, keys, values, scales, cosine, sine = refs[count : count + 7]
+    mixed, whole = refs[-2:]
     raw = project(ids, blocks, own, other, whole)
     length = raw.shape[0]
     rows = length // 2 if length % 16 == 0 else length
@@ -145,14 +147,14 @@
             mixed[first:last, columns] = (product / total).astype(mixed.dtype)
 
 
-def attend(ids, blocks, own, other, keys, values, scales, cosine, sine):
+def attend(ids, blocks, own, other, keys, values, scales, cosine, sine, after=()):
     length = blocks[0].shape[0]
     features = sum(b.shape[1] for b in blocks)
     width = own.shape[1]
     return pl.pallas_call(
         functools.partial(attend_kernel, len(blocks)),
         out_shape=jax.ShapeDtypeStruct((length, width), jnp.bfloat16),
-        in_specs=[SMEM] + [VMEM] * (len(blocks) + 7),
+        in_specs=[SMEM] + [VMEM] * (len(blocks) + 7) + [ANY] * len(after),
         out_specs=VMEM,
         scratch_shapes=[pltpu.VMEM((features, width), own.dtype)],
         compiler_params=params(),
@@ -161,13 +163,13 @@
             bytes_accessed=2 * features * (length + width),
             transcendentals=length * length * width // HEAD_DIM,
         ),
-    )(ids, *blocks, own, other, keys, values, scales, cosine, sine)
+    )(ids, *blocks, own, other, keys, values, scales, cosine, sine, *after)
 
 
 def partial_kernel(count, parts, ids, *refs):
     mixed = refs[:parts]
     own, other = refs[parts : parts + 2]
-    outs = refs[parts + 2 : parts + 2 + count]
+    outs = refs[-1 - count : -1]
     by_owner = refs[-1]
     mine, place = ids[0], ids[1]
     width = by_owner.shape[2]
@@ -188,14 +190,14 @@
         outs[k][...] = by_owner[lax.rem(place + k, count)]
 
 
-def partials(ids, mixed, own, other, count):
+def partials(ids, mixed, own, other, count, after=()):
     length = mixed[0].shape[0]
     width = 2 * own.shape[1] // count
     piece = jax.ShapeDtypeStruct((length, width), jnp.bfloat16)
     return pl.pallas_call(
         functools.partial(partial_kernel, count, len(mixed)),
         out_shape=(piece,) * count,
-        in_specs=[SMEM] + [VMEM] * (len(mixed) + 2),
+        in_specs=[SMEM] + [VMEM] * (len(mixed) + 2) + [ANY] * len(after),
         out_specs=(VMEM,) * count,
         scratch_shapes=[pltpu.VMEM((count, length, width), jnp.bfloat16)],
         compiler_params=params(),
@@ -204,7 +206,7 @@
             bytes_accessed=4 * own.size + 2 * length * (own.shape[0] + 2 * own.shape[1]),
             transcendentals=0,
         ),
-    )(ids, *mixed, own, other)
+    )(ids, *mixed, own, other, *after)
 
 
 def leave_kernel(count, chunks, rows, *refs):
@@ -271,60 +273,61 @@
     quarter = own_out.shape[1] // halves
     out_width = quarter // OUT_CHUNKS
 
-    far_keyval = from_far(own_keyval)
-    near_keyval = from_near(own_keyval)
+    chunks = [own_keyval]
+    for c in range(QUERY_CHUNKS):
+        chunks.append(own_query[:, c * query_width : (c + 1) * query_width])
+    for c in range(OUT_CHUNKS):
+        columns = [
+            own_out[:, h * quarter + c * out_width : h * quarter + (c + 1) * out_width]
+            for h in range(halves)
+        ]
+        chunks.append(jnp.concatenate(columns, axis=1))
+    far = [from_far(chunk) for chunk in chunks]
+    near = [from_near(chunk) for chunk in chunks]
     blocks = [rows] + [permute(rows, "tensor", lambda i, k=k: i - k) for k in range(1, count)]
-    near_query = from_near(own_query)
-    near_out = from_near(own_out)
-    far_query = [
-        from_far(own_query[:, c * query_width : (c + 1) * query_width])
-        for c in range(QUERY_CHUNKS)
-    ]
-    far_out = [
-        from_far(
-            jnp.concatenate(
-                [
-                    own_out[:, h * quarter + c * out_width : h * quarter + (c + 1) * out_width]
-                    for h in range(halves)
-                ],
-                axis=1,
-            )
-        )
-        for c in range(OUT_CHUNKS)
-    ]
     cosine, sine = rope_tables(length, HEAD_DIM)
 
-    keyval_own = combine(shares, near_keyval, far_keyval, lambda j: 0, own_keyval.shape[1])
-    keyval_other = from_other_half(keyval_own)
-    query_own, query_other = [], []
-    for c in range(QUERY_CHUNKS):
-        query_own.append(
-            combine(shares, near_query, far_query[c], lambda j, c=c: c, query_width)
-        )
-        query_other.append(from_other_half(query_own[c]))
-    out_own, out_other = [], []
-    for c in range(OUT_CHUNKS):
-        out_own.append(
-            combine(
-                shares, near_out, far_out[c], lambda j, c=c: j * OUT_CHUNKS + c, out_width
-            )
-        )
-        out_other.append(from_other_half(out_own[c]))
-
-    keys, values, scales = keyval(ids, blocks, keyval_own, keyval_other, cosine, sine)
-    mixed = [
-        attend(
-            ids, blocks, query_own[c], query_other[c], keys, values, scales, cosine, sine
-        )
-        for c in range(QUERY_CHUNKS)
-    ]
-    pieces = []
-    for c in range(OUT_CHUNKS):
-        parts = partials(ids, mixed, out_own[c], out_other[c], count)
-        pieces.append(
-            [parts[0]]
-            + [permute(parts[k], "tensor", lambda i, k=k: i - k) for k in range(1, count)]
-        )
+    own, other, mixed, pieces = [], [], [], []
+    after = {1: blocks[1:2] + blocks[3:], 3: blocks[2:3]}
+    for c in range(len(chunks)):
+        ready = after.get(c, [])
+        if c >= 2:
+            ready = ready + [other[c - 2]]
+        own.append(combine(shares, near[c], far[c], after=ready))
+        other.append(from_other_half(own[c]))
+        work = after.setdefault(c + 1, [])
+        todo = {3: (0, 1), 4: (2, 3), 5: (4,), 6: (5,), 7: (6,), 8: (7, 8)}.get(c, ())
+        for d in todo:
+            if d == 0:
+                keys, values, scales = keyval(
+                    ids, blocks, own[d], other[d], cosine, sine, after=[own[c]]
+                )
+                work.append(scales)
+            elif d <= QUERY_CHUNKS:
+                mixed.append(
+                    attend(
+                        ids,
+                        blocks,
+                        own[d],
+                        other[d],
+                        keys,
+                        values,
+                        scales,
+                        cosine,
+                        sine,
+                        after=[own[c]],
+                    )
+                )
+                work.append(mixed[-1])
+            else:
+                before = [own[c]] + (pieces[-2][1:] if len(pieces) >= 2 else [])
+                parts = partials(ids, mixed, own[d], other[d], count, after=before)
+                pieces.append(
+                    [parts[0]]
+                    + [permute(parts[k], "tensor", lambda i, k=k: i - k) for k in range(1, count)]
+                )
+                work.append(parts[0])
+                after.setdefault(c + 2, []).extend(pieces[-1][1:])
     return leave(rows, pieces)[None]
 
 

time: 236 us -> 168 us (0.71)
  waiting for transfers between devices: 92.2 us -> 61.1 us
  starting transfers between devices: 80.8 us -> 63.8 us
  Pallas kernels: 41.7 us -> 31.6 us
  local copies, waits for them, and re-layouts: 14 us -> 7.18 us
  other arithmetic: 5.49 us -> 3.11 us
    ppermute x36 -> x42, waiting for transfers between devices: 92.2 us -> 61.1 us  [permute(): lax.ppermute(array, axis, [(source(i) % count, i) for i in range(count)])]
    ppermute x36 -> x42, starting transfers between devices: 80.8 us -> 63.8 us  [permute(): lax.ppermute(array, axis, [(source(i) % count, i) for i in range(count)])]
    unnamed x62 -> x38, local copies, waits for them, and re-layouts: 11.8 us -> 2.93 us
    pallas_call x9, Pallas kernels: 17.8 us -> 9.93 us  [combine(): pl.pallas_call(combine_kernel, out_shape=jax.ShapeDtypeStruct(far.shape,...]
    concatenate x4, other arithmetic: 3.51 us -> 1.06 us  [body(): chunks.append(jnp.concatenate(columns, axis=1))]
  transfers between devices with their start and end apart: 36 -> 42, of which waited for: 11 -> 13; matrix products, arithmetic and copies ran while one was open for 3% -> 4% of each run, Pallas kernels for 17% -> 18%
where the time goes in v2:
time: 168 us; the launch traced here: 167 us
  starting transfers between devices  63.8 us (38%)
  waiting for transfers between devices  61.1 us (36%)
  Pallas kernels  31.6 us (19%)
  local copies, waits for them, and re-layouts  7.18 us (4%)
  other arithmetic  3.11 us (2%)
    ppermute x42, starting transfers between devices, permute(): lax.ppermute(array, axis, [(source(i) % count, i) for i in range(count)])  63.8 us
    ppermute x42, waiting for transfers between devices, permute(): lax.ppermute(array, axis, [(source(i) % count, i) for i in range(count)])  61.1 us
    pallas_call x4, Pallas kernels, attend(): pl.pallas_call(functools.partial(attend_kernel, len(blocks)), out_shape=j...  13.5 us
    pallas_call x9, Pallas kernels, combine(): pl.pallas_call(combine_kernel, out_shape=jax.ShapeDtypeStruct(far.shape,...  9.93 us
    pallas_call x4, Pallas kernels, partials(): pl.pallas_call(functools.partial(partial_kernel, count, len(mixed)), out_...  5.19 us
  transfers between devices with their start and end apart: 42, of which 13 were waited for; matrix products, arithmetic and copies ran while one was open for 4% of the time, Pallas kernels for 18%

profile of v2, /device:TPU:0, one launch (start us, length us, event | category | flops | bytes accessed | tf_op | source)
XLA Modules:
  0.0 167.3 jit_solution(12065995892830294432)
XLA Ops:
  0.0 3.0 %collective-permute-start = (bf16[512,512]{1,0:T(8,128)(2,1)}, bf16[512,512]{1,0:T(8,128)(2,1)S(1)}, u32[]{:S(2)}, u32[]{:S(2)}) collective-permute-start(bf16[512,512]{1,0:T(8,128)(2,1)} %bitcast.7), channel_id=1, source_target_pairs={{3,0},{0,1},{1,2},{2,3},{7,4},{4,5},{5,6},{6,7},{11,8},{8,9},{9,10... | collective-permute-start | bytes 1572872 | tf_op jit(solution)/shard_map/ppermute | solution.py:242
  4.6 2.2 %collective-permute-start.2 = (bf16[512,512]{1,0:T(8,128)(2,1)}, bf16[512,512]{1,0:T(8,128)(2,1)S(1)}, u32[]{:S(2)}, u32[]{:S(2)}) collective-permute-start(bf16[512,512]{1,0:T(8,128)(2,1)} %bitcast.8), channel_id=1, source_target_pairs={{1,0},{2,1},{3,2},{0,3},{5,4},{6,5},{7,6},{4,7},{9,8},{10,9},{11,1... | collective-permute-start | bytes 1572872 | tf_op jit(solution)/shard_map/ppermute | solution.py:242
  6.9 2.9 %fusion.4 = (bf16[1024,256]{1,0:T(8,128)(2,1)}, bf16[1024,256]{1,0:T(8,128)(2,1)}, bf16[1024,256]{1,0:T(8,128)(2,1)}, bf16[1024,256]{1,0:T(8,128)(2,1)}) fusion(bf16[1024,1024]{1,0:T(8,128)(2,1)} %bitcast.16), kind=kLoop, calls=%fused_computation.14 | loop fusion | bytes 4194304 | tf_op jit(solution)/shard_map/slice | solution.py:278
  9.8 8.2 %collective-permute-done.rest_0_.refs_1_ = bf16[512,512]{1,0:T(8,128)(2,1)S(1)} collective-permute-done((bf16[512,512]{1,0:T(8,128)(2,1)}, bf16[512,512]{1,0:T(8,128)(2,1)S(1)}, u32[]{:S(2)}, u32[]{:S(2)}) %collective-permute-start) | collective-permute-done | bytes 524320 | tf_op jit(solution)/shard_map/ppermute | solution.py:242
  18.1 1.9 %collective-permute-start.11 = (bf16[1024,256]{1,0:T(8,128)(2,1)}, bf16[1024,256]{1,0:T(8,128)(2,1)S(1)}, u32[]{:S(2)}, u32[]{:S(2)}) collective-permute-start(bf16[1024,256]{1,0:T(8,128)(2,1)} %get-tuple-element.52), channel_id=1, source_target_pairs={{8,0},{0,8},{24,16},{16,24},{9,1},{1,9},{25,17},{17,25},{10,2},{2,... | collective-permute-start | bytes 1572872 | tf_op jit(solution)/shard_map/ppermute | solution.py:242
  20.8 7.6 %collective-permute-done.2.rest_1_.refs_3_ = bf16[512,512]{1,0:T(8,128)(2,1)S(1)} collective-permute-done((bf16[512,512]{1,0:T(8,128)(2,1)}, bf16[512,512]{1,0:T(8,128)(2,1)S(1)}, u32[]{:S(2)}, u32[]{:S(2)}) %collective-permute-start.2) | collective-permute-done | bytes 524320 | tf_op jit(solution)/shard_map/ppermute | solution.py:242
  30.0 3.5 %collective-permute-start.1 = (bf16[512,512]{1,0:T(8,128)(2,1)S(1)}, bf16[512,512]{1,0:T(8,128)(2,1)S(1)}, u32[]{:S(2)}, u32[]{:S(2)}) collective-permute-start(bf16[512,512]{1,0:T(8,128)(2,1)S(1)} %bitcast.9), channel_id=1, source_target_pairs={{2,0},{3,1},{0,2},{1,3},{6,4},{7,5},{4,6},{5,7},{10,8},{11,9},{8,1... | collective-permute-start | bytes 1572872 | tf_op jit(solution)/shard_map/ppermute | solution.py:242
  34.5 2.0 %shard_map.64.refs_4_ = bf16[1024,256]{1,0:T(8,128)(2,1)} custom-call(f32[2]{0:T(128)S(1)} %broadcast_select_fusion.shares, bf16[1024,256]{1,0:T(8,128)(2,1)} %collective-permute-done.3.near, bf16[1024,256]{1,0:T(8,128)(2,1)} %collective-permute-done.4.far, bf16[512,512]{1,0:T(8,128)(2,1)S(1)} %collective-permute-done.rest_0_.refs_1_, ...), custom_call_target="tpu_custom_call" | custom-call | flops 786432 | bytes 1572864 | tf_op jit(solution)/shard_map/pallas_call | solution.py:51
  37.2 6.4 %collective-permute-done.12.far = bf16[1024,256]{1,0:T(8,128)(2,1)} collective-permute-done((bf16[1024,256]{1,0:T(8,128)(2,1)}, bf16[1024,256]{1,0:T(8,128)(2,1)}, u32[]{:S(2)}, u32[]{:S(2)}) %collective-permute-start.12) | collective-permute-done | bytes 524320 | tf_op jit(solution)/shard_map/ppermute | solution.py:242
  43.5 2.0 %collective-permute-start.5 = (bf16[1024,256]{1,0:T(8,128)(2,1)}, bf16[1024,256]{1,0:T(8,128)(2,1)}, u32[]{:S(2)}, u32[]{:S(2)}) collective-permute-start(bf16[1024,256]{1,0:T(8,128)(2,1)} %shard_map.64.refs_4_), channel_id=1, source_target_pairs={{4,0},{0,4},{5,1},{1,5},{6,2},{2,6},{7,3},{3,7},{12,8},{8,12},{13,... | collective-permute-start | bytes 1572872 | tf_op jit(solution)/shard_map/ppermute | solution.py:242
  45.6 1.8 %fusion.2 = (f32[512,64]{1,0:T(8,128)}, f32[512,64]{1,0:T(8,128)}, f32[512,64]{1,0:T(8,128)}) fusion(f32[64]{0:T(128)S(1)} %multiply_exponential_fusion), kind=kLoop, calls=%fused_computation.9 | loop fusion | flops 65536 | bytes 393472 | tf_op jit(solution)/shard_map/neg | solution.py:35
  50.9 6.1 %collective-permute-done.1.rest_0_.refs_2_ = bf16[512,512]{1,0:T(8,128)(2,1)S(1)} collective-permute-done((bf16[512,512]{1,0:T(8,128)(2,1)S(1)}, bf16[512,512]{1,0:T(8,128)(2,1)S(1)}, u32[]{:S(2)}, u32[]{:S(2)}) %collective-permute-start.1) | collective-permute-done | bytes 524320 | tf_op jit(solution)/shard_map/ppermute | solution.py:242
  65.0 1.9 %shard_map.67 = (bf16[512,128]{1,0:T(8,128)(2,1)S(1)}, bf16[512,128]{1,0:T(8,128)(2,1)S(1)}, f32[512,128]{1,0:T(8,128)S(1)}) custom-call(s32[2]{0:T(128)S(1)} %pad_add_fusion.ids, bf16[512,512]{1,0:T(8,128)(2,1)S(1)} %bitcast.10, bf16[512,512]{1,0:T(8,128)(2,1)S(1)} %collective-permute-done.rest_0_.refs_1_, ...), custom_call_target="tpu_custom_call" | custom-call | flops 536870912 | bytes 3145728 | tf_op jit(solution)/shard_map/pallas_call | solution.py:106
  66.8 3.8 %shard_map.68.rest_1_.refs_0_ = bf16[512,256]{1,0:T(8,128)(2,1)S(1)} custom-call(s32[2]{0:T(128)S(1)} %pad_add_fusion.ids, bf16[512,512]{1,0:T(8,128)(2,1)S(1)} %bitcast.11, bf16[512,512]{1,0:T(8,128)(2,1)S(1)} %collective-permute-done.rest_0_.refs_1_, bf16[512,512]{1,0:T(8,128)(2,1)S(1)} %collective-permute-done.1.rest_0_.refs_2_, ...), custom_call_target="tpu_custom_call" | custom-call | flops 738197504 | bytes 3145728 | tf_op jit(solution)/shard_map/pallas_call | solution.py:154
  71.7 1.7 %collective-permute-done.13.rest_2_.refs_5_ = bf16[1024,256]{1,0:T(8,128)(2,1)} collective-permute-done((bf16[1024,256]{1,0:T(8,128)(2,1)S(1)}, bf16[1024,256]{1,0:T(8,128)(2,1)}, u32[]{:S(2)}, u32[]{:S(2)}) %collective-permute-start.13) | collective-permute-done | bytes 524320 | tf_op jit(solution)/shard_map/ppermute | solution.py:242
  75.3 9.2 %collective-permute-done.16.refs_5_.rest_2_ = bf16[1024,256]{1,0:T(8,128)(2,1)S(1)} collective-permute-done((bf16[1024,256]{1,0:T(8,128)(2,1)S(1)}, bf16[1024,256]{1,0:T(8,128)(2,1)S(1)}, u32[]{:S(2)}, u32[]{:S(2)}) %collective-permute-start.16) | collective-permute-done | bytes 524320 | tf_op jit(solution)/shard_map/ppermute | solution.py:242
  84.5 3.6 %shard_map.71.rest_0_.refs_1_ = bf16[512,256]{1,0:T(8,128)(2,1)S(1)} custom-call(s32[2]{0:T(128)S(1)} %pad_add_fusion.ids, bf16[512,512]{1,0:T(8,128)(2,1)S(1)} %bitcast.12, bf16[512,512]{1,0:T(8,128)(2,1)S(1)} %collective-permute-done.rest_0_.refs_1_, bf16[512,512]{1,0:T(8,128)(2,1)S(1)} %collective-permute-done.1.rest_0_.refs_2_, ...), custom_call_target="tpu_custom_call" | custom-call | flops 738197504 | bytes 3145728 | tf_op jit(solution)/shard_map/pallas_call | solution.py:154
  88.1 3.1 %shard_map.72.rest_1_.refs_2_ = bf16[512,256]{1,0:T(8,128)(2,1)S(1)} custom-call(s32[2]{0:T(128)S(1)} %pad_add_fusion.ids, bf16[512,512]{1,0:T(8,128)(2,1)S(1)} %bitcast.13, bf16[512,512]{1,0:T(8,128)(2,1)S(1)} %collective-permute-done.rest_0_.refs_1_, bf16[512,512]{1,0:T(8,128)(2,1)S(1)} %collective-permute-done.1.rest_0_.refs_2_, ...), custom_call_target="tpu_custom_call" | custom-call | flops 738197504 | bytes 3145728 | tf_op jit(solution)/shard_map/pallas_call | solution.py:154
  95.7 3.1 %shard_map.74.rest_0_.refs_3_ = bf16[512,256]{1,0:T(8,128)(2,1)S(1)} custom-call(s32[2]{0:T(128)S(1)} %pad_add_fusion.ids, bf16[512,512]{1,0:T(8,128)(2,1)S(1)} %bitcast.14, bf16[512,512]{1,0:T(8,128)(2,1)S(1)} %collective-permute-done.rest_0_.refs_1_, bf16[512,512]{1,0:T(8,128)(2,1)S(1)} %collective-permute-done.1.rest_0_.refs_2_, ...), custom_call_target="tpu_custom_call" | custom-call | flops 738197504 | bytes 3145728 | tf_op jit(solution)/shard_map/pallas_call | solution.py:154
  100.6 6.5 %collective-permute-done.20.refs_5_.rest_1_ = bf16[1024,256]{1,0:T(8,128)(2,1)S(1)} collective-permute-done((bf16[1024,256]{1,0:T(8,128)(2,1)S(1)}, bf16[1024,256]{1,0:T(8,128)(2,1)S(1)}, u32[]{:S(2)}, u32[]{:S(2)}) %collective-permute-start.20) | collective-permute-done | bytes 524320 | tf_op jit(solution)/shard_map/ppermute | solution.py:242
  110.4 8.7 %collective-permute-start.24 = (bf16[512,128]{1,0:T(8,128)(2,1)S(1)}, bf16[512,128]{1,0:T(8,128)(2,1)S(1)}, u32[]{:S(2)}, u32[]{:S(2)}) collective-permute-start(bf16[512,128]{1,0:T(8,128)(2,1)S(1)} %get-tuple-element.29), channel_id=1, source_target_pairs={{2,0},{3,1},{0,2},{1,3},{6,4},{7,5},{4,6},{5,7},{10,8},{11,9},{8,1... | collective-permute-start | bytes 393224 | tf_op jit(solution)/shard_map/ppermute | solution.py:242
  121.3 1.7 collective-permute-start.32
  124.2 3.4 %collective-permute-done.24.rest_1_.refs_8_.refs_2_ = bf16[512,128]{1,0:T(8,128)(2,1)S(1)} collective-permute-done((bf16[512,128]{1,0:T(8,128)(2,1)S(1)}, bf16[512,128]{1,0:T(8,128)(2,1)S(1)}, u32[]{:S(2)}, u32[]{:S(2)}) %collective-permute-start.24) | collective-permute-done | bytes 131104 | tf_op jit(solution)/shard_map/ppermute | solution.py:242
  128.4 2.2 %collective-permute-start.38 = (bf16[1024,256]{1,0:T(8,128)(2,1)S(1)}, bf16[1024,256]{1,0:T(8,128)(2,1)S(1)}, u32[]{:S(2)}, u32[]{:S(2)}) collective-permute-start(bf16[1024,256]{1,0:T(8,128)(2,1)S(1)} %shard_map.79.refs_6_.refs_4_), channel_id=1, source_target_pairs={{4,0},{0,4},{5,1},{1,5},{6,2},{2,6},{7,3},{3,7},{12,8},{8,12},{13,... | collective-permute-start | bytes 1572872 | tf_op jit(solution)/shard_map/ppermute | solution.py:242
  130.6 3.3 %collective-permute-start.29 = (bf16[512,128]{1,0:T(8,128)(2,1)S(1)}, bf16[512,128]{1,0:T(8,128)(2,1)S(1)}, u32[]{:S(2)}, u32[]{:S(2)}) collective-permute-start(bf16[512,128]{1,0:T(8,128)(2,1)S(1)} %get-tuple-element.32), channel_id=1, source_target_pairs={{3,0},{0,1},{1,2},{2,3},{7,4},{4,5},{5,6},{6,7},{11,8},{8,9},{9,10... | collective-permute-start | bytes 393224 | tf_op jit(solution)/shard_map/ppermute | solution.py:242
  133.9 1.6 collective-permute-start.30
  139.3 4.9 %collective-permute-start.36 = (bf16[512,128]{1,0:T(8,128)(2,1)S(1)}, bf16[512,128]{1,0:T(8,128)(2,1)S(1)}, u32[]{:S(2)}, u32[]{:S(2)}) collective-permute-start(bf16[512,128]{1,0:T(8,128)(2,1)S(1)} %get-tuple-element.37), channel_id=1, source_target_pairs={{2,0},{3,1},{0,2},{1,3},{6,4},{7,5},{4,6},{5,7},{10,8},{11,9},{8,1... | collective-permute-start | bytes 393224 | tf_op jit(solution)/shard_map/ppermute | solution.py:242
  144.3 5.8 %collective-permute-start.37 = (bf16[512,128]{1,0:T(8,128)(2,1)S(1)}, bf16[512,128]{1,0:T(8,128)(2,1)S(1)}, u32[]{:S(2)}, u32[]{:S(2)}) collective-permute-start(bf16[512,128]{1,0:T(8,128)(2,1)S(1)} %get-tuple-element.38), channel_id=1, source_target_pairs={{1,0},{2,1},{3,2},{0,3},{5,4},{6,5},{7,6},{4,7},{9,8},{10,9},{11,1... | collective-permute-start | bytes 393224 | tf_op jit(solution)/shard_map/ppermute | solution.py:242
  151.4 2.7 %collective-permute-start.39 = (bf16[512,128]{1,0:T(8,128)(2,1)S(1)}, bf16[512,128]{1,0:T(8,128)(2,1)S(1)}, u32[]{:S(2)}, u32[]{:S(2)}) collective-permute-start(bf16[512,128]{1,0:T(8,128)(2,1)S(1)} %get-tuple-element.40), channel_id=1, source_target_pairs={{3,0},{0,1},{1,2},{2,3},{7,4},{4,5},{5,6},{6,7},{11,8},{8,9},{9,10... | collective-permute-start | bytes 393224 | tf_op jit(solution)/shard_map/ppermute | solution.py:242
  154.7 1.7 %collective-permute-start.41 = (bf16[512,128]{1,0:T(8,128)(2,1)S(1)}, bf16[512,128]{1,0:T(8,128)(2,1)S(1)}, u32[]{:S(2)}, u32[]{:S(2)}) collective-permute-start(bf16[512,128]{1,0:T(8,128)(2,1)S(1)} %get-tuple-element.42), channel_id=1, source_target_pairs={{1,0},{2,1},{3,2},{0,3},{5,4},{6,5},{7,6},{4,7},{9,8},{10,9},{11,1... | collective-permute-start | bytes 393224 | tf_op jit(solution)/shard_map/ppermute | solution.py:242
  156.5 3.1 %collective-permute-done.39.refs_13_ = bf16[512,128]{1,0:T(8,128)(2,1)S(1)} collective-permute-done((bf16[512,128]{1,0:T(8,128)(2,1)S(1)}, bf16[512,128]{1,0:T(8,128)(2,1)S(1)}, u32[]{:S(2)}, u32[]{:S(2)}) %collective-permute-start.39) | collective-permute-done | bytes 131104 | tf_op jit(solution)/shard_map/ppermute | solution.py:242
  159.5 6.6 %collective-permute-done.40.refs_14_ = bf16[512,128]{1,0:T(8,128)(2,1)S(1)} collective-permute-done((bf16[512,128]{1,0:T(8,128)(2,1)S(1)}, bf16[512,128]{1,0:T(8,128)(2,1)S(1)}, u32[]{:S(2)}, u32[]{:S(2)}) %collective-permute-start.40) | collective-permute-done | bytes 131104 | tf_op jit(solution)/shard_map/ppermute | solution.py:242
  (120 shorter events, 40.7 us)
Async XLA Ops:
  0.0 18.1 %collective-permute-start = (bf16[512,512]{1,0:T(8,128)(2,1)}, bf16[512,512]{1,0:T(8,128)(2,1)S(1)}, u32[]{:S(2)}, u32[]{:S(2)}) collective-permute-start(bf16[512,512]{1,0:T(8,128)(2,1)} %bitcast.7), channel_id=1, source_target_pairs={{3,0},{0,1},{1,2},{2,3},{7,4},{4,5},{5,6},{6,7},{11,8},{8,9},{9,10... | collective-permute-start | bytes 1572872 | tf_op jit(solution)/shard_map/ppermute | solution.py:242
  3.0 15.0 %collective-permute-start.6 = (bf16[1024,256]{1,0:T(8,128)(2,1)}, bf16[1024,256]{1,0:T(8,128)(2,1)S(1)}, u32[]{:S(2)}, u32[]{:S(2)}) collective-permute-start(bf16[1024,256]{1,0:T(8,128)(2,1)} %bitcast.18), channel_id=1, source_target_pairs={{8,0},{0,8},{24,16},{16,24},{9,1},{1,9},{25,17},{17,25},{10,2},{2,... | collective-permute-start | bytes 1572872 | tf_op jit(solution)/shard_map/ppermute | solution.py:242
  3.0 16.9 %collective-permute-start.7 = (bf16[1024,256]{1,0:T(8,128)(2,1)}, bf16[1024,256]{1,0:T(8,128)(2,1)S(1)}, u32[]{:S(2)}, u32[]{:S(2)}) collective-permute-start(bf16[1024,256]{1,0:T(8,128)(2,1)} %bitcast.19), channel_id=1, source_target_pairs={{24,0},{16,8},{8,16},{0,24},{25,1},{17,9},{9,17},{1,25},{26,2},{18... | collective-permute-start | bytes 1572872 | tf_op jit(solution)/shard_map/ppermute | solution.py:242
  4.6 23.8 %collective-permute-start.2 = (bf16[512,512]{1,0:T(8,128)(2,1)}, bf16[512,512]{1,0:T(8,128)(2,1)S(1)}, u32[]{:S(2)}, u32[]{:S(2)}) collective-permute-start(bf16[512,512]{1,0:T(8,128)(2,1)} %bitcast.8), channel_id=1, source_target_pairs={{1,0},{2,1},{3,2},{0,3},{5,4},{6,5},{7,6},{4,7},{9,8},{10,9},{11,1... | collective-permute-start | bytes 1572872 | tf_op jit(solution)/shard_map/ppermute | solution.py:242
  9.8 20.1 %collective-permute-start.3 = (bf16[1024,256]{1,0:T(8,128)(2,1)}, bf16[1024,256]{1,0:T(8,128)(2,1)}, u32[]{:S(2)}, u32[]{:S(2)}) collective-permute-start(bf16[1024,256]{1,0:T(8,128)(2,1)} %get-tuple-element.54), channel_id=1, source_target_pairs={{8,0},{0,8},{24,16},{16,24},{9,1},{1,9},{25,17},{17,25},{10,2},{2,... | collective-permute-start | bytes 1572872 | tf_op jit(solution)/shard_map/ppermute | solution.py:242
  18.1 15.4 %collective-permute-start.4 = (bf16[1024,256]{1,0:T(8,128)(2,1)}, bf16[1024,256]{1,0:T(8,128)(2,1)}, u32[]{:S(2)}, u32[]{:S(2)}) collective-permute-start(bf16[1024,256]{1,0:T(8,128)(2,1)} %get-tuple-element.54), channel_id=1, source_target_pairs={{24,0},{16,8},{8,16},{0,24},{25,1},{17,9},{9,17},{1,25},{26,2},{18... | collective-permute-start | bytes 1572872 | tf_op jit(solution)/shard_map/ppermute | solution.py:242
  18.1 18.4 %collective-permute-start.11 = (bf16[1024,256]{1,0:T(8,128)(2,1)}, bf16[1024,256]{1,0:T(8,128)(2,1)S(1)}, u32[]{:S(2)}, u32[]{:S(2)}) collective-permute-start(bf16[1024,256]{1,0:T(8,128)(2,1)} %get-tuple-element.52), channel_id=1, source_target_pairs={{8,0},{0,8},{24,16},{16,24},{9,1},{1,9},{25,17},{17,25},{10,2},{2,... | collective-permute-start | bytes 1572872 | tf_op jit(solution)/shard_map/ppermute | solution.py:242
  19.9 23.6 %collective-permute-start.12 = (bf16[1024,256]{1,0:T(8,128)(2,1)}, bf16[1024,256]{1,0:T(8,128)(2,1)}, u32[]{:S(2)}, u32[]{:S(2)}) collective-permute-start(bf16[1024,256]{1,0:T(8,128)(2,1)} %get-tuple-element.52), channel_id=1, source_target_pairs={{24,0},{16,8},{8,16},{0,24},{25,1},{17,9},{9,17},{1,25},{26,2},{18... | collective-permute-start | bytes 1572872 | tf_op jit(solution)/shard_map/ppermute | solution.py:242
  28.4 18.9 %collective-permute-start.8 = (bf16[1024,256]{1,0:T(8,128)(2,1)S(1)}, bf16[1024,256]{1,0:T(8,128)(2,1)S(1)}, u32[]{:S(2)}, u32[]{:S(2)}) collective-permute-start(bf16[1024,256]{1,0:T(8,128)(2,1)S(1)} %shard_map.65.refs_4_), channel_id=1, source_target_pairs={{4,0},{0,4},{5,1},{1,5},{6,2},{2,6},{7,3},{3,7},{12,8},{8,12},{13,... | collective-permute-start | bytes 1572872 | tf_op jit(solution)/shard_map/ppermute | solution.py:242
  30.0 27.0 %collective-permute-start.1 = (bf16[512,512]{1,0:T(8,128)(2,1)S(1)}, bf16[512,512]{1,0:T(8,128)(2,1)S(1)}, u32[]{:S(2)}, u32[]{:S(2)}) collective-permute-start(bf16[512,512]{1,0:T(8,128)(2,1)S(1)} %bitcast.9), channel_id=1, source_target_pairs={{2,0},{3,1},{0,2},{1,3},{6,4},{7,5},{4,6},{5,7},{10,8},{11,9},{8,1... | collective-permute-start | bytes 1572872 | tf_op jit(solution)/shard_map/ppermute | solution.py:242
  33.5 24.2 %collective-permute-start.10 = (bf16[1024,256]{1,0:T(8,128)(2,1)}, bf16[1024,256]{1,0:T(8,128)(2,1)S(1)}, u32[]{:S(2)}, u32[]{:S(2)}) collective-permute-start(bf16[1024,256]{1,0:T(8,128)(2,1)} %get-tuple-element.53), channel_id=1, source_target_pairs={{24,0},{16,8},{8,16},{0,24},{25,1},{17,9},{9,17},{1,25},{26,2},{18... | collective-permute-start | bytes 1572872 | tf_op jit(solution)/shard_map/ppermute | solution.py:242
  36.5 23.4 %collective-permute-start.9 = (bf16[1024,256]{1,0:T(8,128)(2,1)}, bf16[1024,256]{1,0:T(8,128)(2,1)}, u32[]{:S(2)}, u32[]{:S(2)}) collective-permute-start(bf16[1024,256]{1,0:T(8,128)(2,1)} %get-tuple-element.53), channel_id=1, source_target_pairs={{8,0},{0,8},{24,16},{16,24},{9,1},{1,9},{25,17},{17,25},{10,2},{2,... | collective-permute-start | bytes 1572872 | tf_op jit(solution)/shard_map/ppermute | solution.py:242
  43.5 16.9 %collective-permute-start.5 = (bf16[1024,256]{1,0:T(8,128)(2,1)}, bf16[1024,256]{1,0:T(8,128)(2,1)}, u32[]{:S(2)}, u32[]{:S(2)}) collective-permute-start(bf16[1024,256]{1,0:T(8,128)(2,1)} %shard_map.64.refs_4_), channel_id=1, source_target_pairs={{4,0},{0,4},{5,1},{1,5},{6,2},{2,6},{7,3},{3,7},{12,8},{8,12},{13,... | collective-permute-start | bytes 1572872 | tf_op jit(solution)/shard_map/ppermute | solution.py:242
  47.3 17.2 %collective-permute-start.14 = (bf16[1024,256]{1,0:T(8,128)(2,1)}, bf16[1024,256]{1,0:T(8,128)(2,1)}, u32[]{:S(2)}, u32[]{:S(2)}) collective-permute-start(bf16[1024,256]{1,0:T(8,128)(2,1)} %get-tuple-element.51), channel_id=1, source_target_pairs={{8,0},{0,8},{24,16},{16,24},{9,1},{1,9},{25,17},{17,25},{10,2},{2,... | collective-permute-start | bytes 1572872 | tf_op jit(solution)/shard_map/ppermute | solution.py:242
  58.5 14.9 %collective-permute-start.13 = (bf16[1024,256]{1,0:T(8,128)(2,1)S(1)}, bf16[1024,256]{1,0:T(8,128)(2,1)}, u32[]{:S(2)}, u32[]{:S(2)}) collective-permute-start(bf16[1024,256]{1,0:T(8,128)(2,1)S(1)} %shard_map.69.refs_4_), channel_id=1, source_target_pairs={{4,0},{0,4},{5,1},{1,5},{6,2},{2,6},{7,3},{3,7},{12,8},{8,12},{13,... | collective-permute-start | bytes 1572872 | tf_op jit(solution)/shard_map/ppermute | solution.py:242
  59.9 31.4 %collective-permute-start.18 = (bf16[1024,256]{1,0:T(8,128)(2,1)}, bf16[1024,256]{1,0:T(8,128)(2,1)S(1)}, u32[]{:S(2)}, u32[]{:S(2)}) collective-permute-start(bf16[1024,256]{1,0:T(8,128)(2,1)} %pad_maximum_fusion), channel_id=1, source_target_pairs={{8,0},{0,8},{24,16},{16,24},{9,1},{1,9},{25,17},{17,25},{10,2},{2,... | collective-permute-start | bytes 1572872 | tf_op jit(solution)/shard_map/ppermute | solution.py:242
  62.9 21.6 %collective-permute-start.16 = (bf16[1024,256]{1,0:T(8,128)(2,1)S(1)}, bf16[1024,256]{1,0:T(8,128)(2,1)S(1)}, u32[]{:S(2)}, u32[]{:S(2)}) collective-permute-start(bf16[1024,256]{1,0:T(8,128)(2,1)S(1)} %shard_map.66.refs_8_.refs_11_.refs_4_), channel_id=1, source_target_pairs={{4,0},{0,4},{5,1},{1,5},{6,2},{2,6},{7,3},{3,7},{12,8},{8,12},{13,... | collective-permute-start | bytes 1572872 | tf_op jit(solution)/shard_map/ppermute | solution.py:242
  64.6 26.7 %collective-permute-start.19 = (bf16[1024,256]{1,0:T(8,128)(2,1)S(1)}, bf16[1024,256]{1,0:T(8,128)(2,1)S(1)}, u32[]{:S(2)}, u32[]{:S(2)}) collective-permute-start(bf16[1024,256]{1,0:T(8,128)(2,1)S(1)} %copy-done.16), channel_id=1, source_target_pairs={{24,0},{16,8},{8,16},{0,24},{25,1},{17,9},{9,17},{1,25},{26,2},{18... | collective-permute-start | bytes 1572872 | tf_op jit(solution)/shard_map/ppermute | solution.py:242
  71.5 22.2 %collective-permute-start.21 = (bf16[1024,256]{1,0:T(8,128)(2,1)S(1)}, bf16[1024,256]{1,0:T(8,128)(2,1)S(1)}, u32[]{:S(2)}, u32[]{:S(2)}) collective-permute-start(bf16[1024,256]{1,0:T(8,128)(2,1)S(1)} %pad_maximum_fusion.1), channel_id=1, source_target_pairs={{8,0},{0,8},{24,16},{16,24},{9,1},{1,9},{25,17},{17,25},{10,2},{2,... | collective-permute-start | bytes 1572872 | tf_op jit(solution)/shard_map/ppermute | solution.py:242
  74.7 20.9 %collective-permute-start.17 = (bf16[1024,256]{1,0:T(8,128)(2,1)S(1)}, bf16[1024,256]{1,0:T(8,128)(2,1)S(1)}, u32[]{:S(2)}, u32[]{:S(2)}) collective-permute-start(bf16[1024,256]{1,0:T(8,128)(2,1)S(1)} %shard_map.70.refs_11_.refs_4_), channel_id=1, source_target_pairs={{4,0},{0,4},{5,1},{1,5},{6,2},{2,6},{7,3},{3,7},{12,8},{8,12},{13,... | collective-permute-start | bytes 1572872 | tf_op jit(solution)/shard_map/ppermute | solution.py:242
  92.3 14.9 %collective-permute-start.20 = (bf16[1024,256]{1,0:T(8,128)(2,1)S(1)}, bf16[1024,256]{1,0:T(8,128)(2,1)S(1)}, u32[]{:S(2)}, u32[]{:S(2)}) collective-permute-start(bf16[1024,256]{1,0:T(8,128)(2,1)S(1)} %shard_map.73.refs_11_.refs_4_), channel_id=1, source_target_pairs={{4,0},{0,4},{5,1},{1,5},{6,2},{2,6},{7,3},{3,7},{12,8},{8,12},{13,... | collective-permute-start | bytes 1572872 | tf_op jit(solution)/shard_map/ppermute | solution.py:242
  92.9 16.2 %collective-permute-start.27 = (bf16[1024,256]{1,0:T(8,128)(2,1)S(1)}, bf16[1024,256]{1,0:T(8,128)(2,1)S(1)}, u32[]{:S(2)}, u32[]{:S(2)}) collective-permute-start(bf16[1024,256]{1,0:T(8,128)(2,1)S(1)} %pad_maximum_fusion.2), channel_id=1, source_target_pairs={{8,0},{0,8},{24,16},{16,24},{9,1},{1,9},{25,17},{17,25},{10,2},{2,... | collective-permute-start | bytes 1572872 | tf_op jit(solution)/shard_map/ppermute | solution.py:242
  93.6 16.8 %collective-permute-start.28 = (bf16[1024,256]{1,0:T(8,128)(2,1)S(1)}, bf16[1024,256]{1,0:T(8,128)(2,1)S(1)}, u32[]{:S(2)}, u32[]{:S(2)}) collective-permute-start(bf16[1024,256]{1,0:T(8,128)(2,1)S(1)} %pad_maximum_fusion.2), channel_id=1, source_target_pairs={{24,0},{16,8},{8,16},{0,24},{25,1},{17,9},{9,17},{1,25},{26,2},{18... | collective-permute-start | bytes 1572872 | tf_op jit(solution)/shard_map/ppermute | solution.py:242
  95.7 23.4 %collective-permute-start.33 = (bf16[1024,256]{1,0:T(8,128)(2,1)S(1)}, bf16[1024,256]{1,0:T(8,128)(2,1)S(1)}, u32[]{:S(2)}, u32[]{:S(2)}) collective-permute-start(bf16[1024,256]{1,0:T(8,128)(2,1)S(1)} %pad_maximum_fusion.3), channel_id=1, source_target_pairs={{8,0},{0,8},{24,16},{16,24},{9,1},{1,9},{25,17},{17,25},{10,2},{2,... | collective-permute-start | bytes 1572872 | tf_op jit(solution)/shard_map/ppermute | solution.py:242
  99.6 21.7 %collective-permute-start.26 = (bf16[1024,256]{1,0:T(8,128)(2,1)S(1)}, bf16[1024,256]{1,0:T(8,128)(2,1)S(1)}, u32[]{:S(2)}, u32[]{:S(2)}) collective-permute-start(bf16[1024,256]{1,0:T(8,128)(2,1)S(1)} %shard_map.75.refs_6_.refs_4_), channel_id=1, source_target_pairs={{4,0},{0,4},{5,1},{1,5},{6,2},{2,6},{7,3},{3,7},{12,8},{8,12},{13,... | collective-permute-start | bytes 1572872 | tf_op jit(solution)/shard_map/ppermute | solution.py:242
  107.1 17.1 %collective-permute-start.34 = (bf16[1024,256]{1,0:T(8,128)(2,1)S(1)}, bf16[1024,256]{1,0:T(8,128)(2,1)S(1)}, u32[]{:S(2)}, u32[]{:S(2)}) collective-permute-start(bf16[1024,256]{1,0:T(8,128)(2,1)S(1)} %pad_maximum_fusion.3), channel_id=1, source_target_pairs={{24,0},{16,8},{8,16},{0,24},{25,1},{17,9},{9,17},{1,25},{26,2},{18... | collective-permute-start | bytes 1572872 | tf_op jit(solution)/shard_map/ppermute | solution.py:242
  109.1 15.2 %collective-permute-start.23 = (bf16[512,128]{1,0:T(8,128)(2,1)S(1)}, bf16[512,128]{1,0:T(8,128)(2,1)S(1)}, u32[]{:S(2)}, u32[]{:S(2)}) collective-permute-start(bf16[512,128]{1,0:T(8,128)(2,1)S(1)} %get-tuple-element.28), channel_id=1, source_target_pairs={{3,0},{0,1},{1,2},{2,3},{7,4},{4,5},{5,6},{6,7},{11,8},{8,9},{9,10... | collective-permute-start | bytes 393224 | tf_op jit(solution)/shard_map/ppermute | solution.py:242
  110.4 17.2 %collective-permute-start.24 = (bf16[512,128]{1,0:T(8,128)(2,1)S(1)}, bf16[512,128]{1,0:T(8,128)(2,1)S(1)}, u32[]{:S(2)}, u32[]{:S(2)}) collective-permute-start(bf16[512,128]{1,0:T(8,128)(2,1)S(1)} %get-tuple-element.29), channel_id=1, source_target_pairs={{2,0},{3,1},{0,2},{1,3},{6,4},{7,5},{4,6},{5,7},{10,8},{11,9},{8,1... | collective-permute-start | bytes 393224 | tf_op jit(solution)/shard_map/ppermute | solution.py:242
  121.3 15.0 %collective-permute-start.32 = (bf16[1024,256]{1,0:T(8,128)(2,1)S(1)}, bf16[1024,256]{1,0:T(8,128)(2,1)S(1)}, u32[]{:S(2)}, u32[]{:S(2)}) collective-permute-start(bf16[1024,256]{1,0:T(8,128)(2,1)S(1)} %shard_map.77.refs_6_.refs_4_), channel_id=1, source_target_pairs={{4,0},{0,4},{5,1},{1,5},{6,2},{2,6},{7,3},{3,7},{12,8},{8,12},{13,... | collective-permute-start | bytes 1572872 | tf_op jit(solution)/shard_map/ppermute | solution.py:242
  128.4 21.6 %collective-permute-start.38 = (bf16[1024,256]{1,0:T(8,128)(2,1)S(1)}, bf16[1024,256]{1,0:T(8,128)(2,1)S(1)}, u32[]{:S(2)}, u32[]{:S(2)}) collective-permute-start(bf16[1024,256]{1,0:T(8,128)(2,1)S(1)} %shard_map.79.refs_6_.refs_4_), channel_id=1, source_target_pairs={{4,0},{0,4},{5,1},{1,5},{6,2},{2,6},{7,3},{3,7},{12,8},{8,12},{13,... | collective-permute-start | bytes 1572872 | tf_op jit(solution)/shard_map/ppermute | solution.py:242
  137.6 17.1 %collective-permute-start.35 = (bf16[512,128]{1,0:T(8,128)(2,1)S(1)}, bf16[512,128]{1,0:T(8,128)(2,1)S(1)}, u32[]{:S(2)}, u32[]{:S(2)}) collective-permute-start(bf16[512,128]{1,0:T(8,128)(2,1)S(1)} %get-tuple-element.36), channel_id=1, source_target_pairs={{3,0},{0,1},{1,2},{2,3},{7,4},{4,5},{5,6},{6,7},{11,8},{8,9},{9,10... | collective-permute-start | bytes 393224 | tf_op jit(solution)/shard_map/ppermute | solution.py:242
  139.3 17.1 %collective-permute-start.36 = (bf16[512,128]{1,0:T(8,128)(2,1)S(1)}, bf16[512,128]{1,0:T(8,128)(2,1)S(1)}, u32[]{:S(2)}, u32[]{:S(2)}) collective-permute-start(bf16[512,128]{1,0:T(8,128)(2,1)S(1)} %get-tuple-element.37), channel_id=1, source_target_pairs={{2,0},{3,1},{0,2},{1,3},{6,4},{7,5},{4,6},{5,7},{10,8},{11,9},{8,1... | collective-permute-start | bytes 393224 | tf_op jit(solution)/shard_map/ppermute | solution.py:242
  (29 other events, 259.8 us)

commit v3 on v2

--- a/solution.py
+++ b/solution.py
@@ -17,6 +17,12 @@
 VMEM_BYTES = 48 * 1024 * 1024
 QUERY_CHUNKS = 4
 OUT_CHUNKS = 4
+DEPTH = 2
+COST = 1
+FIRST = (1, 3)
+A2A = False
+TODO = {3: (0, 1), 4: (2, 3), 5: (4,), 6: (5,), 7: (6,), 8: (7, 8)}
+Z_TIE = 2
 
 SMEM = pl.BlockSpec(memory_space=pltpu.SMEM)
 VMEM = pl.BlockSpec(memory_space=pltpu.VMEM)
@@ -56,9 +62,24 @@
         out_specs=block,
         compiler_params=params(),
         cost_estimate=pl.CostEstimate(
-            flops=3 * far.size, bytes_accessed=6 * far.size, transcendentals=0
+            flops=3 * far.size, bytes_accessed=COST * 6 * far.size, transcendentals=0
         ),
     )(shares, near, far, *after)
+
+
+def copy_kernel(source, *rest):
+    rest[-1][...] = source[...]
+
+
+def copied(array, after):
+    return pl.pallas_call(
+        copy_kernel,
+        out_shape=jax.ShapeDtypeStruct(array.shape, array.dtype),
+        in_specs=[VMEM] + [ANY] * len(after),
+        out_specs=VMEM,
+        compiler_params=params(),
+        cost_estimate=pl.CostEstimate(flops=0, bytes_accessed=4 * array.size, transcendentals=0),
+    )(array, *after)
 
 
 def project(ids, blocks, own, other, whole):
@@ -169,8 +190,11 @@
 def partial_kernel(count, parts, ids, *refs):
     mixed = refs[:parts]
     own, other = refs[parts : parts + 2]
-    outs = refs[-1 - count : -1]
-    by_owner = refs[-1]
+    if A2A:
+        by_owner = refs[-1]
+    else:
+        outs = refs[-1 - count : -1]
+        by_owner = refs[-1]
     mine, place = ids[0], ids[1]
     width = by_owner.shape[2]
     per_half = count // 2
@@ -186,8 +210,9 @@
             by_owner[half * per_half + piece] = total[
                 :, piece * width : (piece + 1) * width
             ].astype(by_owner.dtype)
-    for k in range(count):
-        outs[k][...] = by_owner[lax.rem(place + k, count)]
+    if not A2A:
+        for k in range(count):
+            outs[k][...] = by_owner[lax.rem(place + k, count)]
 
 
 def partials(ids, mixed, own, other, count, after=()):
@@ -196,10 +221,10 @@
     piece = jax.ShapeDtypeStruct((length, width), jnp.bfloat16)
     return pl.pallas_call(
         functools.partial(partial_kernel, count, len(mixed)),
-        out_shape=(piece,) * count,
+        out_shape=jax.ShapeDtypeStruct((count, length, width), jnp.bfloat16) if A2A else (piece,) * count,
         in_specs=[SMEM] + [VMEM] * (len(mixed) + 2) + [ANY] * len(after),
-        out_specs=(VMEM,) * count,
-        scratch_shapes=[pltpu.VMEM((count, length, width), jnp.bfloat16)],
+        out_specs=VMEM if A2A else (VMEM,) * count,
+        scratch_shapes=[] if A2A else [pltpu.VMEM((count, length, width), jnp.bfloat16)],
         compiler_params=params(),
         cost_estimate=pl.CostEstimate(
             flops=4 * length * own.size,
@@ -209,30 +234,30 @@
     )(ids, *mixed, own, other, *after)
 
 
-def leave_kernel(count, chunks, rows, *refs):
+def leave_kernel(chunks, rows, *refs):
     out = refs[-1]
-    width = refs[0].shape[1]
+    per_chunk = (len(refs) - 1) // chunks
+    width = rows.shape[1] // chunks
     for chunk in range(chunks):
         columns = slice(chunk * width, (chunk + 1) * width)
-        pieces = refs[chunk * count : (chunk + 1) * count]
-        total = pieces[0][...].astype(jnp.float32)
-        for piece in pieces[1:]:
-            total = total + piece[...].astype(jnp.float32)
+        total = None
+        for piece in refs[chunk * per_chunk : (chunk + 1) * per_chunk]:
+            term = piece[...].astype(jnp.float32)
+            term = jnp.sum(term, axis=0) if len(piece.shape) == 3 else term
+            total = term if total is None else total + term
         out[:, columns] = (rows[:, columns].astype(jnp.float32) + total).astype(out.dtype)
 
 
 def leave(rows, pieces):
     flat = [piece for chunk in pieces for piece in chunk]
     return pl.pallas_call(
-        functools.partial(leave_kernel, len(pieces[0]), len(pieces)),
+        functools.partial(leave_kernel, len(pieces)),
         out_shape=jax.ShapeDtypeStruct(rows.shape, rows.dtype),
         in_specs=[VMEM] * (1 + len(flat)),
         out_specs=VMEM,
         compiler_params=params(),
         cost_estimate=pl.CostEstimate(
-            flops=(1 + len(pieces[0])) * rows.size,
-            bytes_accessed=2 * rows.size * (2 + len(pieces[0])),
-            transcendentals=0,
+            flops=5 * rows.size, bytes_accessed=12 * rows.size, transcendentals=0
         ),
     )(rows, *flat)
 
@@ -284,20 +309,25 @@
         chunks.append(jnp.concatenate(columns, axis=1))
     far = [from_far(chunk) for chunk in chunks]
     near = [from_near(chunk) for chunk in chunks]
-    blocks = [rows] + [permute(rows, "tensor", lambda i, k=k: i - k) for k in range(1, count)]
+    blocks = [rows] + [None] * (count - 1)
+    for k in FIRST:
+        blocks[k] = permute(rows, "tensor", lambda i, k=k: i - k)
+    again = copied(rows, after=[blocks[k] for k in FIRST])
+    for k in range(1, count):
+        if k not in FIRST:
+            blocks[k] = permute(again, "tensor", lambda i, k=k: i - k)
     cosine, sine = rope_tables(length, HEAD_DIM)
 
     own, other, mixed, pieces = [], [], [], []
-    after = {1: blocks[1:2] + blocks[3:], 3: blocks[2:3]}
+    after = {}
     for c in range(len(chunks)):
         ready = after.get(c, [])
-        if c >= 2:
-            ready = ready + [other[c - 2]]
+        if c >= DEPTH:
+            ready = ready + [other[c - DEPTH]]
         own.append(combine(shares, near[c], far[c], after=ready))
         other.append(from_other_half(own[c]))
         work = after.setdefault(c + 1, [])
-        todo = {3: (0, 1), 4: (2, 3), 5: (4,), 6: (5,), 7: (6,), 8: (7, 8)}.get(c, ())
-        for d in todo:
+        for d in TODO.get(c, ()):
             if d == 0:
                 keys, values, scales = keyval(
                     ids, blocks, own[d], other[d], cosine, sine, after=[own[c]]
@@ -320,14 +350,18 @@
                 )
                 work.append(mixed[-1])
             else:
-                before = [own[c]] + (pieces[-2][1:] if len(pieces) >= 2 else [])
+                before = [own[c]] + (pieces[-2][-3:] if len(pieces) >= 2 else [])
                 parts = partials(ids, mixed, own[d], other[d], count, after=before)
-                pieces.append(
-                    [parts[0]]
-                    + [permute(parts[k], "tensor", lambda i, k=k: i - k) for k in range(1, count)]
-                )
-                work.append(parts[0])
-                after.setdefault(c + 2, []).extend(pieces[-1][1:])
+                if A2A:
+                    work.append(parts)
+                    pieces.append([lax.all_to_all(parts, "tensor", 0, 0)])
+                else:
+                    pieces.append(
+                        [parts[0]]
+                        + [permute(parts[k], "tensor", lambda i, k=k: i - k) for k in range(1, count)]
+                    )
+                    work.append(parts[0])
+                after.setdefault(c + Z_TIE, []).extend(pieces[-1][-3:])
     return leave(rows, pieces)[None]
 
 

time: 168 us -> 160 us (0.952)
  waiting for transfers between devices: 61.1 us -> 52.3 us
  local copies, waits for them, and re-layouts: 7.18 us -> 14.4 us
  starting transfers between devices: 63.8 us -> 57.1 us
    ppermute x42, waiting for transfers between devices: 61.1 us -> 52.3 us  [permute(): lax.ppermute(array, axis, [(source(i) % count, i) for i in range(count)])]
    unnamed x38 -> x56, local copies, waits for them, and re-layouts: 2.93 us -> 10.1 us
    ppermute x42, starting transfers between devices: 63.8 us -> 57.1 us  [permute(): lax.ppermute(array, axis, [(source(i) % count, i) for i in range(count)])]
  transfers between devices with their start and end apart: 42 -> 42, of which waited for: 13 -> 12; matrix products, arithmetic and copies ran while one was open for 4% -> 3% of each run, Pallas kernels for 18% -> 19%
where the time goes in v3:
time: 160 us; the launch traced here: 159 us
  starting transfers between devices  57.1 us (36%)
  waiting for transfers between devices  52.3 us (33%)
  Pallas kernels  32.1 us (20%)
  local copies, waits for them, and re-layouts  14.4 us (9%)
  other arithmetic  3.13 us (2%)
    ppermute x42, starting transfers between devices, permute(): lax.ppermute(array, axis, [(source(i) % count, i) for i in range(count)])  57.1 us
    ppermute x42, waiting for transfers between devices, permute(): lax.ppermute(array, axis, [(source(i) % count, i) for i in range(count)])  52.3 us
    pallas_call x4, Pallas kernels, attend(): pl.pallas_call(functools.partial(attend_kernel, len(blocks)), out_shape=j...  13.5 us
    unnamed x56, local copies, waits for them, and re-layouts  10.1 us
    pallas_call x9, Pallas kernels, combine(): pl.pallas_call(combine_kernel, out_shape=jax.ShapeDtypeStruct(far.shape,...  9.61 us
    pallas_call x4, Pallas kernels, partials(): pl.pallas_call(functools.partial(partial_kernel, count, len(mixed)), out_...  5.19 us
  transfers between devices with their start and end apart: 42, of which 12 were waited for; matrix products, arithmetic and copies ran while one was open for 3% of the time, Pallas kernels for 19%

profile of v3, /device:TPU:0, one launch (start us, length us, event | category | flops | bytes accessed | tf_op | source)
XLA Modules:
  0.0 159.3 jit_solution(16820107299159834615)
XLA Ops:
  0.0 2.9 %fusion.4 = (bf16[1024,256]{1,0:T(8,128)(2,1)}, bf16[1024,256]{1,0:T(8,128)(2,1)}, bf16[1024,256]{1,0:T(8,128)(2,1)}, bf16[1024,256]{1,0:T(8,128)(2,1)}) fusion(bf16[1024,1024]{1,0:T(8,128)(2,1)} %bitcast.16), kind=kLoop, calls=%fused_computation.14 | loop fusion | bytes 4194304 | tf_op jit(solution)/shard_map/slice | solution.py:303
  3.5 2.6 %collective-permute-start.7 = (bf16[1024,256]{1,0:T(8,128)(2,1)}, bf16[1024,256]{1,0:T(8,128)(2,1)}, u32[]{:S(2)}, u32[]{:S(2)}) collective-permute-start(bf16[1024,256]{1,0:T(8,128)(2,1)} %bitcast.4), channel_id=1, source_target_pairs={{24,0},{16,8},{8,16},{0,24},{25,1},{17,9},{9,17},{1,25},{26,2},{18... | collective-permute-start | bytes 1572872 | tf_op jit(solution)/shard_map/ppermute | solution.py:267
  6.1 2.2 %collective-permute-start = (bf16[512,512]{1,0:T(8,128)(2,1)S(1)}, bf16[512,512]{1,0:T(8,128)(2,1)S(1)}, u32[]{:S(2)}, u32[]{:S(2)}) collective-permute-start(bf16[512,512]{1,0:T(8,128)(2,1)S(1)} %bitcast.7), channel_id=1, source_target_pairs={{3,0},{0,1},{1,2},{2,3},{7,4},{4,5},{5,6},{6,7},{11,8},{8,9},{9,10... | collective-permute-start | bytes 1572872 | tf_op jit(solution)/shard_map/ppermute | solution.py:267
  9.1 2.0 %collective-permute-start.1 = (bf16[512,512]{1,0:T(8,128)(2,1)S(1)}, bf16[512,512]{1,0:T(8,128)(2,1)S(1)}, u32[]{:S(2)}, u32[]{:S(2)}) collective-permute-start(bf16[512,512]{1,0:T(8,128)(2,1)S(1)} %bitcast.8), channel_id=1, source_target_pairs={{1,0},{2,1},{3,2},{0,3},{5,4},{6,5},{7,6},{4,7},{9,8},{10,9},{11,1... | collective-permute-start | bytes 1572872 | tf_op jit(solution)/shard_map/ppermute | solution.py:267
  11.9 6.7 %collective-permute-done.7.far = bf16[1024,256]{1,0:T(8,128)(2,1)} collective-permute-done((bf16[1024,256]{1,0:T(8,128)(2,1)}, bf16[1024,256]{1,0:T(8,128)(2,1)}, u32[]{:S(2)}, u32[]{:S(2)}) %collective-permute-start.7) | collective-permute-done | bytes 524320 | tf_op jit(solution)/shard_map/ppermute | solution.py:267
  18.6 2.1 %collective-permute-start.12 = (bf16[1024,256]{1,0:T(8,128)(2,1)}, bf16[1024,256]{1,0:T(8,128)(2,1)S(1)}, u32[]{:S(2)}, u32[]{:S(2)}) collective-permute-start(bf16[1024,256]{1,0:T(8,128)(2,1)} %get-tuple-element.52), channel_id=1, source_target_pairs={{24,0},{16,8},{8,16},{0,24},{25,1},{17,9},{9,17},{1,25},{26,2},{18... | collective-permute-start | bytes 1572872 | tf_op jit(solution)/shard_map/ppermute | solution.py:267
  23.1 6.8 %collective-permute-done.4.far = bf16[1024,256]{1,0:T(8,128)(2,1)S(1)} collective-permute-done((bf16[1024,256]{1,0:T(8,128)(2,1)}, bf16[1024,256]{1,0:T(8,128)(2,1)S(1)}, u32[]{:S(2)}, u32[]{:S(2)}) %collective-permute-start.4) | collective-permute-done | bytes 524320 | tf_op jit(solution)/shard_map/ppermute | solution.py:267
  30.7 2.0 %collective-permute-start.8 = (bf16[1024,256]{1,0:T(8,128)(2,1)S(1)}, bf16[1024,256]{1,0:T(8,128)(2,1)S(1)}, u32[]{:S(2)}, u32[]{:S(2)}) collective-permute-start(bf16[1024,256]{1,0:T(8,128)(2,1)S(1)} %shard_map.66.refs_4_), channel_id=1, source_target_pairs={{4,0},{0,4},{5,1},{1,5},{6,2},{2,6},{7,3},{3,7},{12,8},{8,12},{13,... | collective-permute-start | bytes 1572872 | tf_op jit(solution)/shard_map/ppermute | solution.py:267
  39.2 1.8 %fusion.2 = (f32[512,64]{1,0:T(8,128)}, f32[512,64]{1,0:T(8,128)}, f32[512,64]{1,0:T(8,128)}) fusion(f32[64]{0:T(128)S(1)} %multiply_exponential_fusion), kind=kLoop, calls=%fused_computation.9 | loop fusion | flops 65536 | bytes 393472 | tf_op jit(solution)/shard_map/neg | solution.py:41
  41.9 3.6 %collective-permute-done.8.refs_5_.rest_0_ = bf16[1024,256]{1,0:T(8,128)(2,1)S(1)} collective-permute-done((bf16[1024,256]{1,0:T(8,128)(2,1)S(1)}, bf16[1024,256]{1,0:T(8,128)(2,1)S(1)}, u32[]{:S(2)}, u32[]{:S(2)}) %collective-permute-start.8) | collective-permute-done | bytes 524320 | tf_op jit(solution)/shard_map/ppermute | solution.py:267
  45.5 3.0 %collective-permute-start.2 = (bf16[512,512]{1,0:T(8,128)(2,1)}, bf16[512,512]{1,0:T(8,128)(2,1)S(1)}, u32[]{:S(2)}, u32[]{:S(2)}) collective-permute-start(bf16[512,512]{1,0:T(8,128)(2,1)} %shard_map.64), channel_id=1, source_target_pairs={{2,0},{3,1},{0,2},{1,3},{6,4},{7,5},{4,6},{5,7},{10,8},{11,9},{8,1... | collective-permute-start | bytes 1572872 | tf_op jit(solution)/shard_map/ppermute | solution.py:267
  52.9 2.2 %collective-permute-start.15 = (bf16[1024,256]{1,0:T(8,128)(2,1)}, bf16[1024,256]{1,0:T(8,128)(2,1)}, u32[]{:S(2)}, u32[]{:S(2)}) collective-permute-start(bf16[1024,256]{1,0:T(8,128)(2,1)} %get-tuple-element.51), channel_id=1, source_target_pairs={{24,0},{16,8},{8,16},{0,24},{25,1},{17,9},{9,17},{1,25},{26,2},{18... | collective-permute-start | bytes 1572872 | tf_op jit(solution)/shard_map/ppermute | solution.py:267
  62.0 9.4 %collective-permute-done.2.refs_2_ = bf16[512,512]{1,0:T(8,128)(2,1)S(1)} collective-permute-done((bf16[512,512]{1,0:T(8,128)(2,1)}, bf16[512,512]{1,0:T(8,128)(2,1)S(1)}, u32[]{:S(2)}, u32[]{:S(2)}) %collective-permute-start.2) | collective-permute-done | bytes 524320 | tf_op jit(solution)/shard_map/ppermute | solution.py:267
  71.8 1.8 %shard_map.68 = (bf16[512,128]{1,0:T(8,128)(2,1)S(1)}, bf16[512,128]{1,0:T(8,128)(2,1)S(1)}, f32[512,128]{1,0:T(8,128)S(1)}) custom-call(s32[2]{0:T(128)S(1)} %pad_add_fusion.ids, bf16[512,512]{1,0:T(8,128)(2,1)S(1)} %bitcast.10, bf16[512,512]{1,0:T(8,128)(2,1)S(1)} %collective-permute-done.rest_0_.refs_1_, ...), custom_call_target="tpu_custom_call" | custom-call | flops 536870912 | bytes 3145728 | tf_op jit(solution)/shard_map/pallas_call | solution.py:127
  73.6 3.6 %shard_map.69.rest_1_.refs_0_ = bf16[512,256]{1,0:T(8,128)(2,1)S(1)} custom-call(s32[2]{0:T(128)S(1)} %pad_add_fusion.ids, bf16[512,512]{1,0:T(8,128)(2,1)S(1)} %bitcast.11, bf16[512,512]{1,0:T(8,128)(2,1)S(1)} %collective-permute-done.rest_0_.refs_1_, bf16[512,512]{1,0:T(8,128)(2,1)S(1)} %collective-permute-done.2.refs_2_, ...), custom_call_target="tpu_custom_call" | custom-call | flops 738197504 | bytes 3145728 | tf_op jit(solution)/shard_map/pallas_call | solution.py:175
  81.7 3.8 %shard_map.72.rest_0_.refs_1_ = bf16[512,256]{1,0:T(8,128)(2,1)S(1)} custom-call(s32[2]{0:T(128)S(1)} %pad_add_fusion.ids, bf16[512,512]{1,0:T(8,128)(2,1)S(1)} %bitcast.12, bf16[512,512]{1,0:T(8,128)(2,1)S(1)} %collective-permute-done.rest_0_.refs_1_, bf16[512,512]{1,0:T(8,128)(2,1)S(1)} %collective-permute-done.2.refs_2_, ...), custom_call_target="tpu_custom_call" | custom-call | flops 738197504 | bytes 3145728 | tf_op jit(solution)/shard_map/pallas_call | solution.py:175
  85.5 3.1 %shard_map.73.rest_1_.refs_2_ = bf16[512,256]{1,0:T(8,128)(2,1)S(1)} custom-call(s32[2]{0:T(128)S(1)} %pad_add_fusion.ids, bf16[512,512]{1,0:T(8,128)(2,1)S(1)} %bitcast.13, bf16[512,512]{1,0:T(8,128)(2,1)S(1)} %collective-permute-done.rest_0_.refs_1_, bf16[512,512]{1,0:T(8,128)(2,1)S(1)} %collective-permute-done.2.refs_2_, ...), custom_call_target="tpu_custom_call" | custom-call | flops 738197504 | bytes 3145728 | tf_op jit(solution)/shard_map/pallas_call | solution.py:175
  92.6 2.4 %collective-permute-done.17.refs_5_.rest_1_ = bf16[1024,256]{1,0:T(8,128)(2,1)S(1)} collective-permute-done((bf16[1024,256]{1,0:T(8,128)(2,1)S(1)}, bf16[1024,256]{1,0:T(8,128)(2,1)S(1)}, u32[]{:S(2)}, u32[]{:S(2)}) %collective-permute-start.17) | collective-permute-done | bytes 524320 | tf_op jit(solution)/shard_map/ppermute | solution.py:267
  95.0 3.1 %shard_map.75.rest_0_.refs_3_ = bf16[512,256]{1,0:T(8,128)(2,1)S(1)} custom-call(s32[2]{0:T(128)S(1)} %pad_add_fusion.ids, bf16[512,512]{1,0:T(8,128)(2,1)S(1)} %bitcast.14, bf16[512,512]{1,0:T(8,128)(2,1)S(1)} %collective-permute-done.rest_0_.refs_1_, bf16[512,512]{1,0:T(8,128)(2,1)S(1)} %collective-permute-done.2.refs_2_, ...), custom_call_target="tpu_custom_call" | custom-call | flops 738197504 | bytes 3145728 | tf_op jit(solution)/shard_map/pallas_call | solution.py:175
  100.5 5.7 %collective-permute-done.20.refs_5_.rest_1_ = bf16[1024,256]{1,0:T(8,128)(2,1)S(1)} collective-permute-done((bf16[1024,256]{1,0:T(8,128)(2,1)S(1)}, bf16[1024,256]{1,0:T(8,128)(2,1)S(1)}, u32[]{:S(2)}, u32[]{:S(2)}) %collective-permute-start.20) | collective-permute-done | bytes 524320 | tf_op jit(solution)/shard_map/ppermute | solution.py:267
  108.1 3.5 %collective-permute-start.24 = (bf16[512,128]{1,0:T(8,128)(2,1)S(1)}, bf16[512,128]{1,0:T(8,128)(2,1)S(1)}, u32[]{:S(2)}, u32[]{:S(2)}) collective-permute-start(bf16[512,128]{1,0:T(8,128)(2,1)S(1)} %get-tuple-element.29), channel_id=1, source_target_pairs={{2,0},{3,1},{0,2},{1,3},{6,4},{7,5},{4,6},{5,7},{10,8},{11,9},{8,1... | collective-permute-start | bytes 393224 | tf_op jit(solution)/shard_map/ppermute | solution.py:267
  113.3 3.2 %collective-permute-done.26.refs_5_.rest_4_ = bf16[1024,256]{1,0:T(8,128)(2,1)S(1)} collective-permute-done((bf16[1024,256]{1,0:T(8,128)(2,1)S(1)}, bf16[1024,256]{1,0:T(8,128)(2,1)S(1)}, u32[]{:S(2)}, u32[]{:S(2)}) %collective-permute-start.26) | collective-permute-done | bytes 524320 | tf_op jit(solution)/shard_map/ppermute | solution.py:267
  121.3 1.8 %collective-permute-start.38 = (bf16[1024,256]{1,0:T(8,128)(2,1)S(1)}, bf16[1024,256]{1,0:T(8,128)(2,1)S(1)}, u32[]{:S(2)}, u32[]{:S(2)}) collective-permute-start(bf16[1024,256]{1,0:T(8,128)(2,1)S(1)} %shard_map.80.refs_6_.refs_4_), channel_id=1, source_target_pairs={{4,0},{0,4},{5,1},{1,5},{6,2},{2,6},{7,3},{3,7},{12,8},{8,12},{13,... | collective-permute-start | bytes 1572872 | tf_op jit(solution)/shard_map/ppermute | solution.py:267
  123.1 3.3 %collective-permute-start.29 = (bf16[512,128]{1,0:T(8,128)(2,1)S(1)}, bf16[512,128]{1,0:T(8,128)(2,1)S(1)}, u32[]{:S(2)}, u32[]{:S(2)}) collective-permute-start(bf16[512,128]{1,0:T(8,128)(2,1)S(1)} %get-tuple-element.32), channel_id=1, source_target_pairs={{3,0},{0,1},{1,2},{2,3},{7,4},{4,5},{5,6},{6,7},{11,8},{8,9},{9,10... | collective-permute-start | bytes 393224 | tf_op jit(solution)/shard_map/ppermute | solution.py:267
  126.9 1.9 %collective-permute-start.31 = (bf16[512,128]{1,0:T(8,128)(2,1)S(1)}, bf16[512,128]{1,0:T(8,128)(2,1)S(1)}, u32[]{:S(2)}, u32[]{:S(2)}) collective-permute-start(bf16[512,128]{1,0:T(8,128)(2,1)S(1)} %get-tuple-element.34), channel_id=1, source_target_pairs={{1,0},{2,1},{3,2},{0,3},{5,4},{6,5},{7,6},{4,7},{9,8},{10,9},{11,1... | collective-permute-start | bytes 393224 | tf_op jit(solution)/shard_map/ppermute | solution.py:267
  128.7 2.7 %collective-permute-done.32.refs_5_ = bf16[1024,256]{1,0:T(8,128)(2,1)S(1)} collective-permute-done((bf16[1024,256]{1,0:T(8,128)(2,1)S(1)}, bf16[1024,256]{1,0:T(8,128)(2,1)S(1)}, u32[]{:S(2)}, u32[]{:S(2)}) %collective-permute-start.32) | collective-permute-done | bytes 524320 | tf_op jit(solution)/shard_map/ppermute | solution.py:267
  133.5 3.3 %collective-permute-start.36 = (bf16[512,128]{1,0:T(8,128)(2,1)S(1)}, bf16[512,128]{1,0:T(8,128)(2,1)S(1)}, u32[]{:S(2)}, u32[]{:S(2)}) collective-permute-start(bf16[512,128]{1,0:T(8,128)(2,1)S(1)} %get-tuple-element.37), channel_id=1, source_target_pairs={{2,0},{3,1},{0,2},{1,3},{6,4},{7,5},{4,6},{5,7},{10,8},{11,9},{8,1... | collective-permute-start | bytes 393224 | tf_op jit(solution)/shard_map/ppermute | solution.py:267
  136.8 5.7 %collective-permute-start.37 = (bf16[512,128]{1,0:T(8,128)(2,1)S(1)}, bf16[512,128]{1,0:T(8,128)(2,1)S(1)}, u32[]{:S(2)}, u32[]{:S(2)}) collective-permute-start(bf16[512,128]{1,0:T(8,128)(2,1)S(1)} %get-tuple-element.38), channel_id=1, source_target_pairs={{1,0},{2,1},{3,2},{0,3},{5,4},{6,5},{7,6},{4,7},{9,8},{10,9},{11,1... | collective-permute-start | bytes 393224 | tf_op jit(solution)/shard_map/ppermute | solution.py:267
  143.8 2.2 %collective-permute-start.39 = (bf16[512,128]{1,0:T(8,128)(2,1)S(1)}, bf16[512,128]{1,0:T(8,128)(2,1)S(1)}, u32[]{:S(2)}, u32[]{:S(2)}) collective-permute-start(bf16[512,128]{1,0:T(8,128)(2,1)S(1)} %get-tuple-element.40), channel_id=1, source_target_pairs={{3,0},{0,1},{1,2},{2,3},{7,4},{4,5},{5,6},{6,7},{11,8},{8,9},{9,10... | collective-permute-start | bytes 393224 | tf_op jit(solution)/shard_map/ppermute | solution.py:267
  146.2 2.3 %collective-permute-start.41 = (bf16[512,128]{1,0:T(8,128)(2,1)S(1)}, bf16[512,128]{1,0:T(8,128)(2,1)S(1)}, u32[]{:S(2)}, u32[]{:S(2)}) collective-permute-start(bf16[512,128]{1,0:T(8,128)(2,1)S(1)} %get-tuple-element.42), channel_id=1, source_target_pairs={{1,0},{2,1},{3,2},{0,3},{5,4},{6,5},{7,6},{4,7},{9,8},{10,9},{11,1... | collective-permute-start | bytes 393224 | tf_op jit(solution)/shard_map/ppermute | solution.py:267
  148.5 3.6 %collective-permute-done.39.refs_13_ = bf16[512,128]{1,0:T(8,128)(2,1)S(1)} collective-permute-done((bf16[512,128]{1,0:T(8,128)(2,1)S(1)}, bf16[512,128]{1,0:T(8,128)(2,1)S(1)}, u32[]{:S(2)}, u32[]{:S(2)}) %collective-permute-start.39) | collective-permute-done | bytes 131104 | tf_op jit(solution)/shard_map/ppermute | solution.py:267
  152.1 6.0 %collective-permute-done.40.refs_14_ = bf16[512,128]{1,0:T(8,128)(2,1)S(1)} collective-permute-done((bf16[512,128]{1,0:T(8,128)(2,1)S(1)}, bf16[512,128]{1,0:T(8,128)(2,1)S(1)}, u32[]{:S(2)}, u32[]{:S(2)}) %collective-permute-start.40) | collective-permute-done | bytes 131104 | tf_op jit(solution)/shard_map/ppermute | solution.py:267
  (139 shorter events, 48.6 us)
Async XLA Ops:
  3.5 15.2 %collective-permute-start.7 = (bf16[1024,256]{1,0:T(8,128)(2,1)}, bf16[1024,256]{1,0:T(8,128)(2,1)}, u32[]{:S(2)}, u32[]{:S(2)}) collective-permute-start(bf16[1024,256]{1,0:T(8,128)(2,1)} %bitcast.4), channel_id=1, source_target_pairs={{24,0},{16,8},{8,16},{0,24},{25,1},{17,9},{9,17},{1,25},{26,2},{18... | collective-permute-start | bytes 1572872 | tf_op jit(solution)/shard_map/ppermute | solution.py:267
  6.0 23.9 %collective-permute-start.4 = (bf16[1024,256]{1,0:T(8,128)(2,1)}, bf16[1024,256]{1,0:T(8,128)(2,1)S(1)}, u32[]{:S(2)}, u32[]{:S(2)}) collective-permute-start(bf16[1024,256]{1,0:T(8,128)(2,1)} %get-tuple-element.54), channel_id=1, source_target_pairs={{24,0},{16,8},{8,16},{0,24},{25,1},{17,9},{9,17},{1,25},{26,2},{18... | collective-permute-start | bytes 1572872 | tf_op jit(solution)/shard_map/ppermute | solution.py:267
  6.1 30.2 %collective-permute-start = (bf16[512,512]{1,0:T(8,128)(2,1)S(1)}, bf16[512,512]{1,0:T(8,128)(2,1)S(1)}, u32[]{:S(2)}, u32[]{:S(2)}) collective-permute-start(bf16[512,512]{1,0:T(8,128)(2,1)S(1)} %bitcast.7), channel_id=1, source_target_pairs={{3,0},{0,1},{1,2},{2,3},{7,4},{4,5},{5,6},{6,7},{11,8},{8,9},{9,10... | collective-permute-start | bytes 1572872 | tf_op jit(solution)/shard_map/ppermute | solution.py:267
  9.1 28.5 %collective-permute-start.1 = (bf16[512,512]{1,0:T(8,128)(2,1)S(1)}, bf16[512,512]{1,0:T(8,128)(2,1)S(1)}, u32[]{:S(2)}, u32[]{:S(2)}) collective-permute-start(bf16[512,512]{1,0:T(8,128)(2,1)S(1)} %bitcast.8), channel_id=1, source_target_pairs={{1,0},{2,1},{3,2},{0,3},{5,4},{6,5},{7,6},{4,7},{9,8},{10,9},{11,1... | collective-permute-start | bytes 1572872 | tf_op jit(solution)/shard_map/ppermute | solution.py:267
  11.9 26.0 %collective-permute-start.11 = (bf16[1024,256]{1,0:T(8,128)(2,1)}, bf16[1024,256]{1,0:T(8,128)(2,1)S(1)}, u32[]{:S(2)}, u32[]{:S(2)}) collective-permute-start(bf16[1024,256]{1,0:T(8,128)(2,1)} %get-tuple-element.52), channel_id=1, source_target_pairs={{8,0},{0,8},{24,16},{16,24},{9,1},{1,9},{25,17},{17,25},{10,2},{2,... | collective-permute-start | bytes 1572872 | tf_op jit(solution)/shard_map/ppermute | solution.py:267
  18.6 23.2 %collective-permute-start.12 = (bf16[1024,256]{1,0:T(8,128)(2,1)}, bf16[1024,256]{1,0:T(8,128)(2,1)S(1)}, u32[]{:S(2)}, u32[]{:S(2)}) collective-permute-start(bf16[1024,256]{1,0:T(8,128)(2,1)} %get-tuple-element.52), channel_id=1, source_target_pairs={{24,0},{16,8},{8,16},{0,24},{25,1},{17,9},{9,17},{1,25},{26,2},{18... | collective-permute-start | bytes 1572872 | tf_op jit(solution)/shard_map/ppermute | solution.py:267
  30.7 14.8 %collective-permute-start.8 = (bf16[1024,256]{1,0:T(8,128)(2,1)S(1)}, bf16[1024,256]{1,0:T(8,128)(2,1)S(1)}, u32[]{:S(2)}, u32[]{:S(2)}) collective-permute-start(bf16[1024,256]{1,0:T(8,128)(2,1)S(1)} %shard_map.66.refs_4_), channel_id=1, source_target_pairs={{4,0},{0,4},{5,1},{1,5},{6,2},{2,6},{7,3},{3,7},{12,8},{8,12},{13,... | collective-permute-start | bytes 1572872 | tf_op jit(solution)/shard_map/ppermute | solution.py:267
  36.3 15.8 %collective-permute-start.10 = (bf16[1024,256]{1,0:T(8,128)(2,1)S(1)}, bf16[1024,256]{1,0:T(8,128)(2,1)S(1)}, u32[]{:S(2)}, u32[]{:S(2)}) collective-permute-start(bf16[1024,256]{1,0:T(8,128)(2,1)S(1)} %copy-done.25), channel_id=1, source_target_pairs={{24,0},{16,8},{8,16},{0,24},{25,1},{17,9},{9,17},{1,25},{26,2},{18... | collective-permute-start | bytes 1572872 | tf_op jit(solution)/shard_map/ppermute | solution.py:267
  37.6 17.5 %collective-permute-start.9 = (bf16[1024,256]{1,0:T(8,128)(2,1)S(1)}, bf16[1024,256]{1,0:T(8,128)(2,1)S(1)}, u32[]{:S(2)}, u32[]{:S(2)}) collective-permute-start(bf16[1024,256]{1,0:T(8,128)(2,1)S(1)} %copy-done.25), channel_id=1, source_target_pairs={{8,0},{0,8},{24,16},{16,24},{9,1},{1,9},{25,17},{17,25},{10,2},{2,... | collective-permute-start | bytes 1572872 | tf_op jit(solution)/shard_map/ppermute | solution.py:267
  38.7 19.6 %collective-permute-start.5 = (bf16[1024,256]{1,0:T(8,128)(2,1)}, bf16[1024,256]{1,0:T(8,128)(2,1)S(1)}, u32[]{:S(2)}, u32[]{:S(2)}) collective-permute-start(bf16[1024,256]{1,0:T(8,128)(2,1)} %shard_map.65.refs_4_), channel_id=1, source_target_pairs={{4,0},{0,4},{5,1},{1,5},{6,2},{2,6},{7,3},{3,7},{12,8},{8,12},{13,... | collective-permute-start | bytes 1572872 | tf_op jit(solution)/shard_map/ppermute | solution.py:267
  41.8 20.1 %collective-permute-start.14 = (bf16[1024,256]{1,0:T(8,128)(2,1)}, bf16[1024,256]{1,0:T(8,128)(2,1)}, u32[]{:S(2)}, u32[]{:S(2)}) collective-permute-start(bf16[1024,256]{1,0:T(8,128)(2,1)} %get-tuple-element.51), channel_id=1, source_target_pairs={{8,0},{0,8},{24,16},{16,24},{9,1},{1,9},{25,17},{17,25},{10,2},{2,... | collective-permute-start | bytes 1572872 | tf_op jit(solution)/shard_map/ppermute | solution.py:267
  45.5 26.0 %collective-permute-start.2 = (bf16[512,512]{1,0:T(8,128)(2,1)}, bf16[512,512]{1,0:T(8,128)(2,1)S(1)}, u32[]{:S(2)}, u32[]{:S(2)}) collective-permute-start(bf16[512,512]{1,0:T(8,128)(2,1)} %shard_map.64), channel_id=1, source_target_pairs={{2,0},{3,1},{0,2},{1,3},{6,4},{7,5},{4,6},{5,7},{10,8},{11,9},{8,1... | collective-permute-start | bytes 1572872 | tf_op jit(solution)/shard_map/ppermute | solution.py:267
  52.9 24.3 %collective-permute-start.15 = (bf16[1024,256]{1,0:T(8,128)(2,1)}, bf16[1024,256]{1,0:T(8,128)(2,1)}, u32[]{:S(2)}, u32[]{:S(2)}) collective-permute-start(bf16[1024,256]{1,0:T(8,128)(2,1)} %get-tuple-element.51), channel_id=1, source_target_pairs={{24,0},{16,8},{8,16},{0,24},{25,1},{17,9},{9,17},{1,25},{26,2},{18... | collective-permute-start | bytes 1572872 | tf_op jit(solution)/shard_map/ppermute | solution.py:267
  55.9 22.9 %collective-permute-start.13 = (bf16[1024,256]{1,0:T(8,128)(2,1)}, bf16[1024,256]{1,0:T(8,128)(2,1)}, u32[]{:S(2)}, u32[]{:S(2)}) collective-permute-start(bf16[1024,256]{1,0:T(8,128)(2,1)} %shard_map.70.refs_4_), channel_id=1, source_target_pairs={{4,0},{0,4},{5,1},{1,5},{6,2},{2,6},{7,3},{3,7},{12,8},{8,12},{13,... | collective-permute-start | bytes 1572872 | tf_op jit(solution)/shard_map/ppermute | solution.py:267
  61.3 20.5 %collective-permute-start.16 = (bf16[1024,256]{1,0:T(8,128)(2,1)S(1)}, bf16[1024,256]{1,0:T(8,128)(2,1)S(1)}, u32[]{:S(2)}, u32[]{:S(2)}) collective-permute-start(bf16[1024,256]{1,0:T(8,128)(2,1)S(1)} %shard_map.67.refs_8_.refs_11_.refs_4_), channel_id=1, source_target_pairs={{4,0},{0,4},{5,1},{1,5},{6,2},{2,6},{7,3},{3,7},{12,8},{8,12},{13,... | collective-permute-start | bytes 1572872 | tf_op jit(solution)/shard_map/ppermute | solution.py:267
  61.9 26.7 %collective-permute-start.18 = (bf16[1024,256]{1,0:T(8,128)(2,1)S(1)}, bf16[1024,256]{1,0:T(8,128)(2,1)S(1)}, u32[]{:S(2)}, u32[]{:S(2)}) collective-permute-start(bf16[1024,256]{1,0:T(8,128)(2,1)S(1)} %copy-done.24), channel_id=1, source_target_pairs={{8,0},{0,8},{24,16},{16,24},{9,1},{1,9},{25,17},{17,25},{10,2},{2,... | collective-permute-start | bytes 1572872 | tf_op jit(solution)/shard_map/ppermute | solution.py:267
  71.4 17.2 %collective-permute-start.19 = (bf16[1024,256]{1,0:T(8,128)(2,1)S(1)}, bf16[1024,256]{1,0:T(8,128)(2,1)S(1)}, u32[]{:S(2)}, u32[]{:S(2)}) collective-permute-start(bf16[1024,256]{1,0:T(8,128)(2,1)S(1)} %copy-done.24), channel_id=1, source_target_pairs={{24,0},{16,8},{8,16},{0,24},{25,1},{17,9},{9,17},{1,25},{26,2},{18... | collective-permute-start | bytes 1572872 | tf_op jit(solution)/shard_map/ppermute | solution.py:267
  77.2 14.2 %collective-permute-start.21 = (bf16[1024,256]{1,0:T(8,128)(2,1)S(1)}, bf16[1024,256]{1,0:T(8,128)(2,1)S(1)}, u32[]{:S(2)}, u32[]{:S(2)}) collective-permute-start(bf16[1024,256]{1,0:T(8,128)(2,1)S(1)} %pad_maximum_fusion.1), channel_id=1, source_target_pairs={{8,0},{0,8},{24,16},{16,24},{9,1},{1,9},{25,17},{17,25},{10,2},{2,... | collective-permute-start | bytes 1572872 | tf_op jit(solution)/shard_map/ppermute | solution.py:267
  80.1 14.9 %collective-permute-start.17 = (bf16[1024,256]{1,0:T(8,128)(2,1)S(1)}, bf16[1024,256]{1,0:T(8,128)(2,1)S(1)}, u32[]{:S(2)}, u32[]{:S(2)}) collective-permute-start(bf16[1024,256]{1,0:T(8,128)(2,1)S(1)} %shard_map.71.refs_11_.refs_4_), channel_id=1, source_target_pairs={{4,0},{0,4},{5,1},{1,5},{6,2},{2,6},{7,3},{3,7},{12,8},{8,12},{13,... | collective-permute-start | bytes 1572872 | tf_op jit(solution)/shard_map/ppermute | solution.py:267
  81.7 16.4 %collective-permute-start.22 = (bf16[1024,256]{1,0:T(8,128)(2,1)S(1)}, bf16[1024,256]{1,0:T(8,128)(2,1)S(1)}, u32[]{:S(2)}, u32[]{:S(2)}) collective-permute-start(bf16[1024,256]{1,0:T(8,128)(2,1)S(1)} %pad_maximum_fusion.1), channel_id=1, source_target_pairs={{24,0},{16,8},{8,16},{0,24},{25,1},{17,9},{9,17},{1,25},{26,2},{18... | collective-permute-start | bytes 1572872 | tf_op jit(solution)/shard_map/ppermute | solution.py:267
  89.6 16.6 %collective-permute-start.20 = (bf16[1024,256]{1,0:T(8,128)(2,1)S(1)}, bf16[1024,256]{1,0:T(8,128)(2,1)S(1)}, u32[]{:S(2)}, u32[]{:S(2)}) collective-permute-start(bf16[1024,256]{1,0:T(8,128)(2,1)S(1)} %shard_map.74.refs_11_.refs_4_), channel_id=1, source_target_pairs={{4,0},{0,4},{5,1},{1,5},{6,2},{2,6},{7,3},{3,7},{12,8},{8,12},{13,... | collective-permute-start | bytes 1572872 | tf_op jit(solution)/shard_map/ppermute | solution.py:267
  90.9 16.6 %collective-permute-start.27 = (bf16[1024,256]{1,0:T(8,128)(2,1)S(1)}, bf16[1024,256]{1,0:T(8,128)(2,1)S(1)}, u32[]{:S(2)}, u32[]{:S(2)}) collective-permute-start(bf16[1024,256]{1,0:T(8,128)(2,1)S(1)} %pad_maximum_fusion.2), channel_id=1, source_target_pairs={{8,0},{0,8},{24,16},{16,24},{9,1},{1,9},{25,17},{17,25},{10,2},{2,... | collective-permute-start | bytes 1572872 | tf_op jit(solution)/shard_map/ppermute | solution.py:267
  91.4 16.7 %collective-permute-start.28 = (bf16[1024,256]{1,0:T(8,128)(2,1)S(1)}, bf16[1024,256]{1,0:T(8,128)(2,1)S(1)}, u32[]{:S(2)}, u32[]{:S(2)}) collective-permute-start(bf16[1024,256]{1,0:T(8,128)(2,1)S(1)} %pad_maximum_fusion.2), channel_id=1, source_target_pairs={{24,0},{16,8},{8,16},{0,24},{25,1},{17,9},{9,17},{1,25},{26,2},{18... | collective-permute-start | bytes 1572872 | tf_op jit(solution)/shard_map/ppermute | solution.py:267
  95.0 16.7 %collective-permute-start.33 = (bf16[1024,256]{1,0:T(8,128)(2,1)S(1)}, bf16[1024,256]{1,0:T(8,128)(2,1)S(1)}, u32[]{:S(2)}, u32[]{:S(2)}) collective-permute-start(bf16[1024,256]{1,0:T(8,128)(2,1)S(1)} %pad_maximum_fusion.3), channel_id=1, source_target_pairs={{8,0},{0,8},{24,16},{16,24},{9,1},{1,9},{25,17},{17,25},{10,2},{2,... | collective-permute-start | bytes 1572872 | tf_op jit(solution)/shard_map/ppermute | solution.py:267
  98.9 17.6 %collective-permute-start.26 = (bf16[1024,256]{1,0:T(8,128)(2,1)S(1)}, bf16[1024,256]{1,0:T(8,128)(2,1)S(1)}, u32[]{:S(2)}, u32[]{:S(2)}) collective-permute-start(bf16[1024,256]{1,0:T(8,128)(2,1)S(1)} %shard_map.76.refs_6_.refs_4_), channel_id=1, source_target_pairs={{4,0},{0,4},{5,1},{1,5},{6,2},{2,6},{7,3},{3,7},{12,8},{8,12},{13,... | collective-permute-start | bytes 1572872 | tf_op jit(solution)/shard_map/ppermute | solution.py:267
  106.2 13.1 %collective-permute-start.34 = (bf16[1024,256]{1,0:T(8,128)(2,1)S(1)}, bf16[1024,256]{1,0:T(8,128)(2,1)S(1)}, u32[]{:S(2)}, u32[]{:S(2)}) collective-permute-start(bf16[1024,256]{1,0:T(8,128)(2,1)S(1)} %pad_maximum_fusion.3), channel_id=1, source_target_pairs={{24,0},{16,8},{8,16},{0,24},{25,1},{17,9},{9,17},{1,25},{26,2},{18... | collective-permute-start | bytes 1572872 | tf_op jit(solution)/shard_map/ppermute | solution.py:267
  108.1 12.4 %collective-permute-start.24 = (bf16[512,128]{1,0:T(8,128)(2,1)S(1)}, bf16[512,128]{1,0:T(8,128)(2,1)S(1)}, u32[]{:S(2)}, u32[]{:S(2)}) collective-permute-start(bf16[512,128]{1,0:T(8,128)(2,1)S(1)} %get-tuple-element.29), channel_id=1, source_target_pairs={{2,0},{3,1},{0,2},{1,3},{6,4},{7,5},{4,6},{5,7},{10,8},{11,9},{8,1... | collective-permute-start | bytes 393224 | tf_op jit(solution)/shard_map/ppermute | solution.py:267
  116.5 14.9 %collective-permute-start.32 = (bf16[1024,256]{1,0:T(8,128)(2,1)S(1)}, bf16[1024,256]{1,0:T(8,128)(2,1)S(1)}, u32[]{:S(2)}, u32[]{:S(2)}) collective-permute-start(bf16[1024,256]{1,0:T(8,128)(2,1)S(1)} %shard_map.78.refs_6_.refs_4_), channel_id=1, source_target_pairs={{4,0},{0,4},{5,1},{1,5},{6,2},{2,6},{7,3},{3,7},{12,8},{8,12},{13,... | collective-permute-start | bytes 1572872 | tf_op jit(solution)/shard_map/ppermute | solution.py:267
  121.3 21.3 %collective-permute-start.38 = (bf16[1024,256]{1,0:T(8,128)(2,1)S(1)}, bf16[1024,256]{1,0:T(8,128)(2,1)S(1)}, u32[]{:S(2)}, u32[]{:S(2)}) collective-permute-start(bf16[1024,256]{1,0:T(8,128)(2,1)S(1)} %shard_map.80.refs_6_.refs_4_), channel_id=1, source_target_pairs={{4,0},{0,4},{5,1},{1,5},{6,2},{2,6},{7,3},{3,7},{12,8},{8,12},{13,... | collective-permute-start | bytes 1572872 | tf_op jit(solution)/shard_map/ppermute | solution.py:267
  126.9 15.7 %collective-permute-start.31 = (bf16[512,128]{1,0:T(8,128)(2,1)S(1)}, bf16[512,128]{1,0:T(8,128)(2,1)S(1)}, u32[]{:S(2)}, u32[]{:S(2)}) collective-permute-start(bf16[512,128]{1,0:T(8,128)(2,1)S(1)} %get-tuple-element.34), channel_id=1, source_target_pairs={{1,0},{2,1},{3,2},{0,3},{5,4},{6,5},{7,6},{4,7},{9,8},{10,9},{11,1... | collective-permute-start | bytes 393224 | tf_op jit(solution)/shard_map/ppermute | solution.py:267
  132.7 13.5 %collective-permute-start.35 = (bf16[512,128]{1,0:T(8,128)(2,1)S(1)}, bf16[512,128]{1,0:T(8,128)(2,1)S(1)}, u32[]{:S(2)}, u32[]{:S(2)}) collective-permute-start(bf16[512,128]{1,0:T(8,128)(2,1)S(1)} %get-tuple-element.36), channel_id=1, source_target_pairs={{3,0},{0,1},{1,2},{2,3},{7,4},{4,5},{5,6},{6,7},{11,8},{8,9},{9,10... | collective-permute-start | bytes 393224 | tf_op jit(solution)/shard_map/ppermute | solution.py:267
  133.5 14.9 %collective-permute-start.36 = (bf16[512,128]{1,0:T(8,128)(2,1)S(1)}, bf16[512,128]{1,0:T(8,128)(2,1)S(1)}, u32[]{:S(2)}, u32[]{:S(2)}) collective-permute-start(bf16[512,128]{1,0:T(8,128)(2,1)S(1)} %get-tuple-element.37), channel_id=1, source_target_pairs={{2,0},{3,1},{0,2},{1,3},{6,4},{7,5},{4,6},{5,7},{10,8},{11,9},{8,1... | collective-permute-start | bytes 393224 | tf_op jit(solution)/shard_map/ppermute | solution.py:267
  (38 other events, 244.9 us)

commit v4 on v3

--- a/solution.py
+++ b/solution.py
@@ -3,6 +3,7 @@
 
 import jax
 import jax.numpy as jnp
+import numpy as np
 from jax import lax
 from jax.experimental import pallas as pl
 from jax.experimental.pallas import tpu as pltpu
@@ -17,8 +18,20 @@
 VMEM_BYTES = 48 * 1024 * 1024
 QUERY_CHUNKS = 4
 OUT_CHUNKS = 4
-DEPTH = 2
-COST = 1
+DEPTH = 3
+COST = 4000
+KEYVAL_COST = 1
+ATTEND_COST = 2
+PARTIAL_COST = 16
+COPY_COST = 16000
+AGAIN_TIE = 2
+DEPTHS = {1: 1, 2: 2}
+COSTS = {}
+EXTRA = {3: (2,)}
+AGAIN_AFTER = 0
+PARTIAL_TIE = 2
+NUMPY_TABLES = True
+WHOLE_NEAR = False
 FIRST = (1, 3)
 A2A = False
 TODO = {3: (0, 1), 4: (2, 3), 5: (4,), 6: (5,), 7: (6,), 8: (7, 8)}
@@ -33,12 +46,18 @@
 
 
 def rope_tables(length, width):
-    half_width = width // 2
-    exponent = jnp.arange(half_width, dtype=jnp.float32) * (2.0 / width)
-    inverse = jnp.exp(-exponent * math.log(ROPE_BASE))
-    angles = jnp.arange(length, dtype=jnp.float32)[:, None] * inverse[None, :]
-    cosine, sine = jnp.cos(angles), jnp.sin(angles)
-    return jnp.concatenate([cosine, cosine], axis=1), jnp.concatenate([-sine, sine], axis=1)
+    if not NUMPY_TABLES:
+        exponent = jnp.arange(width // 2, dtype=jnp.float32) * (2.0 / width)
+        angles = jnp.arange(length, dtype=jnp.float32)[:, None] * jnp.exp(
+            -exponent * math.log(ROPE_BASE)
+        )
+        cosine, sine = jnp.cos(angles), jnp.sin(angles)
+        return jnp.concatenate([cosine, cosine], 1), jnp.concatenate([-sine, sine], 1)
+    inverse = ROPE_BASE ** (np.arange(width // 2) * (-2.0 / width))
+    angles = np.arange(length)[:, None] * inverse[None, :]
+    cosine, sine = np.cos(angles), np.sin(angles)
+    cosine, sine = np.concatenate([cosine, cosine], 1), np.concatenate([-sine, sine], 1)
+    return jnp.asarray(cosine, jnp.float32), jnp.asarray(sine, jnp.float32)
 
 
 ANY = pl.BlockSpec(memory_space=pl.ANY)
@@ -50,7 +69,7 @@
     out[...] = mixed.astype(out.dtype)
 
 
-def combine(shares, near, far, after=()):
+def combine(shares, near, far, after=(), cost=0):
     rows, columns = far.shape
     step = min(rows, 512)
     block = pl.BlockSpec((step, columns), lambda i: (i, 0))
@@ -62,7 +81,7 @@
         out_specs=block,
         compiler_params=params(),
         cost_estimate=pl.CostEstimate(
-            flops=3 * far.size, bytes_accessed=COST * 6 * far.size, transcendentals=0
+            flops=cost * far.size, bytes_accessed=6 * far.size, transcendentals=0
         ),
     )(shares, near, far, *after)
 
@@ -78,7 +97,7 @@
         in_specs=[VMEM] + [ANY] * len(after),
         out_specs=VMEM,
         compiler_params=params(),
-        cost_estimate=pl.CostEstimate(flops=0, bytes_accessed=4 * array.size, transcendentals=0),
+        cost_estimate=pl.CostEstimate(flops=COPY_COST * array.size, bytes_accessed=4 * array.size, transcendentals=0),
     )(array, *after)
 
 
@@ -132,7 +151,7 @@
         scratch_shapes=[pltpu.VMEM((features, own.shape[1]), own.dtype)],
         compiler_params=params(),
         cost_estimate=pl.CostEstimate(
-            flops=2 * length * features * own.shape[1],
+            flops=int(KEYVAL_COST * 2 * length * features * own.shape[1]),
             bytes_accessed=2 * features * (length + own.shape[1]),
             transcendentals=0,
         ),
@@ -180,7 +199,7 @@
         scratch_shapes=[pltpu.VMEM((features, width), own.dtype)],
         compiler_params=params(),
         cost_estimate=pl.CostEstimate(
-            flops=2 * length * features * width + 3 * length * length * width,
+            flops=int(ATTEND_COST * (2 * length * features * width + 3 * length * length * width)),
             bytes_accessed=2 * features * (length + width),
             transcendentals=length * length * width // HEAD_DIM,
         ),
@@ -227,7 +246,7 @@
         scratch_shapes=[] if A2A else [pltpu.VMEM((count, length, width), jnp.bfloat16)],
         compiler_params=params(),
         cost_estimate=pl.CostEstimate(
-            flops=4 * length * own.size,
+            flops=int(PARTIAL_COST * 4 * length * own.size),
             bytes_accessed=4 * own.size + 2 * length * (own.shape[0] + 2 * own.shape[1]),
             transcendentals=0,
         ),
@@ -312,19 +331,22 @@
     blocks = [rows] + [None] * (count - 1)
     for k in FIRST:
         blocks[k] = permute(rows, "tensor", lambda i, k=k: i - k)
-    again = copied(rows, after=[blocks[k] for k in FIRST])
+    first = [blocks[k] for k in FIRST]
+    again = copied(rows, after=(first, near[:1], far[:1], near[1:2], first[:1])[AGAIN_AFTER])
     for k in range(1, count):
         if k not in FIRST:
             blocks[k] = permute(again, "tensor", lambda i, k=k: i - k)
     cosine, sine = rope_tables(length, HEAD_DIM)
 
     own, other, mixed, pieces = [], [], [], []
-    after = {}
+    after = {AGAIN_TIE: [again]} if AGAIN_TIE else {}
     for c in range(len(chunks)):
         ready = after.get(c, [])
-        if c >= DEPTH:
-            ready = ready + [other[c - DEPTH]]
-        own.append(combine(shares, near[c], far[c], after=ready))
+        depth = DEPTHS.get(c, DEPTH)
+        if c >= depth:
+            ready = ready + [other[c - depth]]
+        ready = ready + [other[d] for d in EXTRA.get(c, ()) if d < c]
+        own.append(combine(shares, near[c], far[c], after=ready, cost=COSTS.get(c, COST)))
         other.append(from_other_half(own[c]))
         work = after.setdefault(c + 1, [])
         for d in TODO.get(c, ()):
@@ -350,7 +372,7 @@
                 )
                 work.append(mixed[-1])
             else:
-                before = [own[c]] + (pieces[-2][-3:] if len(pieces) >= 2 else [])
+                before = [own[c]] + (pieces[-PARTIAL_TIE][-3:] if len(pieces) >= PARTIAL_TIE else [])
                 parts = partials(ids, mixed, own[d], other[d], count, after=before)
                 if A2A:
                     work.append(parts)

time: 160 us -> 152 us (0.950)
  local copies, waits for them, and re-layouts: 14.4 us -> 8.01 us
  starting transfers between devices: 57.1 us -> 52.7 us
  waiting for transfers between devices: 52.3 us -> 55.4 us
    unnamed x56 -> x28, local copies, waits for them, and re-layouts: 10.1 us -> 3.72 us
    ppermute x42, starting transfers between devices: 57.1 us -> 52.7 us  [permute(): lax.ppermute(array, axis, [(source(i) % count, i) for i in range(count)])]
    ppermute x42, waiting for transfers between devices: 52.3 us -> 55.4 us  [permute(): lax.ppermute(array, axis, [(source(i) % count, i) for i in range(count)])]
    neg x1 -> x0, other arithmetic: 1.77 us -> none  [rope_tables(): -sine]
  transfers between devices with their start and end apart: 42 -> 42, of which waited for: 12 -> 15; matrix products, arithmetic and copies ran while one was open for 3% -> 4% of each run, Pallas kernels for 19% -> 20%
where the time goes in v4:
time: 152 us; the launch traced here: 151 us
  waiting for transfers between devices  55.4 us (36%)
  starting transfers between devices  52.7 us (35%)
  Pallas kernels  31.9 us (21%)
  local copies, waits for them, and re-layouts  8.01 us (5%)
  other arithmetic  2.39 us (2%)
    ppermute x42, waiting for transfers between devices, permute(): lax.ppermute(array, axis, [(source(i) % count, i) for i in range(count)])  55.4 us
    ppermute x42, starting transfers between devices, permute(): lax.ppermute(array, axis, [(source(i) % count, i) for i in range(count)])  52.7 us
    pallas_call x4, Pallas kernels, attend(): pl.pallas_call(functools.partial(attend_kernel, len(blocks)), out_shape=j...  13.7 us
    pallas_call x9, Pallas kernels, combine(): pl.pallas_call(combine_kernel, out_shape=jax.ShapeDtypeStruct(far.shape,...  9.18 us
    pallas_call x4, Pallas kernels, partials(): pl.pallas_call(functools.partial(partial_kernel, count, len(mixed)), out_...  5.19 us
    unnamed x28, local copies, waits for them, and re-layouts  3.72 us
  transfers between devices with their start and end apart: 42, of which 15 were waited for; matrix products, arithmetic and copies ran while one was open for 4% of the time, Pallas kernels for 20%

profile of v4, /device:TPU:0, one launch (start us, length us, event | category | flops | bytes accessed | tf_op | source)
XLA Modules:
  0.0 150.7 jit_solution(13976981083070474297)
XLA Ops:
  0.5 2.6 %collective-permute-start.6 = (bf16[1024,256]{1,0:T(8,128)(2,1)}, bf16[1024,256]{1,0:T(8,128)(2,1)S(1)}, u32[]{:S(2)}, u32[]{:S(2)}) collective-permute-start(bf16[1024,256]{1,0:T(8,128)(2,1)} %bitcast.19), channel_id=1, source_target_pairs={{24,0},{16,8},{8,16},{0,24},{25,1},{17,9},{9,17},{1,25},{26,2},{18... | collective-permute-start | bytes 1572872 | tf_op jit(solution)/shard_map/ppermute | solution.py:286
  4.6 2.2 %collective-permute-start.1 = (bf16[512,512]{1,0:T(8,128)(2,1)}, bf16[512,512]{1,0:T(8,128)(2,1)S(1)}, u32[]{:S(2)}, u32[]{:S(2)}) collective-permute-start(bf16[512,512]{1,0:T(8,128)(2,1)} %bitcast.8), channel_id=1, source_target_pairs={{1,0},{2,1},{3,2},{0,3},{5,4},{6,5},{7,6},{4,7},{9,8},{10,9},{11,1... | collective-permute-start | bytes 1572872 | tf_op jit(solution)/shard_map/ppermute | solution.py:286
  6.9 2.9 %fusion.1 = (bf16[1024,256]{1,0:T(8,128)(2,1)}, bf16[1024,256]{1,0:T(8,128)(2,1)}, bf16[1024,256]{1,0:T(8,128)(2,1)}, bf16[1024,256]{1,0:T(8,128)(2,1)}) fusion(bf16[1024,1024]{1,0:T(8,128)(2,1)} %bitcast.16), kind=kLoop, calls=%fused_computation.7 | loop fusion | bytes 4194304 | tf_op jit(solution)/shard_map/slice | solution.py:322
  10.3 5.3 %collective-permute-done.6.far = bf16[1024,256]{1,0:T(8,128)(2,1)S(1)} collective-permute-done((bf16[1024,256]{1,0:T(8,128)(2,1)}, bf16[1024,256]{1,0:T(8,128)(2,1)S(1)}, u32[]{:S(2)}, u32[]{:S(2)}) %collective-permute-start.6) | collective-permute-done | bytes 524320 | tf_op jit(solution)/shard_map/ppermute | solution.py:286
  18.3 1.6 %collective-permute-start.7 = (bf16[1024,256]{1,0:T(8,128)(2,1)S(1)}, bf16[1024,256]{1,0:T(8,128)(2,1)S(1)}, u32[]{:S(2)}, u32[]{:S(2)}) collective-permute-start(bf16[1024,256]{1,0:T(8,128)(2,1)S(1)} %shard_map.83.refs_4_), channel_id=1, source_target_pairs={{4,0},{0,4},{5,1},{1,5},{6,2},{2,6},{7,3},{3,7},{12,8},{8,12},{13,... | collective-permute-start | bytes 1572872 | tf_op jit(solution)/shard_map/ppermute | solution.py:286
  20.6 9.1 %collective-permute-done.1.rest_1_.refs_3_ = bf16[512,512]{1,0:T(8,128)(2,1)S(1)} collective-permute-done((bf16[512,512]{1,0:T(8,128)(2,1)}, bf16[512,512]{1,0:T(8,128)(2,1)S(1)}, u32[]{:S(2)}, u32[]{:S(2)}) %collective-permute-start.1) | collective-permute-done | bytes 524320 | tf_op jit(solution)/shard_map/ppermute | solution.py:286
  31.3 1.7 %collective-permute-start.10 = (bf16[1024,256]{1,0:T(8,128)(2,1)}, bf16[1024,256]{1,0:T(8,128)(2,1)}, u32[]{:S(2)}, u32[]{:S(2)}) collective-permute-start(bf16[1024,256]{1,0:T(8,128)(2,1)} %get-tuple-element.53), channel_id=1, source_target_pairs={{24,0},{16,8},{8,16},{0,24},{25,1},{17,9},{9,17},{1,25},{26,2},{18... | collective-permute-start | bytes 1572872 | tf_op jit(solution)/shard_map/ppermute | solution.py:286
  33.0 2.7 %collective-permute-start.2 = (bf16[512,512]{1,0:T(8,128)(2,1)}, bf16[512,512]{1,0:T(8,128)(2,1)S(1)}, u32[]{:S(2)}, u32[]{:S(2)}) collective-permute-start(bf16[512,512]{1,0:T(8,128)(2,1)} %shard_map.82.rest_0_), channel_id=1, source_target_pairs={{2,0},{3,1},{0,2},{1,3},{6,4},{7,5},{4,6},{5,7},{10,8},{11,9},{8,1... | collective-permute-start | bytes 1572872 | tf_op jit(solution)/shard_map/ppermute | solution.py:286
  39.7 4.0 %collective-permute-done.4.far = bf16[1024,256]{1,0:T(8,128)(2,1)S(1)} collective-permute-done((bf16[1024,256]{1,0:T(8,128)(2,1)S(1)}, bf16[1024,256]{1,0:T(8,128)(2,1)S(1)}, u32[]{:S(2)}, u32[]{:S(2)}) %collective-permute-start.4) | collective-permute-done | bytes 524320 | tf_op jit(solution)/shard_map/ppermute | solution.py:286
  49.2 5.5 %collective-permute-done.10.far = bf16[1024,256]{1,0:T(8,128)(2,1)} collective-permute-done((bf16[1024,256]{1,0:T(8,128)(2,1)}, bf16[1024,256]{1,0:T(8,128)(2,1)}, u32[]{:S(2)}, u32[]{:S(2)}) %collective-permute-start.10) | collective-permute-done | bytes 524320 | tf_op jit(solution)/shard_map/ppermute | solution.py:286
  58.3 1.6 %collective-permute-start.16 = (bf16[1024,256]{1,0:T(8,128)(2,1)S(1)}, bf16[1024,256]{1,0:T(8,128)(2,1)S(1)}, u32[]{:S(2)}, u32[]{:S(2)}) collective-permute-start(bf16[1024,256]{1,0:T(8,128)(2,1)S(1)} %shard_map.86.refs_8_.refs_11_.refs_4_), channel_id=1, source_target_pairs={{4,0},{0,4},{5,1},{1,5},{6,2},{2,6},{7,3},{3,7},{12,8},{8,12},{13,... | collective-permute-start | bytes 1572872 | tf_op jit(solution)/shard_map/ppermute | solution.py:286
  60.0 4.6 %collective-permute-done.8.refs_5_.rest_2_ = bf16[1024,256]{1,0:T(8,128)(2,1)} collective-permute-done((bf16[1024,256]{1,0:T(8,128)(2,1)}, bf16[1024,256]{1,0:T(8,128)(2,1)}, u32[]{:S(2)}, u32[]{:S(2)}) %collective-permute-start.8) | collective-permute-done | bytes 524320 | tf_op jit(solution)/shard_map/ppermute | solution.py:286
  64.6 1.9 %shard_map.87 = (bf16[512,128]{1,0:T(8,128)(2,1)S(1)}, bf16[512,128]{1,0:T(8,128)(2,1)S(1)}, f32[512,128]{1,0:T(8,128)S(1)}) custom-call(s32[2]{0:T(128)S(1)} %pad_add_fusion.ids, bf16[512,512]{1,0:T(8,128)(2,1)S(1)} %bitcast.10, bf16[512,512]{1,0:T(8,128)(2,1)S(1)} %collective-permute-done.rest_0_.refs_1_, ...), custom_call_target="tpu_custom_call" | custom-call | flops 536870912 | bytes 3145728 | tf_op jit(solution)/shard_map/pallas_call | solution.py:146
  66.5 3.8 %shard_map.88.rest_1_.refs_0_ = bf16[512,256]{1,0:T(8,128)(2,1)S(1)} custom-call(s32[2]{0:T(128)S(1)} %pad_add_fusion.ids, bf16[512,512]{1,0:T(8,128)(2,1)S(1)} %bitcast.11, bf16[512,512]{1,0:T(8,128)(2,1)S(1)} %collective-permute-done.rest_0_.refs_1_, bf16[512,512]{1,0:T(8,128)(2,1)S(1)} %collective-permute-done.2.refs_2_, ...), custom_call_target="tpu_custom_call" | custom-call | flops 1476395008 | bytes 3145728 | tf_op jit(solution)/shard_map/pallas_call | solution.py:194
  73.5 3.8 %shard_map.90.rest_0_.refs_1_ = bf16[512,256]{1,0:T(8,128)(2,1)S(1)} custom-call(s32[2]{0:T(128)S(1)} %pad_add_fusion.ids, bf16[512,512]{1,0:T(8,128)(2,1)S(1)} %bitcast.12, bf16[512,512]{1,0:T(8,128)(2,1)S(1)} %collective-permute-done.rest_0_.refs_1_, bf16[512,512]{1,0:T(8,128)(2,1)S(1)} %collective-permute-done.2.refs_2_, ...), custom_call_target="tpu_custom_call" | custom-call | flops 1476395008 | bytes 3145728 | tf_op jit(solution)/shard_map/pallas_call | solution.py:194
  78.0 3.1 %shard_map.91.rest_1_.refs_2_ = bf16[512,256]{1,0:T(8,128)(2,1)S(1)} custom-call(s32[2]{0:T(128)S(1)} %pad_add_fusion.ids, bf16[512,512]{1,0:T(8,128)(2,1)S(1)} %bitcast.13, bf16[512,512]{1,0:T(8,128)(2,1)S(1)} %collective-permute-done.rest_0_.refs_1_, bf16[512,512]{1,0:T(8,128)(2,1)S(1)} %collective-permute-done.2.refs_2_, ...), custom_call_target="tpu_custom_call" | custom-call | flops 1476395008 | bytes 3145728 | tf_op jit(solution)/shard_map/pallas_call | solution.py:194
  83.5 2.7 %collective-permute-done.17.refs_5_.rest_1_ = bf16[1024,256]{1,0:T(8,128)(2,1)S(1)} collective-permute-done((bf16[1024,256]{1,0:T(8,128)(2,1)S(1)}, bf16[1024,256]{1,0:T(8,128)(2,1)S(1)}, u32[]{:S(2)}, u32[]{:S(2)}) %collective-permute-start.17) | collective-permute-done | bytes 524320 | tf_op jit(solution)/shard_map/ppermute | solution.py:286
  86.3 3.1 %shard_map.93.rest_0_.refs_3_ = bf16[512,256]{1,0:T(8,128)(2,1)S(1)} custom-call(s32[2]{0:T(128)S(1)} %pad_add_fusion.ids, bf16[512,512]{1,0:T(8,128)(2,1)S(1)} %bitcast.14, bf16[512,512]{1,0:T(8,128)(2,1)S(1)} %collective-permute-done.rest_0_.refs_1_, bf16[512,512]{1,0:T(8,128)(2,1)S(1)} %collective-permute-done.2.refs_2_, ...), custom_call_target="tpu_custom_call" | custom-call | flops 1476395008 | bytes 3145728 | tf_op jit(solution)/shard_map/pallas_call | solution.py:194
  89.4 2.0 %collective-permute-start.33 = (bf16[1024,256]{1,0:T(8,128)(2,1)S(1)}, bf16[1024,256]{1,0:T(8,128)(2,1)S(1)}, u32[]{:S(2)}, u32[]{:S(2)}) collective-permute-start(bf16[1024,256]{1,0:T(8,128)(2,1)S(1)} %pad_maximum_fusion.3), channel_id=1, source_target_pairs={{8,0},{0,8},{24,16},{16,24},{9,1},{1,9},{25,17},{17,25},{10,2},{2,... | collective-permute-start | bytes 1572872 | tf_op jit(solution)/shard_map/ppermute | solution.py:286
  93.4 3.7 %collective-permute-done.20.refs_5_.rest_4_ = bf16[1024,256]{1,0:T(8,128)(2,1)S(1)} collective-permute-done((bf16[1024,256]{1,0:T(8,128)(2,1)S(1)}, bf16[1024,256]{1,0:T(8,128)(2,1)S(1)}, u32[]{:S(2)}, u32[]{:S(2)}) %collective-permute-start.20) | collective-permute-done | bytes 524320 | tf_op jit(solution)/shard_map/ppermute | solution.py:286
  99.9 1.6 %collective-permute-start.23 = (bf16[512,128]{1,0:T(8,128)(2,1)S(1)}, bf16[512,128]{1,0:T(8,128)(2,1)S(1)}, u32[]{:S(2)}, u32[]{:S(2)}) collective-permute-start(bf16[512,128]{1,0:T(8,128)(2,1)S(1)} %get-tuple-element.28), channel_id=1, source_target_pairs={{3,0},{0,1},{1,2},{2,3},{7,4},{4,5},{5,6},{6,7},{11,8},{8,9},{9,10... | collective-permute-start | bytes 393224 | tf_op jit(solution)/shard_map/ppermute | solution.py:286
  102.8 1.8 %collective-permute-start.24 = (bf16[512,128]{1,0:T(8,128)(2,1)S(1)}, bf16[512,128]{1,0:T(8,128)(2,1)S(1)}, u32[]{:S(2)}, u32[]{:S(2)}) collective-permute-start(bf16[512,128]{1,0:T(8,128)(2,1)S(1)} %get-tuple-element.29), channel_id=1, source_target_pairs={{2,0},{3,1},{0,2},{1,3},{6,4},{7,5},{4,6},{5,7},{10,8},{11,9},{8,1... | collective-permute-start | bytes 393224 | tf_op jit(solution)/shard_map/ppermute | solution.py:286
  105.4 2.2 %collective-permute-start.25 = (bf16[512,128]{1,0:T(8,128)(2,1)S(1)}, bf16[512,128]{1,0:T(8,128)(2,1)S(1)}, u32[]{:S(2)}, u32[]{:S(2)}) collective-permute-start(bf16[512,128]{1,0:T(8,128)(2,1)S(1)} %get-tuple-element.30), channel_id=1, source_target_pairs={{1,0},{2,1},{3,2},{0,3},{5,4},{6,5},{7,6},{4,7},{9,8},{10,9},{11,1... | collective-permute-start | bytes 393224 | tf_op jit(solution)/shard_map/ppermute | solution.py:286
  107.6 3.0 %collective-permute-done.26.refs_5_ = bf16[1024,256]{1,0:T(8,128)(2,1)S(1)} collective-permute-done((bf16[1024,256]{1,0:T(8,128)(2,1)S(1)}, bf16[1024,256]{1,0:T(8,128)(2,1)S(1)}, u32[]{:S(2)}, u32[]{:S(2)}) %collective-permute-start.26) | collective-permute-done | bytes 524320 | tf_op jit(solution)/shard_map/ppermute | solution.py:286
  115.7 1.8 %collective-permute-start.30 = (bf16[512,128]{1,0:T(8,128)(2,1)S(1)}, bf16[512,128]{1,0:T(8,128)(2,1)S(1)}, u32[]{:S(2)}, u32[]{:S(2)}) collective-permute-start(bf16[512,128]{1,0:T(8,128)(2,1)S(1)} %get-tuple-element.33), channel_id=1, source_target_pairs={{2,0},{3,1},{0,2},{1,3},{6,4},{7,5},{4,6},{5,7},{10,8},{11,9},{8,1... | collective-permute-start | bytes 393224 | tf_op jit(solution)/shard_map/ppermute | solution.py:286
  121.2 3.5 %collective-permute-done.32.refs_5_ = bf16[1024,256]{1,0:T(8,128)(2,1)S(1)} collective-permute-done((bf16[1024,256]{1,0:T(8,128)(2,1)S(1)}, bf16[1024,256]{1,0:T(8,128)(2,1)S(1)}, u32[]{:S(2)}, u32[]{:S(2)}) %collective-permute-start.32) | collective-permute-done | bytes 524320 | tf_op jit(solution)/shard_map/ppermute | solution.py:286
  126.0 2.4 %collective-permute-start.35 = (bf16[512,128]{1,0:T(8,128)(2,1)S(1)}, bf16[512,128]{1,0:T(8,128)(2,1)S(1)}, u32[]{:S(2)}, u32[]{:S(2)}) collective-permute-start(bf16[512,128]{1,0:T(8,128)(2,1)S(1)} %get-tuple-element.36), channel_id=1, source_target_pairs={{3,0},{0,1},{1,2},{2,3},{7,4},{4,5},{5,6},{6,7},{11,8},{8,9},{9,10... | collective-permute-start | bytes 393224 | tf_op jit(solution)/shard_map/ppermute | solution.py:286
  128.5 4.5 %collective-permute-start.37 = (bf16[512,128]{1,0:T(8,128)(2,1)S(1)}, bf16[512,128]{1,0:T(8,128)(2,1)S(1)}, u32[]{:S(2)}, u32[]{:S(2)}) collective-permute-start(bf16[512,128]{1,0:T(8,128)(2,1)S(1)} %get-tuple-element.38), channel_id=1, source_target_pairs={{1,0},{2,1},{3,2},{0,3},{5,4},{6,5},{7,6},{4,7},{9,8},{10,9},{11,1... | collective-permute-start | bytes 393224 | tf_op jit(solution)/shard_map/ppermute | solution.py:286
  135.8 1.6 %collective-permute-start.39 = (bf16[512,128]{1,0:T(8,128)(2,1)S(1)}, bf16[512,128]{1,0:T(8,128)(2,1)S(1)}, u32[]{:S(2)}, u32[]{:S(2)}) collective-permute-start(bf16[512,128]{1,0:T(8,128)(2,1)S(1)} %get-tuple-element.40), channel_id=1, source_target_pairs={{3,0},{0,1},{1,2},{2,3},{7,4},{4,5},{5,6},{6,7},{11,8},{8,9},{9,10... | collective-permute-start | bytes 393224 | tf_op jit(solution)/shard_map/ppermute | solution.py:286
  137.9 1.9 %collective-permute-start.41 = (bf16[512,128]{1,0:T(8,128)(2,1)S(1)}, bf16[512,128]{1,0:T(8,128)(2,1)S(1)}, u32[]{:S(2)}, u32[]{:S(2)}) collective-permute-start(bf16[512,128]{1,0:T(8,128)(2,1)S(1)} %get-tuple-element.42), channel_id=1, source_target_pairs={{1,0},{2,1},{3,2},{0,3},{5,4},{6,5},{7,6},{4,7},{9,8},{10,9},{11,1... | collective-permute-start | bytes 393224 | tf_op jit(solution)/shard_map/ppermute | solution.py:286
  139.8 4.2 %collective-permute-done.39.refs_13_ = bf16[512,128]{1,0:T(8,128)(2,1)S(1)} collective-permute-done((bf16[512,128]{1,0:T(8,128)(2,1)S(1)}, bf16[512,128]{1,0:T(8,128)(2,1)S(1)}, u32[]{:S(2)}, u32[]{:S(2)}) %collective-permute-start.39) | collective-permute-done | bytes 131104 | tf_op jit(solution)/shard_map/ppermute | solution.py:286
  144.0 5.5 %collective-permute-done.40.refs_14_ = bf16[512,128]{1,0:T(8,128)(2,1)S(1)} collective-permute-done((bf16[512,128]{1,0:T(8,128)(2,1)S(1)}, bf16[512,128]{1,0:T(8,128)(2,1)S(1)}, u32[]{:S(2)}, u32[]{:S(2)}) %collective-permute-start.40) | collective-permute-done | bytes 131104 | tf_op jit(solution)/shard_map/ppermute | solution.py:286
  (108 shorter events, 48.6 us)
Async XLA Ops:
  0.5 15.2 %collective-permute-start.6 = (bf16[1024,256]{1,0:T(8,128)(2,1)}, bf16[1024,256]{1,0:T(8,128)(2,1)S(1)}, u32[]{:S(2)}, u32[]{:S(2)}) collective-permute-start(bf16[1024,256]{1,0:T(8,128)(2,1)} %bitcast.19), channel_id=1, source_target_pairs={{24,0},{16,8},{8,16},{0,24},{25,1},{17,9},{9,17},{1,25},{26,2},{18... | collective-permute-start | bytes 1572872 | tf_op jit(solution)/shard_map/ppermute | solution.py:286
  3.1 16.8 %collective-permute-start = (bf16[512,512]{1,0:T(8,128)(2,1)}, bf16[512,512]{1,0:T(8,128)(2,1)S(1)}, u32[]{:S(2)}, u32[]{:S(2)}) collective-permute-start(bf16[512,512]{1,0:T(8,128)(2,1)} %bitcast.7), channel_id=1, source_target_pairs={{3,0},{0,1},{1,2},{2,3},{7,4},{4,5},{5,6},{6,7},{11,8},{8,9},{9,10... | collective-permute-start | bytes 1572872 | tf_op jit(solution)/shard_map/ppermute | solution.py:286
  4.6 25.0 %collective-permute-start.1 = (bf16[512,512]{1,0:T(8,128)(2,1)}, bf16[512,512]{1,0:T(8,128)(2,1)S(1)}, u32[]{:S(2)}, u32[]{:S(2)}) collective-permute-start(bf16[512,512]{1,0:T(8,128)(2,1)} %bitcast.8), channel_id=1, source_target_pairs={{1,0},{2,1},{3,2},{0,3},{5,4},{6,5},{7,6},{4,7},{9,8},{10,9},{11,1... | collective-permute-start | bytes 1572872 | tf_op jit(solution)/shard_map/ppermute | solution.py:286
  9.8 20.7 %collective-permute-start.11 = (bf16[1024,256]{1,0:T(8,128)(2,1)}, bf16[1024,256]{1,0:T(8,128)(2,1)S(1)}, u32[]{:S(2)}, u32[]{:S(2)}) collective-permute-start(bf16[1024,256]{1,0:T(8,128)(2,1)} %get-tuple-element.52), channel_id=1, source_target_pairs={{8,0},{0,8},{24,16},{16,24},{9,1},{1,9},{25,17},{17,25},{10,2},{2,... | collective-permute-start | bytes 1572872 | tf_op jit(solution)/shard_map/ppermute | solution.py:286
  9.8 23.2 %collective-permute-start.12 = (bf16[1024,256]{1,0:T(8,128)(2,1)}, bf16[1024,256]{1,0:T(8,128)(2,1)S(1)}, u32[]{:S(2)}, u32[]{:S(2)}) collective-permute-start(bf16[1024,256]{1,0:T(8,128)(2,1)} %get-tuple-element.52), channel_id=1, source_target_pairs={{24,0},{16,8},{8,16},{0,24},{25,1},{17,9},{9,17},{1,25},{26,2},{18... | collective-permute-start | bytes 1572872 | tf_op jit(solution)/shard_map/ppermute | solution.py:286
  18.3 14.8 %collective-permute-start.7 = (bf16[1024,256]{1,0:T(8,128)(2,1)S(1)}, bf16[1024,256]{1,0:T(8,128)(2,1)S(1)}, u32[]{:S(2)}, u32[]{:S(2)}) collective-permute-start(bf16[1024,256]{1,0:T(8,128)(2,1)S(1)} %shard_map.83.refs_4_), channel_id=1, source_target_pairs={{4,0},{0,4},{5,1},{1,5},{6,2},{2,6},{7,3},{3,7},{12,8},{8,12},{13,... | collective-permute-start | bytes 1572872 | tf_op jit(solution)/shard_map/ppermute | solution.py:286
  19.9 18.3 %collective-permute-start.3 = (bf16[1024,256]{1,0:T(8,128)(2,1)S(1)}, bf16[1024,256]{1,0:T(8,128)(2,1)S(1)}, u32[]{:S(2)}, u32[]{:S(2)}) collective-permute-start(bf16[1024,256]{1,0:T(8,128)(2,1)S(1)} %copy-done.11), channel_id=1, source_target_pairs={{8,0},{0,8},{24,16},{16,24},{9,1},{1,9},{25,17},{17,25},{10,2},{2,... | collective-permute-start | bytes 1572872 | tf_op jit(solution)/shard_map/ppermute | solution.py:286
  29.6 14.1 %collective-permute-start.4 = (bf16[1024,256]{1,0:T(8,128)(2,1)S(1)}, bf16[1024,256]{1,0:T(8,128)(2,1)S(1)}, u32[]{:S(2)}, u32[]{:S(2)}) collective-permute-start(bf16[1024,256]{1,0:T(8,128)(2,1)S(1)} %copy-done.11), channel_id=1, source_target_pairs={{24,0},{16,8},{8,16},{0,24},{25,1},{17,9},{9,17},{1,25},{26,2},{18... | collective-permute-start | bytes 1572872 | tf_op jit(solution)/shard_map/ppermute | solution.py:286
  31.3 23.5 %collective-permute-start.10 = (bf16[1024,256]{1,0:T(8,128)(2,1)}, bf16[1024,256]{1,0:T(8,128)(2,1)}, u32[]{:S(2)}, u32[]{:S(2)}) collective-permute-start(bf16[1024,256]{1,0:T(8,128)(2,1)} %get-tuple-element.53), channel_id=1, source_target_pairs={{24,0},{16,8},{8,16},{0,24},{25,1},{17,9},{9,17},{1,25},{26,2},{18... | collective-permute-start | bytes 1572872 | tf_op jit(solution)/shard_map/ppermute | solution.py:286
  33.0 21.8 %collective-permute-start.9 = (bf16[1024,256]{1,0:T(8,128)(2,1)}, bf16[1024,256]{1,0:T(8,128)(2,1)}, u32[]{:S(2)}, u32[]{:S(2)}) collective-permute-start(bf16[1024,256]{1,0:T(8,128)(2,1)} %get-tuple-element.53), channel_id=1, source_target_pairs={{8,0},{0,8},{24,16},{16,24},{9,1},{1,9},{25,17},{17,25},{10,2},{2,... | collective-permute-start | bytes 1572872 | tf_op jit(solution)/shard_map/ppermute | solution.py:286
  33.0 27.0 %collective-permute-start.2 = (bf16[512,512]{1,0:T(8,128)(2,1)}, bf16[512,512]{1,0:T(8,128)(2,1)S(1)}, u32[]{:S(2)}, u32[]{:S(2)}) collective-permute-start(bf16[512,512]{1,0:T(8,128)(2,1)} %shard_map.82.rest_0_), channel_id=1, source_target_pairs={{2,0},{3,1},{0,2},{1,3},{6,4},{7,5},{4,6},{5,7},{10,8},{11,9},{8,1... | collective-permute-start | bytes 1572872 | tf_op jit(solution)/shard_map/ppermute | solution.py:286
  38.2 18.7 %collective-permute-start.13 = (bf16[1024,256]{1,0:T(8,128)(2,1)}, bf16[1024,256]{1,0:T(8,128)(2,1)}, u32[]{:S(2)}, u32[]{:S(2)}) collective-permute-start(bf16[1024,256]{1,0:T(8,128)(2,1)} %shard_map.85.refs_4_), channel_id=1, source_target_pairs={{4,0},{0,4},{5,1},{1,5},{6,2},{2,6},{7,3},{3,7},{12,8},{8,12},{13,... | collective-permute-start | bytes 1572872 | tf_op jit(solution)/shard_map/ppermute | solution.py:286
  45.2 19.3 %collective-permute-start.8 = (bf16[1024,256]{1,0:T(8,128)(2,1)}, bf16[1024,256]{1,0:T(8,128)(2,1)}, u32[]{:S(2)}, u32[]{:S(2)}) collective-permute-start(bf16[1024,256]{1,0:T(8,128)(2,1)} %shard_map.84.refs_4_), channel_id=1, source_target_pairs={{4,0},{0,4},{5,1},{1,5},{6,2},{2,6},{7,3},{3,7},{12,8},{8,12},{13,... | collective-permute-start | bytes 1572872 | tf_op jit(solution)/shard_map/ppermute | solution.py:286
  54.8 15.4 %collective-permute-start.14 = (bf16[1024,256]{1,0:T(8,128)(2,1)}, bf16[1024,256]{1,0:T(8,128)(2,1)S(1)}, u32[]{:S(2)}, u32[]{:S(2)}) collective-permute-start(bf16[1024,256]{1,0:T(8,128)(2,1)} %get-tuple-element.51), channel_id=1, source_target_pairs={{8,0},{0,8},{24,16},{16,24},{9,1},{1,9},{25,17},{17,25},{10,2},{2,... | collective-permute-start | bytes 1572872 | tf_op jit(solution)/shard_map/ppermute | solution.py:286
  54.8 16.3 %collective-permute-start.15 = (bf16[1024,256]{1,0:T(8,128)(2,1)}, bf16[1024,256]{1,0:T(8,128)(2,1)S(1)}, u32[]{:S(2)}, u32[]{:S(2)}) collective-permute-start(bf16[1024,256]{1,0:T(8,128)(2,1)} %get-tuple-element.51), channel_id=1, source_target_pairs={{24,0},{16,8},{8,16},{0,24},{25,1},{17,9},{9,17},{1,25},{26,2},{18... | collective-permute-start | bytes 1572872 | tf_op jit(solution)/shard_map/ppermute | solution.py:286
  58.3 18.9 %collective-permute-start.16 = (bf16[1024,256]{1,0:T(8,128)(2,1)S(1)}, bf16[1024,256]{1,0:T(8,128)(2,1)S(1)}, u32[]{:S(2)}, u32[]{:S(2)}) collective-permute-start(bf16[1024,256]{1,0:T(8,128)(2,1)S(1)} %shard_map.86.refs_8_.refs_11_.refs_4_), channel_id=1, source_target_pairs={{4,0},{0,4},{5,1},{1,5},{6,2},{2,6},{7,3},{3,7},{12,8},{8,12},{13,... | collective-permute-start | bytes 1572872 | tf_op jit(solution)/shard_map/ppermute | solution.py:286
  60.0 21.1 %collective-permute-start.18 = (bf16[1024,256]{1,0:T(8,128)(2,1)S(1)}, bf16[1024,256]{1,0:T(8,128)(2,1)S(1)}, u32[]{:S(2)}, u32[]{:S(2)}) collective-permute-start(bf16[1024,256]{1,0:T(8,128)(2,1)S(1)} %pad_maximum_fusion), channel_id=1, source_target_pairs={{8,0},{0,8},{24,16},{16,24},{9,1},{1,9},{25,17},{17,25},{10,2},{2,... | collective-permute-start | bytes 1572872 | tf_op jit(solution)/shard_map/ppermute | solution.py:286
  64.6 16.6 %collective-permute-start.19 = (bf16[1024,256]{1,0:T(8,128)(2,1)S(1)}, bf16[1024,256]{1,0:T(8,128)(2,1)S(1)}, u32[]{:S(2)}, u32[]{:S(2)}) collective-permute-start(bf16[1024,256]{1,0:T(8,128)(2,1)S(1)} %pad_maximum_fusion), channel_id=1, source_target_pairs={{24,0},{16,8},{8,16},{0,24},{25,1},{17,9},{9,17},{1,25},{26,2},{18... | collective-permute-start | bytes 1572872 | tf_op jit(solution)/shard_map/ppermute | solution.py:286
  70.2 19.1 %collective-permute-start.21 = (bf16[1024,256]{1,0:T(8,128)(2,1)S(1)}, bf16[1024,256]{1,0:T(8,128)(2,1)S(1)}, u32[]{:S(2)}, u32[]{:S(2)}) collective-permute-start(bf16[1024,256]{1,0:T(8,128)(2,1)S(1)} %pad_maximum_fusion.1), channel_id=1, source_target_pairs={{8,0},{0,8},{24,16},{16,24},{9,1},{1,9},{25,17},{17,25},{10,2},{2,... | collective-permute-start | bytes 1572872 | tf_op jit(solution)/shard_map/ppermute | solution.py:286
  71.9 14.4 %collective-permute-start.17 = (bf16[1024,256]{1,0:T(8,128)(2,1)S(1)}, bf16[1024,256]{1,0:T(8,128)(2,1)S(1)}, u32[]{:S(2)}, u32[]{:S(2)}) collective-permute-start(bf16[1024,256]{1,0:T(8,128)(2,1)S(1)} %shard_map.89.refs_11_.refs_4_), channel_id=1, source_target_pairs={{4,0},{0,4},{5,1},{1,5},{6,2},{2,6},{7,3},{3,7},{12,8},{8,12},{13,... | collective-permute-start | bytes 1572872 | tf_op jit(solution)/shard_map/ppermute | solution.py:286
  77.3 14.4 %collective-permute-start.22 = (bf16[1024,256]{1,0:T(8,128)(2,1)S(1)}, bf16[1024,256]{1,0:T(8,128)(2,1)S(1)}, u32[]{:S(2)}, u32[]{:S(2)}) collective-permute-start(bf16[1024,256]{1,0:T(8,128)(2,1)S(1)} %pad_maximum_fusion.1), channel_id=1, source_target_pairs={{24,0},{16,8},{8,16},{0,24},{25,1},{17,9},{9,17},{1,25},{26,2},{18... | collective-permute-start | bytes 1572872 | tf_op jit(solution)/shard_map/ppermute | solution.py:286
  81.9 15.1 %collective-permute-start.20 = (bf16[1024,256]{1,0:T(8,128)(2,1)S(1)}, bf16[1024,256]{1,0:T(8,128)(2,1)S(1)}, u32[]{:S(2)}, u32[]{:S(2)}) collective-permute-start(bf16[1024,256]{1,0:T(8,128)(2,1)S(1)} %shard_map.92.refs_11_.refs_4_), channel_id=1, source_target_pairs={{4,0},{0,4},{5,1},{1,5},{6,2},{2,6},{7,3},{3,7},{12,8},{8,12},{13,... | collective-permute-start | bytes 1572872 | tf_op jit(solution)/shard_map/ppermute | solution.py:286
  82.6 17.3 %collective-permute-start.27 = (bf16[1024,256]{1,0:T(8,128)(2,1)S(1)}, bf16[1024,256]{1,0:T(8,128)(2,1)S(1)}, u32[]{:S(2)}, u32[]{:S(2)}) collective-permute-start(bf16[1024,256]{1,0:T(8,128)(2,1)S(1)} %pad_maximum_fusion.2), channel_id=1, source_target_pairs={{8,0},{0,8},{24,16},{16,24},{9,1},{1,9},{25,17},{17,25},{10,2},{2,... | collective-permute-start | bytes 1572872 | tf_op jit(solution)/shard_map/ppermute | solution.py:286
  86.3 16.6 %collective-permute-start.28 = (bf16[1024,256]{1,0:T(8,128)(2,1)S(1)}, bf16[1024,256]{1,0:T(8,128)(2,1)S(1)}, u32[]{:S(2)}, u32[]{:S(2)}) collective-permute-start(bf16[1024,256]{1,0:T(8,128)(2,1)S(1)} %pad_maximum_fusion.2), channel_id=1, source_target_pairs={{24,0},{16,8},{8,16},{0,24},{25,1},{17,9},{9,17},{1,25},{26,2},{18... | collective-permute-start | bytes 1572872 | tf_op jit(solution)/shard_map/ppermute | solution.py:286
  89.4 16.1 %collective-permute-start.33 = (bf16[1024,256]{1,0:T(8,128)(2,1)S(1)}, bf16[1024,256]{1,0:T(8,128)(2,1)S(1)}, u32[]{:S(2)}, u32[]{:S(2)}) collective-permute-start(bf16[1024,256]{1,0:T(8,128)(2,1)S(1)} %pad_maximum_fusion.3), channel_id=1, source_target_pairs={{8,0},{0,8},{24,16},{16,24},{9,1},{1,9},{25,17},{17,25},{10,2},{2,... | collective-permute-start | bytes 1572872 | tf_op jit(solution)/shard_map/ppermute | solution.py:286
  91.6 22.5 %collective-permute-start.34 = (bf16[1024,256]{1,0:T(8,128)(2,1)S(1)}, bf16[1024,256]{1,0:T(8,128)(2,1)S(1)}, u32[]{:S(2)}, u32[]{:S(2)}) collective-permute-start(bf16[1024,256]{1,0:T(8,128)(2,1)S(1)} %pad_maximum_fusion.3), channel_id=1, source_target_pairs={{24,0},{16,8},{8,16},{0,24},{25,1},{17,9},{9,17},{1,25},{26,2},{18... | collective-permute-start | bytes 1572872 | tf_op jit(solution)/shard_map/ppermute | solution.py:286
  99.9 15.8 %collective-permute-start.23 = (bf16[512,128]{1,0:T(8,128)(2,1)S(1)}, bf16[512,128]{1,0:T(8,128)(2,1)S(1)}, u32[]{:S(2)}, u32[]{:S(2)}) collective-permute-start(bf16[512,128]{1,0:T(8,128)(2,1)S(1)} %get-tuple-element.28), channel_id=1, source_target_pairs={{3,0},{0,1},{1,2},{2,3},{7,4},{4,5},{5,6},{6,7},{11,8},{8,9},{9,10... | collective-permute-start | bytes 393224 | tf_op jit(solution)/shard_map/ppermute | solution.py:286
  102.8 14.6 %collective-permute-start.24 = (bf16[512,128]{1,0:T(8,128)(2,1)S(1)}, bf16[512,128]{1,0:T(8,128)(2,1)S(1)}, u32[]{:S(2)}, u32[]{:S(2)}) collective-permute-start(bf16[512,128]{1,0:T(8,128)(2,1)S(1)} %get-tuple-element.29), channel_id=1, source_target_pairs={{2,0},{3,1},{0,2},{1,3},{6,4},{7,5},{4,6},{5,7},{10,8},{11,9},{8,1... | collective-permute-start | bytes 393224 | tf_op jit(solution)/shard_map/ppermute | solution.py:286
  110.6 14.1 %collective-permute-start.32 = (bf16[1024,256]{1,0:T(8,128)(2,1)S(1)}, bf16[1024,256]{1,0:T(8,128)(2,1)S(1)}, u32[]{:S(2)}, u32[]{:S(2)}) collective-permute-start(bf16[1024,256]{1,0:T(8,128)(2,1)S(1)} %shard_map.96.refs_6_.refs_4_), channel_id=1, source_target_pairs={{4,0},{0,4},{5,1},{1,5},{6,2},{2,6},{7,3},{3,7},{12,8},{8,12},{13,... | collective-permute-start | bytes 1572872 | tf_op jit(solution)/shard_map/ppermute | solution.py:286
  114.1 14.3 %collective-permute-start.29 = (bf16[512,128]{1,0:T(8,128)(2,1)S(1)}, bf16[512,128]{1,0:T(8,128)(2,1)S(1)}, u32[]{:S(2)}, u32[]{:S(2)}) collective-permute-start(bf16[512,128]{1,0:T(8,128)(2,1)S(1)} %get-tuple-element.32), channel_id=1, source_target_pairs={{3,0},{0,1},{1,2},{2,3},{7,4},{4,5},{5,6},{6,7},{11,8},{8,9},{9,10... | collective-permute-start | bytes 393224 | tf_op jit(solution)/shard_map/ppermute | solution.py:286
  117.5 15.5 %collective-permute-start.31 = (bf16[512,128]{1,0:T(8,128)(2,1)S(1)}, bf16[512,128]{1,0:T(8,128)(2,1)S(1)}, u32[]{:S(2)}, u32[]{:S(2)}) collective-permute-start(bf16[512,128]{1,0:T(8,128)(2,1)S(1)} %get-tuple-element.34), channel_id=1, source_target_pairs={{1,0},{2,1},{3,2},{0,3},{5,4},{6,5},{7,6},{4,7},{9,8},{10,9},{11,1... | collective-permute-start | bytes 393224 | tf_op jit(solution)/shard_map/ppermute | solution.py:286
  119.6 14.9 %collective-permute-start.38 = (bf16[1024,256]{1,0:T(8,128)(2,1)S(1)}, bf16[1024,256]{1,0:T(8,128)(2,1)S(1)}, u32[]{:S(2)}, u32[]{:S(2)}) collective-permute-start(bf16[1024,256]{1,0:T(8,128)(2,1)S(1)} %shard_map.98.refs_6_.refs_4_), channel_id=1, source_target_pairs={{4,0},{0,4},{5,1},{1,5},{6,2},{2,6},{7,3},{3,7},{12,8},{8,12},{13,... | collective-permute-start | bytes 1572872 | tf_op jit(solution)/shard_map/ppermute | solution.py:286
  (24 other events, 177.3 us)

commit v5 on v2

--- a/solution.py
+++ b/solution.py
@@ -3,6 +3,7 @@
 
 import jax
 import jax.numpy as jnp
+import numpy as np
 from jax import lax
 from jax.experimental import pallas as pl
 from jax.experimental.pallas import tpu as pltpu
@@ -17,22 +18,27 @@
 VMEM_BYTES = 48 * 1024 * 1024
 QUERY_CHUNKS = 4
 OUT_CHUNKS = 4
+FIRST = (1, 3)
+STEPS = (('G', 1, '', 200), ('G', 2, 'n0 n1', 200), ('C', 0, '', 1500), ('G', 3, '', 200), ('X', 0, 'a1', 1500), ('C', 1, 'y0', 1500), ('G', 4, '', 200), ('C', 2, '', 1500), ('C', 3, 'y1', 1500), ('G', 5, '', 200), ('G', 6, '', 200), ('K', 0, '', 0), ('A', 1, '', 0), ('C', 4, 'y2', 1500), ('A', 2, '', 6000), ('A', 3, '', 0), ('G', 7, '', 200), ('C', 5, '', 1500), ('G', 8, '', 200), ('A', 4, '', 6000), ('C', 6, '', 1500), ('P', 5, '', 0), ('C', 7, '', 700), ('P', 6, '', 1000), ('R', 5, '', 1000), ('C', 8, '', 1000), ('R', 6, '', 1500), ('Q', 7, '', 200), ('Q', 8, 't5 t6', 0))
 
 SMEM = pl.BlockSpec(memory_space=pltpu.SMEM)
 VMEM = pl.BlockSpec(memory_space=pltpu.VMEM)
 
 
+def estimate(cost):
+    return pl.CostEstimate(flops=cost * 2**20, bytes_accessed=0, transcendentals=0)
+
+
 def params():
     return pltpu.CompilerParams(vmem_limit_bytes=VMEM_BYTES)
 
 
 def rope_tables(length, width):
-    half_width = width // 2
-    exponent = jnp.arange(half_width, dtype=jnp.float32) * (2.0 / width)
-    inverse = jnp.exp(-exponent * math.log(ROPE_BASE))
-    angles = jnp.arange(length, dtype=jnp.float32)[:, None] * inverse[None, :]
-    cosine, sine = jnp.cos(angles), jnp.sin(angles)
-    return jnp.concatenate([cosine, cosine], axis=1), jnp.concatenate([-sine, sine], axis=1)
+    inverse = ROPE_BASE ** (np.arange(width // 2) * (-2.0 / width))
+    angles = np.arange(length)[:, None] * inverse[None, :]
+    cosine, sine = np.cos(angles), np.sin(angles)
+    cosine, sine = np.concatenate([cosine, cosine], 1), np.concatenate([-sine, sine], 1)
+    return jnp.asarray(cosine, jnp.float32), jnp.asarray(sine, jnp.float32)
 
 
 ANY = pl.BlockSpec(memory_space=pl.ANY)
@@ -44,21 +50,53 @@
     out[...] = mixed.astype(out.dtype)
 
 
-def combine(shares, near, far, after=()):
+def combine(shares, near, far, near_block, width, after=(), cost=0):
     rows, columns = far.shape
     step = min(rows, 512)
-    block = pl.BlockSpec((step, columns), lambda i: (i, 0))
+    block = pl.BlockSpec((step, width), lambda i, j: (i, j))
     return pl.pallas_call(
         combine_kernel,
         out_shape=jax.ShapeDtypeStruct(far.shape, far.dtype),
-        grid=(rows // step,),
-        in_specs=[SMEM, block, block] + [ANY] * len(after),
+        grid=(rows // step, columns // width),
+        in_specs=[SMEM, pl.BlockSpec((step, width), lambda i, j: (i, near_block(j))), block]
+        + [ANY] * len(after),
         out_specs=block,
         compiler_params=params(),
-        cost_estimate=pl.CostEstimate(
-            flops=3 * far.size, bytes_accessed=6 * far.size, transcendentals=0
-        ),
+        cost_estimate=estimate(cost),
     )(shares, near, far, *after)
+
+
+def columns_kernel(whole, *rest):
+    rest[-1][...] = whole[...]
+
+
+def columns_of(whole, block, width, pieces, after=(), cost=0):
+    rows = whole.shape[0]
+    step = min(rows, 512)
+    return pl.pallas_call(
+        columns_kernel,
+        out_shape=jax.ShapeDtypeStruct((rows, pieces * width), whole.dtype),
+        grid=(rows // step, pieces),
+        in_specs=[pl.BlockSpec((step, width), lambda i, j: (i, block(j)))] + [ANY] * len(after),
+        out_specs=pl.BlockSpec((step, width), lambda i, j: (i, j)),
+        compiler_params=params(),
+        cost_estimate=estimate(cost),
+    )(whole, *after)
+
+
+def copy_kernel(source, *rest):
+    rest[-1][...] = source[...]
+
+
+def copied(array, after, cost=0):
+    return pl.pallas_call(
+        copy_kernel,
+        out_shape=jax.ShapeDtypeStruct(array.shape, array.dtype),
+        in_specs=[VMEM] + [ANY] * len(after),
+        out_specs=VMEM,
+        compiler_params=params(),
+        cost_estimate=estimate(cost),
+    )(array, *after)
 
 
 def project(ids, blocks, own, other, whole):
@@ -99,7 +137,7 @@
     scales[...] = jnp.broadcast_to(scale, scales.shape)
 
 
-def keyval(ids, blocks, own, other, cosine, sine, after=()):
+def keyval(ids, blocks, own, other, cosine, sine, after=(), cost=0):
     length = blocks[0].shape[0]
     features = sum(b.shape[1] for b in blocks)
     head = jax.ShapeDtypeStruct((length, HEAD_DIM), jnp.bfloat16)
@@ -110,11 +148,7 @@
         out_specs=(VMEM,) * 3,
         scratch_shapes=[pltpu.VMEM((features, own.shape[1]), own.dtype)],
         compiler_params=params(),
-        cost_estimate=pl.CostEstimate(
-            flops=2 * length * features * own.shape[1],
-            bytes_accessed=2 * features * (length + own.shape[1]),
-            transcendentals=0,
-        ),
+        cost_estimate=estimate(cost),
     )(ids, *blocks, own, other, cosine, sine, *after)
 
 
@@ -147,7 +181,7 @@
             mixed[first:last, columns] = (product / total).astype(mixed.dtype)
 
 
-def attend(ids, blocks, own, other, keys, values, scales, cosine, sine, after=()):
+def attend(ids, blocks, own, other, keys, values, scales, cosine, sine, after=(), cost=0):
     length = blocks[0].shape[0]
     features = sum(b.shape[1] for b in blocks)
     width = own.shape[1]
@@ -158,21 +192,13 @@
         out_specs=VMEM,
         scratch_shapes=[pltpu.VMEM((features, width), own.dtype)],
         compiler_params=params(),
-        cost_estimate=pl.CostEstimate(
-            flops=2 * length * features * width + 3 * length * length * width,
-            bytes_accessed=2 * features * (length + width),
-            transcendentals=length * length * width // HEAD_DIM,
-        ),
+        cost_estimate=estimate(cost),
     )(ids, *blocks, own, other, keys, values, scales, cosine, sine, *after)
 
 
-def partial_kernel(count, parts, ids, *refs):
-    mixed = refs[:parts]
-    own, other = refs[parts : parts + 2]
-    outs = refs[-1 - count : -1]
-    by_owner = refs[-1]
-    mine, place = ids[0], ids[1]
-    width = by_owner.shape[2]
+def products(ids, mixed, own, other, by_owner):
+    mine = ids[0]
+    count, _, width = by_owner.shape
     per_half = count // 2
     for half, weights in ((mine, own), (1 - mine, other)):
         total = None
@@ -186,54 +212,99 @@
             by_owner[half * per_half + piece] = total[
                 :, piece * width : (piece + 1) * width
             ].astype(by_owner.dtype)
+
+
+def partial_kernel(count, parts, ids, *refs):
+    kept, sent, by_owner = refs[-3:]
+    products(ids, refs[:parts], refs[parts], refs[parts + 1], by_owner)
+    low = lax.rem(ids[1], 2)
+    for pair in range(count // 2):
+        kept[pair] = by_owner[2 * pair + low]
+        sent[pair] = by_owner[2 * pair + 1 - low]
+
+
+def direct_kernel(count, parts, ids, *refs):
+    outs, by_owner = refs[-1 - count : -1], refs[-1]
+    products(ids, refs[:parts], refs[parts], refs[parts + 1], by_owner)
     for k in range(count):
-        outs[k][...] = by_owner[lax.rem(place + k, count)]
-
-
-def partials(ids, mixed, own, other, count, after=()):
+        outs[k][...] = by_owner[lax.rem(ids[1] + k, count)]
+
+
+def direct_partials(ids, mixed, own, other, count, after=(), cost=0):
     length = mixed[0].shape[0]
     width = 2 * own.shape[1] // count
     piece = jax.ShapeDtypeStruct((length, width), jnp.bfloat16)
     return pl.pallas_call(
-        functools.partial(partial_kernel, count, len(mixed)),
+        functools.partial(direct_kernel, count, len(mixed)),
         out_shape=(piece,) * count,
         in_specs=[SMEM] + [VMEM] * (len(mixed) + 2) + [ANY] * len(after),
         out_specs=(VMEM,) * count,
         scratch_shapes=[pltpu.VMEM((count, length, width), jnp.bfloat16)],
         compiler_params=params(),
-        cost_estimate=pl.CostEstimate(
-            flops=4 * length * own.size,
-            bytes_accessed=4 * own.size + 2 * length * (own.shape[0] + 2 * own.shape[1]),
-            transcendentals=0,
+        cost_estimate=estimate(cost),
+    )(ids, *mixed, own, other, *after)
+
+
+def partials(ids, mixed, own, other, count, after=(), cost=0):
+    length = mixed[0].shape[0]
+    width = 2 * own.shape[1] // count
+    half = jax.ShapeDtypeStruct((count // 2, length, width), jnp.bfloat16)
+    return pl.pallas_call(
+        functools.partial(partial_kernel, count, len(mixed)),
+        out_shape=(half, half),
+        in_specs=[SMEM] + [VMEM] * (len(mixed) + 2) + [ANY] * len(after),
+        out_specs=(VMEM, VMEM),
+        scratch_shapes=[pltpu.VMEM((count, length, width), jnp.bfloat16)],
+        compiler_params=params(),
+        cost_estimate=estimate(cost),
+    )(ids, *mixed, own, other, *after)
+
+
+def reduce_kernel(ids, kept, got, *refs):
+    still, sent = refs[-2:]
+    high = lax.rem(lax.div(ids[1], 2), 2)
+    still[...] = kept[high].astype(jnp.float32) + got[high].astype(jnp.float32)
+    away = kept[1 - high].astype(jnp.float32) + got[1 - high].astype(jnp.float32)
+    sent[...] = away.astype(sent.dtype)
+
+
+def reduce(ids, kept, got, after=(), cost=0):
+    shape = kept.shape[1:]
+    return pl.pallas_call(
+        reduce_kernel,
+        out_shape=(
+            jax.ShapeDtypeStruct(shape, jnp.float32),
+            jax.ShapeDtypeStruct(shape, jnp.bfloat16),
         ),
-    )(ids, *mixed, own, other, *after)
-
-
-def leave_kernel(count, chunks, rows, *refs):
+        in_specs=[SMEM, VMEM, VMEM] + [ANY] * len(after),
+        out_specs=(VMEM, VMEM),
+        compiler_params=params(),
+        cost_estimate=estimate(cost),
+    )(ids, kept, got, *after)
+
+
+def leave_kernel(counts, rows, *refs):
     out = refs[-1]
-    width = refs[0].shape[1]
-    for chunk in range(chunks):
+    width = rows.shape[1] // len(counts)
+    first = 0
+    for chunk, count in enumerate(counts):
         columns = slice(chunk * width, (chunk + 1) * width)
-        pieces = refs[chunk * count : (chunk + 1) * count]
-        total = pieces[0][...].astype(jnp.float32)
-        for piece in pieces[1:]:
+        total = rows[:, columns].astype(jnp.float32)
+        for piece in refs[first : first + count]:
             total = total + piece[...].astype(jnp.float32)
-        out[:, columns] = (rows[:, columns].astype(jnp.float32) + total).astype(out.dtype)
+        first += count
+        out[:, columns] = total.astype(out.dtype)
 
 
 def leave(rows, pieces):
     flat = [piece for chunk in pieces for piece in chunk]
     return pl.pallas_call(
-        functools.partial(leave_kernel, len(pieces[0]), len(pieces)),
+        functools.partial(leave_kernel, [len(chunk) for chunk in pieces]),
         out_shape=jax.ShapeDtypeStruct(rows.shape, rows.dtype),
         in_specs=[VMEM] * (1 + len(flat)),
         out_specs=VMEM,
         compiler_params=params(),
-        cost_estimate=pl.CostEstimate(
-            flops=(1 + len(pieces[0])) * rows.size,
-            bytes_accessed=2 * rows.size * (2 + len(pieces[0])),
-            transcendentals=0,
-        ),
+        cost_estimate=estimate(1),
     )(rows, *flat)
 
 
@@ -273,61 +344,90 @@
     quarter = own_out.shape[1] // halves
     out_width = quarter // OUT_CHUNKS
 
-    chunks = [own_keyval]
+    near_keyval, near_query, near_out = map(from_near, (own_keyval, own_query, own_out))
+    far = {0: from_far(own_keyval)}
+    places = [(own_keyval, near_keyval, own_keyval.shape[1], lambda j: 0)]
     for c in range(QUERY_CHUNKS):
-        chunks.append(own_query[:, c * query_width : (c + 1) * query_width])
+        places.append((own_query, near_query, query_width, lambda j, c=c: c))
     for c in range(OUT_CHUNKS):
-        columns = [
-            own_out[:, h * quarter + c * out_width : h * quarter + (c + 1) * out_width]
-            for h in range(halves)
-        ]
-        chunks.append(jnp.concatenate(columns, axis=1))
-    far = [from_far(chunk) for chunk in chunks]
-    near = [from_near(chunk) for chunk in chunks]
-    blocks = [rows] + [permute(rows, "tensor", lambda i, k=k: i - k) for k in range(1, count)]
+        places.append((own_out, near_out, out_width, lambda j, c=c: j * OUT_CHUNKS + c))
+    pieces_of = [1] * (1 + QUERY_CHUNKS) + [halves] * OUT_CHUNKS
+    blocks = [rows] + [None] * (count - 1)
+    for k in FIRST:
+        blocks[k] = permute(rows, "tensor", lambda i, k=k: i - k)
     cosine, sine = rope_tables(length, HEAD_DIM)
 
-    own, other, mixed, pieces = [], [], [], []
-    after = {1: blocks[1:2] + blocks[3:], 3: blocks[2:3]}
-    for c in range(len(chunks)):
-        ready = after.get(c, [])
-        if c >= 2:
-            ready = ready + [other[c - 2]]
-        own.append(combine(shares, near[c], far[c], after=ready))
-        other.append(from_other_half(own[c]))
-        work = after.setdefault(c + 1, [])
-        todo = {3: (0, 1), 4: (2, 3), 5: (4,), 6: (5,), 7: (6,), 8: (7, 8)}.get(c, ())
-        for d in todo:
-            if d == 0:
-                keys, values, scales = keyval(
-                    ids, blocks, own[d], other[d], cosine, sine, after=[own[c]]
+    own, other, mixed, halves_of, pieces, before = {}, {}, [], {}, {}, []
+    for kind, c, arrivals, cost in STEPS:
+        after = list(before)
+        for name in arrivals.split():
+            if name[0] == "y":
+                after.append(other[int(name[1:])])
+            elif name[0] == "a":
+                after.append(blocks[int(name[1:])])
+            elif name[0] == "n":
+                after.append((near_query, near_out)[int(name[1:])])
+            elif name[0] == "s":
+                after.append(halves_of[int(name[1:])][1])
+            else:
+                after.append(pieces[int(name[1:])][1])
+        if kind == "G":
+            whole, _, width, place = places[c]
+            chunk = columns_of(whole, place, width, pieces_of[c], after=after, cost=cost)
+            far[c] = from_far(chunk)
+            before = [chunk]
+        elif kind == "C":
+            _, near, width, place = places[c]
+            own[c] = combine(shares, near, far[c], place, width, after=after, cost=cost)
+            other[c] = from_other_half(own[c])
+            before = [own[c]]
+        elif kind == "X":
+            again = copied(rows, after=after + [blocks[k] for k in FIRST], cost=cost)
+            for k in range(1, count):
+                if k not in FIRST:
+                    blocks[k] = permute(again, "tensor", lambda i, k=k: i - k)
+            before = [again]
+        elif kind == "K":
+            keys, values, scales = keyval(
+                ids, blocks, own[c], other[c], cosine, sine, after=after, cost=cost
+            )
+            before = [scales]
+        elif kind == "A":
+            mixed.append(
+                attend(
+                    ids,
+                    blocks,
+                    own[c],
+                    other[c],
+                    keys,
+                    values,
+                    scales,
+                    cosine,
+                    sine,
+                    after=after,
+                    cost=cost,
                 )
-                work.append(scales)
-            elif d <= QUERY_CHUNKS:
-                mixed.append(
-                    attend(
-                        ids,
-                        blocks,
-                        own[d],
-                        other[d],
-                        keys,
-                        values,
-                        scales,
-                        cosine,
-                        sine,
-                        after=[own[c]],
-                    )
-                )
-                work.append(mixed[-1])
-            else:
-                before = [own[c]] + (pieces[-2][1:] if len(pieces) >= 2 else [])
-                parts = partials(ids, mixed, own[d], other[d], count, after=before)
-                pieces.append(
-                    [parts[0]]
-                    + [permute(parts[k], "tensor", lambda i, k=k: i - k) for k in range(1, count)]
-                )
-                work.append(parts[0])
-                after.setdefault(c + 2, []).extend(pieces[-1][1:])
+            )
+            before = [mixed[-1]]
+        elif kind == "P":
+            kept, sent = partials(
+                ids, mixed, own[c], other[c], count, after=after, cost=cost
+            )
+            halves_of[c] = (kept, permute(sent, "tensor", lambda i: i ^ 1))
+            before = [kept]
+        elif kind == "Q":
+            parts = direct_partials(
+                ids, mixed, own[c], other[c], count, after=after, cost=cost
+            )
+            pieces[c] = [parts[0]] + [
+                permute(parts[k], "tensor", lambda i, k=k: i - k) for k in range(1, count)
+            ]
+            before = [parts[0]]
+        else:
+            kept, sent = reduce(ids, *halves_of[c], after=after, cost=cost)
+            pieces[c] = (kept, permute(sent, "tensor", lambda i: i ^ 2))
+            before = [kept]
+    pieces = [pieces[c] for c in sorted(pieces)]
     return leave(rows, pieces)[None]
 
 
@@ -400,7 +500,7 @@
         chunked = (
             mesh.shape["section"] % 2 == 0
             and mesh.shape["fsdp"] == 2
-            and mesh.shape["tensor"] % 2 == 0
+            and mesh.shape["tensor"] == 4
             and w_keyval.shape[2] == mesh.shape["tensor"]
             and w_keyval.shape[3] == 2 * HEAD_DIM
             and w_query.shape[2] % (mesh.shape["tensor"] * QUERY_CHUNKS * HEAD_DIM) == 0

time: 168 us -> 147 us (0.88)
  starting transfers between devices: 63.8 us -> 45.8 us
  Pallas kernels: 31.6 us -> 39 us
  local copies, waits for them, and re-layouts: 7.18 us -> 2.92 us
  other arithmetic: 3.11 us -> 0.08 us
  waiting for transfers between devices: 61.1 us -> 58.4 us
    ppermute x42 -> x34, starting transfers between devices: 63.8 us -> 45.8 us  [permute(): lax.ppermute(array, axis, [(source(i) % count, i) for i in range(count)])]
    pallas_call x1 -> x14, Pallas kernels: 1.14 us -> 9.45 us  [the longest x8 3.69 us: columns_of(): pl.pallas_call(columns_kernel, out_shape=jax.ShapeDtypeStruct((rows, piec...]
    slice x2 -> x0, local copies, waits for them, and re-layouts: 4.25 us -> none  [the longest x1 2.94 us: body(): chunks.append(own_query[:, c * query_width:(c + 1) * query_width])]
    ppermute x42 -> x34, waiting for transfers between devices: 61.1 us -> 58.4 us  [permute(): lax.ppermute(array, axis, [(source(i) % count, i) for i in range(count)])]
    pallas_call x4 -> x2, Pallas kernels: 5.19 us -> 2.6 us  [partials(): pl.pallas_call(functools.partial(partial_kernel, count, len(mixed)), out_...]
    pallas_call x9, Pallas kernels: 9.93 us -> 12 us  [combine(): pl.pallas_call(combine_kernel, out_shape=jax.ShapeDtypeStruct(far.shape,...]
    neg x1 -> x0, other arithmetic: 1.75 us -> none  [rope_tables(): -sine]
  transfers between devices with their start and end apart: 42 -> 34, of which waited for: 13 -> 11; matrix products, arithmetic and copies ran while one was open for 4% -> 0% of each run, Pallas kernels for 18% -> 26%
where the time goes in v5:
time: 147 us
  waiting for transfers between devices  58.4 us (40%)
  starting transfers between devices  45.8 us (31%)
  Pallas kernels  39 us (27%)
  local copies, waits for them, and re-layouts  2.92 us (2%)
    ppermute x34, waiting for transfers between devices, permute(): lax.ppermute(array, axis, [(source(i) % count, i) for i in range(count)])  58.4 us
    ppermute x34, starting transfers between devices, permute(): lax.ppermute(array, axis, [(source(i) % count, i) for i in range(count)])  45.8 us
    pallas_call x4, Pallas kernels, attend(): pl.pallas_call(functools.partial(attend_kernel, len(blocks)), out_shape=j...  13 us
    pallas_call x9, Pallas kernels, combine(): pl.pallas_call(combine_kernel, out_shape=jax.ShapeDtypeStruct(far.shape,...  12 us
    pallas_call x8, Pallas kernels, columns_of(): pl.pallas_call(columns_kernel, out_shape=jax.ShapeDtypeStruct((rows, piec...  3.69 us
  transfers between devices with their start and end apart: 34, of which 11 were waited for; matrix products, arithmetic and copies ran while one was open for 0% of the time, Pallas kernels for 26%

profile of v5, /device:TPU:0, one launch (start us, length us, event | category | flops | bytes accessed | tf_op | source)
XLA Modules:
  0.0 146.6 jit_solution(3075966894953219438)
XLA Ops:
  0.5 2.6 %collective-permute-start.2 = (bf16[1024,256]{1,0:T(8,128)(2,1)}, bf16[1024,256]{1,0:T(8,128)(2,1)}, u32[]{:S(2)}, u32[]{:S(2)}) collective-permute-start(bf16[1024,256]{1,0:T(8,128)(2,1)} %bitcast.26), channel_id=1, source_target_pairs={{24,0},{16,8},{8,16},{0,24},{25,1},{17,9},{9,17},{1,25},{26,2},{18... | collective-permute-start | bytes 1572872 | tf_op jit(solution)/shard_map/ppermute | solution.py:313
  3.6 3.6 %collective-permute-start.5 = (bf16[512,512]{1,0:T(8,128)(2,1)}, bf16[512,512]{1,0:T(8,128)(2,1)S(1)}, u32[]{:S(2)}, u32[]{:S(2)}) collective-permute-start(bf16[512,512]{1,0:T(8,128)(2,1)} %bitcast.17), channel_id=1, source_target_pairs={{1,0},{2,1},{3,2},{0,3},{5,4},{6,5},{7,6},{4,7},{9,8},{10,9},{11,1... | collective-permute-start | bytes 1572872 | tf_op jit(solution)/shard_map/ppermute | solution.py:313
  7.2 1.6 %copy-done = bf16[1,1024,1024]{2,1,0:T(8,128)(2,1)S(1)} copy-done((bf16[1,1024,1024]{2,1,0:T(8,128)(2,1)S(1)}, bf16[1,1024,1024]{2,1,0:T(8,128)(2,1)}, u32[]{:S(2)}) %copy-start) | copy-done | bytes 2097176
  11.3 4.4 %collective-permute-done.2.far = bf16[1024,256]{1,0:T(8,128)(2,1)} collective-permute-done((bf16[1024,256]{1,0:T(8,128)(2,1)}, bf16[1024,256]{1,0:T(8,128)(2,1)}, u32[]{:S(2)}, u32[]{:S(2)}) %collective-permute-start.2) | collective-permute-done | bytes 524320 | tf_op jit(solution)/shard_map/ppermute | solution.py:313
  17.1 2.1 %collective-permute-start.8 = (bf16[1024,256]{1,0:T(8,128)(2,1)S(1)}, bf16[1024,256]{1,0:T(8,128)(2,1)S(1)}, u32[]{:S(2)}, u32[]{:S(2)}) collective-permute-start(bf16[1024,256]{1,0:T(8,128)(2,1)S(1)} %shard_map.84.rest_0_.refs_4_), channel_id=1, source_target_pairs={{4,0},{0,4},{5,1},{1,5},{6,2},{2,6},{7,3},{3,7},{12,8},{8,12},{13,... | collective-permute-start | bytes 1572872 | tf_op jit(solution)/shard_map/ppermute | solution.py:313
  21.8 9.1 %collective-permute-done.rest_1_.rest_2_.refs_1_ = bf16[512,512]{1,0:T(8,128)(2,1)S(1)} collective-permute-done((bf16[512,512]{1,0:T(8,128)(2,1)S(1)}, bf16[512,512]{1,0:T(8,128)(2,1)S(1)}, u32[]{:S(2)}, u32[]{:S(2)}) %collective-permute-start) | collective-permute-done | bytes 524320 | tf_op jit(solution)/shard_map/ppermute | solution.py:313
  33.4 1.6 %collective-permute-start.9 = (bf16[1024,256]{1,0:T(8,128)(2,1)S(1)}, bf16[1024,256]{1,0:T(8,128)(2,1)S(1)}, u32[]{:S(2)}, u32[]{:S(2)}) collective-permute-start(bf16[1024,256]{1,0:T(8,128)(2,1)S(1)} %shard_map.87.rest_0_.refs_4_), channel_id=1, source_target_pairs={{4,0},{0,4},{5,1},{1,5},{6,2},{2,6},{7,3},{3,7},{12,8},{8,12},{13,... | collective-permute-start | bytes 1572872 | tf_op jit(solution)/shard_map/ppermute | solution.py:313
  35.0 2.6 %collective-permute-start.6 = (bf16[512,512]{1,0:T(8,128)(2,1)}, bf16[512,512]{1,0:T(8,128)(2,1)S(1)}, u32[]{:S(2)}, u32[]{:S(2)}) collective-permute-start(bf16[512,512]{1,0:T(8,128)(2,1)} %shard_map.86.rest_0_), channel_id=1, source_target_pairs={{2,0},{3,1},{0,2},{1,3},{6,4},{7,5},{4,6},{5,7},{10,8},{11,9},{8,1... | collective-permute-start | bytes 1572872 | tf_op jit(solution)/shard_map/ppermute | solution.py:313
  38.7 1.9 %shard_map.89.rest_0_.refs_4_ = bf16[1024,256]{1,0:T(8,128)(2,1)} custom-call(f32[2]{0:T(128)S(1)} %broadcast_select_fusion.shares, bf16[1024,1024]{1,0:T(8,128)(2,1)} %collective-permute-done.3.rest_1_.near, bf16[1024,256]{1,0:T(8,128)(2,1)S(1)} %collective-permute-done.11.far, bf16[1024,256]{1,0:T(8,128)(2,1)} %shard_map.88.rest_0_), custom_call_target="tpu_custom_call" | custom-call | flops 1572864000 | tf_op jit(solution)/shard_map/pallas_call | solution.py:57
  42.1 7.4 %collective-permute-done.10.far = bf16[1024,256]{1,0:T(8,128)(2,1)} collective-permute-done((bf16[1024,256]{1,0:T(8,128)(2,1)}, bf16[1024,256]{1,0:T(8,128)(2,1)}, u32[]{:S(2)}, u32[]{:S(2)}) %collective-permute-start.10) | collective-permute-done | bytes 524320 | tf_op jit(solution)/shard_map/ppermute | solution.py:313
  49.5 1.5 %shard_map.90.rest_0_.refs_4_ = bf16[1024,256]{1,0:T(8,128)(2,1)S(1)} custom-call(f32[2]{0:T(128)S(1)} %broadcast_select_fusion.shares, bf16[1024,1024]{1,0:T(8,128)(2,1)} %collective-permute-done.3.rest_1_.near, bf16[1024,256]{1,0:T(8,128)(2,1)} %collective-permute-done.10.far, bf16[1024,256]{1,0:T(8,128)(2,1)} %shard_map.89.rest_0_.refs_4_, ...), custom_call_target="tpu_custom_call" | custom-call | flops 1572864000 | tf_op jit(solution)/shard_map/pallas_call | solution.py:57
  51.0 2.1 %collective-permute-start.14 = (bf16[1024,256]{1,0:T(8,128)(2,1)S(1)}, bf16[1024,256]{1,0:T(8,128)(2,1)S(1)}, u32[]{:S(2)}, u32[]{:S(2)}) collective-permute-start(bf16[1024,256]{1,0:T(8,128)(2,1)S(1)} %shard_map.90.rest_0_.refs_4_), channel_id=1, source_target_pairs={{4,0},{0,4},{5,1},{1,5},{6,2},{2,6},{7,3},{3,7},{12,8},{8,12},{13,... | collective-permute-start | bytes 1572872 | tf_op jit(solution)/shard_map/ppermute | solution.py:313
  55.4 5.3 %collective-permute-done.6.refs_2_ = bf16[512,512]{1,0:T(8,128)(2,1)S(1)} collective-permute-done((bf16[512,512]{1,0:T(8,128)(2,1)}, bf16[512,512]{1,0:T(8,128)(2,1)S(1)}, u32[]{:S(2)}, u32[]{:S(2)}) %collective-permute-start.6) | collective-permute-done | bytes 524320 | tf_op jit(solution)/shard_map/ppermute | solution.py:313
  60.7 1.9 %shard_map.93 = (bf16[512,128]{1,0:T(8,128)(2,1)S(1)}, bf16[512,128]{1,0:T(8,128)(2,1)S(1)}, f32[512,128]{1,0:T(8,128)S(1)}) custom-call(s32[2]{0:T(128)S(1)} %pad_add_fusion.ids, bf16[512,512]{1,0:T(8,128)(2,1)S(1)} %bitcast.20, bf16[512,512]{1,0:T(8,128)(2,1)S(1)} %copy-done.7, bf16[512,512]{1,0:T(8,128)(2,1)S(1)} %collective-permute-done.6.refs_2_, ...), custom_call_target="tpu_custom_call" | custom-call | tf_op jit(solution)/shard_map/pallas_call | solution.py:144
  62.6 3.1 %shard_map.94.rest_0_.refs_0_ = bf16[512,256]{1,0:T(8,128)(2,1)S(1)} custom-call(s32[2]{0:T(128)S(1)} %pad_add_fusion.ids, bf16[512,512]{1,0:T(8,128)(2,1)S(1)} %bitcast.21, bf16[512,512]{1,0:T(8,128)(2,1)S(1)} %copy-done.7, bf16[512,512]{1,0:T(8,128)(2,1)S(1)} %collective-permute-done.6.refs_2_, ...), custom_call_target="tpu_custom_call" | custom-call | tf_op jit(solution)/shard_map/pallas_call | solution.py:188
  67.6 3.8 %shard_map.96.refs_11_.refs_1_ = bf16[512,256]{1,0:T(8,128)(2,1)S(1)} custom-call(s32[2]{0:T(128)S(1)} %pad_add_fusion.ids, bf16[512,512]{1,0:T(8,128)(2,1)S(1)} %bitcast.22, bf16[512,512]{1,0:T(8,128)(2,1)S(1)} %copy-done.7, bf16[512,512]{1,0:T(8,128)(2,1)S(1)} %collective-permute-done.6.refs_2_, ...), custom_call_target="tpu_custom_call" | custom-call | flops 6291456000 | tf_op jit(solution)/shard_map/pallas_call | solution.py:188
  71.4 3.1 %shard_map.97.rest_0_.refs_2_ = bf16[512,256]{1,0:T(8,128)(2,1)S(1)} custom-call(s32[2]{0:T(128)S(1)} %pad_add_fusion.ids, bf16[512,512]{1,0:T(8,128)(2,1)S(1)} %bitcast.23, bf16[512,512]{1,0:T(8,128)(2,1)S(1)} %copy-done.7, bf16[512,512]{1,0:T(8,128)(2,1)S(1)} %collective-permute-done.6.refs_2_, ...), custom_call_target="tpu_custom_call" | custom-call | tf_op jit(solution)/shard_map/pallas_call | solution.py:188
  74.9 1.5 %collective-permute-start.21 = (bf16[1024,256]{1,0:T(8,128)(2,1)S(1)}, bf16[1024,256]{1,0:T(8,128)(2,1)S(1)}, u32[]{:S(2)}, u32[]{:S(2)}) collective-permute-start(bf16[1024,256]{1,0:T(8,128)(2,1)S(1)} %shard_map.98.rest_0_), channel_id=1, source_target_pairs={{24,0},{16,8},{8,16},{0,24},{25,1},{17,9},{9,17},{1,25},{26,2},{18... | collective-permute-start | bytes 1572872 | tf_op jit(solution)/shard_map/ppermute | solution.py:313
  77.6 1.6 %collective-permute-start.17 = (bf16[1024,256]{1,0:T(8,128)(2,1)S(1)}, bf16[1024,256]{1,0:T(8,128)(2,1)S(1)}, u32[]{:S(2)}, u32[]{:S(2)}) collective-permute-start(bf16[1024,256]{1,0:T(8,128)(2,1)S(1)} %shard_map.99.rest_0_.refs_4_), channel_id=1, source_target_pairs={{4,0},{0,4},{5,1},{1,5},{6,2},{2,6},{7,3},{3,7},{12,8},{8,12},{13,... | collective-permute-start | bytes 1572872 | tf_op jit(solution)/shard_map/ppermute | solution.py:313
  79.5 1.9 %collective-permute-done.15.refs_5_ = bf16[1024,256]{1,0:T(8,128)(2,1)S(1)} collective-permute-done((bf16[1024,256]{1,0:T(8,128)(2,1)S(1)}, bf16[1024,256]{1,0:T(8,128)(2,1)S(1)}, u32[]{:S(2)}, u32[]{:S(2)}) %collective-permute-start.15) | collective-permute-done | bytes 524320 | tf_op jit(solution)/shard_map/ppermute | solution.py:313
  81.5 3.1 %shard_map.101.rest_0_.refs_3_ = bf16[512,256]{1,0:T(8,128)(2,1)S(1)} custom-call(s32[2]{0:T(128)S(1)} %pad_add_fusion.ids, bf16[512,512]{1,0:T(8,128)(2,1)S(1)} %bitcast.24, bf16[512,512]{1,0:T(8,128)(2,1)S(1)} %copy-done.7, bf16[512,512]{1,0:T(8,128)(2,1)S(1)} %collective-permute-done.6.refs_2_, ...), custom_call_target="tpu_custom_call" | custom-call | flops 6291456000 | tf_op jit(solution)/shard_map/pallas_call | solution.py:188
  87.7 5.0 %collective-permute-done.17.refs_5_ = bf16[1024,256]{1,0:T(8,128)(2,1)S(1)} collective-permute-done((bf16[1024,256]{1,0:T(8,128)(2,1)S(1)}, bf16[1024,256]{1,0:T(8,128)(2,1)S(1)}, u32[]{:S(2)}, u32[]{:S(2)}) %collective-permute-start.17) | collective-permute-done | bytes 524320 | tf_op jit(solution)/shard_map/ppermute | solution.py:313
  94.0 2.2 %collective-permute-start.19 = (bf16[2,512,128]{2,1,0:T(8,128)(2,1)S(1)}, bf16[2,512,128]{2,1,0:T(8,128)(2,1)S(1)}, u32[]{:S(2)}, u32[]{:S(2)}) collective-permute-start(bf16[2,512,128]{2,1,0:T(8,128)(2,1)S(1)} %get-tuple-element.28), channel_id=1, source_target_pairs={{1,0},{0,1},{3,2},{2,3},{5,4},{4,5},{7,6},{6,7},{9,8},{8,9},{11,10... | collective-permute-start | bytes 786440 | tf_op jit(solution)/shard_map/ppermute | solution.py:313
  98.0 5.9 %collective-permute-done.20.refs_5_ = bf16[1024,256]{1,0:T(8,128)(2,1)S(1)} collective-permute-done((bf16[1024,256]{1,0:T(8,128)(2,1)S(1)}, bf16[1024,256]{1,0:T(8,128)(2,1)S(1)}, u32[]{:S(2)}, u32[]{:S(2)}) %collective-permute-start.20) | collective-permute-done | bytes 524320 | tf_op jit(solution)/shard_map/ppermute | solution.py:313
  105.3 2.2 %collective-permute-start.23 = (bf16[2,512,128]{2,1,0:T(8,128)(2,1)S(1)}, bf16[2,512,128]{2,1,0:T(8,128)(2,1)S(1)}, u32[]{:S(2)}, u32[]{:S(2)}) collective-permute-start(bf16[2,512,128]{2,1,0:T(8,128)(2,1)S(1)} %get-tuple-element.32), channel_id=1, source_target_pairs={{1,0},{0,1},{3,2},{2,3},{5,4},{4,5},{7,6},{6,7},{9,8},{8,9},{11,10... | collective-permute-start | bytes 786440 | tf_op jit(solution)/shard_map/ppermute | solution.py:313
  109.9 3.2 %collective-permute-start.22 = (bf16[512,128]{1,0:T(8,128)(2,1)S(1)}, bf16[512,128]{1,0:T(8,128)(2,1)S(1)}, u32[]{:S(2)}, u32[]{:S(2)}) collective-permute-start(bf16[512,128]{1,0:T(8,128)(2,1)S(1)} %get-tuple-element.31), channel_id=1, source_target_pairs={{2,0},{3,1},{0,2},{1,3},{6,4},{7,5},{4,6},{5,7},{10,8},{11,9},{8,1... | collective-permute-start | bytes 393224 | tf_op jit(solution)/shard_map/ppermute | solution.py:313
  113.1 4.2 %collective-permute-done.23.got = bf16[2,512,128]{2,1,0:T(8,128)(2,1)S(1)} collective-permute-done((bf16[2,512,128]{2,1,0:T(8,128)(2,1)S(1)}, bf16[2,512,128]{2,1,0:T(8,128)(2,1)S(1)}, u32[]{:S(2)}, u32[]{:S(2)}) %collective-permute-start.23) | collective-permute-done | bytes 262176 | tf_op jit(solution)/shard_map/ppermute | solution.py:313
  122.3 2.8 %collective-permute-start.29 = (bf16[512,128]{1,0:T(8,128)(2,1)S(1)}, bf16[512,128]{1,0:T(8,128)(2,1)S(1)}, u32[]{:S(2)}, u32[]{:S(2)}) collective-permute-start(bf16[512,128]{1,0:T(8,128)(2,1)S(1)} %get-tuple-element.38), channel_id=1, source_target_pairs={{1,0},{2,1},{3,2},{0,3},{5,4},{6,5},{7,6},{4,7},{9,8},{10,9},{11,1... | collective-permute-start | bytes 393224 | tf_op jit(solution)/shard_map/ppermute | solution.py:313
  125.2 6.0 %collective-permute-done.25.refs_8_.refs_3_ = bf16[512,128]{1,0:T(8,128)(2,1)S(1)} collective-permute-done((bf16[512,128]{1,0:T(8,128)(2,1)S(1)}, bf16[512,128]{1,0:T(8,128)(2,1)S(1)}, u32[]{:S(2)}, u32[]{:S(2)}) %collective-permute-start.25) | collective-permute-done | bytes 131104 | tf_op jit(solution)/shard_map/ppermute | solution.py:313
  132.8 3.6 %collective-permute-start.33 = (bf16[512,128]{1,0:T(8,128)(2,1)S(1)}, bf16[512,128]{1,0:T(8,128)(2,1)S(1)}, u32[]{:S(2)}, u32[]{:S(2)}) collective-permute-start(bf16[512,128]{1,0:T(8,128)(2,1)S(1)} %get-tuple-element.42), channel_id=1, source_target_pairs={{1,0},{2,1},{3,2},{0,3},{5,4},{6,5},{7,6},{4,7},{9,8},{10,9},{11,1... | collective-permute-start | bytes 393224 | tf_op jit(solution)/shard_map/ppermute | solution.py:313
  136.4 4.4 %collective-permute-done.31.refs_9_ = bf16[512,128]{1,0:T(8,128)(2,1)S(1)} collective-permute-done((bf16[512,128]{1,0:T(8,128)(2,1)S(1)}, bf16[512,128]{1,0:T(8,128)(2,1)S(1)}, u32[]{:S(2)}, u32[]{:S(2)}) %collective-permute-start.31) | collective-permute-done | bytes 131104 | tf_op jit(solution)/shard_map/ppermute | solution.py:313
  140.8 4.7 %collective-permute-done.32.refs_10_ = bf16[512,128]{1,0:T(8,128)(2,1)S(1)} collective-permute-done((bf16[512,128]{1,0:T(8,128)(2,1)S(1)}, bf16[512,128]{1,0:T(8,128)(2,1)S(1)}, u32[]{:S(2)}, u32[]{:S(2)}) %collective-permute-start.32) | collective-permute-done | bytes 131104 | tf_op jit(solution)/shard_map/ppermute | solution.py:313
  (104 shorter events, 36.2 us)
Async XLA Ops:
  0.5 9.4 %collective-permute-start.4 = (bf16[1024,1024]{1,0:T(8,128)(2,1)}, bf16[1024,1024]{1,0:T(8,128)(2,1)S(1)}, u32[]{:S(2)}, u32[]{:S(2)}) collective-permute-start(bf16[1024,1024]{1,0:T(8,128)(2,1)} %bitcast.12), channel_id=1, source_target_pairs={{8,0},{0,8},{24,16},{16,24},{9,1},{1,9},{25,17},{17,25},{10,2},{2,... | collective-permute-start | bytes 6291464 | tf_op jit(solution)/shard_map/ppermute | solution.py:313
  0.5 15.2 %collective-permute-start.2 = (bf16[1024,256]{1,0:T(8,128)(2,1)}, bf16[1024,256]{1,0:T(8,128)(2,1)}, u32[]{:S(2)}, u32[]{:S(2)}) collective-permute-start(bf16[1024,256]{1,0:T(8,128)(2,1)} %bitcast.26), channel_id=1, source_target_pairs={{24,0},{16,8},{8,16},{0,24},{25,1},{17,9},{9,17},{1,25},{26,2},{18... | collective-permute-start | bytes 1572872 | tf_op jit(solution)/shard_map/ppermute | solution.py:313
  3.1 12.6 %collective-permute-start.1 = (bf16[1024,256]{1,0:T(8,128)(2,1)}, bf16[1024,256]{1,0:T(8,128)(2,1)}, u32[]{:S(2)}, u32[]{:S(2)}) collective-permute-start(bf16[1024,256]{1,0:T(8,128)(2,1)} %bitcast.27), channel_id=1, source_target_pairs={{8,0},{0,8},{24,16},{16,24},{9,1},{1,9},{25,17},{17,25},{10,2},{2,... | collective-permute-start | bytes 1572872 | tf_op jit(solution)/shard_map/ppermute | solution.py:313
  3.6 17.8 %collective-permute-start.5 = (bf16[512,512]{1,0:T(8,128)(2,1)}, bf16[512,512]{1,0:T(8,128)(2,1)S(1)}, u32[]{:S(2)}, u32[]{:S(2)}) collective-permute-start(bf16[512,512]{1,0:T(8,128)(2,1)} %bitcast.17), channel_id=1, source_target_pairs={{1,0},{2,1},{3,2},{0,3},{5,4},{6,5},{7,6},{4,7},{9,8},{10,9},{11,1... | collective-permute-start | bytes 1572872 | tf_op jit(solution)/shard_map/ppermute | solution.py:313
  9.8 21.1 %collective-permute-start = (bf16[512,512]{1,0:T(8,128)(2,1)S(1)}, bf16[512,512]{1,0:T(8,128)(2,1)S(1)}, u32[]{:S(2)}, u32[]{:S(2)}) collective-permute-start(bf16[512,512]{1,0:T(8,128)(2,1)S(1)} %bitcast.18), channel_id=1, source_target_pairs={{3,0},{0,1},{1,2},{2,3},{7,4},{4,5},{5,6},{6,7},{11,8},{8,9},{9,10... | collective-permute-start | bytes 1572872 | tf_op jit(solution)/shard_map/ppermute | solution.py:313
  9.8 22.1 %collective-permute-start.7 = (bf16[1024,256]{1,0:T(8,128)(2,1)S(1)}, bf16[1024,256]{1,0:T(8,128)(2,1)S(1)}, u32[]{:S(2)}, u32[]{:S(2)}) collective-permute-start(bf16[1024,256]{1,0:T(8,128)(2,1)S(1)} %shard_map.82.rest_0_), channel_id=1, source_target_pairs={{24,0},{16,8},{8,16},{0,24},{25,1},{17,9},{9,17},{1,25},{26,2},{18... | collective-permute-start | bytes 1572872 | tf_op jit(solution)/shard_map/ppermute | solution.py:313
  17.1 14.8 %collective-permute-start.8 = (bf16[1024,256]{1,0:T(8,128)(2,1)S(1)}, bf16[1024,256]{1,0:T(8,128)(2,1)S(1)}, u32[]{:S(2)}, u32[]{:S(2)}) collective-permute-start(bf16[1024,256]{1,0:T(8,128)(2,1)S(1)} %shard_map.84.rest_0_.refs_4_), channel_id=1, source_target_pairs={{4,0},{0,4},{5,1},{1,5},{6,2},{2,6},{7,3},{3,7},{12,8},{8,12},{13,... | collective-permute-start | bytes 1572872 | tf_op jit(solution)/shard_map/ppermute | solution.py:313
  19.2 19.6 %collective-permute-start.11 = (bf16[1024,256]{1,0:T(8,128)(2,1)S(1)}, bf16[1024,256]{1,0:T(8,128)(2,1)S(1)}, u32[]{:S(2)}, u32[]{:S(2)}) collective-permute-start(bf16[1024,256]{1,0:T(8,128)(2,1)S(1)} %shard_map.83.rest_0_), channel_id=1, source_target_pairs={{24,0},{16,8},{8,16},{0,24},{25,1},{17,9},{9,17},{1,25},{26,2},{18... | collective-permute-start | bytes 1572872 | tf_op jit(solution)/shard_map/ppermute | solution.py:313
  21.4 28.1 %collective-permute-start.10 = (bf16[1024,256]{1,0:T(8,128)(2,1)}, bf16[1024,256]{1,0:T(8,128)(2,1)}, u32[]{:S(2)}, u32[]{:S(2)}) collective-permute-start(bf16[1024,256]{1,0:T(8,128)(2,1)} %shard_map.85.rest_0_), channel_id=1, source_target_pairs={{24,0},{16,8},{8,16},{0,24},{25,1},{17,9},{9,17},{1,25},{26,2},{18... | collective-permute-start | bytes 1572872 | tf_op jit(solution)/shard_map/ppermute | solution.py:313
  33.4 16.1 %collective-permute-start.9 = (bf16[1024,256]{1,0:T(8,128)(2,1)S(1)}, bf16[1024,256]{1,0:T(8,128)(2,1)S(1)}, u32[]{:S(2)}, u32[]{:S(2)}) collective-permute-start(bf16[1024,256]{1,0:T(8,128)(2,1)S(1)} %shard_map.87.rest_0_.refs_4_), channel_id=1, source_target_pairs={{4,0},{0,4},{5,1},{1,5},{6,2},{2,6},{7,3},{3,7},{12,8},{8,12},{13,... | collective-permute-start | bytes 1572872 | tf_op jit(solution)/shard_map/ppermute | solution.py:313
  35.0 25.7 %collective-permute-start.6 = (bf16[512,512]{1,0:T(8,128)(2,1)}, bf16[512,512]{1,0:T(8,128)(2,1)S(1)}, u32[]{:S(2)}, u32[]{:S(2)}) collective-permute-start(bf16[512,512]{1,0:T(8,128)(2,1)} %shard_map.86.rest_0_), channel_id=1, source_target_pairs={{2,0},{3,1},{0,2},{1,3},{6,4},{7,5},{4,6},{5,7},{10,8},{11,9},{8,1... | collective-permute-start | bytes 1572872 | tf_op jit(solution)/shard_map/ppermute | solution.py:313
  38.5 27.2 %collective-permute-start.13 = (bf16[1024,256]{1,0:T(8,128)(2,1)}, bf16[1024,256]{1,0:T(8,128)(2,1)}, u32[]{:S(2)}, u32[]{:S(2)}) collective-permute-start(bf16[1024,256]{1,0:T(8,128)(2,1)} %shard_map.88.rest_0_), channel_id=1, source_target_pairs={{24,0},{16,8},{8,16},{0,24},{25,1},{17,9},{9,17},{1,25},{26,2},{18... | collective-permute-start | bytes 1572872 | tf_op jit(solution)/shard_map/ppermute | solution.py:313
  40.7 25.0 %collective-permute-start.12 = (bf16[1024,256]{1,0:T(8,128)(2,1)}, bf16[1024,256]{1,0:T(8,128)(2,1)}, u32[]{:S(2)}, u32[]{:S(2)}) collective-permute-start(bf16[1024,256]{1,0:T(8,128)(2,1)} %shard_map.89.rest_0_.refs_4_), channel_id=1, source_target_pairs={{4,0},{0,4},{5,1},{1,5},{6,2},{2,6},{7,3},{3,7},{12,8},{8,12},{13,... | collective-permute-start | bytes 1572872 | tf_op jit(solution)/shard_map/ppermute | solution.py:313
  51.0 20.4 %collective-permute-start.14 = (bf16[1024,256]{1,0:T(8,128)(2,1)S(1)}, bf16[1024,256]{1,0:T(8,128)(2,1)S(1)}, u32[]{:S(2)}, u32[]{:S(2)}) collective-permute-start(bf16[1024,256]{1,0:T(8,128)(2,1)S(1)} %shard_map.90.rest_0_.refs_4_), channel_id=1, source_target_pairs={{4,0},{0,4},{5,1},{1,5},{6,2},{2,6},{7,3},{3,7},{12,8},{8,12},{13,... | collective-permute-start | bytes 1572872 | tf_op jit(solution)/shard_map/ppermute | solution.py:313
  53.5 22.9 %collective-permute-start.16 = (bf16[1024,256]{1,0:T(8,128)(2,1)S(1)}, bf16[1024,256]{1,0:T(8,128)(2,1)S(1)}, u32[]{:S(2)}, u32[]{:S(2)}) collective-permute-start(bf16[1024,256]{1,0:T(8,128)(2,1)S(1)} %shard_map.91.rest_0_), channel_id=1, source_target_pairs={{24,0},{16,8},{8,16},{0,24},{25,1},{17,9},{9,17},{1,25},{26,2},{18... | collective-permute-start | bytes 1572872 | tf_op jit(solution)/shard_map/ppermute | solution.py:313
  60.7 23.9 %collective-permute-start.18 = (bf16[1024,256]{1,0:T(8,128)(2,1)S(1)}, bf16[1024,256]{1,0:T(8,128)(2,1)S(1)}, u32[]{:S(2)}, u32[]{:S(2)}) collective-permute-start(bf16[1024,256]{1,0:T(8,128)(2,1)S(1)} %shard_map.92.refs_8_), channel_id=1, source_target_pairs={{24,0},{16,8},{8,16},{0,24},{25,1},{17,9},{9,17},{1,25},{26,2},{18... | collective-permute-start | bytes 1572872 | tf_op jit(solution)/shard_map/ppermute | solution.py:313
  67.1 14.4 %collective-permute-start.15 = (bf16[1024,256]{1,0:T(8,128)(2,1)S(1)}, bf16[1024,256]{1,0:T(8,128)(2,1)S(1)}, u32[]{:S(2)}, u32[]{:S(2)}) collective-permute-start(bf16[1024,256]{1,0:T(8,128)(2,1)S(1)} %shard_map.95.refs_11_.refs_4_), channel_id=1, source_target_pairs={{4,0},{0,4},{5,1},{1,5},{6,2},{2,6},{7,3},{3,7},{12,8},{8,12},{13,... | collective-permute-start | bytes 1572872 | tf_op jit(solution)/shard_map/ppermute | solution.py:313
  74.9 21.3 %collective-permute-start.21 = (bf16[1024,256]{1,0:T(8,128)(2,1)S(1)}, bf16[1024,256]{1,0:T(8,128)(2,1)S(1)}, u32[]{:S(2)}, u32[]{:S(2)}) collective-permute-start(bf16[1024,256]{1,0:T(8,128)(2,1)S(1)} %shard_map.98.rest_0_), channel_id=1, source_target_pairs={{24,0},{16,8},{8,16},{0,24},{25,1},{17,9},{9,17},{1,25},{26,2},{18... | collective-permute-start | bytes 1572872 | tf_op jit(solution)/shard_map/ppermute | solution.py:313
  77.6 15.1 %collective-permute-start.17 = (bf16[1024,256]{1,0:T(8,128)(2,1)S(1)}, bf16[1024,256]{1,0:T(8,128)(2,1)S(1)}, u32[]{:S(2)}, u32[]{:S(2)}) collective-permute-start(bf16[1024,256]{1,0:T(8,128)(2,1)S(1)} %shard_map.99.rest_0_.refs_4_), channel_id=1, source_target_pairs={{4,0},{0,4},{5,1},{1,5},{6,2},{2,6},{7,3},{3,7},{12,8},{8,12},{13,... | collective-permute-start | bytes 1572872 | tf_op jit(solution)/shard_map/ppermute | solution.py:313
  85.7 18.2 %collective-permute-start.20 = (bf16[1024,256]{1,0:T(8,128)(2,1)S(1)}, bf16[1024,256]{1,0:T(8,128)(2,1)S(1)}, u32[]{:S(2)}, u32[]{:S(2)}) collective-permute-start(bf16[1024,256]{1,0:T(8,128)(2,1)S(1)} %shard_map.102.refs_6_.refs_4_), channel_id=1, source_target_pairs={{4,0},{0,4},{5,1},{1,5},{6,2},{2,6},{7,3},{3,7},{12,8},{8,12},{13,... | collective-permute-start | bytes 1572872 | tf_op jit(solution)/shard_map/ppermute | solution.py:313
  86.3 21.8 %collective-permute-start.24 = (bf16[1024,256]{1,0:T(8,128)(2,1)S(1)}, bf16[1024,256]{1,0:T(8,128)(2,1)S(1)}, u32[]{:S(2)}, u32[]{:S(2)}) collective-permute-start(bf16[1024,256]{1,0:T(8,128)(2,1)S(1)} %shard_map.100.refs_11_), channel_id=1, source_target_pairs={{24,0},{16,8},{8,16},{0,24},{25,1},{17,9},{9,17},{1,25},{26,2},{18... | collective-permute-start | bytes 1572872 | tf_op jit(solution)/shard_map/ppermute | solution.py:313
  94.0 13.5 %collective-permute-start.19 = (bf16[2,512,128]{2,1,0:T(8,128)(2,1)S(1)}, bf16[2,512,128]{2,1,0:T(8,128)(2,1)S(1)}, u32[]{:S(2)}, u32[]{:S(2)}) collective-permute-start(bf16[2,512,128]{2,1,0:T(8,128)(2,1)S(1)} %get-tuple-element.28), channel_id=1, source_target_pairs={{1,0},{0,1},{3,2},{2,3},{5,4},{4,5},{7,6},{6,7},{9,8},{8,9},{11,10... | collective-permute-start | bytes 786440 | tf_op jit(solution)/shard_map/ppermute | solution.py:313
  97.4 21.3 %collective-permute-start.26 = (bf16[1024,256]{1,0:T(8,128)(2,1)S(1)}, bf16[1024,256]{1,0:T(8,128)(2,1)S(1)}, u32[]{:S(2)}, u32[]{:S(2)}) collective-permute-start(bf16[1024,256]{1,0:T(8,128)(2,1)S(1)} %shard_map.104.refs_6_.refs_4_), channel_id=1, source_target_pairs={{4,0},{0,4},{5,1},{1,5},{6,2},{2,6},{7,3},{3,7},{12,8},{8,12},{13,... | collective-permute-start | bytes 1572872 | tf_op jit(solution)/shard_map/ppermute | solution.py:313
  105.3 12.0 %collective-permute-start.23 = (bf16[2,512,128]{2,1,0:T(8,128)(2,1)S(1)}, bf16[2,512,128]{2,1,0:T(8,128)(2,1)S(1)}, u32[]{:S(2)}, u32[]{:S(2)}) collective-permute-start(bf16[2,512,128]{2,1,0:T(8,128)(2,1)S(1)} %get-tuple-element.32), channel_id=1, source_target_pairs={{1,0},{0,1},{3,2},{2,3},{5,4},{4,5},{7,6},{6,7},{9,8},{8,9},{11,10... | collective-permute-start | bytes 786440 | tf_op jit(solution)/shard_map/ppermute | solution.py:313
  109.3 22.0 %collective-permute-start.30 = (bf16[1024,256]{1,0:T(8,128)(2,1)S(1)}, bf16[1024,256]{1,0:T(8,128)(2,1)S(1)}, u32[]{:S(2)}, u32[]{:S(2)}) collective-permute-start(bf16[1024,256]{1,0:T(8,128)(2,1)S(1)} %shard_map.107.refs_0_.refs_4_), channel_id=1, source_target_pairs={{4,0},{0,4},{5,1},{1,5},{6,2},{2,6},{7,3},{3,7},{12,8},{8,12},{13,... | collective-permute-start | bytes 1572872 | tf_op jit(solution)/shard_map/ppermute | solution.py:313
  109.9 12.4 %collective-permute-start.22 = (bf16[512,128]{1,0:T(8,128)(2,1)S(1)}, bf16[512,128]{1,0:T(8,128)(2,1)S(1)}, u32[]{:S(2)}, u32[]{:S(2)}) collective-permute-start(bf16[512,128]{1,0:T(8,128)(2,1)S(1)} %get-tuple-element.31), channel_id=1, source_target_pairs={{2,0},{3,1},{0,2},{1,3},{6,4},{7,5},{4,6},{5,7},{10,8},{11,9},{8,1... | collective-permute-start | bytes 393224 | tf_op jit(solution)/shard_map/ppermute | solution.py:313
  117.9 13.3 %collective-permute-start.25 = (bf16[512,128]{1,0:T(8,128)(2,1)S(1)}, bf16[512,128]{1,0:T(8,128)(2,1)S(1)}, u32[]{:S(2)}, u32[]{:S(2)}) collective-permute-start(bf16[512,128]{1,0:T(8,128)(2,1)S(1)} %get-tuple-element.34), channel_id=1, source_target_pairs={{2,0},{3,1},{0,2},{1,3},{6,4},{7,5},{4,6},{5,7},{10,8},{11,9},{8,1... | collective-permute-start | bytes 393224 | tf_op jit(solution)/shard_map/ppermute | solution.py:313
  119.9 12.9 %collective-permute-start.27 = (bf16[512,128]{1,0:T(8,128)(2,1)S(1)}, bf16[512,128]{1,0:T(8,128)(2,1)S(1)}, u32[]{:S(2)}, u32[]{:S(2)}) collective-permute-start(bf16[512,128]{1,0:T(8,128)(2,1)S(1)} %get-tuple-element.36), channel_id=1, source_target_pairs={{3,0},{0,1},{1,2},{2,3},{7,4},{4,5},{5,6},{6,7},{11,8},{8,9},{9,10... | collective-permute-start | bytes 393224 | tf_op jit(solution)/shard_map/ppermute | solution.py:313
  121.4 15.0 %collective-permute-start.28 = (bf16[512,128]{1,0:T(8,128)(2,1)S(1)}, bf16[512,128]{1,0:T(8,128)(2,1)S(1)}, u32[]{:S(2)}, u32[]{:S(2)}) collective-permute-start(bf16[512,128]{1,0:T(8,128)(2,1)S(1)} %get-tuple-element.37), channel_id=1, source_target_pairs={{2,0},{3,1},{0,2},{1,3},{6,4},{7,5},{4,6},{5,7},{10,8},{11,9},{8,1... | collective-permute-start | bytes 393224 | tf_op jit(solution)/shard_map/ppermute | solution.py:313
  122.3 14.1 %collective-permute-start.29 = (bf16[512,128]{1,0:T(8,128)(2,1)S(1)}, bf16[512,128]{1,0:T(8,128)(2,1)S(1)}, u32[]{:S(2)}, u32[]{:S(2)}) collective-permute-start(bf16[512,128]{1,0:T(8,128)(2,1)S(1)} %get-tuple-element.38), channel_id=1, source_target_pairs={{1,0},{2,1},{3,2},{0,3},{5,4},{6,5},{7,6},{4,7},{9,8},{10,9},{11,1... | collective-permute-start | bytes 393224 | tf_op jit(solution)/shard_map/ppermute | solution.py:313
  132.6 12.9 %collective-permute-start.32 = (bf16[512,128]{1,0:T(8,128)(2,1)S(1)}, bf16[512,128]{1,0:T(8,128)(2,1)S(1)}, u32[]{:S(2)}, u32[]{:S(2)}) collective-permute-start(bf16[512,128]{1,0:T(8,128)(2,1)S(1)} %get-tuple-element.41), channel_id=1, source_target_pairs={{2,0},{3,1},{0,2},{1,3},{6,4},{7,5},{4,6},{5,7},{10,8},{11,9},{8,1... | collective-permute-start | bytes 393224 | tf_op jit(solution)/shard_map/ppermute | solution.py:313
  132.8 12.7 %collective-permute-start.33 = (bf16[512,128]{1,0:T(8,128)(2,1)S(1)}, bf16[512,128]{1,0:T(8,128)(2,1)S(1)}, u32[]{:S(2)}, u32[]{:S(2)}) collective-permute-start(bf16[512,128]{1,0:T(8,128)(2,1)S(1)} %get-tuple-element.42), channel_id=1, source_target_pairs={{1,0},{2,1},{3,2},{0,3},{5,4},{6,5},{7,6},{4,7},{9,8},{10,9},{11,1... | collective-permute-start | bytes 393224 | tf_op jit(solution)/shard_map/ppermute | solution.py:313
  (20 other events, 115.6 us)

commit v6 on v5

--- a/solution.py
+++ b/solution.py
@@ -19,7 +19,7 @@
 QUERY_CHUNKS = 4
 OUT_CHUNKS = 4
 FIRST = (1, 3)
-STEPS = (('G', 1, '', 200), ('G', 2, 'n0 n1', 200), ('C', 0, '', 1500), ('G', 3, '', 200), ('X', 0, 'a1', 1500), ('C', 1, 'y0', 1500), ('G', 4, '', 200), ('C', 2, '', 1500), ('C', 3, 'y1', 1500), ('G', 5, '', 200), ('G', 6, '', 200), ('K', 0, '', 0), ('A', 1, '', 0), ('C', 4, 'y2', 1500), ('A', 2, '', 6000), ('A', 3, '', 0), ('G', 7, '', 200), ('C', 5, '', 1500), ('G', 8, '', 200), ('A', 4, '', 6000), ('C', 6, '', 1500), ('P', 5, '', 0), ('C', 7, '', 700), ('P', 6, '', 1000), ('R', 5, '', 1000), ('C', 8, '', 1000), ('R', 6, '', 1500), ('Q', 7, '', 200), ('Q', 8, 't5 t6', 0))
+STEPS = (('G', 2, '', 1500), ('G', 1, 'n1', 700), ('G', 3, '', 3000), ('C', 0, '', 700), ('C', 1, '', 700), ('X', 0, '', 1000), ('G', 4, '', 50), ('C', 2, 'y0', 700), ('C', 3, 'y1', 700), ('G', 5, '', 4000), ('G', 6, '', 50), ('K', 0, '', 4000), ('C', 4, '', 700), ('A', 1, 'n0', 4000), ('A', 2, '', 700), ('G', 7, '', 1000), ('C', 5, 'y2', 700), ('A', 3, '', 4000), ('C', 6, 'a3', 700), ('A', 4, '', 1500), ('P', 5, '', 2000), ('G', 8, '', 50), ('C', 7, '', 700), ('R', 5, 'a2 y5 y6', 0), ('P', 6, '', 2000), ('C', 8, '', 700), ('P', 7, 't5 y3', 6000), ('R', 6, 'y4', 700), ('R', 7, 'a1 s7', 1500), ('Q', 8, '', 50))
 
 SMEM = pl.BlockSpec(memory_space=pltpu.SMEM)
 VMEM = pl.BlockSpec(memory_space=pltpu.VMEM)

time: 147 us -> 143 us (0.973)
  waiting for transfers between devices: 58.4 us -> 41.3 us
  starting transfers between devices: 45.8 us -> 55.1 us
  Pallas kernels: 39 us -> 43 us
    ppermute x34 -> x33, waiting for transfers between devices: 58.4 us -> 41.3 us  [permute(): lax.ppermute(array, axis, [(source(i) % count, i) for i in range(count)])]
    ppermute x34 -> x33, starting transfers between devices: 45.8 us -> 55.1 us  [permute(): lax.ppermute(array, axis, [(source(i) % count, i) for i in range(count)])]
    pallas_call x4, Pallas kernels: 13 us -> 15.1 us  [attend(): pl.pallas_call(functools.partial(attend_kernel, len(blocks)), out_shape=j...]
    pallas_call x2 -> x3, Pallas kernels: 2.6 us -> 3.89 us  [partials(): pl.pallas_call(functools.partial(partial_kernel, count, len(mixed)), out_...]
  transfers between devices with their start and end apart: 34 -> 33, of which waited for: 11 -> 13; matrix products, arithmetic and copies ran while one was open for 0% -> 0% of each run, Pallas kernels for 26% -> 30%
where the time goes in v6:
time: 143 us; the launch traced here: 142 us
  starting transfers between devices  55.1 us (39%)
  Pallas kernels  43 us (30%)
  waiting for transfers between devices  41.3 us (29%)
  local copies, waits for them, and re-layouts  2.42 us (2%)
    ppermute x33, starting transfers between devices, permute(): lax.ppermute(array, axis, [(source(i) % count, i) for i in range(count)])  55.1 us
    ppermute x33, waiting for transfers between devices, permute(): lax.ppermute(array, axis, [(source(i) % count, i) for i in range(count)])  41.3 us
    pallas_call x4, Pallas kernels, attend(): pl.pallas_call(functools.partial(attend_kernel, len(blocks)), out_shape=j...  15.1 us
    pallas_call x9, Pallas kernels, combine(): pl.pallas_call(combine_kernel, out_shape=jax.ShapeDtypeStruct(far.shape,...  12.3 us
    pallas_call x8, Pallas kernels, columns_of(): pl.pallas_call(columns_kernel, out_shape=jax.ShapeDtypeStruct((rows, piec...  4.84 us
    pallas_call x3, Pallas kernels, partials(): pl.pallas_call(functools.partial(partial_kernel, count, len(mixed)), out_...  3.89 us
  transfers between devices with their start and end apart: 33, of which 13 were waited for; matrix products, arithmetic and copies ran while one was open for 0% of the time, Pallas kernels for 30%

profile of v6, /device:TPU:0, one launch (start us, length us, event | category | flops | bytes accessed | tf_op | source)
XLA Modules:
  0.0 142.1 jit_solution(1097885363326980256)
XLA Ops:
  1.0 2.6 %collective-permute-start.5 = (bf16[1024,256]{1,0:T(8,128)(2,1)}, bf16[1024,256]{1,0:T(8,128)(2,1)}, u32[]{:S(2)}, u32[]{:S(2)}) collective-permute-start(bf16[1024,256]{1,0:T(8,128)(2,1)} %bitcast.27), channel_id=1, source_target_pairs={{24,0},{16,8},{8,16},{0,24},{25,1},{17,9},{9,17},{1,25},{26,2},{18... | collective-permute-start | bytes 1572872 | tf_op jit(solution)/shard_map/ppermute | solution.py:313
  7.8 2.4 %collective-permute-start.3 = (bf16[1024,256]{1,0:T(8,128)(2,1)S(1)}, bf16[1024,256]{1,0:T(8,128)(2,1)S(1)}, u32[]{:S(2)}, u32[]{:S(2)}) collective-permute-start(bf16[1024,256]{1,0:T(8,128)(2,1)S(1)} %shard_map.83.rest_0_), channel_id=1, source_target_pairs={{24,0},{16,8},{8,16},{0,24},{25,1},{17,9},{9,17},{1,25},{26,2},{18... | collective-permute-start | bytes 1572872 | tf_op jit(solution)/shard_map/ppermute | solution.py:313
  11.1 3.6 %collective-permute-start.6 = (bf16[512,512]{1,0:T(8,128)(2,1)S(1)}, bf16[512,512]{1,0:T(8,128)(2,1)S(1)}, u32[]{:S(2)}, u32[]{:S(2)}) collective-permute-start(bf16[512,512]{1,0:T(8,128)(2,1)S(1)} %bitcast.18), channel_id=1, source_target_pairs={{1,0},{2,1},{3,2},{0,3},{5,4},{6,5},{7,6},{4,7},{9,8},{10,9},{11,1... | collective-permute-start | bytes 1572872 | tf_op jit(solution)/shard_map/ppermute | solution.py:313
  16.2 2.2 %collective-permute-start.11 = (bf16[1024,256]{1,0:T(8,128)(2,1)}, bf16[1024,256]{1,0:T(8,128)(2,1)}, u32[]{:S(2)}, u32[]{:S(2)}) collective-permute-start(bf16[1024,256]{1,0:T(8,128)(2,1)} %shard_map.82.rest_0_), channel_id=1, source_target_pairs={{24,0},{16,8},{8,16},{0,24},{25,1},{17,9},{9,17},{1,25},{26,2},{18... | collective-permute-start | bytes 1572872 | tf_op jit(solution)/shard_map/ppermute | solution.py:313
  18.4 1.9 %shard_map.85.rest_0_.refs_4_ = bf16[1024,256]{1,0:T(8,128)(2,1)} custom-call(f32[2]{0:T(128)S(1)} %broadcast_select_fusion.shares, bf16[1024,256]{1,0:T(8,128)(2,1)S(1)} %copy-done.9, bf16[1024,256]{1,0:T(8,128)(2,1)} %collective-permute-done.5.far, bf16[1024,256]{1,0:T(8,128)(2,1)} %shard_map.84.rest_0_), custom_call_target="tpu_custom_call" | custom-call | flops 734003200 | tf_op jit(solution)/shard_map/pallas_call | solution.py:57
  21.8 5.5 %collective-permute-done.3.far = bf16[1024,256]{1,0:T(8,128)(2,1)S(1)} collective-permute-done((bf16[1024,256]{1,0:T(8,128)(2,1)S(1)}, bf16[1024,256]{1,0:T(8,128)(2,1)S(1)}, u32[]{:S(2)}, u32[]{:S(2)}) %collective-permute-start.3) | collective-permute-done | bytes 524320 | tf_op jit(solution)/shard_map/ppermute | solution.py:313
  27.3 2.3 %collective-permute-start.10 = (bf16[1024,256]{1,0:T(8,128)(2,1)}, bf16[1024,256]{1,0:T(8,128)(2,1)}, u32[]{:S(2)}, u32[]{:S(2)}) collective-permute-start(bf16[1024,256]{1,0:T(8,128)(2,1)} %shard_map.84.rest_0_), channel_id=1, source_target_pairs={{24,0},{16,8},{8,16},{0,24},{25,1},{17,9},{9,17},{1,25},{26,2},{18... | collective-permute-start | bytes 1572872 | tf_op jit(solution)/shard_map/ppermute | solution.py:313
  29.6 1.9 %shard_map.86.rest_0_.refs_4_ = bf16[1024,256]{1,0:T(8,128)(2,1)} custom-call(f32[2]{0:T(128)S(1)} %broadcast_select_fusion.shares, bf16[1024,1024]{1,0:T(8,128)(2,1)} %collective-permute-done.1.near.refs_12_, bf16[1024,256]{1,0:T(8,128)(2,1)S(1)} %collective-permute-done.3.far, bf16[1024,256]{1,0:T(8,128)(2,1)} %shard_map.85.rest_0_.refs_4_), custom_call_target="tpu_custom_call" | custom-call | flops 734003200 | tf_op jit(solution)/shard_map/pallas_call | solution.py:57
  33.1 2.7 %collective-permute-start.7 = (bf16[512,512]{1,0:T(8,128)(2,1)S(1)}, bf16[512,512]{1,0:T(8,128)(2,1)S(1)}, u32[]{:S(2)}, u32[]{:S(2)}) collective-permute-start(bf16[512,512]{1,0:T(8,128)(2,1)S(1)} %shard_map.87.rest_0_), channel_id=1, source_target_pairs={{2,0},{3,1},{0,2},{1,3},{6,4},{7,5},{4,6},{5,7},{10,8},{11,9},{8,1... | collective-permute-start | bytes 1572872 | tf_op jit(solution)/shard_map/ppermute | solution.py:313
  36.0 2.7 %collective-permute-done.11.far = bf16[1024,256]{1,0:T(8,128)(2,1)} collective-permute-done((bf16[1024,256]{1,0:T(8,128)(2,1)}, bf16[1024,256]{1,0:T(8,128)(2,1)}, u32[]{:S(2)}, u32[]{:S(2)}) %collective-permute-start.11) | collective-permute-done | bytes 524320 | tf_op jit(solution)/shard_map/ppermute | solution.py:313
  38.6 2.2 %collective-permute-start.12 = (bf16[1024,256]{1,0:T(8,128)(2,1)S(1)}, bf16[1024,256]{1,0:T(8,128)(2,1)S(1)}, u32[]{:S(2)}, u32[]{:S(2)}) collective-permute-start(bf16[1024,256]{1,0:T(8,128)(2,1)S(1)} %shard_map.88.rest_0_), channel_id=1, source_target_pairs={{24,0},{16,8},{8,16},{0,24},{25,1},{17,9},{9,17},{1,25},{26,2},{18... | collective-permute-start | bytes 1572872 | tf_op jit(solution)/shard_map/ppermute | solution.py:313
  43.8 6.1 %collective-permute-done.10.far = bf16[1024,256]{1,0:T(8,128)(2,1)} collective-permute-done((bf16[1024,256]{1,0:T(8,128)(2,1)}, bf16[1024,256]{1,0:T(8,128)(2,1)}, u32[]{:S(2)}, u32[]{:S(2)}) %collective-permute-start.10) | collective-permute-done | bytes 524320 | tf_op jit(solution)/shard_map/ppermute | solution.py:313
  53.2 1.8 %collective-permute-start.15 = (bf16[1024,256]{1,0:T(8,128)(2,1)S(1)}, bf16[1024,256]{1,0:T(8,128)(2,1)S(1)}, u32[]{:S(2)}, u32[]{:S(2)}) collective-permute-start(bf16[1024,256]{1,0:T(8,128)(2,1)S(1)} %shard_map.91.rest_0_), channel_id=1, source_target_pairs={{24,0},{16,8},{8,16},{0,24},{25,1},{17,9},{9,17},{1,25},{26,2},{18... | collective-permute-start | bytes 1572872 | tf_op jit(solution)/shard_map/ppermute | solution.py:313
  57.9 2.7 %shard_map.93 = (bf16[512,128]{1,0:T(8,128)(2,1)S(1)}, bf16[512,128]{1,0:T(8,128)(2,1)S(1)}, f32[512,128]{1,0:T(8,128)S(1)}) custom-call(s32[2]{0:T(128)S(1)} %pad_add_fusion.ids, bf16[512,512]{1,0:T(8,128)(2,1)S(1)} %bitcast.20, bf16[512,512]{1,0:T(8,128)(2,1)} %collective-permute-done.rest_1_.refs_1_, ...), custom_call_target="tpu_custom_call" | custom-call | flops 4194304000 | tf_op jit(solution)/shard_map/pallas_call | solution.py:144
  63.8 3.9 %shard_map.95.refs_11_.refs_0_ = bf16[512,256]{1,0:T(8,128)(2,1)S(1)} custom-call(s32[2]{0:T(128)S(1)} %pad_add_fusion.ids, bf16[512,512]{1,0:T(8,128)(2,1)S(1)} %bitcast.21, bf16[512,512]{1,0:T(8,128)(2,1)} %collective-permute-done.rest_1_.refs_1_, bf16[512,512]{1,0:T(8,128)(2,1)S(1)} %collective-permute-done.7.refs_2_.refs_1_, ...), custom_call_target="tpu_custom_call" | custom-call | flops 4194304000 | tf_op jit(solution)/shard_map/pallas_call | solution.py:188
  67.7 3.6 %shard_map.96.rest_0_.refs_1_ = bf16[512,256]{1,0:T(8,128)(2,1)S(1)} custom-call(s32[2]{0:T(128)S(1)} %pad_add_fusion.ids, bf16[512,512]{1,0:T(8,128)(2,1)S(1)} %bitcast.22, bf16[512,512]{1,0:T(8,128)(2,1)} %collective-permute-done.rest_1_.refs_1_, bf16[512,512]{1,0:T(8,128)(2,1)S(1)} %collective-permute-done.7.refs_2_.refs_1_, ...), custom_call_target="tpu_custom_call" | custom-call | flops 734003200 | tf_op jit(solution)/shard_map/pallas_call | solution.py:188
  71.7 2.1 %collective-permute-start.20 = (bf16[1024,256]{1,0:T(8,128)(2,1)S(1)}, bf16[1024,256]{1,0:T(8,128)(2,1)S(1)}, u32[]{:S(2)}, u32[]{:S(2)}) collective-permute-start(bf16[1024,256]{1,0:T(8,128)(2,1)S(1)} %shard_map.97.rest_0_), channel_id=1, source_target_pairs={{24,0},{16,8},{8,16},{0,24},{25,1},{17,9},{9,17},{1,25},{26,2},{18... | collective-permute-start | bytes 1572872 | tf_op jit(solution)/shard_map/ppermute | solution.py:313
  75.5 3.8 %shard_map.99.rest_0_.refs_2_ = bf16[512,256]{1,0:T(8,128)(2,1)S(1)} custom-call(s32[2]{0:T(128)S(1)} %pad_add_fusion.ids, bf16[512,512]{1,0:T(8,128)(2,1)S(1)} %bitcast.23, bf16[512,512]{1,0:T(8,128)(2,1)} %collective-permute-done.rest_1_.refs_1_, bf16[512,512]{1,0:T(8,128)(2,1)S(1)} %collective-permute-done.7.refs_2_.refs_1_, ...), custom_call_target="tpu_custom_call" | custom-call | flops 4194304000 | tf_op jit(solution)/shard_map/pallas_call | solution.py:188
  79.3 4.3 %collective-permute-done.17.far = bf16[1024,256]{1,0:T(8,128)(2,1)S(1)} collective-permute-done((bf16[1024,256]{1,0:T(8,128)(2,1)}, bf16[1024,256]{1,0:T(8,128)(2,1)S(1)}, u32[]{:S(2)}, u32[]{:S(2)}) %collective-permute-start.17) | collective-permute-done | bytes 524320 | tf_op jit(solution)/shard_map/ppermute | solution.py:313
  86.3 3.8 %shard_map.101.refs_3_.refs_6_ = bf16[512,256]{1,0:T(8,128)(2,1)S(1)} custom-call(s32[2]{0:T(128)S(1)} %pad_add_fusion.ids, bf16[512,512]{1,0:T(8,128)(2,1)S(1)} %bitcast.24, bf16[512,512]{1,0:T(8,128)(2,1)} %collective-permute-done.rest_1_.refs_1_, bf16[512,512]{1,0:T(8,128)(2,1)S(1)} %collective-permute-done.7.refs_2_.refs_1_, ...), custom_call_target="tpu_custom_call" | custom-call | flops 1572864000 | tf_op jit(solution)/shard_map/pallas_call | solution.py:188
  92.0 1.7 %collective-permute-start.25 = (bf16[1024,256]{1,0:T(8,128)(2,1)S(1)}, bf16[1024,256]{1,0:T(8,128)(2,1)S(1)}, u32[]{:S(2)}, u32[]{:S(2)}) collective-permute-start(bf16[1024,256]{1,0:T(8,128)(2,1)S(1)} %shard_map.103.rest_0_), channel_id=1, source_target_pairs={{24,0},{16,8},{8,16},{0,24},{25,1},{17,9},{9,17},{1,25},{26,2},{18... | collective-permute-start | bytes 1572872 | tf_op jit(solution)/shard_map/ppermute | solution.py:313
  97.5 4.1 %collective-permute-done.21.refs_3_.refs_5_ = bf16[1024,256]{1,0:T(8,128)(2,1)S(1)} collective-permute-done((bf16[1024,256]{1,0:T(8,128)(2,1)S(1)}, bf16[1024,256]{1,0:T(8,128)(2,1)S(1)}, u32[]{:S(2)}, u32[]{:S(2)}) %collective-permute-start.21) | collective-permute-done | bytes 524320 | tf_op jit(solution)/shard_map/ppermute | solution.py:313
  102.1 2.4 %collective-permute-start.22 = (bf16[512,128]{1,0:T(8,128)(2,1)S(1)}, bf16[512,128]{1,0:T(8,128)(2,1)S(1)}, u32[]{:S(2)}, u32[]{:S(2)}) collective-permute-start(bf16[512,128]{1,0:T(8,128)(2,1)S(1)} %get-tuple-element.30), channel_id=1, source_target_pairs={{2,0},{3,1},{0,2},{1,3},{6,4},{7,5},{4,6},{5,7},{10,8},{11,9},{8,1... | collective-permute-start | bytes 393224 | tf_op jit(solution)/shard_map/ppermute | solution.py:313
  105.9 1.6 %collective-permute-start.23 = (bf16[2,512,128]{2,1,0:T(8,128)(2,1)S(1)}, bf16[2,512,128]{2,1,0:T(8,128)(2,1)S(1)}, u32[]{:S(2)}, u32[]{:S(2)}) collective-permute-start(bf16[2,512,128]{2,1,0:T(8,128)(2,1)S(1)} %get-tuple-element.32), channel_id=1, source_target_pairs={{1,0},{0,1},{3,2},{2,3},{5,4},{4,5},{7,6},{6,7},{9,8},{8,9},{11,10... | collective-permute-start | bytes 786440 | tf_op jit(solution)/shard_map/ppermute | solution.py:313
  110.3 2.5 %collective-permute-done.24.refs_5_ = bf16[1024,256]{1,0:T(8,128)(2,1)S(1)} collective-permute-done((bf16[1024,256]{1,0:T(8,128)(2,1)S(1)}, bf16[1024,256]{1,0:T(8,128)(2,1)S(1)}, u32[]{:S(2)}, u32[]{:S(2)}) %collective-permute-start.24) | collective-permute-done | bytes 524320 | tf_op jit(solution)/shard_map/ppermute | solution.py:313
  116.1 2.7 %collective-permute-start.26 = (bf16[512,128]{1,0:T(8,128)(2,1)S(1)}, bf16[512,128]{1,0:T(8,128)(2,1)S(1)}, u32[]{:S(2)}, u32[]{:S(2)}) collective-permute-start(bf16[512,128]{1,0:T(8,128)(2,1)S(1)} %get-tuple-element.35), channel_id=1, source_target_pairs={{2,0},{3,1},{0,2},{1,3},{6,4},{7,5},{4,6},{5,7},{10,8},{11,9},{8,1... | collective-permute-start | bytes 393224 | tf_op jit(solution)/shard_map/ppermute | solution.py:313
  118.8 5.1 %collective-permute-done.27.got.refs_2_ = bf16[2,512,128]{2,1,0:T(8,128)(2,1)S(1)} collective-permute-done((bf16[2,512,128]{2,1,0:T(8,128)(2,1)S(1)}, bf16[2,512,128]{2,1,0:T(8,128)(2,1)S(1)}, u32[]{:S(2)}, u32[]{:S(2)}) %collective-permute-start.27) | collective-permute-done | bytes 262176 | tf_op jit(solution)/shard_map/ppermute | solution.py:313
  124.5 1.9 %collective-permute-start.28 = (bf16[512,128]{1,0:T(8,128)(2,1)S(1)}, bf16[512,128]{1,0:T(8,128)(2,1)S(1)}, u32[]{:S(2)}, u32[]{:S(2)}) collective-permute-start(bf16[512,128]{1,0:T(8,128)(2,1)S(1)} %get-tuple-element.38), channel_id=1, source_target_pairs={{2,0},{3,1},{0,2},{1,3},{6,4},{7,5},{4,6},{5,7},{10,8},{11,9},{8,1... | collective-permute-start | bytes 393224 | tf_op jit(solution)/shard_map/ppermute | solution.py:313
  127.7 2.5 %collective-permute-start.30 = (bf16[512,128]{1,0:T(8,128)(2,1)S(1)}, bf16[512,128]{1,0:T(8,128)(2,1)S(1)}, u32[]{:S(2)}, u32[]{:S(2)}) collective-permute-start(bf16[512,128]{1,0:T(8,128)(2,1)S(1)} %get-tuple-element.40), channel_id=1, source_target_pairs={{3,0},{0,1},{1,2},{2,3},{7,4},{4,5},{5,6},{6,7},{11,8},{8,9},{9,10... | collective-permute-start | bytes 393224 | tf_op jit(solution)/shard_map/ppermute | solution.py:313
  130.3 2.4 %collective-permute-start.32 = (bf16[512,128]{1,0:T(8,128)(2,1)S(1)}, bf16[512,128]{1,0:T(8,128)(2,1)S(1)}, u32[]{:S(2)}, u32[]{:S(2)}) collective-permute-start(bf16[512,128]{1,0:T(8,128)(2,1)S(1)} %get-tuple-element.42), channel_id=1, source_target_pairs={{1,0},{2,1},{3,2},{0,3},{5,4},{6,5},{7,6},{4,7},{9,8},{10,9},{11,1... | collective-permute-start | bytes 393224 | tf_op jit(solution)/shard_map/ppermute | solution.py:313
  132.7 5.6 %collective-permute-done.28.refs_5_ = bf16[512,128]{1,0:T(8,128)(2,1)S(1)} collective-permute-done((bf16[512,128]{1,0:T(8,128)(2,1)S(1)}, bf16[512,128]{1,0:T(8,128)(2,1)S(1)}, u32[]{:S(2)}, u32[]{:S(2)}) %collective-permute-start.28) | collective-permute-done | bytes 131104 | tf_op jit(solution)/shard_map/ppermute | solution.py:313
  138.3 2.8 %collective-permute-done.31.refs_8_ = bf16[512,128]{1,0:T(8,128)(2,1)S(1)} collective-permute-done((bf16[512,128]{1,0:T(8,128)(2,1)S(1)}, bf16[512,128]{1,0:T(8,128)(2,1)S(1)}, u32[]{:S(2)}, u32[]{:S(2)}) %collective-permute-start.31) | collective-permute-done | bytes 131104 | tf_op jit(solution)/shard_map/ppermute | solution.py:313
  (91 shorter events, 44.5 us)
Async XLA Ops:
  0.5 19.8 %collective-permute-start.1 = (bf16[1024,1024]{1,0:T(8,128)(2,1)}, bf16[1024,1024]{1,0:T(8,128)(2,1)}, u32[]{:S(2)}, u32[]{:S(2)}) collective-permute-start(bf16[1024,1024]{1,0:T(8,128)(2,1)} %bitcast.7), channel_id=1, source_target_pairs={{8,0},{0,8},{24,16},{16,24},{9,1},{1,9},{25,17},{17,25},{10,2},{2,... | collective-permute-start | bytes 6291464 | tf_op jit(solution)/shard_map/ppermute | solution.py:313
  0.5 9.8 %collective-permute-start.4 = (bf16[1024,256]{1,0:T(8,128)(2,1)}, bf16[1024,256]{1,0:T(8,128)(2,1)S(1)}, u32[]{:S(2)}, u32[]{:S(2)}) collective-permute-start(bf16[1024,256]{1,0:T(8,128)(2,1)} %bitcast.26), channel_id=1, source_target_pairs={{8,0},{0,8},{24,16},{16,24},{9,1},{1,9},{25,17},{17,25},{10,2},{2,... | collective-permute-start | bytes 1572872 | tf_op jit(solution)/shard_map/ppermute | solution.py:313
  1.0 15.2 %collective-permute-start.5 = (bf16[1024,256]{1,0:T(8,128)(2,1)}, bf16[1024,256]{1,0:T(8,128)(2,1)}, u32[]{:S(2)}, u32[]{:S(2)}) collective-permute-start(bf16[1024,256]{1,0:T(8,128)(2,1)} %bitcast.27), channel_id=1, source_target_pairs={{24,0},{16,8},{8,16},{0,24},{25,1},{17,9},{9,17},{1,25},{26,2},{18... | collective-permute-start | bytes 1572872 | tf_op jit(solution)/shard_map/ppermute | solution.py:313
  3.6 27.9 %collective-permute-start = (bf16[512,512]{1,0:T(8,128)(2,1)}, bf16[512,512]{1,0:T(8,128)(2,1)}, u32[]{:S(2)}, u32[]{:S(2)}) collective-permute-start(bf16[512,512]{1,0:T(8,128)(2,1)} %bitcast.17), channel_id=1, source_target_pairs={{3,0},{0,1},{1,2},{2,3},{7,4},{4,5},{5,6},{6,7},{11,8},{8,9},{9,10... | collective-permute-start | bytes 1572872 | tf_op jit(solution)/shard_map/ppermute | solution.py:313
  7.8 19.5 %collective-permute-start.3 = (bf16[1024,256]{1,0:T(8,128)(2,1)S(1)}, bf16[1024,256]{1,0:T(8,128)(2,1)S(1)}, u32[]{:S(2)}, u32[]{:S(2)}) collective-permute-start(bf16[1024,256]{1,0:T(8,128)(2,1)S(1)} %shard_map.83.rest_0_), channel_id=1, source_target_pairs={{24,0},{16,8},{8,16},{0,24},{25,1},{17,9},{9,17},{1,25},{26,2},{18... | collective-permute-start | bytes 1572872 | tf_op jit(solution)/shard_map/ppermute | solution.py:313
  11.1 22.0 %collective-permute-start.6 = (bf16[512,512]{1,0:T(8,128)(2,1)S(1)}, bf16[512,512]{1,0:T(8,128)(2,1)S(1)}, u32[]{:S(2)}, u32[]{:S(2)}) collective-permute-start(bf16[512,512]{1,0:T(8,128)(2,1)S(1)} %bitcast.18), channel_id=1, source_target_pairs={{1,0},{2,1},{3,2},{0,3},{5,4},{6,5},{7,6},{4,7},{9,8},{10,9},{11,1... | collective-permute-start | bytes 1572872 | tf_op jit(solution)/shard_map/ppermute | solution.py:313
  16.2 22.5 %collective-permute-start.11 = (bf16[1024,256]{1,0:T(8,128)(2,1)}, bf16[1024,256]{1,0:T(8,128)(2,1)}, u32[]{:S(2)}, u32[]{:S(2)}) collective-permute-start(bf16[1024,256]{1,0:T(8,128)(2,1)} %shard_map.82.rest_0_), channel_id=1, source_target_pairs={{24,0},{16,8},{8,16},{0,24},{25,1},{17,9},{9,17},{1,25},{26,2},{18... | collective-permute-start | bytes 1572872 | tf_op jit(solution)/shard_map/ppermute | solution.py:313
  20.2 20.6 %collective-permute-start.9 = (bf16[1024,256]{1,0:T(8,128)(2,1)}, bf16[1024,256]{1,0:T(8,128)(2,1)}, u32[]{:S(2)}, u32[]{:S(2)}) collective-permute-start(bf16[1024,256]{1,0:T(8,128)(2,1)} %shard_map.85.rest_0_.refs_4_), channel_id=1, source_target_pairs={{4,0},{0,4},{5,1},{1,5},{6,2},{2,6},{7,3},{3,7},{12,8},{8,12},{13,... | collective-permute-start | bytes 1572872 | tf_op jit(solution)/shard_map/ppermute | solution.py:313
  27.3 22.6 %collective-permute-start.10 = (bf16[1024,256]{1,0:T(8,128)(2,1)}, bf16[1024,256]{1,0:T(8,128)(2,1)}, u32[]{:S(2)}, u32[]{:S(2)}) collective-permute-start(bf16[1024,256]{1,0:T(8,128)(2,1)} %shard_map.84.rest_0_), channel_id=1, source_target_pairs={{24,0},{16,8},{8,16},{0,24},{25,1},{17,9},{9,17},{1,25},{26,2},{18... | collective-permute-start | bytes 1572872 | tf_op jit(solution)/shard_map/ppermute | solution.py:313
  31.5 18.4 %collective-permute-start.8 = (bf16[1024,256]{1,0:T(8,128)(2,1)}, bf16[1024,256]{1,0:T(8,128)(2,1)}, u32[]{:S(2)}, u32[]{:S(2)}) collective-permute-start(bf16[1024,256]{1,0:T(8,128)(2,1)} %shard_map.86.rest_0_.refs_4_), channel_id=1, source_target_pairs={{4,0},{0,4},{5,1},{1,5},{6,2},{2,6},{7,3},{3,7},{12,8},{8,12},{13,... | collective-permute-start | bytes 1572872 | tf_op jit(solution)/shard_map/ppermute | solution.py:313
  33.1 24.7 %collective-permute-start.7 = (bf16[512,512]{1,0:T(8,128)(2,1)S(1)}, bf16[512,512]{1,0:T(8,128)(2,1)S(1)}, u32[]{:S(2)}, u32[]{:S(2)}) collective-permute-start(bf16[512,512]{1,0:T(8,128)(2,1)S(1)} %shard_map.87.rest_0_), channel_id=1, source_target_pairs={{2,0},{3,1},{0,2},{1,3},{6,4},{7,5},{4,6},{5,7},{10,8},{11,9},{8,1... | collective-permute-start | bytes 1572872 | tf_op jit(solution)/shard_map/ppermute | solution.py:313
  38.6 22.4 %collective-permute-start.12 = (bf16[1024,256]{1,0:T(8,128)(2,1)S(1)}, bf16[1024,256]{1,0:T(8,128)(2,1)S(1)}, u32[]{:S(2)}, u32[]{:S(2)}) collective-permute-start(bf16[1024,256]{1,0:T(8,128)(2,1)S(1)} %shard_map.88.rest_0_), channel_id=1, source_target_pairs={{24,0},{16,8},{8,16},{0,24},{25,1},{17,9},{9,17},{1,25},{26,2},{18... | collective-permute-start | bytes 1572872 | tf_op jit(solution)/shard_map/ppermute | solution.py:313
  42.2 25.5 %collective-permute-start.13 = (bf16[1024,256]{1,0:T(8,128)(2,1)S(1)}, bf16[1024,256]{1,0:T(8,128)(2,1)S(1)}, u32[]{:S(2)}, u32[]{:S(2)}) collective-permute-start(bf16[1024,256]{1,0:T(8,128)(2,1)S(1)} %shard_map.89.rest_0_.refs_4_), channel_id=1, source_target_pairs={{4,0},{0,4},{5,1},{1,5},{6,2},{2,6},{7,3},{3,7},{12,8},{8,12},{13,... | collective-permute-start | bytes 1572872 | tf_op jit(solution)/shard_map/ppermute | solution.py:313
  51.7 23.9 %collective-permute-start.14 = (bf16[1024,256]{1,0:T(8,128)(2,1)S(1)}, bf16[1024,256]{1,0:T(8,128)(2,1)}, u32[]{:S(2)}, u32[]{:S(2)}) collective-permute-start(bf16[1024,256]{1,0:T(8,128)(2,1)S(1)} %shard_map.90.rest_0_.refs_4_), channel_id=1, source_target_pairs={{4,0},{0,4},{5,1},{1,5},{6,2},{2,6},{7,3},{3,7},{12,8},{8,12},{13,... | collective-permute-start | bytes 1572872 | tf_op jit(solution)/shard_map/ppermute | solution.py:313
  53.2 20.6 %collective-permute-start.15 = (bf16[1024,256]{1,0:T(8,128)(2,1)S(1)}, bf16[1024,256]{1,0:T(8,128)(2,1)S(1)}, u32[]{:S(2)}, u32[]{:S(2)}) collective-permute-start(bf16[1024,256]{1,0:T(8,128)(2,1)S(1)} %shard_map.91.rest_0_), channel_id=1, source_target_pairs={{24,0},{16,8},{8,16},{0,24},{25,1},{17,9},{9,17},{1,25},{26,2},{18... | collective-permute-start | bytes 1572872 | tf_op jit(solution)/shard_map/ppermute | solution.py:313
  57.9 25.7 %collective-permute-start.17 = (bf16[1024,256]{1,0:T(8,128)(2,1)}, bf16[1024,256]{1,0:T(8,128)(2,1)S(1)}, u32[]{:S(2)}, u32[]{:S(2)}) collective-permute-start(bf16[1024,256]{1,0:T(8,128)(2,1)} %shard_map.92.refs_8_), channel_id=1, source_target_pairs={{24,0},{16,8},{8,16},{0,24},{25,1},{17,9},{9,17},{1,25},{26,2},{18... | collective-permute-start | bytes 1572872 | tf_op jit(solution)/shard_map/ppermute | solution.py:313
  62.2 24.1 %collective-permute-start.16 = (bf16[1024,256]{1,0:T(8,128)(2,1)S(1)}, bf16[1024,256]{1,0:T(8,128)(2,1)S(1)}, u32[]{:S(2)}, u32[]{:S(2)}) collective-permute-start(bf16[1024,256]{1,0:T(8,128)(2,1)S(1)} %shard_map.94.refs_11_.refs_4_), channel_id=1, source_target_pairs={{4,0},{0,4},{5,1},{1,5},{6,2},{2,6},{7,3},{3,7},{12,8},{8,12},{13,... | collective-permute-start | bytes 1572872 | tf_op jit(solution)/shard_map/ppermute | solution.py:313
  71.7 23.6 %collective-permute-start.20 = (bf16[1024,256]{1,0:T(8,128)(2,1)S(1)}, bf16[1024,256]{1,0:T(8,128)(2,1)S(1)}, u32[]{:S(2)}, u32[]{:S(2)}) collective-permute-start(bf16[1024,256]{1,0:T(8,128)(2,1)S(1)} %shard_map.97.rest_0_), channel_id=1, source_target_pairs={{24,0},{16,8},{8,16},{0,24},{25,1},{17,9},{9,17},{1,25},{26,2},{18... | collective-permute-start | bytes 1572872 | tf_op jit(solution)/shard_map/ppermute | solution.py:313
  75.0 15.3 %collective-permute-start.18 = (bf16[1024,256]{1,0:T(8,128)(2,1)S(1)}, bf16[1024,256]{1,0:T(8,128)(2,1)S(1)}, u32[]{:S(2)}, u32[]{:S(2)}) collective-permute-start(bf16[1024,256]{1,0:T(8,128)(2,1)S(1)} %shard_map.98.refs_11_.refs_4_), channel_id=1, source_target_pairs={{4,0},{0,4},{5,1},{1,5},{6,2},{2,6},{7,3},{3,7},{12,8},{8,12},{13,... | collective-permute-start | bytes 1572872 | tf_op jit(solution)/shard_map/ppermute | solution.py:313
  84.7 16.8 %collective-permute-start.21 = (bf16[1024,256]{1,0:T(8,128)(2,1)S(1)}, bf16[1024,256]{1,0:T(8,128)(2,1)S(1)}, u32[]{:S(2)}, u32[]{:S(2)}) collective-permute-start(bf16[1024,256]{1,0:T(8,128)(2,1)S(1)} %shard_map.100.refs_11_.refs_4_), channel_id=1, source_target_pairs={{4,0},{0,4},{5,1},{1,5},{6,2},{2,6},{7,3},{3,7},{12,8},{8,12},{13,... | collective-permute-start | bytes 1572872 | tf_op jit(solution)/shard_map/ppermute | solution.py:313
  92.0 15.5 %collective-permute-start.25 = (bf16[1024,256]{1,0:T(8,128)(2,1)S(1)}, bf16[1024,256]{1,0:T(8,128)(2,1)S(1)}, u32[]{:S(2)}, u32[]{:S(2)}) collective-permute-start(bf16[1024,256]{1,0:T(8,128)(2,1)S(1)} %shard_map.103.rest_0_), channel_id=1, source_target_pairs={{24,0},{16,8},{8,16},{0,24},{25,1},{17,9},{9,17},{1,25},{26,2},{18... | collective-permute-start | bytes 1572872 | tf_op jit(solution)/shard_map/ppermute | solution.py:313
  93.7 7.8 %collective-permute-start.19 = (bf16[2,512,128]{2,1,0:T(8,128)(2,1)S(1)}, bf16[2,512,128]{2,1,0:T(8,128)(2,1)S(1)}, u32[]{:S(2)}, u32[]{:S(2)}) collective-permute-start(bf16[2,512,128]{2,1,0:T(8,128)(2,1)S(1)} %get-tuple-element.28), channel_id=1, source_target_pairs={{1,0},{0,1},{3,2},{2,3},{5,4},{4,5},{7,6},{6,7},{9,8},{8,9},{11,10... | collective-permute-start | bytes 786440 | tf_op jit(solution)/shard_map/ppermute | solution.py:313
  96.6 16.2 %collective-permute-start.24 = (bf16[1024,256]{1,0:T(8,128)(2,1)S(1)}, bf16[1024,256]{1,0:T(8,128)(2,1)S(1)}, u32[]{:S(2)}, u32[]{:S(2)}) collective-permute-start(bf16[1024,256]{1,0:T(8,128)(2,1)S(1)} %shard_map.104.refs_0_.refs_4_), channel_id=1, source_target_pairs={{4,0},{0,4},{5,1},{1,5},{6,2},{2,6},{7,3},{3,7},{12,8},{8,12},{13,... | collective-permute-start | bytes 1572872 | tf_op jit(solution)/shard_map/ppermute | solution.py:313
  102.1 8.2 %collective-permute-start.22 = (bf16[512,128]{1,0:T(8,128)(2,1)S(1)}, bf16[512,128]{1,0:T(8,128)(2,1)S(1)}, u32[]{:S(2)}, u32[]{:S(2)}) collective-permute-start(bf16[512,128]{1,0:T(8,128)(2,1)S(1)} %get-tuple-element.30), channel_id=1, source_target_pairs={{2,0},{3,1},{0,2},{1,3},{6,4},{7,5},{4,6},{5,7},{10,8},{11,9},{8,1... | collective-permute-start | bytes 393224 | tf_op jit(solution)/shard_map/ppermute | solution.py:313
  105.9 9.6 %collective-permute-start.23 = (bf16[2,512,128]{2,1,0:T(8,128)(2,1)S(1)}, bf16[2,512,128]{2,1,0:T(8,128)(2,1)S(1)}, u32[]{:S(2)}, u32[]{:S(2)}) collective-permute-start(bf16[2,512,128]{2,1,0:T(8,128)(2,1)S(1)} %get-tuple-element.32), channel_id=1, source_target_pairs={{1,0},{0,1},{3,2},{2,3},{5,4},{4,5},{7,6},{6,7},{9,8},{8,9},{11,10... | collective-permute-start | bytes 786440 | tf_op jit(solution)/shard_map/ppermute | solution.py:313
  108.7 17.8 %collective-permute-start.29 = (bf16[1024,256]{1,0:T(8,128)(2,1)S(1)}, bf16[1024,256]{1,0:T(8,128)(2,1)S(1)}, u32[]{:S(2)}, u32[]{:S(2)}) collective-permute-start(bf16[1024,256]{1,0:T(8,128)(2,1)S(1)} %shard_map.107.refs_6_.refs_4_), channel_id=1, source_target_pairs={{4,0},{0,4},{5,1},{1,5},{6,2},{2,6},{7,3},{3,7},{12,8},{8,12},{13,... | collective-permute-start | bytes 1572872 | tf_op jit(solution)/shard_map/ppermute | solution.py:313
  114.1 9.8 %collective-permute-start.27 = (bf16[2,512,128]{2,1,0:T(8,128)(2,1)S(1)}, bf16[2,512,128]{2,1,0:T(8,128)(2,1)S(1)}, u32[]{:S(2)}, u32[]{:S(2)}) collective-permute-start(bf16[2,512,128]{2,1,0:T(8,128)(2,1)S(1)} %get-tuple-element.36), channel_id=1, source_target_pairs={{1,0},{0,1},{3,2},{2,3},{5,4},{4,5},{7,6},{6,7},{9,8},{8,9},{11,10... | collective-permute-start | bytes 786440 | tf_op jit(solution)/shard_map/ppermute | solution.py:313
  116.1 16.6 %collective-permute-start.26 = (bf16[512,128]{1,0:T(8,128)(2,1)S(1)}, bf16[512,128]{1,0:T(8,128)(2,1)S(1)}, u32[]{:S(2)}, u32[]{:S(2)}) collective-permute-start(bf16[512,128]{1,0:T(8,128)(2,1)S(1)} %get-tuple-element.35), channel_id=1, source_target_pairs={{2,0},{3,1},{0,2},{1,3},{6,4},{7,5},{4,6},{5,7},{10,8},{11,9},{8,1... | collective-permute-start | bytes 393224 | tf_op jit(solution)/shard_map/ppermute | solution.py:313
  124.5 13.8 %collective-permute-start.28 = (bf16[512,128]{1,0:T(8,128)(2,1)S(1)}, bf16[512,128]{1,0:T(8,128)(2,1)S(1)}, u32[]{:S(2)}, u32[]{:S(2)}) collective-permute-start(bf16[512,128]{1,0:T(8,128)(2,1)S(1)} %get-tuple-element.38), channel_id=1, source_target_pairs={{2,0},{3,1},{0,2},{1,3},{6,4},{7,5},{4,6},{5,7},{10,8},{11,9},{8,1... | collective-permute-start | bytes 393224 | tf_op jit(solution)/shard_map/ppermute | solution.py:313
  127.7 10.6 %collective-permute-start.30 = (bf16[512,128]{1,0:T(8,128)(2,1)S(1)}, bf16[512,128]{1,0:T(8,128)(2,1)S(1)}, u32[]{:S(2)}, u32[]{:S(2)}) collective-permute-start(bf16[512,128]{1,0:T(8,128)(2,1)S(1)} %get-tuple-element.40), channel_id=1, source_target_pairs={{3,0},{0,1},{1,2},{2,3},{7,4},{4,5},{5,6},{6,7},{11,8},{8,9},{9,10... | collective-permute-start | bytes 393224 | tf_op jit(solution)/shard_map/ppermute | solution.py:313
  130.3 10.8 %collective-permute-start.31 = (bf16[512,128]{1,0:T(8,128)(2,1)S(1)}, bf16[512,128]{1,0:T(8,128)(2,1)S(1)}, u32[]{:S(2)}, u32[]{:S(2)}) collective-permute-start(bf16[512,128]{1,0:T(8,128)(2,1)S(1)} %get-tuple-element.41), channel_id=1, source_target_pairs={{2,0},{3,1},{0,2},{1,3},{6,4},{7,5},{4,6},{5,7},{10,8},{11,9},{8,1... | collective-permute-start | bytes 393224 | tf_op jit(solution)/shard_map/ppermute | solution.py:313
  130.3 10.8 %collective-permute-start.32 = (bf16[512,128]{1,0:T(8,128)(2,1)S(1)}, bf16[512,128]{1,0:T(8,128)(2,1)S(1)}, u32[]{:S(2)}, u32[]{:S(2)}) collective-permute-start(bf16[512,128]{1,0:T(8,128)(2,1)S(1)} %get-tuple-element.42), channel_id=1, source_target_pairs={{1,0},{2,1},{3,2},{0,3},{5,4},{6,5},{7,6},{4,7},{9,8},{10,9},{11,1... | collective-permute-start | bytes 393224 | tf_op jit(solution)/shard_map/ppermute | solution.py:313
  (13 other events, 57.3 us)

commit v7 on v6

--- a/solution.py
+++ b/solution.py
@@ -19,7 +19,7 @@
 QUERY_CHUNKS = 4
 OUT_CHUNKS = 4
 FIRST = (1, 3)
-STEPS = (('G', 2, '', 1500), ('G', 1, 'n1', 700), ('G', 3, '', 3000), ('C', 0, '', 700), ('C', 1, '', 700), ('X', 0, '', 1000), ('G', 4, '', 50), ('C', 2, 'y0', 700), ('C', 3, 'y1', 700), ('G', 5, '', 4000), ('G', 6, '', 50), ('K', 0, '', 4000), ('C', 4, '', 700), ('A', 1, 'n0', 4000), ('A', 2, '', 700), ('G', 7, '', 1000), ('C', 5, 'y2', 700), ('A', 3, '', 4000), ('C', 6, 'a3', 700), ('A', 4, '', 1500), ('P', 5, '', 2000), ('G', 8, '', 50), ('C', 7, '', 700), ('R', 5, 'a2 y5 y6', 0), ('P', 6, '', 2000), ('C', 8, '', 700), ('P', 7, 't5 y3', 6000), ('R', 6, 'y4', 700), ('R', 7, 'a1 s7', 1500), ('Q', 8, '', 50))
+STEPS = (('G', 1, 'n1', 6000), ('G', 2, '', 6000), ('C', 0, '', 700), ('G', 3, '', 6000), ('C', 1, '', 4000), ('X', 0, '', 200), ('G', 4, '', 6000), ('C', 2, '', 0), ('G', 5, 'y0', 6000), ('C', 3, 'y1', 4000), ('K', 0, '', 6000), ('G', 6, '', 6000), ('C', 4, '', 0), ('A', 1, 'a1', 0), ('A', 2, 'a3', 2000), ('A', 3, '', 1000), ('C', 5, '', 4000), ('A', 4, '', 2000), ('G', 8, '', 6000), ('G', 7, '', 6000), ('C', 6, '', 0), ('P', 5, '', 3000), ('C', 7, '', 4000), ('R', 5, 'y3', 1000), ('P', 6, '', 6000), ('C', 8, '', 0), ('P', 7, 't5', 3000), ('R', 6, 'y4', 50), ('R', 7, '', 1000), ('Q', 8, 'a2', 4000))
 
 SMEM = pl.BlockSpec(memory_space=pltpu.SMEM)
 VMEM = pl.BlockSpec(memory_space=pltpu.VMEM)

time: 143 us -> 142 us (level)
  Pallas kernels: 43 us -> 36.6 us
  waiting for transfers between devices: 41.3 us -> 47.1 us
    ppermute x33, waiting for transfers between devices: 41.3 us -> 47.1 us  [permute(): lax.ppermute(array, axis, [(source(i) % count, i) for i in range(count)])]
    pallas_call x4, Pallas kernels: 15.1 us -> 12.9 us  [attend(): pl.pallas_call(functools.partial(attend_kernel, len(blocks)), out_shape=j...]
    pallas_call x8, Pallas kernels: 4.84 us -> 2.98 us  [columns_of(): pl.pallas_call(columns_kernel, out_shape=jax.ShapeDtypeStruct((rows, piec...]
    pallas_call x9, Pallas kernels: 12.3 us -> 10.8 us  [combine(): pl.pallas_call(combine_kernel, out_shape=jax.ShapeDtypeStruct(far.shape,...]
    unnamed x24 -> x16, local copies, waits for them, and re-layouts: 2.42 us -> 3.22 us
  transfers between devices with their start and end apart: 33 -> 33, of which waited for: 13 -> 13; matrix products, arithmetic and copies ran while one was open for 0% -> 1% of each run, Pallas kernels for 30% -> 25%
where the time goes in v7:
time: 142 us
  starting transfers between devices  54 us (38%)
  waiting for transfers between devices  47.1 us (33%)
  Pallas kernels  36.6 us (26%)
  local copies, waits for them, and re-layouts  3.22 us (2%)
    ppermute x33, starting transfers between devices, permute(): lax.ppermute(array, axis, [(source(i) % count, i) for i in range(count)])  54 us
    ppermute x33, waiting for transfers between devices, permute(): lax.ppermute(array, axis, [(source(i) % count, i) for i in range(count)])  47.1 us
    pallas_call x4, Pallas kernels, attend(): pl.pallas_call(functools.partial(attend_kernel, len(blocks)), out_shape=j...  12.9 us
    pallas_call x9, Pallas kernels, combine(): pl.pallas_call(combine_kernel, out_shape=jax.ShapeDtypeStruct(far.shape,...  10.8 us
    pallas_call x3, Pallas kernels, partials(): pl.pallas_call(functools.partial(partial_kernel, count, len(mixed)), out_...  3.9 us
    unnamed x16, local copies, waits for them, and re-layouts  3.22 us
    pallas_call x8, Pallas kernels, columns_of(): pl.pallas_call(columns_kernel, out_shape=jax.ShapeDtypeStruct((rows, piec...  2.98 us
  transfers between devices with their start and end apart: 33, of which 13 were waited for; matrix products, arithmetic and copies ran while one was open for 1% of the time, Pallas kernels for 25%

profile of v7, /device:TPU:0, one launch (start us, length us, event | category | flops | bytes accessed | tf_op | source)
XLA Modules:
  0.0 142.0 jit_solution(11645323303431976839)
XLA Ops:
  0.5 2.5 %collective-permute-start.5 = (bf16[1024,256]{1,0:T(8,128)(2,1)}, bf16[1024,256]{1,0:T(8,128)(2,1)}, u32[]{:S(2)}, u32[]{:S(2)}) collective-permute-start(bf16[1024,256]{1,0:T(8,128)(2,1)} %bitcast.27), channel_id=1, source_target_pairs={{24,0},{16,8},{8,16},{0,24},{25,1},{17,9},{9,17},{1,25},{26,2},{18... | collective-permute-start | bytes 1572872 | tf_op jit(solution)/shard_map/ppermute | solution.py:313
  5.6 3.8 %collective-permute-start.6 = (bf16[512,512]{1,0:T(8,128)(2,1)}, bf16[512,512]{1,0:T(8,128)(2,1)S(1)}, u32[]{:S(2)}, u32[]{:S(2)}) collective-permute-start(bf16[512,512]{1,0:T(8,128)(2,1)} %bitcast.8), channel_id=1, source_target_pairs={{1,0},{2,1},{3,2},{0,3},{5,4},{6,5},{7,6},{4,7},{9,8},{10,9},{11,1... | collective-permute-start | bytes 1572872 | tf_op jit(solution)/shard_map/ppermute | solution.py:313
  12.4 3.3 %collective-permute-done.5.far = bf16[1024,256]{1,0:T(8,128)(2,1)} collective-permute-done((bf16[1024,256]{1,0:T(8,128)(2,1)}, bf16[1024,256]{1,0:T(8,128)(2,1)}, u32[]{:S(2)}, u32[]{:S(2)}) %collective-permute-start.5) | collective-permute-done | bytes 524320 | tf_op jit(solution)/shard_map/ppermute | solution.py:313
  17.8 2.2 %collective-permute-start.9 = (bf16[1024,256]{1,0:T(8,128)(2,1)S(1)}, bf16[1024,256]{1,0:T(8,128)(2,1)S(1)}, u32[]{:S(2)}, u32[]{:S(2)}) collective-permute-start(bf16[1024,256]{1,0:T(8,128)(2,1)S(1)} %shard_map.84.rest_0_.refs_4_), channel_id=1, source_target_pairs={{4,0},{0,4},{5,1},{1,5},{6,2},{2,6},{7,3},{3,7},{12,8},{8,12},{13,... | collective-permute-start | bytes 1572872 | tf_op jit(solution)/shard_map/ppermute | solution.py:313
  21.2 5.7 %collective-permute-done.3.far = bf16[1024,256]{1,0:T(8,128)(2,1)S(1)} collective-permute-done((bf16[1024,256]{1,0:T(8,128)(2,1)S(1)}, bf16[1024,256]{1,0:T(8,128)(2,1)S(1)}, u32[]{:S(2)}, u32[]{:S(2)}) %collective-permute-start.3) | collective-permute-done | bytes 524320 | tf_op jit(solution)/shard_map/ppermute | solution.py:313
  26.8 2.2 %collective-permute-start.10 = (bf16[1024,256]{1,0:T(8,128)(2,1)}, bf16[1024,256]{1,0:T(8,128)(2,1)}, u32[]{:S(2)}, u32[]{:S(2)}) collective-permute-start(bf16[1024,256]{1,0:T(8,128)(2,1)} %shard_map.85.rest_0_), channel_id=1, source_target_pairs={{24,0},{16,8},{8,16},{0,24},{25,1},{17,9},{9,17},{1,25},{26,2},{18... | collective-permute-start | bytes 1572872 | tf_op jit(solution)/shard_map/ppermute | solution.py:313
  31.9 2.7 %collective-permute-start.7 = (bf16[512,512]{1,0:T(8,128)(2,1)S(1)}, bf16[512,512]{1,0:T(8,128)(2,1)S(1)}, u32[]{:S(2)}, u32[]{:S(2)}) collective-permute-start(bf16[512,512]{1,0:T(8,128)(2,1)S(1)} %shard_map.87.rest_0_), channel_id=1, source_target_pairs={{2,0},{3,1},{0,2},{1,3},{6,4},{7,5},{4,6},{5,7},{10,8},{11,9},{8,1... | collective-permute-start | bytes 1572872 | tf_op jit(solution)/shard_map/ppermute | solution.py:313
  34.7 3.3 %collective-permute-done.11.far = bf16[1024,256]{1,0:T(8,128)(2,1)S(1)} collective-permute-done((bf16[1024,256]{1,0:T(8,128)(2,1)S(1)}, bf16[1024,256]{1,0:T(8,128)(2,1)S(1)}, u32[]{:S(2)}, u32[]{:S(2)}) %collective-permute-start.11) | collective-permute-done | bytes 524320 | tf_op jit(solution)/shard_map/ppermute | solution.py:313
  38.1 2.3 %collective-permute-start.12 = (bf16[1024,256]{1,0:T(8,128)(2,1)S(1)}, bf16[1024,256]{1,0:T(8,128)(2,1)S(1)}, u32[]{:S(2)}, u32[]{:S(2)}) collective-permute-start(bf16[1024,256]{1,0:T(8,128)(2,1)S(1)} %shard_map.88.rest_0_), channel_id=1, source_target_pairs={{24,0},{16,8},{8,16},{0,24},{25,1},{17,9},{9,17},{1,25},{26,2},{18... | collective-permute-start | bytes 1572872 | tf_op jit(solution)/shard_map/ppermute | solution.py:313
  43.6 5.8 %collective-permute-done.10.far = bf16[1024,256]{1,0:T(8,128)(2,1)} collective-permute-done((bf16[1024,256]{1,0:T(8,128)(2,1)}, bf16[1024,256]{1,0:T(8,128)(2,1)}, u32[]{:S(2)}, u32[]{:S(2)}) %collective-permute-start.10) | collective-permute-done | bytes 524320 | tf_op jit(solution)/shard_map/ppermute | solution.py:313
  49.4 2.2 %collective-permute-start.16 = (bf16[1024,256]{1,0:T(8,128)(2,1)S(1)}, bf16[1024,256]{1,0:T(8,128)(2,1)S(1)}, u32[]{:S(2)}, u32[]{:S(2)}) collective-permute-start(bf16[1024,256]{1,0:T(8,128)(2,1)S(1)} %shard_map.90.rest_0_), channel_id=1, source_target_pairs={{24,0},{16,8},{8,16},{0,24},{25,1},{17,9},{9,17},{1,25},{26,2},{18... | collective-permute-start | bytes 1572872 | tf_op jit(solution)/shard_map/ppermute | solution.py:313
  54.5 3.1 %collective-permute-done.7.refs_2_.refs_7_ = bf16[512,512]{1,0:T(8,128)(2,1)S(1)} collective-permute-done((bf16[512,512]{1,0:T(8,128)(2,1)S(1)}, bf16[512,512]{1,0:T(8,128)(2,1)S(1)}, u32[]{:S(2)}, u32[]{:S(2)}) %collective-permute-start.7) | collective-permute-done | bytes 524320 | tf_op jit(solution)/shard_map/ppermute | solution.py:313
  57.7 1.9 %shard_map.92 = (bf16[512,128]{1,0:T(8,128)(2,1)S(1)}, bf16[512,128]{1,0:T(8,128)(2,1)S(1)}, f32[512,128]{1,0:T(8,128)S(1)}) custom-call(s32[2]{0:T(128)S(1)} %pad_add_fusion.ids, bf16[512,512]{1,0:T(8,128)(2,1)S(1)} %bitcast.10, bf16[512,512]{1,0:T(8,128)(2,1)S(1)} %collective-permute-done.rest_1_.refs_1_.refs_12_, ...), custom_call_target="tpu_custom_call" | custom-call | flops 6291456000 | tf_op jit(solution)/shard_map/pallas_call | solution.py:144
  63.9 3.1 %shard_map.95.refs_11_.refs_0_ = bf16[512,256]{1,0:T(8,128)(2,1)S(1)} custom-call(s32[2]{0:T(128)S(1)} %pad_add_fusion.ids, bf16[512,512]{1,0:T(8,128)(2,1)S(1)} %bitcast.11, bf16[512,512]{1,0:T(8,128)(2,1)S(1)} %collective-permute-done.rest_1_.refs_1_.refs_12_, bf16[512,512]{1,0:T(8,128)(2,1)S(1)} %collective-permute-done.7.refs_2_.refs_7_, ...), custom_call_target="tpu_custom_call" | custom-call | tf_op jit(solution)/shard_map/pallas_call | solution.py:188
  67.0 3.6 %shard_map.96.refs_11_.refs_1_ = bf16[512,256]{1,0:T(8,128)(2,1)S(1)} custom-call(s32[2]{0:T(128)S(1)} %pad_add_fusion.ids, bf16[512,512]{1,0:T(8,128)(2,1)S(1)} %bitcast.12, bf16[512,512]{1,0:T(8,128)(2,1)S(1)} %collective-permute-done.rest_1_.refs_1_.refs_12_, bf16[512,512]{1,0:T(8,128)(2,1)S(1)} %collective-permute-done.7.refs_2_.refs_7_, ...), custom_call_target="tpu_custom_call" | custom-call | flops 2097152000 | tf_op jit(solution)/shard_map/pallas_call | solution.py:188
  70.7 3.1 %shard_map.97.rest_0_.refs_2_ = bf16[512,256]{1,0:T(8,128)(2,1)S(1)} custom-call(s32[2]{0:T(128)S(1)} %pad_add_fusion.ids, bf16[512,512]{1,0:T(8,128)(2,1)S(1)} %bitcast.13, bf16[512,512]{1,0:T(8,128)(2,1)S(1)} %collective-permute-done.rest_1_.refs_1_.refs_12_, bf16[512,512]{1,0:T(8,128)(2,1)S(1)} %collective-permute-done.7.refs_2_.refs_7_, ...), custom_call_target="tpu_custom_call" | custom-call | flops 1048576000 | tf_op jit(solution)/shard_map/pallas_call | solution.py:188
  76.0 2.4 %collective-permute-done.15.refs_5_.refs_1_ = bf16[1024,256]{1,0:T(8,128)(2,1)S(1)} collective-permute-done((bf16[1024,256]{1,0:T(8,128)(2,1)S(1)}, bf16[1024,256]{1,0:T(8,128)(2,1)S(1)}, u32[]{:S(2)}, u32[]{:S(2)}) %collective-permute-start.15) | collective-permute-done | bytes 524320 | tf_op jit(solution)/shard_map/ppermute | solution.py:313
  78.3 3.1 %shard_map.99.rest_0_.refs_3_ = bf16[512,256]{1,0:T(8,128)(2,1)S(1)} custom-call(s32[2]{0:T(128)S(1)} %pad_add_fusion.ids, bf16[512,512]{1,0:T(8,128)(2,1)S(1)} %bitcast.14, bf16[512,512]{1,0:T(8,128)(2,1)S(1)} %collective-permute-done.rest_1_.refs_1_.refs_12_, bf16[512,512]{1,0:T(8,128)(2,1)S(1)} %collective-permute-done.7.refs_2_.refs_7_, ...), custom_call_target="tpu_custom_call" | custom-call | flops 2097152000 | tf_op jit(solution)/shard_map/pallas_call | solution.py:188
  85.4 2.0 %collective-permute-start.22 = (bf16[1024,256]{1,0:T(8,128)(2,1)S(1)}, bf16[1024,256]{1,0:T(8,128)(2,1)S(1)}, u32[]{:S(2)}, u32[]{:S(2)}) collective-permute-start(bf16[1024,256]{1,0:T(8,128)(2,1)S(1)} %shard_map.102.refs_6_.refs_4_), channel_id=1, source_target_pairs={{4,0},{0,4},{5,1},{1,5},{6,2},{2,6},{7,3},{3,7},{12,8},{8,12},{13,... | collective-permute-start | bytes 1572872 | tf_op jit(solution)/shard_map/ppermute | solution.py:313
  87.4 2.4 %collective-permute-done.17.refs_5_ = bf16[1024,256]{1,0:T(8,128)(2,1)S(1)} collective-permute-done((bf16[1024,256]{1,0:T(8,128)(2,1)S(1)}, bf16[1024,256]{1,0:T(8,128)(2,1)S(1)}, u32[]{:S(2)}, u32[]{:S(2)}) %collective-permute-start.17) | collective-permute-done | bytes 524320 | tf_op jit(solution)/shard_map/ppermute | solution.py:313
  92.7 3.8 %collective-permute-done.20.far = bf16[1024,256]{1,0:T(8,128)(2,1)S(1)} collective-permute-done((bf16[1024,256]{1,0:T(8,128)(2,1)S(1)}, bf16[1024,256]{1,0:T(8,128)(2,1)S(1)}, u32[]{:S(2)}, u32[]{:S(2)}) %collective-permute-start.20) | collective-permute-done | bytes 524320 | tf_op jit(solution)/shard_map/ppermute | solution.py:313
  97.6 2.0 %collective-permute-start.24 = (bf16[1024,256]{1,0:T(8,128)(2,1)S(1)}, bf16[1024,256]{1,0:T(8,128)(2,1)S(1)}, u32[]{:S(2)}, u32[]{:S(2)}) collective-permute-start(bf16[1024,256]{1,0:T(8,128)(2,1)S(1)} %shard_map.104.refs_0_.refs_4_), channel_id=1, source_target_pairs={{4,0},{0,4},{5,1},{1,5},{6,2},{2,6},{7,3},{3,7},{12,8},{8,12},{13,... | collective-permute-start | bytes 1572872 | tf_op jit(solution)/shard_map/ppermute | solution.py:313
  100.3 2.9 %collective-permute-start.21 = (bf16[512,128]{1,0:T(8,128)(2,1)S(1)}, bf16[512,128]{1,0:T(8,128)(2,1)S(1)}, u32[]{:S(2)}, u32[]{:S(2)}) collective-permute-start(bf16[512,128]{1,0:T(8,128)(2,1)S(1)} %get-tuple-element.30), channel_id=1, source_target_pairs={{2,0},{3,1},{0,2},{1,3},{6,4},{7,5},{4,6},{5,7},{10,8},{11,9},{8,1... | collective-permute-start | bytes 393224 | tf_op jit(solution)/shard_map/ppermute | solution.py:313
  109.9 2.6 %collective-permute-done.24.refs_5_ = bf16[1024,256]{1,0:T(8,128)(2,1)S(1)} collective-permute-done((bf16[1024,256]{1,0:T(8,128)(2,1)S(1)}, bf16[1024,256]{1,0:T(8,128)(2,1)S(1)}, u32[]{:S(2)}, u32[]{:S(2)}) %collective-permute-start.24) | collective-permute-done | bytes 524320 | tf_op jit(solution)/shard_map/ppermute | solution.py:313
  113.9 1.9 %collective-permute-start.27 = (bf16[2,512,128]{2,1,0:T(8,128)(2,1)S(1)}, bf16[2,512,128]{2,1,0:T(8,128)(2,1)S(1)}, u32[]{:S(2)}, u32[]{:S(2)}) collective-permute-start(bf16[2,512,128]{2,1,0:T(8,128)(2,1)S(1)} %get-tuple-element.36), channel_id=1, source_target_pairs={{1,0},{0,1},{3,2},{2,3},{5,4},{4,5},{7,6},{6,7},{9,8},{8,9},{11,10... | collective-permute-start | bytes 786440 | tf_op jit(solution)/shard_map/ppermute | solution.py:313
  116.3 2.5 %collective-permute-start.26 = (bf16[512,128]{1,0:T(8,128)(2,1)S(1)}, bf16[512,128]{1,0:T(8,128)(2,1)S(1)}, u32[]{:S(2)}, u32[]{:S(2)}) collective-permute-start(bf16[512,128]{1,0:T(8,128)(2,1)S(1)} %get-tuple-element.35), channel_id=1, source_target_pairs={{2,0},{3,1},{0,2},{1,3},{6,4},{7,5},{4,6},{5,7},{10,8},{11,9},{8,1... | collective-permute-start | bytes 393224 | tf_op jit(solution)/shard_map/ppermute | solution.py:313
  118.8 4.7 %collective-permute-done.27.got = bf16[2,512,128]{2,1,0:T(8,128)(2,1)S(1)} collective-permute-done((bf16[2,512,128]{2,1,0:T(8,128)(2,1)S(1)}, bf16[2,512,128]{2,1,0:T(8,128)(2,1)S(1)}, u32[]{:S(2)}, u32[]{:S(2)}) %collective-permute-start.27) | collective-permute-done | bytes 262176 | tf_op jit(solution)/shard_map/ppermute | solution.py:313
  124.2 1.7 %collective-permute-start.28 = (bf16[512,128]{1,0:T(8,128)(2,1)S(1)}, bf16[512,128]{1,0:T(8,128)(2,1)S(1)}, u32[]{:S(2)}, u32[]{:S(2)}) collective-permute-start(bf16[512,128]{1,0:T(8,128)(2,1)S(1)} %get-tuple-element.38), channel_id=1, source_target_pairs={{2,0},{3,1},{0,2},{1,3},{6,4},{7,5},{4,6},{5,7},{10,8},{11,9},{8,1... | collective-permute-start | bytes 393224 | tf_op jit(solution)/shard_map/ppermute | solution.py:313
  127.2 2.5 %collective-permute-start.30 = (bf16[512,128]{1,0:T(8,128)(2,1)S(1)}, bf16[512,128]{1,0:T(8,128)(2,1)S(1)}, u32[]{:S(2)}, u32[]{:S(2)}) collective-permute-start(bf16[512,128]{1,0:T(8,128)(2,1)S(1)} %get-tuple-element.40), channel_id=1, source_target_pairs={{3,0},{0,1},{1,2},{2,3},{7,4},{4,5},{5,6},{6,7},{11,8},{8,9},{9,10... | collective-permute-start | bytes 393224 | tf_op jit(solution)/shard_map/ppermute | solution.py:313
  129.7 2.4 %collective-permute-start.32 = (bf16[512,128]{1,0:T(8,128)(2,1)S(1)}, bf16[512,128]{1,0:T(8,128)(2,1)S(1)}, u32[]{:S(2)}, u32[]{:S(2)}) collective-permute-start(bf16[512,128]{1,0:T(8,128)(2,1)S(1)} %get-tuple-element.42), channel_id=1, source_target_pairs={{1,0},{2,1},{3,2},{0,3},{5,4},{6,5},{7,6},{4,7},{9,8},{10,9},{11,1... | collective-permute-start | bytes 393224 | tf_op jit(solution)/shard_map/ppermute | solution.py:313
  132.1 6.0 %collective-permute-done.28.refs_5_ = bf16[512,128]{1,0:T(8,128)(2,1)S(1)} collective-permute-done((bf16[512,128]{1,0:T(8,128)(2,1)S(1)}, bf16[512,128]{1,0:T(8,128)(2,1)S(1)}, u32[]{:S(2)}, u32[]{:S(2)}) %collective-permute-start.28) | collective-permute-done | bytes 131104 | tf_op jit(solution)/shard_map/ppermute | solution.py:313
  138.2 2.8 %collective-permute-done.31.refs_8_ = bf16[512,128]{1,0:T(8,128)(2,1)S(1)} collective-permute-done((bf16[512,128]{1,0:T(8,128)(2,1)S(1)}, bf16[512,128]{1,0:T(8,128)(2,1)S(1)}, u32[]{:S(2)}, u32[]{:S(2)}) %collective-permute-start.31) | collective-permute-done | bytes 131104 | tf_op jit(solution)/shard_map/ppermute | solution.py:313
  (83 shorter events, 45.2 us)
Async XLA Ops:
  0.5 10.9 %collective-permute-start.4 = (bf16[1024,256]{1,0:T(8,128)(2,1)}, bf16[1024,256]{1,0:T(8,128)(2,1)S(1)}, u32[]{:S(2)}, u32[]{:S(2)}) collective-permute-start(bf16[1024,256]{1,0:T(8,128)(2,1)} %bitcast.26), channel_id=1, source_target_pairs={{8,0},{0,8},{24,16},{16,24},{9,1},{1,9},{25,17},{17,25},{10,2},{2,... | collective-permute-start | bytes 1572872 | tf_op jit(solution)/shard_map/ppermute | solution.py:313
  0.5 15.2 %collective-permute-start.5 = (bf16[1024,256]{1,0:T(8,128)(2,1)}, bf16[1024,256]{1,0:T(8,128)(2,1)}, u32[]{:S(2)}, u32[]{:S(2)}) collective-permute-start(bf16[1024,256]{1,0:T(8,128)(2,1)} %bitcast.27), channel_id=1, source_target_pairs={{24,0},{16,8},{8,16},{0,24},{25,1},{17,9},{9,17},{1,25},{26,2},{18... | collective-permute-start | bytes 1572872 | tf_op jit(solution)/shard_map/ppermute | solution.py:313
  3.1 27.2 %collective-permute-start = (bf16[512,512]{1,0:T(8,128)(2,1)}, bf16[512,512]{1,0:T(8,128)(2,1)S(1)}, u32[]{:S(2)}, u32[]{:S(2)}) collective-permute-start(bf16[512,512]{1,0:T(8,128)(2,1)} %bitcast.7), channel_id=1, source_target_pairs={{3,0},{0,1},{1,2},{2,3},{7,4},{4,5},{5,6},{6,7},{11,8},{8,9},{9,10... | collective-permute-start | bytes 1572872 | tf_op jit(solution)/shard_map/ppermute | solution.py:313
  4.6 15.3 %collective-permute-start.1 = (bf16[1024,1024]{1,0:T(8,128)(2,1)}, bf16[1024,1024]{1,0:T(8,128)(2,1)}, u32[]{:S(2)}, u32[]{:S(2)}) collective-permute-start(bf16[1024,1024]{1,0:T(8,128)(2,1)} %bitcast.16), channel_id=1, source_target_pairs={{8,0},{0,8},{24,16},{16,24},{9,1},{1,9},{25,17},{17,25},{10,2},{2,... | collective-permute-start | bytes 6291464 | tf_op jit(solution)/shard_map/ppermute | solution.py:313
  5.6 26.2 %collective-permute-start.6 = (bf16[512,512]{1,0:T(8,128)(2,1)}, bf16[512,512]{1,0:T(8,128)(2,1)S(1)}, u32[]{:S(2)}, u32[]{:S(2)}) collective-permute-start(bf16[512,512]{1,0:T(8,128)(2,1)} %bitcast.8), channel_id=1, source_target_pairs={{1,0},{2,1},{3,2},{0,3},{5,4},{6,5},{7,6},{4,7},{9,8},{10,9},{11,1... | collective-permute-start | bytes 1572872 | tf_op jit(solution)/shard_map/ppermute | solution.py:313
  11.4 15.4 %collective-permute-start.3 = (bf16[1024,256]{1,0:T(8,128)(2,1)S(1)}, bf16[1024,256]{1,0:T(8,128)(2,1)S(1)}, u32[]{:S(2)}, u32[]{:S(2)}) collective-permute-start(bf16[1024,256]{1,0:T(8,128)(2,1)S(1)} %shard_map.82.rest_0_), channel_id=1, source_target_pairs={{24,0},{16,8},{8,16},{0,24},{25,1},{17,9},{9,17},{1,25},{26,2},{18... | collective-permute-start | bytes 1572872 | tf_op jit(solution)/shard_map/ppermute | solution.py:313
  17.8 23.8 %collective-permute-start.9 = (bf16[1024,256]{1,0:T(8,128)(2,1)S(1)}, bf16[1024,256]{1,0:T(8,128)(2,1)S(1)}, u32[]{:S(2)}, u32[]{:S(2)}) collective-permute-start(bf16[1024,256]{1,0:T(8,128)(2,1)S(1)} %shard_map.84.rest_0_.refs_4_), channel_id=1, source_target_pairs={{4,0},{0,4},{5,1},{1,5},{6,2},{2,6},{7,3},{3,7},{12,8},{8,12},{13,... | collective-permute-start | bytes 1572872 | tf_op jit(solution)/shard_map/ppermute | solution.py:313
  20.0 18.1 %collective-permute-start.11 = (bf16[1024,256]{1,0:T(8,128)(2,1)S(1)}, bf16[1024,256]{1,0:T(8,128)(2,1)S(1)}, u32[]{:S(2)}, u32[]{:S(2)}) collective-permute-start(bf16[1024,256]{1,0:T(8,128)(2,1)S(1)} %shard_map.83.rest_0_), channel_id=1, source_target_pairs={{24,0},{16,8},{8,16},{0,24},{25,1},{17,9},{9,17},{1,25},{26,2},{18... | collective-permute-start | bytes 1572872 | tf_op jit(solution)/shard_map/ppermute | solution.py:313
  26.8 22.6 %collective-permute-start.10 = (bf16[1024,256]{1,0:T(8,128)(2,1)}, bf16[1024,256]{1,0:T(8,128)(2,1)}, u32[]{:S(2)}, u32[]{:S(2)}) collective-permute-start(bf16[1024,256]{1,0:T(8,128)(2,1)} %shard_map.85.rest_0_), channel_id=1, source_target_pairs={{24,0},{16,8},{8,16},{0,24},{25,1},{17,9},{9,17},{1,25},{26,2},{18... | collective-permute-start | bytes 1572872 | tf_op jit(solution)/shard_map/ppermute | solution.py:313
  30.2 21.4 %collective-permute-start.8 = (bf16[1024,256]{1,0:T(8,128)(2,1)S(1)}, bf16[1024,256]{1,0:T(8,128)(2,1)S(1)}, u32[]{:S(2)}, u32[]{:S(2)}) collective-permute-start(bf16[1024,256]{1,0:T(8,128)(2,1)S(1)} %shard_map.86.rest_0_.refs_4_), channel_id=1, source_target_pairs={{4,0},{0,4},{5,1},{1,5},{6,2},{2,6},{7,3},{3,7},{12,8},{8,12},{13,... | collective-permute-start | bytes 1572872 | tf_op jit(solution)/shard_map/ppermute | solution.py:313
  31.9 25.8 %collective-permute-start.7 = (bf16[512,512]{1,0:T(8,128)(2,1)S(1)}, bf16[512,512]{1,0:T(8,128)(2,1)S(1)}, u32[]{:S(2)}, u32[]{:S(2)}) collective-permute-start(bf16[512,512]{1,0:T(8,128)(2,1)S(1)} %shard_map.87.rest_0_), channel_id=1, source_target_pairs={{2,0},{3,1},{0,2},{1,3},{6,4},{7,5},{4,6},{5,7},{10,8},{11,9},{8,1... | collective-permute-start | bytes 1572872 | tf_op jit(solution)/shard_map/ppermute | solution.py:313
  38.1 23.5 %collective-permute-start.12 = (bf16[1024,256]{1,0:T(8,128)(2,1)S(1)}, bf16[1024,256]{1,0:T(8,128)(2,1)S(1)}, u32[]{:S(2)}, u32[]{:S(2)}) collective-permute-start(bf16[1024,256]{1,0:T(8,128)(2,1)S(1)} %shard_map.88.rest_0_), channel_id=1, source_target_pairs={{24,0},{16,8},{8,16},{0,24},{25,1},{17,9},{9,17},{1,25},{26,2},{18... | collective-permute-start | bytes 1572872 | tf_op jit(solution)/shard_map/ppermute | solution.py:313
  41.6 25.5 %collective-permute-start.13 = (bf16[1024,256]{1,0:T(8,128)(2,1)S(1)}, bf16[1024,256]{1,0:T(8,128)(2,1)}, u32[]{:S(2)}, u32[]{:S(2)}) collective-permute-start(bf16[1024,256]{1,0:T(8,128)(2,1)S(1)} %shard_map.89.rest_0_.refs_4_), channel_id=1, source_target_pairs={{4,0},{0,4},{5,1},{1,5},{6,2},{2,6},{7,3},{3,7},{12,8},{8,12},{13,... | collective-permute-start | bytes 1572872 | tf_op jit(solution)/shard_map/ppermute | solution.py:313
  49.4 24.4 %collective-permute-start.16 = (bf16[1024,256]{1,0:T(8,128)(2,1)S(1)}, bf16[1024,256]{1,0:T(8,128)(2,1)S(1)}, u32[]{:S(2)}, u32[]{:S(2)}) collective-permute-start(bf16[1024,256]{1,0:T(8,128)(2,1)S(1)} %shard_map.90.rest_0_), channel_id=1, source_target_pairs={{24,0},{16,8},{8,16},{0,24},{25,1},{17,9},{9,17},{1,25},{26,2},{18... | collective-permute-start | bytes 1572872 | tf_op jit(solution)/shard_map/ppermute | solution.py:313
  52.9 17.7 %collective-permute-start.14 = (bf16[1024,256]{1,0:T(8,128)(2,1)S(1)}, bf16[1024,256]{1,0:T(8,128)(2,1)S(1)}, u32[]{:S(2)}, u32[]{:S(2)}) collective-permute-start(bf16[1024,256]{1,0:T(8,128)(2,1)S(1)} %shard_map.91.refs_8_.refs_4_), channel_id=1, source_target_pairs={{4,0},{0,4},{5,1},{1,5},{6,2},{2,6},{7,3},{3,7},{12,8},{8,12},{13,... | collective-permute-start | bytes 1572872 | tf_op jit(solution)/shard_map/ppermute | solution.py:313
  61.5 22.6 %collective-permute-start.18 = (bf16[1024,256]{1,0:T(8,128)(2,1)S(1)}, bf16[1024,256]{1,0:T(8,128)(2,1)S(1)}, u32[]{:S(2)}, u32[]{:S(2)}) collective-permute-start(bf16[1024,256]{1,0:T(8,128)(2,1)S(1)} %shard_map.93.rest_0_), channel_id=1, source_target_pairs={{24,0},{16,8},{8,16},{0,24},{25,1},{17,9},{9,17},{1,25},{26,2},{18... | collective-permute-start | bytes 1572872 | tf_op jit(solution)/shard_map/ppermute | solution.py:313
  62.8 15.5 %collective-permute-start.15 = (bf16[1024,256]{1,0:T(8,128)(2,1)S(1)}, bf16[1024,256]{1,0:T(8,128)(2,1)S(1)}, u32[]{:S(2)}, u32[]{:S(2)}) collective-permute-start(bf16[1024,256]{1,0:T(8,128)(2,1)S(1)} %shard_map.94.refs_11_.refs_4_), channel_id=1, source_target_pairs={{4,0},{0,4},{5,1},{1,5},{6,2},{2,6},{7,3},{3,7},{12,8},{8,12},{13,... | collective-permute-start | bytes 1572872 | tf_op jit(solution)/shard_map/ppermute | solution.py:313
  74.9 14.8 %collective-permute-start.17 = (bf16[1024,256]{1,0:T(8,128)(2,1)S(1)}, bf16[1024,256]{1,0:T(8,128)(2,1)S(1)}, u32[]{:S(2)}, u32[]{:S(2)}) collective-permute-start(bf16[1024,256]{1,0:T(8,128)(2,1)S(1)} %shard_map.98.refs_11_.refs_4_), channel_id=1, source_target_pairs={{4,0},{0,4},{5,1},{1,5},{6,2},{2,6},{7,3},{3,7},{12,8},{8,12},{13,... | collective-permute-start | bytes 1572872 | tf_op jit(solution)/shard_map/ppermute | solution.py:313
  82.3 14.2 %collective-permute-start.20 = (bf16[1024,256]{1,0:T(8,128)(2,1)S(1)}, bf16[1024,256]{1,0:T(8,128)(2,1)S(1)}, u32[]{:S(2)}, u32[]{:S(2)}) collective-permute-start(bf16[1024,256]{1,0:T(8,128)(2,1)S(1)} %shard_map.101.rest_0_), channel_id=1, source_target_pairs={{24,0},{16,8},{8,16},{0,24},{25,1},{17,9},{9,17},{1,25},{26,2},{18... | collective-permute-start | bytes 1572872 | tf_op jit(solution)/shard_map/ppermute | solution.py:313
  82.6 24.5 %collective-permute-start.25 = (bf16[1024,256]{1,0:T(8,128)(2,1)S(1)}, bf16[1024,256]{1,0:T(8,128)(2,1)S(1)}, u32[]{:S(2)}, u32[]{:S(2)}) collective-permute-start(bf16[1024,256]{1,0:T(8,128)(2,1)S(1)} %shard_map.100.rest_0_), channel_id=1, source_target_pairs={{24,0},{16,8},{8,16},{0,24},{25,1},{17,9},{9,17},{1,25},{26,2},{18... | collective-permute-start | bytes 1572872 | tf_op jit(solution)/shard_map/ppermute | solution.py:313
  85.4 17.8 %collective-permute-start.22 = (bf16[1024,256]{1,0:T(8,128)(2,1)S(1)}, bf16[1024,256]{1,0:T(8,128)(2,1)S(1)}, u32[]{:S(2)}, u32[]{:S(2)}) collective-permute-start(bf16[1024,256]{1,0:T(8,128)(2,1)S(1)} %shard_map.102.refs_6_.refs_4_), channel_id=1, source_target_pairs={{4,0},{0,4},{5,1},{1,5},{6,2},{2,6},{7,3},{3,7},{12,8},{8,12},{13,... | collective-permute-start | bytes 1572872 | tf_op jit(solution)/shard_map/ppermute | solution.py:313
  91.1 8.6 %collective-permute-start.19 = (bf16[2,512,128]{2,1,0:T(8,128)(2,1)S(1)}, bf16[2,512,128]{2,1,0:T(8,128)(2,1)S(1)}, u32[]{:S(2)}, u32[]{:S(2)}) collective-permute-start(bf16[2,512,128]{2,1,0:T(8,128)(2,1)S(1)} %get-tuple-element.28), channel_id=1, source_target_pairs={{1,0},{0,1},{3,2},{2,3},{5,4},{4,5},{7,6},{6,7},{9,8},{8,9},{11,10... | collective-permute-start | bytes 786440 | tf_op jit(solution)/shard_map/ppermute | solution.py:313
  97.6 14.9 %collective-permute-start.24 = (bf16[1024,256]{1,0:T(8,128)(2,1)S(1)}, bf16[1024,256]{1,0:T(8,128)(2,1)S(1)}, u32[]{:S(2)}, u32[]{:S(2)}) collective-permute-start(bf16[1024,256]{1,0:T(8,128)(2,1)S(1)} %shard_map.104.refs_0_.refs_4_), channel_id=1, source_target_pairs={{4,0},{0,4},{5,1},{1,5},{6,2},{2,6},{7,3},{3,7},{12,8},{8,12},{13,... | collective-permute-start | bytes 1572872 | tf_op jit(solution)/shard_map/ppermute | solution.py:313
  100.3 9.7 %collective-permute-start.21 = (bf16[512,128]{1,0:T(8,128)(2,1)S(1)}, bf16[512,128]{1,0:T(8,128)(2,1)S(1)}, u32[]{:S(2)}, u32[]{:S(2)}) collective-permute-start(bf16[512,128]{1,0:T(8,128)(2,1)S(1)} %get-tuple-element.30), channel_id=1, source_target_pairs={{2,0},{3,1},{0,2},{1,3},{6,4},{7,5},{4,6},{5,7},{10,8},{11,9},{8,1... | collective-permute-start | bytes 393224 | tf_op jit(solution)/shard_map/ppermute | solution.py:313
  104.5 11.2 %collective-permute-start.23 = (bf16[2,512,128]{2,1,0:T(8,128)(2,1)S(1)}, bf16[2,512,128]{2,1,0:T(8,128)(2,1)S(1)}, u32[]{:S(2)}, u32[]{:S(2)}) collective-permute-start(bf16[2,512,128]{2,1,0:T(8,128)(2,1)S(1)} %get-tuple-element.32), channel_id=1, source_target_pairs={{1,0},{0,1},{3,2},{2,3},{5,4},{4,5},{7,6},{6,7},{9,8},{8,9},{11,10... | collective-permute-start | bytes 786440 | tf_op jit(solution)/shard_map/ppermute | solution.py:313
  108.3 17.6 %collective-permute-start.29 = (bf16[1024,256]{1,0:T(8,128)(2,1)S(1)}, bf16[1024,256]{1,0:T(8,128)(2,1)S(1)}, u32[]{:S(2)}, u32[]{:S(2)}) collective-permute-start(bf16[1024,256]{1,0:T(8,128)(2,1)S(1)} %shard_map.107.refs_6_.refs_4_), channel_id=1, source_target_pairs={{4,0},{0,4},{5,1},{1,5},{6,2},{2,6},{7,3},{3,7},{12,8},{8,12},{13,... | collective-permute-start | bytes 1572872 | tf_op jit(solution)/shard_map/ppermute | solution.py:313
  113.9 9.7 %collective-permute-start.27 = (bf16[2,512,128]{2,1,0:T(8,128)(2,1)S(1)}, bf16[2,512,128]{2,1,0:T(8,128)(2,1)S(1)}, u32[]{:S(2)}, u32[]{:S(2)}) collective-permute-start(bf16[2,512,128]{2,1,0:T(8,128)(2,1)S(1)} %get-tuple-element.36), channel_id=1, source_target_pairs={{1,0},{0,1},{3,2},{2,3},{5,4},{4,5},{7,6},{6,7},{9,8},{8,9},{11,10... | collective-permute-start | bytes 786440 | tf_op jit(solution)/shard_map/ppermute | solution.py:313
  116.3 15.8 %collective-permute-start.26 = (bf16[512,128]{1,0:T(8,128)(2,1)S(1)}, bf16[512,128]{1,0:T(8,128)(2,1)S(1)}, u32[]{:S(2)}, u32[]{:S(2)}) collective-permute-start(bf16[512,128]{1,0:T(8,128)(2,1)S(1)} %get-tuple-element.35), channel_id=1, source_target_pairs={{2,0},{3,1},{0,2},{1,3},{6,4},{7,5},{4,6},{5,7},{10,8},{11,9},{8,1... | collective-permute-start | bytes 393224 | tf_op jit(solution)/shard_map/ppermute | solution.py:313
  124.2 14.0 %collective-permute-start.28 = (bf16[512,128]{1,0:T(8,128)(2,1)S(1)}, bf16[512,128]{1,0:T(8,128)(2,1)S(1)}, u32[]{:S(2)}, u32[]{:S(2)}) collective-permute-start(bf16[512,128]{1,0:T(8,128)(2,1)S(1)} %get-tuple-element.38), channel_id=1, source_target_pairs={{2,0},{3,1},{0,2},{1,3},{6,4},{7,5},{4,6},{5,7},{10,8},{11,9},{8,1... | collective-permute-start | bytes 393224 | tf_op jit(solution)/shard_map/ppermute | solution.py:313
  127.2 11.0 %collective-permute-start.30 = (bf16[512,128]{1,0:T(8,128)(2,1)S(1)}, bf16[512,128]{1,0:T(8,128)(2,1)S(1)}, u32[]{:S(2)}, u32[]{:S(2)}) collective-permute-start(bf16[512,128]{1,0:T(8,128)(2,1)S(1)} %get-tuple-element.40), channel_id=1, source_target_pairs={{3,0},{0,1},{1,2},{2,3},{7,4},{4,5},{5,6},{6,7},{11,8},{8,9},{9,10... | collective-permute-start | bytes 393224 | tf_op jit(solution)/shard_map/ppermute | solution.py:313
  129.7 11.3 %collective-permute-start.31 = (bf16[512,128]{1,0:T(8,128)(2,1)S(1)}, bf16[512,128]{1,0:T(8,128)(2,1)S(1)}, u32[]{:S(2)}, u32[]{:S(2)}) collective-permute-start(bf16[512,128]{1,0:T(8,128)(2,1)S(1)} %get-tuple-element.41), channel_id=1, source_target_pairs={{2,0},{3,1},{0,2},{1,3},{6,4},{7,5},{4,6},{5,7},{10,8},{11,9},{8,1... | collective-permute-start | bytes 393224 | tf_op jit(solution)/shard_map/ppermute | solution.py:313
  129.7 11.2 %collective-permute-start.32 = (bf16[512,128]{1,0:T(8,128)(2,1)S(1)}, bf16[512,128]{1,0:T(8,128)(2,1)S(1)}, u32[]{:S(2)}, u32[]{:S(2)}) collective-permute-start(bf16[512,128]{1,0:T(8,128)(2,1)S(1)} %get-tuple-element.42), channel_id=1, source_target_pairs={{1,0},{2,1},{3,2},{0,3},{5,4},{6,5},{7,6},{4,7},{9,8},{10,9},{11,1... | collective-permute-start | bytes 393224 | tf_op jit(solution)/shard_map/ppermute | solution.py:313
  (9 other events, 71.5 us)

commit v8 on v7

--- a/solution.py
+++ b/solution.py
@@ -420,7 +420,7 @@
                 ids, mixed, own[c], other[c], count, after=after, cost=cost
             )
             pieces[c] = [parts[0]] + [
-                permute(parts[k], "tensor", lambda i, k=k: i - k) for k in range(1, count)
+                permute(parts[k], "tensor", lambda i, k=k: i - k) for k in sorted(range(1, count), key=lambda k: -min(k, count - k))
             ]
             before = [parts[0]]
         else:

time: 142 us -> 142 us (level)
  no operation moved by 1% of the time
where the time goes in v8:
time: 142 us
  starting transfers between devices  54.2 us (38%)
  waiting for transfers between devices  46.9 us (33%)
  Pallas kernels  36.6 us (26%)
  local copies, waits for them, and re-layouts  3.22 us (2%)
    ppermute x33, starting transfers between devices, permute(): lax.ppermute(array, axis, [(source(i) % count, i) for i in range(count)])  54.2 us
    ppermute x33, waiting for transfers between devices, permute(): lax.ppermute(array, axis, [(source(i) % count, i) for i in range(count)])  46.9 us
    pallas_call x4, Pallas kernels, attend(): pl.pallas_call(functools.partial(attend_kernel, len(blocks)), out_shape=j...  12.9 us
    pallas_call x9, Pallas kernels, combine(): pl.pallas_call(combine_kernel, out_shape=jax.ShapeDtypeStruct(far.shape,...  10.8 us
    pallas_call x3, Pallas kernels, partials(): pl.pallas_call(functools.partial(partial_kernel, count, len(mixed)), out_...  3.9 us
    unnamed x16, local copies, waits for them, and re-layouts  3.22 us
    pallas_call x8, Pallas kernels, columns_of(): pl.pallas_call(columns_kernel, out_shape=jax.ShapeDtypeStruct((rows, piec...  2.98 us
  transfers between devices with their start and end apart: 33, of which 13 were waited for; matrix products, arithmetic and copies ran while one was open for 1% of the time, Pallas kernels for 25%

profile of v8, /device:TPU:0, one launch (start us, length us, event | category | flops | bytes accessed | tf_op | source)
XLA Modules:
  0.0 142.0 jit_solution(13024698729748748581)
XLA Ops:
  0.5 2.5 %collective-permute-start.5 = (bf16[1024,256]{1,0:T(8,128)(2,1)}, bf16[1024,256]{1,0:T(8,128)(2,1)}, u32[]{:S(2)}, u32[]{:S(2)}) collective-permute-start(bf16[1024,256]{1,0:T(8,128)(2,1)} %bitcast.27), channel_id=1, source_target_pairs={{24,0},{16,8},{8,16},{0,24},{25,1},{17,9},{9,17},{1,25},{26,2},{18... | collective-permute-start | bytes 1572872 | tf_op jit(solution)/shard_map/ppermute | solution.py:313
  5.6 3.8 %collective-permute-start.6 = (bf16[512,512]{1,0:T(8,128)(2,1)}, bf16[512,512]{1,0:T(8,128)(2,1)S(1)}, u32[]{:S(2)}, u32[]{:S(2)}) collective-permute-start(bf16[512,512]{1,0:T(8,128)(2,1)} %bitcast.8), channel_id=1, source_target_pairs={{1,0},{2,1},{3,2},{0,3},{5,4},{6,5},{7,6},{4,7},{9,8},{10,9},{11,1... | collective-permute-start | bytes 1572872 | tf_op jit(solution)/shard_map/ppermute | solution.py:313
  12.4 3.3 %collective-permute-done.5.far = bf16[1024,256]{1,0:T(8,128)(2,1)} collective-permute-done((bf16[1024,256]{1,0:T(8,128)(2,1)}, bf16[1024,256]{1,0:T(8,128)(2,1)}, u32[]{:S(2)}, u32[]{:S(2)}) %collective-permute-start.5) | collective-permute-done | bytes 524320 | tf_op jit(solution)/shard_map/ppermute | solution.py:313
  17.8 2.2 %collective-permute-start.9 = (bf16[1024,256]{1,0:T(8,128)(2,1)S(1)}, bf16[1024,256]{1,0:T(8,128)(2,1)S(1)}, u32[]{:S(2)}, u32[]{:S(2)}) collective-permute-start(bf16[1024,256]{1,0:T(8,128)(2,1)S(1)} %shard_map.84.rest_0_.refs_4_), channel_id=1, source_target_pairs={{4,0},{0,4},{5,1},{1,5},{6,2},{2,6},{7,3},{3,7},{12,8},{8,12},{13,... | collective-permute-start | bytes 1572872 | tf_op jit(solution)/shard_map/ppermute | solution.py:313
  21.2 5.7 %collective-permute-done.3.far = bf16[1024,256]{1,0:T(8,128)(2,1)S(1)} collective-permute-done((bf16[1024,256]{1,0:T(8,128)(2,1)S(1)}, bf16[1024,256]{1,0:T(8,128)(2,1)S(1)}, u32[]{:S(2)}, u32[]{:S(2)}) %collective-permute-start.3) | collective-permute-done | bytes 524320 | tf_op jit(solution)/shard_map/ppermute | solution.py:313
  26.8 2.2 %collective-permute-start.10 = (bf16[1024,256]{1,0:T(8,128)(2,1)}, bf16[1024,256]{1,0:T(8,128)(2,1)}, u32[]{:S(2)}, u32[]{:S(2)}) collective-permute-start(bf16[1024,256]{1,0:T(8,128)(2,1)} %shard_map.85.rest_0_), channel_id=1, source_target_pairs={{24,0},{16,8},{8,16},{0,24},{25,1},{17,9},{9,17},{1,25},{26,2},{18... | collective-permute-start | bytes 1572872 | tf_op jit(solution)/shard_map/ppermute | solution.py:313
  31.9 2.7 %collective-permute-start.7 = (bf16[512,512]{1,0:T(8,128)(2,1)S(1)}, bf16[512,512]{1,0:T(8,128)(2,1)S(1)}, u32[]{:S(2)}, u32[]{:S(2)}) collective-permute-start(bf16[512,512]{1,0:T(8,128)(2,1)S(1)} %shard_map.87.rest_0_), channel_id=1, source_target_pairs={{2,0},{3,1},{0,2},{1,3},{6,4},{7,5},{4,6},{5,7},{10,8},{11,9},{8,1... | collective-permute-start | bytes 1572872 | tf_op jit(solution)/shard_map/ppermute | solution.py:313
  34.7 3.3 %collective-permute-done.11.far = bf16[1024,256]{1,0:T(8,128)(2,1)S(1)} collective-permute-done((bf16[1024,256]{1,0:T(8,128)(2,1)S(1)}, bf16[1024,256]{1,0:T(8,128)(2,1)S(1)}, u32[]{:S(2)}, u32[]{:S(2)}) %collective-permute-start.11) | collective-permute-done | bytes 524320 | tf_op jit(solution)/shard_map/ppermute | solution.py:313
  38.1 2.3 %collective-permute-start.12 = (bf16[1024,256]{1,0:T(8,128)(2,1)S(1)}, bf16[1024,256]{1,0:T(8,128)(2,1)S(1)}, u32[]{:S(2)}, u32[]{:S(2)}) collective-permute-start(bf16[1024,256]{1,0:T(8,128)(2,1)S(1)} %shard_map.88.rest_0_), channel_id=1, source_target_pairs={{24,0},{16,8},{8,16},{0,24},{25,1},{17,9},{9,17},{1,25},{26,2},{18... | collective-permute-start | bytes 1572872 | tf_op jit(solution)/shard_map/ppermute | solution.py:313
  43.6 5.8 %collective-permute-done.10.far = bf16[1024,256]{1,0:T(8,128)(2,1)} collective-permute-done((bf16[1024,256]{1,0:T(8,128)(2,1)}, bf16[1024,256]{1,0:T(8,128)(2,1)}, u32[]{:S(2)}, u32[]{:S(2)}) %collective-permute-start.10) | collective-permute-done | bytes 524320 | tf_op jit(solution)/shard_map/ppermute | solution.py:313
  49.4 2.2 %collective-permute-start.16 = (bf16[1024,256]{1,0:T(8,128)(2,1)S(1)}, bf16[1024,256]{1,0:T(8,128)(2,1)S(1)}, u32[]{:S(2)}, u32[]{:S(2)}) collective-permute-start(bf16[1024,256]{1,0:T(8,128)(2,1)S(1)} %shard_map.90.rest_0_), channel_id=1, source_target_pairs={{24,0},{16,8},{8,16},{0,24},{25,1},{17,9},{9,17},{1,25},{26,2},{18... | collective-permute-start | bytes 1572872 | tf_op jit(solution)/shard_map/ppermute | solution.py:313
  54.5 3.1 %collective-permute-done.7.refs_2_.refs_7_ = bf16[512,512]{1,0:T(8,128)(2,1)S(1)} collective-permute-done((bf16[512,512]{1,0:T(8,128)(2,1)S(1)}, bf16[512,512]{1,0:T(8,128)(2,1)S(1)}, u32[]{:S(2)}, u32[]{:S(2)}) %collective-permute-start.7) | collective-permute-done | bytes 524320 | tf_op jit(solution)/shard_map/ppermute | solution.py:313
  57.7 1.9 %shard_map.92 = (bf16[512,128]{1,0:T(8,128)(2,1)S(1)}, bf16[512,128]{1,0:T(8,128)(2,1)S(1)}, f32[512,128]{1,0:T(8,128)S(1)}) custom-call(s32[2]{0:T(128)S(1)} %pad_add_fusion.ids, bf16[512,512]{1,0:T(8,128)(2,1)S(1)} %bitcast.10, bf16[512,512]{1,0:T(8,128)(2,1)S(1)} %collective-permute-done.rest_1_.refs_1_.refs_12_, ...), custom_call_target="tpu_custom_call" | custom-call | flops 6291456000 | tf_op jit(solution)/shard_map/pallas_call | solution.py:144
  63.9 3.1 %shard_map.95.refs_11_.refs_0_ = bf16[512,256]{1,0:T(8,128)(2,1)S(1)} custom-call(s32[2]{0:T(128)S(1)} %pad_add_fusion.ids, bf16[512,512]{1,0:T(8,128)(2,1)S(1)} %bitcast.11, bf16[512,512]{1,0:T(8,128)(2,1)S(1)} %collective-permute-done.rest_1_.refs_1_.refs_12_, bf16[512,512]{1,0:T(8,128)(2,1)S(1)} %collective-permute-done.7.refs_2_.refs_7_, ...), custom_call_target="tpu_custom_call" | custom-call | tf_op jit(solution)/shard_map/pallas_call | solution.py:188
  67.0 3.6 %shard_map.96.refs_11_.refs_1_ = bf16[512,256]{1,0:T(8,128)(2,1)S(1)} custom-call(s32[2]{0:T(128)S(1)} %pad_add_fusion.ids, bf16[512,512]{1,0:T(8,128)(2,1)S(1)} %bitcast.12, bf16[512,512]{1,0:T(8,128)(2,1)S(1)} %collective-permute-done.rest_1_.refs_1_.refs_12_, bf16[512,512]{1,0:T(8,128)(2,1)S(1)} %collective-permute-done.7.refs_2_.refs_7_, ...), custom_call_target="tpu_custom_call" | custom-call | flops 2097152000 | tf_op jit(solution)/shard_map/pallas_call | solution.py:188
  70.7 3.1 %shard_map.97.rest_0_.refs_2_ = bf16[512,256]{1,0:T(8,128)(2,1)S(1)} custom-call(s32[2]{0:T(128)S(1)} %pad_add_fusion.ids, bf16[512,512]{1,0:T(8,128)(2,1)S(1)} %bitcast.13, bf16[512,512]{1,0:T(8,128)(2,1)S(1)} %collective-permute-done.rest_1_.refs_1_.refs_12_, bf16[512,512]{1,0:T(8,128)(2,1)S(1)} %collective-permute-done.7.refs_2_.refs_7_, ...), custom_call_target="tpu_custom_call" | custom-call | flops 1048576000 | tf_op jit(solution)/shard_map/pallas_call | solution.py:188
  76.0 2.4 %collective-permute-done.15.refs_5_.refs_1_ = bf16[1024,256]{1,0:T(8,128)(2,1)S(1)} collective-permute-done((bf16[1024,256]{1,0:T(8,128)(2,1)S(1)}, bf16[1024,256]{1,0:T(8,128)(2,1)S(1)}, u32[]{:S(2)}, u32[]{:S(2)}) %collective-permute-start.15) | collective-permute-done | bytes 524320 | tf_op jit(solution)/shard_map/ppermute | solution.py:313
  78.3 3.1 %shard_map.99.rest_0_.refs_3_ = bf16[512,256]{1,0:T(8,128)(2,1)S(1)} custom-call(s32[2]{0:T(128)S(1)} %pad_add_fusion.ids, bf16[512,512]{1,0:T(8,128)(2,1)S(1)} %bitcast.14, bf16[512,512]{1,0:T(8,128)(2,1)S(1)} %collective-permute-done.rest_1_.refs_1_.refs_12_, bf16[512,512]{1,0:T(8,128)(2,1)S(1)} %collective-permute-done.7.refs_2_.refs_7_, ...), custom_call_target="tpu_custom_call" | custom-call | flops 2097152000 | tf_op jit(solution)/shard_map/pallas_call | solution.py:188
  85.4 2.0 %collective-permute-start.22 = (bf16[1024,256]{1,0:T(8,128)(2,1)S(1)}, bf16[1024,256]{1,0:T(8,128)(2,1)S(1)}, u32[]{:S(2)}, u32[]{:S(2)}) collective-permute-start(bf16[1024,256]{1,0:T(8,128)(2,1)S(1)} %shard_map.102.refs_6_.refs_4_), channel_id=1, source_target_pairs={{4,0},{0,4},{5,1},{1,5},{6,2},{2,6},{7,3},{3,7},{12,8},{8,12},{13,... | collective-permute-start | bytes 1572872 | tf_op jit(solution)/shard_map/ppermute | solution.py:313
  87.4 2.4 %collective-permute-done.17.refs_5_ = bf16[1024,256]{1,0:T(8,128)(2,1)S(1)} collective-permute-done((bf16[1024,256]{1,0:T(8,128)(2,1)S(1)}, bf16[1024,256]{1,0:T(8,128)(2,1)S(1)}, u32[]{:S(2)}, u32[]{:S(2)}) %collective-permute-start.17) | collective-permute-done | bytes 524320 | tf_op jit(solution)/shard_map/ppermute | solution.py:313
  92.7 3.8 %collective-permute-done.20.far = bf16[1024,256]{1,0:T(8,128)(2,1)S(1)} collective-permute-done((bf16[1024,256]{1,0:T(8,128)(2,1)S(1)}, bf16[1024,256]{1,0:T(8,128)(2,1)S(1)}, u32[]{:S(2)}, u32[]{:S(2)}) %collective-permute-start.20) | collective-permute-done | bytes 524320 | tf_op jit(solution)/shard_map/ppermute | solution.py:313
  97.6 2.0 %collective-permute-start.24 = (bf16[1024,256]{1,0:T(8,128)(2,1)S(1)}, bf16[1024,256]{1,0:T(8,128)(2,1)S(1)}, u32[]{:S(2)}, u32[]{:S(2)}) collective-permute-start(bf16[1024,256]{1,0:T(8,128)(2,1)S(1)} %shard_map.104.refs_0_.refs_4_), channel_id=1, source_target_pairs={{4,0},{0,4},{5,1},{1,5},{6,2},{2,6},{7,3},{3,7},{12,8},{8,12},{13,... | collective-permute-start | bytes 1572872 | tf_op jit(solution)/shard_map/ppermute | solution.py:313
  100.3 2.9 %collective-permute-start.21 = (bf16[512,128]{1,0:T(8,128)(2,1)S(1)}, bf16[512,128]{1,0:T(8,128)(2,1)S(1)}, u32[]{:S(2)}, u32[]{:S(2)}) collective-permute-start(bf16[512,128]{1,0:T(8,128)(2,1)S(1)} %get-tuple-element.30), channel_id=1, source_target_pairs={{2,0},{3,1},{0,2},{1,3},{6,4},{7,5},{4,6},{5,7},{10,8},{11,9},{8,1... | collective-permute-start | bytes 393224 | tf_op jit(solution)/shard_map/ppermute | solution.py:313
  108.3 1.7 %collective-permute-start.29 = (bf16[1024,256]{1,0:T(8,128)(2,1)S(1)}, bf16[1024,256]{1,0:T(8,128)(2,1)S(1)}, u32[]{:S(2)}, u32[]{:S(2)}) collective-permute-start(bf16[1024,256]{1,0:T(8,128)(2,1)S(1)} %shard_map.107.refs_6_.refs_4_), channel_id=1, source_target_pairs={{4,0},{0,4},{5,1},{1,5},{6,2},{2,6},{7,3},{3,7},{12,8},{8,12},{13,... | collective-permute-start | bytes 1572872 | tf_op jit(solution)/shard_map/ppermute | solution.py:313
  109.9 2.6 %collective-permute-done.24.refs_5_ = bf16[1024,256]{1,0:T(8,128)(2,1)S(1)} collective-permute-done((bf16[1024,256]{1,0:T(8,128)(2,1)S(1)}, bf16[1024,256]{1,0:T(8,128)(2,1)S(1)}, u32[]{:S(2)}, u32[]{:S(2)}) %collective-permute-start.24) | collective-permute-done | bytes 524320 | tf_op jit(solution)/shard_map/ppermute | solution.py:313
  113.9 1.9 %collective-permute-start.27 = (bf16[2,512,128]{2,1,0:T(8,128)(2,1)S(1)}, bf16[2,512,128]{2,1,0:T(8,128)(2,1)S(1)}, u32[]{:S(2)}, u32[]{:S(2)}) collective-permute-start(bf16[2,512,128]{2,1,0:T(8,128)(2,1)S(1)} %get-tuple-element.36), channel_id=1, source_target_pairs={{1,0},{0,1},{3,2},{2,3},{5,4},{4,5},{7,6},{6,7},{9,8},{8,9},{11,10... | collective-permute-start | bytes 786440 | tf_op jit(solution)/shard_map/ppermute | solution.py:313
  116.3 2.5 %collective-permute-start.26 = (bf16[512,128]{1,0:T(8,128)(2,1)S(1)}, bf16[512,128]{1,0:T(8,128)(2,1)S(1)}, u32[]{:S(2)}, u32[]{:S(2)}) collective-permute-start(bf16[512,128]{1,0:T(8,128)(2,1)S(1)} %get-tuple-element.35), channel_id=1, source_target_pairs={{2,0},{3,1},{0,2},{1,3},{6,4},{7,5},{4,6},{5,7},{10,8},{11,9},{8,1... | collective-permute-start | bytes 393224 | tf_op jit(solution)/shard_map/ppermute | solution.py:313
  118.8 4.7 %collective-permute-done.27.got = bf16[2,512,128]{2,1,0:T(8,128)(2,1)S(1)} collective-permute-done((bf16[2,512,128]{2,1,0:T(8,128)(2,1)S(1)}, bf16[2,512,128]{2,1,0:T(8,128)(2,1)S(1)}, u32[]{:S(2)}, u32[]{:S(2)}) %collective-permute-start.27) | collective-permute-done | bytes 262176 | tf_op jit(solution)/shard_map/ppermute | solution.py:313
  124.2 1.7 %collective-permute-start.28 = (bf16[512,128]{1,0:T(8,128)(2,1)S(1)}, bf16[512,128]{1,0:T(8,128)(2,1)S(1)}, u32[]{:S(2)}, u32[]{:S(2)}) collective-permute-start(bf16[512,128]{1,0:T(8,128)(2,1)S(1)} %get-tuple-element.38), channel_id=1, source_target_pairs={{2,0},{3,1},{0,2},{1,3},{6,4},{7,5},{4,6},{5,7},{10,8},{11,9},{8,1... | collective-permute-start | bytes 393224 | tf_op jit(solution)/shard_map/ppermute | solution.py:313
  129.8 2.6 %collective-permute-start.32 = (bf16[512,128]{1,0:T(8,128)(2,1)S(1)}, bf16[512,128]{1,0:T(8,128)(2,1)S(1)}, u32[]{:S(2)}, u32[]{:S(2)}) collective-permute-start(bf16[512,128]{1,0:T(8,128)(2,1)S(1)} %get-tuple-element.42), channel_id=1, source_target_pairs={{1,0},{2,1},{3,2},{0,3},{5,4},{6,5},{7,6},{4,7},{9,8},{10,9},{11,1... | collective-permute-start | bytes 393224 | tf_op jit(solution)/shard_map/ppermute | solution.py:313
  132.4 6.2 %collective-permute-done.28.refs_5_ = bf16[512,128]{1,0:T(8,128)(2,1)S(1)} collective-permute-done((bf16[512,128]{1,0:T(8,128)(2,1)S(1)}, bf16[512,128]{1,0:T(8,128)(2,1)S(1)}, u32[]{:S(2)}, u32[]{:S(2)}) %collective-permute-start.28) | collective-permute-done | bytes 131104 | tf_op jit(solution)/shard_map/ppermute | solution.py:313
  138.5 2.5 %collective-permute-done.30.refs_7_ = bf16[512,128]{1,0:T(8,128)(2,1)S(1)} collective-permute-done((bf16[512,128]{1,0:T(8,128)(2,1)S(1)}, bf16[512,128]{1,0:T(8,128)(2,1)S(1)}, u32[]{:S(2)}, u32[]{:S(2)}) %collective-permute-start.30) | collective-permute-done | bytes 131104 | tf_op jit(solution)/shard_map/ppermute | solution.py:313
  (83 shorter events, 46.1 us)
Async XLA Ops:
  0.5 10.9 %collective-permute-start.4 = (bf16[1024,256]{1,0:T(8,128)(2,1)}, bf16[1024,256]{1,0:T(8,128)(2,1)S(1)}, u32[]{:S(2)}, u32[]{:S(2)}) collective-permute-start(bf16[1024,256]{1,0:T(8,128)(2,1)} %bitcast.26), channel_id=1, source_target_pairs={{8,0},{0,8},{24,16},{16,24},{9,1},{1,9},{25,17},{17,25},{10,2},{2,... | collective-permute-start | bytes 1572872 | tf_op jit(solution)/shard_map/ppermute | solution.py:313
  0.5 15.2 %collective-permute-start.5 = (bf16[1024,256]{1,0:T(8,128)(2,1)}, bf16[1024,256]{1,0:T(8,128)(2,1)}, u32[]{:S(2)}, u32[]{:S(2)}) collective-permute-start(bf16[1024,256]{1,0:T(8,128)(2,1)} %bitcast.27), channel_id=1, source_target_pairs={{24,0},{16,8},{8,16},{0,24},{25,1},{17,9},{9,17},{1,25},{26,2},{18... | collective-permute-start | bytes 1572872 | tf_op jit(solution)/shard_map/ppermute | solution.py:313
  3.1 27.2 %collective-permute-start = (bf16[512,512]{1,0:T(8,128)(2,1)}, bf16[512,512]{1,0:T(8,128)(2,1)S(1)}, u32[]{:S(2)}, u32[]{:S(2)}) collective-permute-start(bf16[512,512]{1,0:T(8,128)(2,1)} %bitcast.7), channel_id=1, source_target_pairs={{3,0},{0,1},{1,2},{2,3},{7,4},{4,5},{5,6},{6,7},{11,8},{8,9},{9,10... | collective-permute-start | bytes 1572872 | tf_op jit(solution)/shard_map/ppermute | solution.py:313
  4.6 15.3 %collective-permute-start.1 = (bf16[1024,1024]{1,0:T(8,128)(2,1)}, bf16[1024,1024]{1,0:T(8,128)(2,1)}, u32[]{:S(2)}, u32[]{:S(2)}) collective-permute-start(bf16[1024,1024]{1,0:T(8,128)(2,1)} %bitcast.16), channel_id=1, source_target_pairs={{8,0},{0,8},{24,16},{16,24},{9,1},{1,9},{25,17},{17,25},{10,2},{2,... | collective-permute-start | bytes 6291464 | tf_op jit(solution)/shard_map/ppermute | solution.py:313
  5.6 26.2 %collective-permute-start.6 = (bf16[512,512]{1,0:T(8,128)(2,1)}, bf16[512,512]{1,0:T(8,128)(2,1)S(1)}, u32[]{:S(2)}, u32[]{:S(2)}) collective-permute-start(bf16[512,512]{1,0:T(8,128)(2,1)} %bitcast.8), channel_id=1, source_target_pairs={{1,0},{2,1},{3,2},{0,3},{5,4},{6,5},{7,6},{4,7},{9,8},{10,9},{11,1... | collective-permute-start | bytes 1572872 | tf_op jit(solution)/shard_map/ppermute | solution.py:313
  11.4 15.4 %collective-permute-start.3 = (bf16[1024,256]{1,0:T(8,128)(2,1)S(1)}, bf16[1024,256]{1,0:T(8,128)(2,1)S(1)}, u32[]{:S(2)}, u32[]{:S(2)}) collective-permute-start(bf16[1024,256]{1,0:T(8,128)(2,1)S(1)} %shard_map.82.rest_0_), channel_id=1, source_target_pairs={{24,0},{16,8},{8,16},{0,24},{25,1},{17,9},{9,17},{1,25},{26,2},{18... | collective-permute-start | bytes 1572872 | tf_op jit(solution)/shard_map/ppermute | solution.py:313
  17.8 23.8 %collective-permute-start.9 = (bf16[1024,256]{1,0:T(8,128)(2,1)S(1)}, bf16[1024,256]{1,0:T(8,128)(2,1)S(1)}, u32[]{:S(2)}, u32[]{:S(2)}) collective-permute-start(bf16[1024,256]{1,0:T(8,128)(2,1)S(1)} %shard_map.84.rest_0_.refs_4_), channel_id=1, source_target_pairs={{4,0},{0,4},{5,1},{1,5},{6,2},{2,6},{7,3},{3,7},{12,8},{8,12},{13,... | collective-permute-start | bytes 1572872 | tf_op jit(solution)/shard_map/ppermute | solution.py:313
  20.0 18.1 %collective-permute-start.11 = (bf16[1024,256]{1,0:T(8,128)(2,1)S(1)}, bf16[1024,256]{1,0:T(8,128)(2,1)S(1)}, u32[]{:S(2)}, u32[]{:S(2)}) collective-permute-start(bf16[1024,256]{1,0:T(8,128)(2,1)S(1)} %shard_map.83.rest_0_), channel_id=1, source_target_pairs={{24,0},{16,8},{8,16},{0,24},{25,1},{17,9},{9,17},{1,25},{26,2},{18... | collective-permute-start | bytes 1572872 | tf_op jit(solution)/shard_map/ppermute | solution.py:313
  26.8 22.6 %collective-permute-start.10 = (bf16[1024,256]{1,0:T(8,128)(2,1)}, bf16[1024,256]{1,0:T(8,128)(2,1)}, u32[]{:S(2)}, u32[]{:S(2)}) collective-permute-start(bf16[1024,256]{1,0:T(8,128)(2,1)} %shard_map.85.rest_0_), channel_id=1, source_target_pairs={{24,0},{16,8},{8,16},{0,24},{25,1},{17,9},{9,17},{1,25},{26,2},{18... | collective-permute-start | bytes 1572872 | tf_op jit(solution)/shard_map/ppermute | solution.py:313
  30.2 21.4 %collective-permute-start.8 = (bf16[1024,256]{1,0:T(8,128)(2,1)S(1)}, bf16[1024,256]{1,0:T(8,128)(2,1)S(1)}, u32[]{:S(2)}, u32[]{:S(2)}) collective-permute-start(bf16[1024,256]{1,0:T(8,128)(2,1)S(1)} %shard_map.86.rest_0_.refs_4_), channel_id=1, source_target_pairs={{4,0},{0,4},{5,1},{1,5},{6,2},{2,6},{7,3},{3,7},{12,8},{8,12},{13,... | collective-permute-start | bytes 1572872 | tf_op jit(solution)/shard_map/ppermute | solution.py:313
  31.9 25.8 %collective-permute-start.7 = (bf16[512,512]{1,0:T(8,128)(2,1)S(1)}, bf16[512,512]{1,0:T(8,128)(2,1)S(1)}, u32[]{:S(2)}, u32[]{:S(2)}) collective-permute-start(bf16[512,512]{1,0:T(8,128)(2,1)S(1)} %shard_map.87.rest_0_), channel_id=1, source_target_pairs={{2,0},{3,1},{0,2},{1,3},{6,4},{7,5},{4,6},{5,7},{10,8},{11,9},{8,1... | collective-permute-start | bytes 1572872 | tf_op jit(solution)/shard_map/ppermute | solution.py:313
  38.1 23.5 %collective-permute-start.12 = (bf16[1024,256]{1,0:T(8,128)(2,1)S(1)}, bf16[1024,256]{1,0:T(8,128)(2,1)S(1)}, u32[]{:S(2)}, u32[]{:S(2)}) collective-permute-start(bf16[1024,256]{1,0:T(8,128)(2,1)S(1)} %shard_map.88.rest_0_), channel_id=1, source_target_pairs={{24,0},{16,8},{8,16},{0,24},{25,1},{17,9},{9,17},{1,25},{26,2},{18... | collective-permute-start | bytes 1572872 | tf_op jit(solution)/shard_map/ppermute | solution.py:313
  41.6 25.5 %collective-permute-start.13 = (bf16[1024,256]{1,0:T(8,128)(2,1)S(1)}, bf16[1024,256]{1,0:T(8,128)(2,1)}, u32[]{:S(2)}, u32[]{:S(2)}) collective-permute-start(bf16[1024,256]{1,0:T(8,128)(2,1)S(1)} %shard_map.89.rest_0_.refs_4_), channel_id=1, source_target_pairs={{4,0},{0,4},{5,1},{1,5},{6,2},{2,6},{7,3},{3,7},{12,8},{8,12},{13,... | collective-permute-start | bytes 1572872 | tf_op jit(solution)/shard_map/ppermute | solution.py:313
  49.4 24.4 %collective-permute-start.16 = (bf16[1024,256]{1,0:T(8,128)(2,1)S(1)}, bf16[1024,256]{1,0:T(8,128)(2,1)S(1)}, u32[]{:S(2)}, u32[]{:S(2)}) collective-permute-start(bf16[1024,256]{1,0:T(8,128)(2,1)S(1)} %shard_map.90.rest_0_), channel_id=1, source_target_pairs={{24,0},{16,8},{8,16},{0,24},{25,1},{17,9},{9,17},{1,25},{26,2},{18... | collective-permute-start | bytes 1572872 | tf_op jit(solution)/shard_map/ppermute | solution.py:313
  52.9 17.7 %collective-permute-start.14 = (bf16[1024,256]{1,0:T(8,128)(2,1)S(1)}, bf16[1024,256]{1,0:T(8,128)(2,1)S(1)}, u32[]{:S(2)}, u32[]{:S(2)}) collective-permute-start(bf16[1024,256]{1,0:T(8,128)(2,1)S(1)} %shard_map.91.refs_8_.refs_4_), channel_id=1, source_target_pairs={{4,0},{0,4},{5,1},{1,5},{6,2},{2,6},{7,3},{3,7},{12,8},{8,12},{13,... | collective-permute-start | bytes 1572872 | tf_op jit(solution)/shard_map/ppermute | solution.py:313
  61.5 22.6 %collective-permute-start.18 = (bf16[1024,256]{1,0:T(8,128)(2,1)S(1)}, bf16[1024,256]{1,0:T(8,128)(2,1)S(1)}, u32[]{:S(2)}, u32[]{:S(2)}) collective-permute-start(bf16[1024,256]{1,0:T(8,128)(2,1)S(1)} %shard_map.93.rest_0_), channel_id=1, source_target_pairs={{24,0},{16,8},{8,16},{0,24},{25,1},{17,9},{9,17},{1,25},{26,2},{18... | collective-permute-start | bytes 1572872 | tf_op jit(solution)/shard_map/ppermute | solution.py:313
  62.8 15.5 %collective-permute-start.15 = (bf16[1024,256]{1,0:T(8,128)(2,1)S(1)}, bf16[1024,256]{1,0:T(8,128)(2,1)S(1)}, u32[]{:S(2)}, u32[]{:S(2)}) collective-permute-start(bf16[1024,256]{1,0:T(8,128)(2,1)S(1)} %shard_map.94.refs_11_.refs_4_), channel_id=1, source_target_pairs={{4,0},{0,4},{5,1},{1,5},{6,2},{2,6},{7,3},{3,7},{12,8},{8,12},{13,... | collective-permute-start | bytes 1572872 | tf_op jit(solution)/shard_map/ppermute | solution.py:313
  74.9 14.8 %collective-permute-start.17 = (bf16[1024,256]{1,0:T(8,128)(2,1)S(1)}, bf16[1024,256]{1,0:T(8,128)(2,1)S(1)}, u32[]{:S(2)}, u32[]{:S(2)}) collective-permute-start(bf16[1024,256]{1,0:T(8,128)(2,1)S(1)} %shard_map.98.refs_11_.refs_4_), channel_id=1, source_target_pairs={{4,0},{0,4},{5,1},{1,5},{6,2},{2,6},{7,3},{3,7},{12,8},{8,12},{13,... | collective-permute-start | bytes 1572872 | tf_op jit(solution)/shard_map/ppermute | solution.py:313
  82.3 14.2 %collective-permute-start.20 = (bf16[1024,256]{1,0:T(8,128)(2,1)S(1)}, bf16[1024,256]{1,0:T(8,128)(2,1)S(1)}, u32[]{:S(2)}, u32[]{:S(2)}) collective-permute-start(bf16[1024,256]{1,0:T(8,128)(2,1)S(1)} %shard_map.101.rest_0_), channel_id=1, source_target_pairs={{24,0},{16,8},{8,16},{0,24},{25,1},{17,9},{9,17},{1,25},{26,2},{18... | collective-permute-start | bytes 1572872 | tf_op jit(solution)/shard_map/ppermute | solution.py:313
  82.6 24.5 %collective-permute-start.25 = (bf16[1024,256]{1,0:T(8,128)(2,1)S(1)}, bf16[1024,256]{1,0:T(8,128)(2,1)S(1)}, u32[]{:S(2)}, u32[]{:S(2)}) collective-permute-start(bf16[1024,256]{1,0:T(8,128)(2,1)S(1)} %shard_map.100.rest_0_), channel_id=1, source_target_pairs={{24,0},{16,8},{8,16},{0,24},{25,1},{17,9},{9,17},{1,25},{26,2},{18... | collective-permute-start | bytes 1572872 | tf_op jit(solution)/shard_map/ppermute | solution.py:313
  85.4 17.8 %collective-permute-start.22 = (bf16[1024,256]{1,0:T(8,128)(2,1)S(1)}, bf16[1024,256]{1,0:T(8,128)(2,1)S(1)}, u32[]{:S(2)}, u32[]{:S(2)}) collective-permute-start(bf16[1024,256]{1,0:T(8,128)(2,1)S(1)} %shard_map.102.refs_6_.refs_4_), channel_id=1, source_target_pairs={{4,0},{0,4},{5,1},{1,5},{6,2},{2,6},{7,3},{3,7},{12,8},{8,12},{13,... | collective-permute-start | bytes 1572872 | tf_op jit(solution)/shard_map/ppermute | solution.py:313
  91.1 8.6 %collective-permute-start.19 = (bf16[2,512,128]{2,1,0:T(8,128)(2,1)S(1)}, bf16[2,512,128]{2,1,0:T(8,128)(2,1)S(1)}, u32[]{:S(2)}, u32[]{:S(2)}) collective-permute-start(bf16[2,512,128]{2,1,0:T(8,128)(2,1)S(1)} %get-tuple-element.28), channel_id=1, source_target_pairs={{1,0},{0,1},{3,2},{2,3},{5,4},{4,5},{7,6},{6,7},{9,8},{8,9},{11,10... | collective-permute-start | bytes 786440 | tf_op jit(solution)/shard_map/ppermute | solution.py:313
  97.6 14.9 %collective-permute-start.24 = (bf16[1024,256]{1,0:T(8,128)(2,1)S(1)}, bf16[1024,256]{1,0:T(8,128)(2,1)S(1)}, u32[]{:S(2)}, u32[]{:S(2)}) collective-permute-start(bf16[1024,256]{1,0:T(8,128)(2,1)S(1)} %shard_map.104.refs_0_.refs_4_), channel_id=1, source_target_pairs={{4,0},{0,4},{5,1},{1,5},{6,2},{2,6},{7,3},{3,7},{12,8},{8,12},{13,... | collective-permute-start | bytes 1572872 | tf_op jit(solution)/shard_map/ppermute | solution.py:313
  100.3 9.7 %collective-permute-start.21 = (bf16[512,128]{1,0:T(8,128)(2,1)S(1)}, bf16[512,128]{1,0:T(8,128)(2,1)S(1)}, u32[]{:S(2)}, u32[]{:S(2)}) collective-permute-start(bf16[512,128]{1,0:T(8,128)(2,1)S(1)} %get-tuple-element.30), channel_id=1, source_target_pairs={{2,0},{3,1},{0,2},{1,3},{6,4},{7,5},{4,6},{5,7},{10,8},{11,9},{8,1... | collective-permute-start | bytes 393224 | tf_op jit(solution)/shard_map/ppermute | solution.py:313
  104.5 11.2 %collective-permute-start.23 = (bf16[2,512,128]{2,1,0:T(8,128)(2,1)S(1)}, bf16[2,512,128]{2,1,0:T(8,128)(2,1)S(1)}, u32[]{:S(2)}, u32[]{:S(2)}) collective-permute-start(bf16[2,512,128]{2,1,0:T(8,128)(2,1)S(1)} %get-tuple-element.32), channel_id=1, source_target_pairs={{1,0},{0,1},{3,2},{2,3},{5,4},{4,5},{7,6},{6,7},{9,8},{8,9},{11,10... | collective-permute-start | bytes 786440 | tf_op jit(solution)/shard_map/ppermute | solution.py:313
  108.3 17.6 %collective-permute-start.29 = (bf16[1024,256]{1,0:T(8,128)(2,1)S(1)}, bf16[1024,256]{1,0:T(8,128)(2,1)S(1)}, u32[]{:S(2)}, u32[]{:S(2)}) collective-permute-start(bf16[1024,256]{1,0:T(8,128)(2,1)S(1)} %shard_map.107.refs_6_.refs_4_), channel_id=1, source_target_pairs={{4,0},{0,4},{5,1},{1,5},{6,2},{2,6},{7,3},{3,7},{12,8},{8,12},{13,... | collective-permute-start | bytes 1572872 | tf_op jit(solution)/shard_map/ppermute | solution.py:313
  113.9 9.7 %collective-permute-start.27 = (bf16[2,512,128]{2,1,0:T(8,128)(2,1)S(1)}, bf16[2,512,128]{2,1,0:T(8,128)(2,1)S(1)}, u32[]{:S(2)}, u32[]{:S(2)}) collective-permute-start(bf16[2,512,128]{2,1,0:T(8,128)(2,1)S(1)} %get-tuple-element.36), channel_id=1, source_target_pairs={{1,0},{0,1},{3,2},{2,3},{5,4},{4,5},{7,6},{6,7},{9,8},{8,9},{11,10... | collective-permute-start | bytes 786440 | tf_op jit(solution)/shard_map/ppermute | solution.py:313
  116.3 16.0 %collective-permute-start.26 = (bf16[512,128]{1,0:T(8,128)(2,1)S(1)}, bf16[512,128]{1,0:T(8,128)(2,1)S(1)}, u32[]{:S(2)}, u32[]{:S(2)}) collective-permute-start(bf16[512,128]{1,0:T(8,128)(2,1)S(1)} %get-tuple-element.35), channel_id=1, source_target_pairs={{2,0},{3,1},{0,2},{1,3},{6,4},{7,5},{4,6},{5,7},{10,8},{11,9},{8,1... | collective-permute-start | bytes 393224 | tf_op jit(solution)/shard_map/ppermute | solution.py:313
  124.2 14.4 %collective-permute-start.28 = (bf16[512,128]{1,0:T(8,128)(2,1)S(1)}, bf16[512,128]{1,0:T(8,128)(2,1)S(1)}, u32[]{:S(2)}, u32[]{:S(2)}) collective-permute-start(bf16[512,128]{1,0:T(8,128)(2,1)S(1)} %get-tuple-element.38), channel_id=1, source_target_pairs={{2,0},{3,1},{0,2},{1,3},{6,4},{7,5},{4,6},{5,7},{10,8},{11,9},{8,1... | collective-permute-start | bytes 393224 | tf_op jit(solution)/shard_map/ppermute | solution.py:313
  127.2 13.8 %collective-permute-start.30 = (bf16[512,128]{1,0:T(8,128)(2,1)S(1)}, bf16[512,128]{1,0:T(8,128)(2,1)S(1)}, u32[]{:S(2)}, u32[]{:S(2)}) collective-permute-start(bf16[512,128]{1,0:T(8,128)(2,1)S(1)} %get-tuple-element.40), channel_id=1, source_target_pairs={{2,0},{3,1},{0,2},{1,3},{6,4},{7,5},{4,6},{5,7},{10,8},{11,9},{8,1... | collective-permute-start | bytes 393224 | tf_op jit(solution)/shard_map/ppermute | solution.py:313
  128.5 12.5 %collective-permute-start.31 = (bf16[512,128]{1,0:T(8,128)(2,1)S(1)}, bf16[512,128]{1,0:T(8,128)(2,1)S(1)}, u32[]{:S(2)}, u32[]{:S(2)}) collective-permute-start(bf16[512,128]{1,0:T(8,128)(2,1)S(1)} %get-tuple-element.41), channel_id=1, source_target_pairs={{3,0},{0,1},{1,2},{2,3},{7,4},{4,5},{5,6},{6,7},{11,8},{8,9},{9,10... | collective-permute-start | bytes 393224 | tf_op jit(solution)/shard_map/ppermute | solution.py:313
  129.8 11.2 %collective-permute-start.32 = (bf16[512,128]{1,0:T(8,128)(2,1)S(1)}, bf16[512,128]{1,0:T(8,128)(2,1)S(1)}, u32[]{:S(2)}, u32[]{:S(2)}) collective-permute-start(bf16[512,128]{1,0:T(8,128)(2,1)S(1)} %get-tuple-element.42), channel_id=1, source_target_pairs={{1,0},{2,1},{3,2},{0,3},{5,4},{6,5},{7,6},{4,7},{9,8},{10,9},{11,1... | collective-permute-start | bytes 393224 | tf_op jit(solution)/shard_map/ppermute | solution.py:313
  (9 other events, 71.5 us)

commit v9 on v8

--- a/solution.py
+++ b/solution.py
@@ -200,14 +200,9 @@
     mine = ids[0]
     count, _, width = by_owner.shape
     per_half = count // 2
+    rows = jnp.concatenate([part[...] for part in mixed], axis=1)
     for half, weights in ((mine, own), (1 - mine, other)):
-        total = None
-        depth = 0
-        for part in mixed:
-            rows = slice(depth, depth + part.shape[1])
-            depth += part.shape[1]
-            term = jnp.dot(part[...], weights[rows, :], preferred_element_type=jnp.float32)
-            total = term if total is None else total + term
+        total = jnp.dot(rows, weights[...], preferred_element_type=jnp.float32)
         for piece in range(per_half):
             by_owner[half * per_half + piece] = total[
                 :, piece * width : (piece + 1) * width

time: 142 us -> 142 us (level)
  no operation moved by 1% of the time
where the time goes in v9:
time: 142 us
  starting transfers between devices  54.2 us (38%)
  waiting for transfers between devices  46.9 us (33%)
  Pallas kernels  36.6 us (26%)
  local copies, waits for them, and re-layouts  3.22 us (2%)
    ppermute x33, starting transfers between devices, permute(): lax.ppermute(array, axis, [(source(i) % count, i) for i in range(count)])  54.2 us
    ppermute x33, waiting for transfers between devices, permute(): lax.ppermute(array, axis, [(source(i) % count, i) for i in range(count)])  46.9 us
    pallas_call x4, Pallas kernels, attend(): pl.pallas_call(functools.partial(attend_kernel, len(blocks)), out_shape=j...  12.9 us
    pallas_call x9, Pallas kernels, combine(): pl.pallas_call(combine_kernel, out_shape=jax.ShapeDtypeStruct(far.shape,...  10.8 us
    pallas_call x3, Pallas kernels, partials(): pl.pallas_call(functools.partial(partial_kernel, count, len(mixed)), out_...  3.9 us
    unnamed x16, local copies, waits for them, and re-layouts  3.22 us
    pallas_call x8, Pallas kernels, columns_of(): pl.pallas_call(columns_kernel, out_shape=jax.ShapeDtypeStruct((rows, piec...  2.98 us
  transfers between devices with their start and end apart: 33, of which 13 were waited for; matrix products, arithmetic and copies ran while one was open for 1% of the time, Pallas kernels for 25%

profile of v9, /device:TPU:0, one launch (start us, length us, event | category | flops | bytes accessed | tf_op | source)
XLA Modules:
  0.0 142.0 jit_solution(4134162826461235664)
XLA Ops:
  0.5 2.5 %collective-permute-start.5 = (bf16[1024,256]{1,0:T(8,128)(2,1)}, bf16[1024,256]{1,0:T(8,128)(2,1)}, u32[]{:S(2)}, u32[]{:S(2)}) collective-permute-start(bf16[1024,256]{1,0:T(8,128)(2,1)} %bitcast.27), channel_id=1, source_target_pairs={{24,0},{16,8},{8,16},{0,24},{25,1},{17,9},{9,17},{1,25},{26,2},{18... | collective-permute-start | bytes 1572872 | tf_op jit(solution)/shard_map/ppermute | solution.py:308
  5.6 3.8 %collective-permute-start.6 = (bf16[512,512]{1,0:T(8,128)(2,1)}, bf16[512,512]{1,0:T(8,128)(2,1)S(1)}, u32[]{:S(2)}, u32[]{:S(2)}) collective-permute-start(bf16[512,512]{1,0:T(8,128)(2,1)} %bitcast.8), channel_id=1, source_target_pairs={{1,0},{2,1},{3,2},{0,3},{5,4},{6,5},{7,6},{4,7},{9,8},{10,9},{11,1... | collective-permute-start | bytes 1572872 | tf_op jit(solution)/shard_map/ppermute | solution.py:308
  12.4 3.3 %collective-permute-done.5.far = bf16[1024,256]{1,0:T(8,128)(2,1)} collective-permute-done((bf16[1024,256]{1,0:T(8,128)(2,1)}, bf16[1024,256]{1,0:T(8,128)(2,1)}, u32[]{:S(2)}, u32[]{:S(2)}) %collective-permute-start.5) | collective-permute-done | bytes 524320 | tf_op jit(solution)/shard_map/ppermute | solution.py:308
  17.8 2.2 %collective-permute-start.9 = (bf16[1024,256]{1,0:T(8,128)(2,1)S(1)}, bf16[1024,256]{1,0:T(8,128)(2,1)S(1)}, u32[]{:S(2)}, u32[]{:S(2)}) collective-permute-start(bf16[1024,256]{1,0:T(8,128)(2,1)S(1)} %shard_map.84.rest_0_.refs_4_), channel_id=1, source_target_pairs={{4,0},{0,4},{5,1},{1,5},{6,2},{2,6},{7,3},{3,7},{12,8},{8,12},{13,... | collective-permute-start | bytes 1572872 | tf_op jit(solution)/shard_map/ppermute | solution.py:308
  21.2 5.7 %collective-permute-done.3.far = bf16[1024,256]{1,0:T(8,128)(2,1)S(1)} collective-permute-done((bf16[1024,256]{1,0:T(8,128)(2,1)S(1)}, bf16[1024,256]{1,0:T(8,128)(2,1)S(1)}, u32[]{:S(2)}, u32[]{:S(2)}) %collective-permute-start.3) | collective-permute-done | bytes 524320 | tf_op jit(solution)/shard_map/ppermute | solution.py:308
  26.8 2.2 %collective-permute-start.10 = (bf16[1024,256]{1,0:T(8,128)(2,1)}, bf16[1024,256]{1,0:T(8,128)(2,1)}, u32[]{:S(2)}, u32[]{:S(2)}) collective-permute-start(bf16[1024,256]{1,0:T(8,128)(2,1)} %shard_map.85.rest_0_), channel_id=1, source_target_pairs={{24,0},{16,8},{8,16},{0,24},{25,1},{17,9},{9,17},{1,25},{26,2},{18... | collective-permute-start | bytes 1572872 | tf_op jit(solution)/shard_map/ppermute | solution.py:308
  31.9 2.7 %collective-permute-start.7 = (bf16[512,512]{1,0:T(8,128)(2,1)S(1)}, bf16[512,512]{1,0:T(8,128)(2,1)S(1)}, u32[]{:S(2)}, u32[]{:S(2)}) collective-permute-start(bf16[512,512]{1,0:T(8,128)(2,1)S(1)} %shard_map.87.rest_0_), channel_id=1, source_target_pairs={{2,0},{3,1},{0,2},{1,3},{6,4},{7,5},{4,6},{5,7},{10,8},{11,9},{8,1... | collective-permute-start | bytes 1572872 | tf_op jit(solution)/shard_map/ppermute | solution.py:308
  34.7 3.3 %collective-permute-done.11.far = bf16[1024,256]{1,0:T(8,128)(2,1)S(1)} collective-permute-done((bf16[1024,256]{1,0:T(8,128)(2,1)S(1)}, bf16[1024,256]{1,0:T(8,128)(2,1)S(1)}, u32[]{:S(2)}, u32[]{:S(2)}) %collective-permute-start.11) | collective-permute-done | bytes 524320 | tf_op jit(solution)/shard_map/ppermute | solution.py:308
  38.1 2.3 %collective-permute-start.12 = (bf16[1024,256]{1,0:T(8,128)(2,1)S(1)}, bf16[1024,256]{1,0:T(8,128)(2,1)S(1)}, u32[]{:S(2)}, u32[]{:S(2)}) collective-permute-start(bf16[1024,256]{1,0:T(8,128)(2,1)S(1)} %shard_map.88.rest_0_), channel_id=1, source_target_pairs={{24,0},{16,8},{8,16},{0,24},{25,1},{17,9},{9,17},{1,25},{26,2},{18... | collective-permute-start | bytes 1572872 | tf_op jit(solution)/shard_map/ppermute | solution.py:308
  43.6 5.8 %collective-permute-done.10.far = bf16[1024,256]{1,0:T(8,128)(2,1)} collective-permute-done((bf16[1024,256]{1,0:T(8,128)(2,1)}, bf16[1024,256]{1,0:T(8,128)(2,1)}, u32[]{:S(2)}, u32[]{:S(2)}) %collective-permute-start.10) | collective-permute-done | bytes 524320 | tf_op jit(solution)/shard_map/ppermute | solution.py:308
  49.4 2.2 %collective-permute-start.16 = (bf16[1024,256]{1,0:T(8,128)(2,1)S(1)}, bf16[1024,256]{1,0:T(8,128)(2,1)S(1)}, u32[]{:S(2)}, u32[]{:S(2)}) collective-permute-start(bf16[1024,256]{1,0:T(8,128)(2,1)S(1)} %shard_map.90.rest_0_), channel_id=1, source_target_pairs={{24,0},{16,8},{8,16},{0,24},{25,1},{17,9},{9,17},{1,25},{26,2},{18... | collective-permute-start | bytes 1572872 | tf_op jit(solution)/shard_map/ppermute | solution.py:308
  54.5 3.1 %collective-permute-done.7.refs_2_.refs_7_ = bf16[512,512]{1,0:T(8,128)(2,1)S(1)} collective-permute-done((bf16[512,512]{1,0:T(8,128)(2,1)S(1)}, bf16[512,512]{1,0:T(8,128)(2,1)S(1)}, u32[]{:S(2)}, u32[]{:S(2)}) %collective-permute-start.7) | collective-permute-done | bytes 524320 | tf_op jit(solution)/shard_map/ppermute | solution.py:308
  57.7 1.9 %shard_map.92 = (bf16[512,128]{1,0:T(8,128)(2,1)S(1)}, bf16[512,128]{1,0:T(8,128)(2,1)S(1)}, f32[512,128]{1,0:T(8,128)S(1)}) custom-call(s32[2]{0:T(128)S(1)} %pad_add_fusion.ids, bf16[512,512]{1,0:T(8,128)(2,1)S(1)} %bitcast.10, bf16[512,512]{1,0:T(8,128)(2,1)S(1)} %collective-permute-done.rest_1_.refs_1_.refs_12_, ...), custom_call_target="tpu_custom_call" | custom-call | flops 6291456000 | tf_op jit(solution)/shard_map/pallas_call | solution.py:144
  63.9 3.1 %shard_map.95.refs_11_.refs_0_ = bf16[512,256]{1,0:T(8,128)(2,1)S(1)} custom-call(s32[2]{0:T(128)S(1)} %pad_add_fusion.ids, bf16[512,512]{1,0:T(8,128)(2,1)S(1)} %bitcast.11, bf16[512,512]{1,0:T(8,128)(2,1)S(1)} %collective-permute-done.rest_1_.refs_1_.refs_12_, bf16[512,512]{1,0:T(8,128)(2,1)S(1)} %collective-permute-done.7.refs_2_.refs_7_, ...), custom_call_target="tpu_custom_call" | custom-call | tf_op jit(solution)/shard_map/pallas_call | solution.py:188
  67.0 3.6 %shard_map.96.refs_11_.refs_1_ = bf16[512,256]{1,0:T(8,128)(2,1)S(1)} custom-call(s32[2]{0:T(128)S(1)} %pad_add_fusion.ids, bf16[512,512]{1,0:T(8,128)(2,1)S(1)} %bitcast.12, bf16[512,512]{1,0:T(8,128)(2,1)S(1)} %collective-permute-done.rest_1_.refs_1_.refs_12_, bf16[512,512]{1,0:T(8,128)(2,1)S(1)} %collective-permute-done.7.refs_2_.refs_7_, ...), custom_call_target="tpu_custom_call" | custom-call | flops 2097152000 | tf_op jit(solution)/shard_map/pallas_call | solution.py:188
  70.7 3.1 %shard_map.97.rest_0_.refs_2_ = bf16[512,256]{1,0:T(8,128)(2,1)S(1)} custom-call(s32[2]{0:T(128)S(1)} %pad_add_fusion.ids, bf16[512,512]{1,0:T(8,128)(2,1)S(1)} %bitcast.13, bf16[512,512]{1,0:T(8,128)(2,1)S(1)} %collective-permute-done.rest_1_.refs_1_.refs_12_, bf16[512,512]{1,0:T(8,128)(2,1)S(1)} %collective-permute-done.7.refs_2_.refs_7_, ...), custom_call_target="tpu_custom_call" | custom-call | flops 1048576000 | tf_op jit(solution)/shard_map/pallas_call | solution.py:188
  76.0 2.4 %collective-permute-done.15.refs_5_.refs_1_ = bf16[1024,256]{1,0:T(8,128)(2,1)S(1)} collective-permute-done((bf16[1024,256]{1,0:T(8,128)(2,1)S(1)}, bf16[1024,256]{1,0:T(8,128)(2,1)S(1)}, u32[]{:S(2)}, u32[]{:S(2)}) %collective-permute-start.15) | collective-permute-done | bytes 524320 | tf_op jit(solution)/shard_map/ppermute | solution.py:308
  78.3 3.1 %shard_map.99.rest_0_.refs_3_ = bf16[512,256]{1,0:T(8,128)(2,1)S(1)} custom-call(s32[2]{0:T(128)S(1)} %pad_add_fusion.ids, bf16[512,512]{1,0:T(8,128)(2,1)S(1)} %bitcast.14, bf16[512,512]{1,0:T(8,128)(2,1)S(1)} %collective-permute-done.rest_1_.refs_1_.refs_12_, bf16[512,512]{1,0:T(8,128)(2,1)S(1)} %collective-permute-done.7.refs_2_.refs_7_, ...), custom_call_target="tpu_custom_call" | custom-call | flops 2097152000 | tf_op jit(solution)/shard_map/pallas_call | solution.py:188
  85.4 2.0 %collective-permute-start.22 = (bf16[1024,256]{1,0:T(8,128)(2,1)S(1)}, bf16[1024,256]{1,0:T(8,128)(2,1)S(1)}, u32[]{:S(2)}, u32[]{:S(2)}) collective-permute-start(bf16[1024,256]{1,0:T(8,128)(2,1)S(1)} %shard_map.102.refs_6_.refs_4_), channel_id=1, source_target_pairs={{4,0},{0,4},{5,1},{1,5},{6,2},{2,6},{7,3},{3,7},{12,8},{8,12},{13,... | collective-permute-start | bytes 1572872 | tf_op jit(solution)/shard_map/ppermute | solution.py:308
  87.4 2.4 %collective-permute-done.17.refs_5_ = bf16[1024,256]{1,0:T(8,128)(2,1)S(1)} collective-permute-done((bf16[1024,256]{1,0:T(8,128)(2,1)S(1)}, bf16[1024,256]{1,0:T(8,128)(2,1)S(1)}, u32[]{:S(2)}, u32[]{:S(2)}) %collective-permute-start.17) | collective-permute-done | bytes 524320 | tf_op jit(solution)/shard_map/ppermute | solution.py:308
  92.7 3.8 %collective-permute-done.20.far = bf16[1024,256]{1,0:T(8,128)(2,1)S(1)} collective-permute-done((bf16[1024,256]{1,0:T(8,128)(2,1)S(1)}, bf16[1024,256]{1,0:T(8,128)(2,1)S(1)}, u32[]{:S(2)}, u32[]{:S(2)}) %collective-permute-start.20) | collective-permute-done | bytes 524320 | tf_op jit(solution)/shard_map/ppermute | solution.py:308
  97.6 2.0 %collective-permute-start.24 = (bf16[1024,256]{1,0:T(8,128)(2,1)S(1)}, bf16[1024,256]{1,0:T(8,128)(2,1)S(1)}, u32[]{:S(2)}, u32[]{:S(2)}) collective-permute-start(bf16[1024,256]{1,0:T(8,128)(2,1)S(1)} %shard_map.104.refs_0_.refs_4_), channel_id=1, source_target_pairs={{4,0},{0,4},{5,1},{1,5},{6,2},{2,6},{7,3},{3,7},{12,8},{8,12},{13,... | collective-permute-start | bytes 1572872 | tf_op jit(solution)/shard_map/ppermute | solution.py:308
  100.3 2.9 %collective-permute-start.21 = (bf16[512,128]{1,0:T(8,128)(2,1)S(1)}, bf16[512,128]{1,0:T(8,128)(2,1)S(1)}, u32[]{:S(2)}, u32[]{:S(2)}) collective-permute-start(bf16[512,128]{1,0:T(8,128)(2,1)S(1)} %get-tuple-element.30), channel_id=1, source_target_pairs={{2,0},{3,1},{0,2},{1,3},{6,4},{7,5},{4,6},{5,7},{10,8},{11,9},{8,1... | collective-permute-start | bytes 393224 | tf_op jit(solution)/shard_map/ppermute | solution.py:308
  108.3 1.7 %collective-permute-start.29 = (bf16[1024,256]{1,0:T(8,128)(2,1)S(1)}, bf16[1024,256]{1,0:T(8,128)(2,1)S(1)}, u32[]{:S(2)}, u32[]{:S(2)}) collective-permute-start(bf16[1024,256]{1,0:T(8,128)(2,1)S(1)} %shard_map.107.refs_6_.refs_4_), channel_id=1, source_target_pairs={{4,0},{0,4},{5,1},{1,5},{6,2},{2,6},{7,3},{3,7},{12,8},{8,12},{13,... | collective-permute-start | bytes 1572872 | tf_op jit(solution)/shard_map/ppermute | solution.py:308
  109.9 2.6 %collective-permute-done.24.refs_5_ = bf16[1024,256]{1,0:T(8,128)(2,1)S(1)} collective-permute-done((bf16[1024,256]{1,0:T(8,128)(2,1)S(1)}, bf16[1024,256]{1,0:T(8,128)(2,1)S(1)}, u32[]{:S(2)}, u32[]{:S(2)}) %collective-permute-start.24) | collective-permute-done | bytes 524320 | tf_op jit(solution)/shard_map/ppermute | solution.py:308
  113.9 1.9 %collective-permute-start.27 = (bf16[2,512,128]{2,1,0:T(8,128)(2,1)S(1)}, bf16[2,512,128]{2,1,0:T(8,128)(2,1)S(1)}, u32[]{:S(2)}, u32[]{:S(2)}) collective-permute-start(bf16[2,512,128]{2,1,0:T(8,128)(2,1)S(1)} %get-tuple-element.36), channel_id=1, source_target_pairs={{1,0},{0,1},{3,2},{2,3},{5,4},{4,5},{7,6},{6,7},{9,8},{8,9},{11,10... | collective-permute-start | bytes 786440 | tf_op jit(solution)/shard_map/ppermute | solution.py:308
  116.3 2.5 %collective-permute-start.26 = (bf16[512,128]{1,0:T(8,128)(2,1)S(1)}, bf16[512,128]{1,0:T(8,128)(2,1)S(1)}, u32[]{:S(2)}, u32[]{:S(2)}) collective-permute-start(bf16[512,128]{1,0:T(8,128)(2,1)S(1)} %get-tuple-element.35), channel_id=1, source_target_pairs={{2,0},{3,1},{0,2},{1,3},{6,4},{7,5},{4,6},{5,7},{10,8},{11,9},{8,1... | collective-permute-start | bytes 393224 | tf_op jit(solution)/shard_map/ppermute | solution.py:308
  118.8 4.7 %collective-permute-done.27.got = bf16[2,512,128]{2,1,0:T(8,128)(2,1)S(1)} collective-permute-done((bf16[2,512,128]{2,1,0:T(8,128)(2,1)S(1)}, bf16[2,512,128]{2,1,0:T(8,128)(2,1)S(1)}, u32[]{:S(2)}, u32[]{:S(2)}) %collective-permute-start.27) | collective-permute-done | bytes 262176 | tf_op jit(solution)/shard_map/ppermute | solution.py:308
  124.2 1.7 %collective-permute-start.28 = (bf16[512,128]{1,0:T(8,128)(2,1)S(1)}, bf16[512,128]{1,0:T(8,128)(2,1)S(1)}, u32[]{:S(2)}, u32[]{:S(2)}) collective-permute-start(bf16[512,128]{1,0:T(8,128)(2,1)S(1)} %get-tuple-element.38), channel_id=1, source_target_pairs={{2,0},{3,1},{0,2},{1,3},{6,4},{7,5},{4,6},{5,7},{10,8},{11,9},{8,1... | collective-permute-start | bytes 393224 | tf_op jit(solution)/shard_map/ppermute | solution.py:308
  129.8 2.6 %collective-permute-start.32 = (bf16[512,128]{1,0:T(8,128)(2,1)S(1)}, bf16[512,128]{1,0:T(8,128)(2,1)S(1)}, u32[]{:S(2)}, u32[]{:S(2)}) collective-permute-start(bf16[512,128]{1,0:T(8,128)(2,1)S(1)} %get-tuple-element.42), channel_id=1, source_target_pairs={{1,0},{2,1},{3,2},{0,3},{5,4},{6,5},{7,6},{4,7},{9,8},{10,9},{11,1... | collective-permute-start | bytes 393224 | tf_op jit(solution)/shard_map/ppermute | solution.py:308
  132.4 6.2 %collective-permute-done.28.refs_5_ = bf16[512,128]{1,0:T(8,128)(2,1)S(1)} collective-permute-done((bf16[512,128]{1,0:T(8,128)(2,1)S(1)}, bf16[512,128]{1,0:T(8,128)(2,1)S(1)}, u32[]{:S(2)}, u32[]{:S(2)}) %collective-permute-start.28) | collective-permute-done | bytes 131104 | tf_op jit(solution)/shard_map/ppermute | solution.py:308
  138.5 2.5 %collective-permute-done.30.refs_7_ = bf16[512,128]{1,0:T(8,128)(2,1)S(1)} collective-permute-done((bf16[512,128]{1,0:T(8,128)(2,1)S(1)}, bf16[512,128]{1,0:T(8,128)(2,1)S(1)}, u32[]{:S(2)}, u32[]{:S(2)}) %collective-permute-start.30) | collective-permute-done | bytes 131104 | tf_op jit(solution)/shard_map/ppermute | solution.py:308
  (83 shorter events, 46.1 us)
Async XLA Ops:
  0.5 10.9 %collective-permute-start.4 = (bf16[1024,256]{1,0:T(8,128)(2,1)}, bf16[1024,256]{1,0:T(8,128)(2,1)S(1)}, u32[]{:S(2)}, u32[]{:S(2)}) collective-permute-start(bf16[1024,256]{1,0:T(8,128)(2,1)} %bitcast.26), channel_id=1, source_target_pairs={{8,0},{0,8},{24,16},{16,24},{9,1},{1,9},{25,17},{17,25},{10,2},{2,... | collective-permute-start | bytes 1572872 | tf_op jit(solution)/shard_map/ppermute | solution.py:308
  0.5 15.2 %collective-permute-start.5 = (bf16[1024,256]{1,0:T(8,128)(2,1)}, bf16[1024,256]{1,0:T(8,128)(2,1)}, u32[]{:S(2)}, u32[]{:S(2)}) collective-permute-start(bf16[1024,256]{1,0:T(8,128)(2,1)} %bitcast.27), channel_id=1, source_target_pairs={{24,0},{16,8},{8,16},{0,24},{25,1},{17,9},{9,17},{1,25},{26,2},{18... | collective-permute-start | bytes 1572872 | tf_op jit(solution)/shard_map/ppermute | solution.py:308
  3.1 27.2 %collective-permute-start = (bf16[512,512]{1,0:T(8,128)(2,1)}, bf16[512,512]{1,0:T(8,128)(2,1)S(1)}, u32[]{:S(2)}, u32[]{:S(2)}) collective-permute-start(bf16[512,512]{1,0:T(8,128)(2,1)} %bitcast.7), channel_id=1, source_target_pairs={{3,0},{0,1},{1,2},{2,3},{7,4},{4,5},{5,6},{6,7},{11,8},{8,9},{9,10... | collective-permute-start | bytes 1572872 | tf_op jit(solution)/shard_map/ppermute | solution.py:308
  4.6 15.3 %collective-permute-start.1 = (bf16[1024,1024]{1,0:T(8,128)(2,1)}, bf16[1024,1024]{1,0:T(8,128)(2,1)}, u32[]{:S(2)}, u32[]{:S(2)}) collective-permute-start(bf16[1024,1024]{1,0:T(8,128)(2,1)} %bitcast.16), channel_id=1, source_target_pairs={{8,0},{0,8},{24,16},{16,24},{9,1},{1,9},{25,17},{17,25},{10,2},{2,... | collective-permute-start | bytes 6291464 | tf_op jit(solution)/shard_map/ppermute | solution.py:308
  5.6 26.2 %collective-permute-start.6 = (bf16[512,512]{1,0:T(8,128)(2,1)}, bf16[512,512]{1,0:T(8,128)(2,1)S(1)}, u32[]{:S(2)}, u32[]{:S(2)}) collective-permute-start(bf16[512,512]{1,0:T(8,128)(2,1)} %bitcast.8), channel_id=1, source_target_pairs={{1,0},{2,1},{3,2},{0,3},{5,4},{6,5},{7,6},{4,7},{9,8},{10,9},{11,1... | collective-permute-start | bytes 1572872 | tf_op jit(solution)/shard_map/ppermute | solution.py:308
  11.4 15.4 %collective-permute-start.3 = (bf16[1024,256]{1,0:T(8,128)(2,1)S(1)}, bf16[1024,256]{1,0:T(8,128)(2,1)S(1)}, u32[]{:S(2)}, u32[]{:S(2)}) collective-permute-start(bf16[1024,256]{1,0:T(8,128)(2,1)S(1)} %shard_map.82.rest_0_), channel_id=1, source_target_pairs={{24,0},{16,8},{8,16},{0,24},{25,1},{17,9},{9,17},{1,25},{26,2},{18... | collective-permute-start | bytes 1572872 | tf_op jit(solution)/shard_map/ppermute | solution.py:308
  17.8 23.8 %collective-permute-start.9 = (bf16[1024,256]{1,0:T(8,128)(2,1)S(1)}, bf16[1024,256]{1,0:T(8,128)(2,1)S(1)}, u32[]{:S(2)}, u32[]{:S(2)}) collective-permute-start(bf16[1024,256]{1,0:T(8,128)(2,1)S(1)} %shard_map.84.rest_0_.refs_4_), channel_id=1, source_target_pairs={{4,0},{0,4},{5,1},{1,5},{6,2},{2,6},{7,3},{3,7},{12,8},{8,12},{13,... | collective-permute-start | bytes 1572872 | tf_op jit(solution)/shard_map/ppermute | solution.py:308
  20.0 18.1 %collective-permute-start.11 = (bf16[1024,256]{1,0:T(8,128)(2,1)S(1)}, bf16[1024,256]{1,0:T(8,128)(2,1)S(1)}, u32[]{:S(2)}, u32[]{:S(2)}) collective-permute-start(bf16[1024,256]{1,0:T(8,128)(2,1)S(1)} %shard_map.83.rest_0_), channel_id=1, source_target_pairs={{24,0},{16,8},{8,16},{0,24},{25,1},{17,9},{9,17},{1,25},{26,2},{18... | collective-permute-start | bytes 1572872 | tf_op jit(solution)/shard_map/ppermute | solution.py:308
  26.8 22.6 %collective-permute-start.10 = (bf16[1024,256]{1,0:T(8,128)(2,1)}, bf16[1024,256]{1,0:T(8,128)(2,1)}, u32[]{:S(2)}, u32[]{:S(2)}) collective-permute-start(bf16[1024,256]{1,0:T(8,128)(2,1)} %shard_map.85.rest_0_), channel_id=1, source_target_pairs={{24,0},{16,8},{8,16},{0,24},{25,1},{17,9},{9,17},{1,25},{26,2},{18... | collective-permute-start | bytes 1572872 | tf_op jit(solution)/shard_map/ppermute | solution.py:308
  30.2 21.4 %collective-permute-start.8 = (bf16[1024,256]{1,0:T(8,128)(2,1)S(1)}, bf16[1024,256]{1,0:T(8,128)(2,1)S(1)}, u32[]{:S(2)}, u32[]{:S(2)}) collective-permute-start(bf16[1024,256]{1,0:T(8,128)(2,1)S(1)} %shard_map.86.rest_0_.refs_4_), channel_id=1, source_target_pairs={{4,0},{0,4},{5,1},{1,5},{6,2},{2,6},{7,3},{3,7},{12,8},{8,12},{13,... | collective-permute-start | bytes 1572872 | tf_op jit(solution)/shard_map/ppermute | solution.py:308
  31.9 25.8 %collective-permute-start.7 = (bf16[512,512]{1,0:T(8,128)(2,1)S(1)}, bf16[512,512]{1,0:T(8,128)(2,1)S(1)}, u32[]{:S(2)}, u32[]{:S(2)}) collective-permute-start(bf16[512,512]{1,0:T(8,128)(2,1)S(1)} %shard_map.87.rest_0_), channel_id=1, source_target_pairs={{2,0},{3,1},{0,2},{1,3},{6,4},{7,5},{4,6},{5,7},{10,8},{11,9},{8,1... | collective-permute-start | bytes 1572872 | tf_op jit(solution)/shard_map/ppermute | solution.py:308
  38.1 23.5 %collective-permute-start.12 = (bf16[1024,256]{1,0:T(8,128)(2,1)S(1)}, bf16[1024,256]{1,0:T(8,128)(2,1)S(1)}, u32[]{:S(2)}, u32[]{:S(2)}) collective-permute-start(bf16[1024,256]{1,0:T(8,128)(2,1)S(1)} %shard_map.88.rest_0_), channel_id=1, source_target_pairs={{24,0},{16,8},{8,16},{0,24},{25,1},{17,9},{9,17},{1,25},{26,2},{18... | collective-permute-start | bytes 1572872 | tf_op jit(solution)/shard_map/ppermute | solution.py:308
  41.6 25.5 %collective-permute-start.13 = (bf16[1024,256]{1,0:T(8,128)(2,1)S(1)}, bf16[1024,256]{1,0:T(8,128)(2,1)}, u32[]{:S(2)}, u32[]{:S(2)}) collective-permute-start(bf16[1024,256]{1,0:T(8,128)(2,1)S(1)} %shard_map.89.rest_0_.refs_4_), channel_id=1, source_target_pairs={{4,0},{0,4},{5,1},{1,5},{6,2},{2,6},{7,3},{3,7},{12,8},{8,12},{13,... | collective-permute-start | bytes 1572872 | tf_op jit(solution)/shard_map/ppermute | solution.py:308
  49.4 24.4 %collective-permute-start.16 = (bf16[1024,256]{1,0:T(8,128)(2,1)S(1)}, bf16[1024,256]{1,0:T(8,128)(2,1)S(1)}, u32[]{:S(2)}, u32[]{:S(2)}) collective-permute-start(bf16[1024,256]{1,0:T(8,128)(2,1)S(1)} %shard_map.90.rest_0_), channel_id=1, source_target_pairs={{24,0},{16,8},{8,16},{0,24},{25,1},{17,9},{9,17},{1,25},{26,2},{18... | collective-permute-start | bytes 1572872 | tf_op jit(solution)/shard_map/ppermute | solution.py:308
  52.9 17.7 %collective-permute-start.14 = (bf16[1024,256]{1,0:T(8,128)(2,1)S(1)}, bf16[1024,256]{1,0:T(8,128)(2,1)S(1)}, u32[]{:S(2)}, u32[]{:S(2)}) collective-permute-start(bf16[1024,256]{1,0:T(8,128)(2,1)S(1)} %shard_map.91.refs_8_.refs_4_), channel_id=1, source_target_pairs={{4,0},{0,4},{5,1},{1,5},{6,2},{2,6},{7,3},{3,7},{12,8},{8,12},{13,... | collective-permute-start | bytes 1572872 | tf_op jit(solution)/shard_map/ppermute | solution.py:308
  61.5 22.6 %collective-permute-start.18 = (bf16[1024,256]{1,0:T(8,128)(2,1)S(1)}, bf16[1024,256]{1,0:T(8,128)(2,1)S(1)}, u32[]{:S(2)}, u32[]{:S(2)}) collective-permute-start(bf16[1024,256]{1,0:T(8,128)(2,1)S(1)} %shard_map.93.rest_0_), channel_id=1, source_target_pairs={{24,0},{16,8},{8,16},{0,24},{25,1},{17,9},{9,17},{1,25},{26,2},{18... | collective-permute-start | bytes 1572872 | tf_op jit(solution)/shard_map/ppermute | solution.py:308
  62.8 15.5 %collective-permute-start.15 = (bf16[1024,256]{1,0:T(8,128)(2,1)S(1)}, bf16[1024,256]{1,0:T(8,128)(2,1)S(1)}, u32[]{:S(2)}, u32[]{:S(2)}) collective-permute-start(bf16[1024,256]{1,0:T(8,128)(2,1)S(1)} %shard_map.94.refs_11_.refs_4_), channel_id=1, source_target_pairs={{4,0},{0,4},{5,1},{1,5},{6,2},{2,6},{7,3},{3,7},{12,8},{8,12},{13,... | collective-permute-start | bytes 1572872 | tf_op jit(solution)/shard_map/ppermute | solution.py:308
  74.9 14.8 %collective-permute-start.17 = (bf16[1024,256]{1,0:T(8,128)(2,1)S(1)}, bf16[1024,256]{1,0:T(8,128)(2,1)S(1)}, u32[]{:S(2)}, u32[]{:S(2)}) collective-permute-start(bf16[1024,256]{1,0:T(8,128)(2,1)S(1)} %shard_map.98.refs_11_.refs_4_), channel_id=1, source_target_pairs={{4,0},{0,4},{5,1},{1,5},{6,2},{2,6},{7,3},{3,7},{12,8},{8,12},{13,... | collective-permute-start | bytes 1572872 | tf_op jit(solution)/shard_map/ppermute | solution.py:308
  82.3 14.2 %collective-permute-start.20 = (bf16[1024,256]{1,0:T(8,128)(2,1)S(1)}, bf16[1024,256]{1,0:T(8,128)(2,1)S(1)}, u32[]{:S(2)}, u32[]{:S(2)}) collective-permute-start(bf16[1024,256]{1,0:T(8,128)(2,1)S(1)} %shard_map.101.rest_0_), channel_id=1, source_target_pairs={{24,0},{16,8},{8,16},{0,24},{25,1},{17,9},{9,17},{1,25},{26,2},{18... | collective-permute-start | bytes 1572872 | tf_op jit(solution)/shard_map/ppermute | solution.py:308
  82.6 24.5 %collective-permute-start.25 = (bf16[1024,256]{1,0:T(8,128)(2,1)S(1)}, bf16[1024,256]{1,0:T(8,128)(2,1)S(1)}, u32[]{:S(2)}, u32[]{:S(2)}) collective-permute-start(bf16[1024,256]{1,0:T(8,128)(2,1)S(1)} %shard_map.100.rest_0_), channel_id=1, source_target_pairs={{24,0},{16,8},{8,16},{0,24},{25,1},{17,9},{9,17},{1,25},{26,2},{18... | collective-permute-start | bytes 1572872 | tf_op jit(solution)/shard_map/ppermute | solution.py:308
  85.4 17.8 %collective-permute-start.22 = (bf16[1024,256]{1,0:T(8,128)(2,1)S(1)}, bf16[1024,256]{1,0:T(8,128)(2,1)S(1)}, u32[]{:S(2)}, u32[]{:S(2)}) collective-permute-start(bf16[1024,256]{1,0:T(8,128)(2,1)S(1)} %shard_map.102.refs_6_.refs_4_), channel_id=1, source_target_pairs={{4,0},{0,4},{5,1},{1,5},{6,2},{2,6},{7,3},{3,7},{12,8},{8,12},{13,... | collective-permute-start | bytes 1572872 | tf_op jit(solution)/shard_map/ppermute | solution.py:308
  91.1 8.6 %collective-permute-start.19 = (bf16[2,512,128]{2,1,0:T(8,128)(2,1)S(1)}, bf16[2,512,128]{2,1,0:T(8,128)(2,1)S(1)}, u32[]{:S(2)}, u32[]{:S(2)}) collective-permute-start(bf16[2,512,128]{2,1,0:T(8,128)(2,1)S(1)} %get-tuple-element.28), channel_id=1, source_target_pairs={{1,0},{0,1},{3,2},{2,3},{5,4},{4,5},{7,6},{6,7},{9,8},{8,9},{11,10... | collective-permute-start | bytes 786440 | tf_op jit(solution)/shard_map/ppermute | solution.py:308
  97.6 14.9 %collective-permute-start.24 = (bf16[1024,256]{1,0:T(8,128)(2,1)S(1)}, bf16[1024,256]{1,0:T(8,128)(2,1)S(1)}, u32[]{:S(2)}, u32[]{:S(2)}) collective-permute-start(bf16[1024,256]{1,0:T(8,128)(2,1)S(1)} %shard_map.104.refs_0_.refs_4_), channel_id=1, source_target_pairs={{4,0},{0,4},{5,1},{1,5},{6,2},{2,6},{7,3},{3,7},{12,8},{8,12},{13,... | collective-permute-start | bytes 1572872 | tf_op jit(solution)/shard_map/ppermute | solution.py:308
  100.3 9.7 %collective-permute-start.21 = (bf16[512,128]{1,0:T(8,128)(2,1)S(1)}, bf16[512,128]{1,0:T(8,128)(2,1)S(1)}, u32[]{:S(2)}, u32[]{:S(2)}) collective-permute-start(bf16[512,128]{1,0:T(8,128)(2,1)S(1)} %get-tuple-element.30), channel_id=1, source_target_pairs={{2,0},{3,1},{0,2},{1,3},{6,4},{7,5},{4,6},{5,7},{10,8},{11,9},{8,1... | collective-permute-start | bytes 393224 | tf_op jit(solution)/shard_map/ppermute | solution.py:308
  104.5 11.2 %collective-permute-start.23 = (bf16[2,512,128]{2,1,0:T(8,128)(2,1)S(1)}, bf16[2,512,128]{2,1,0:T(8,128)(2,1)S(1)}, u32[]{:S(2)}, u32[]{:S(2)}) collective-permute-start(bf16[2,512,128]{2,1,0:T(8,128)(2,1)S(1)} %get-tuple-element.32), channel_id=1, source_target_pairs={{1,0},{0,1},{3,2},{2,3},{5,4},{4,5},{7,6},{6,7},{9,8},{8,9},{11,10... | collective-permute-start | bytes 786440 | tf_op jit(solution)/shard_map/ppermute | solution.py:308
  108.3 17.6 %collective-permute-start.29 = (bf16[1024,256]{1,0:T(8,128)(2,1)S(1)}, bf16[1024,256]{1,0:T(8,128)(2,1)S(1)}, u32[]{:S(2)}, u32[]{:S(2)}) collective-permute-start(bf16[1024,256]{1,0:T(8,128)(2,1)S(1)} %shard_map.107.refs_6_.refs_4_), channel_id=1, source_target_pairs={{4,0},{0,4},{5,1},{1,5},{6,2},{2,6},{7,3},{3,7},{12,8},{8,12},{13,... | collective-permute-start | bytes 1572872 | tf_op jit(solution)/shard_map/ppermute | solution.py:308
  113.9 9.7 %collective-permute-start.27 = (bf16[2,512,128]{2,1,0:T(8,128)(2,1)S(1)}, bf16[2,512,128]{2,1,0:T(8,128)(2,1)S(1)}, u32[]{:S(2)}, u32[]{:S(2)}) collective-permute-start(bf16[2,512,128]{2,1,0:T(8,128)(2,1)S(1)} %get-tuple-element.36), channel_id=1, source_target_pairs={{1,0},{0,1},{3,2},{2,3},{5,4},{4,5},{7,6},{6,7},{9,8},{8,9},{11,10... | collective-permute-start | bytes 786440 | tf_op jit(solution)/shard_map/ppermute | solution.py:308
  116.3 16.0 %collective-permute-start.26 = (bf16[512,128]{1,0:T(8,128)(2,1)S(1)}, bf16[512,128]{1,0:T(8,128)(2,1)S(1)}, u32[]{:S(2)}, u32[]{:S(2)}) collective-permute-start(bf16[512,128]{1,0:T(8,128)(2,1)S(1)} %get-tuple-element.35), channel_id=1, source_target_pairs={{2,0},{3,1},{0,2},{1,3},{6,4},{7,5},{4,6},{5,7},{10,8},{11,9},{8,1... | collective-permute-start | bytes 393224 | tf_op jit(solution)/shard_map/ppermute | solution.py:308
  124.2 14.4 %collective-permute-start.28 = (bf16[512,128]{1,0:T(8,128)(2,1)S(1)}, bf16[512,128]{1,0:T(8,128)(2,1)S(1)}, u32[]{:S(2)}, u32[]{:S(2)}) collective-permute-start(bf16[512,128]{1,0:T(8,128)(2,1)S(1)} %get-tuple-element.38), channel_id=1, source_target_pairs={{2,0},{3,1},{0,2},{1,3},{6,4},{7,5},{4,6},{5,7},{10,8},{11,9},{8,1... | collective-permute-start | bytes 393224 | tf_op jit(solution)/shard_map/ppermute | solution.py:308
  127.2 13.8 %collective-permute-start.30 = (bf16[512,128]{1,0:T(8,128)(2,1)S(1)}, bf16[512,128]{1,0:T(8,128)(2,1)S(1)}, u32[]{:S(2)}, u32[]{:S(2)}) collective-permute-start(bf16[512,128]{1,0:T(8,128)(2,1)S(1)} %get-tuple-element.40), channel_id=1, source_target_pairs={{2,0},{3,1},{0,2},{1,3},{6,4},{7,5},{4,6},{5,7},{10,8},{11,9},{8,1... | collective-permute-start | bytes 393224 | tf_op jit(solution)/shard_map/ppermute | solution.py:308
  128.5 12.5 %collective-permute-start.31 = (bf16[512,128]{1,0:T(8,128)(2,1)S(1)}, bf16[512,128]{1,0:T(8,128)(2,1)S(1)}, u32[]{:S(2)}, u32[]{:S(2)}) collective-permute-start(bf16[512,128]{1,0:T(8,128)(2,1)S(1)} %get-tuple-element.41), channel_id=1, source_target_pairs={{3,0},{0,1},{1,2},{2,3},{7,4},{4,5},{5,6},{6,7},{11,8},{8,9},{9,10... | collective-permute-start | bytes 393224 | tf_op jit(solution)/shard_map/ppermute | solution.py:308
  129.8 11.2 %collective-permute-start.32 = (bf16[512,128]{1,0:T(8,128)(2,1)S(1)}, bf16[512,128]{1,0:T(8,128)(2,1)S(1)}, u32[]{:S(2)}, u32[]{:S(2)}) collective-permute-start(bf16[512,128]{1,0:T(8,128)(2,1)S(1)} %get-tuple-element.42), channel_id=1, source_target_pairs={{1,0},{2,1},{3,2},{0,3},{5,4},{6,5},{7,6},{4,7},{9,8},{10,9},{11,1... | collective-permute-start | bytes 393224 | tf_op jit(solution)/shard_map/ppermute | solution.py:308
  (9 other events, 71.5 us)
